TPU v7x, 512 devices: a whole 4x8x8 slice. The times are simulated.
512 devices in a mesh: seq: 64 (over y, z), head: 8 (over x, core).
Axes of the slice: x: 4, y: 8, z: 8, core: 2. Of those that a mesh axis runs over, the one named last changes fastest.
Arguments:
- queries: bfloat16 [32768, 1024], P('seq', 'head'), may hold values from -6 to 6
- key_rows: bfloat16 [32768, 1024], P('seq', 'head'), may hold values from -6 to 6
- value_rows: bfloat16 [32768, 1024], P('seq', 'head'), may hold values from -6 to 6
- query_gain: float32 [1024], P('head'), may hold values from 1.2 to 2.4
- key_gain: float32 [1024], P('head'), may hold values from 1.2 to 2.4
- out_grad: bfloat16 [32768, 1024], P('seq', 'head'), may hold values from -6 to 6
Outputs:
- attended: bfloat16 [32768, 1024], P('seq', 'head')
- query_grad: bfloat16 [32768, 1024], P('seq', 'head')
- key_grad: bfloat16 [32768, 1024], P('seq', 'head')
- value_grad: bfloat16 [32768, 1024], P('seq', 'head')
All inputs are finite; a program needn't handle non-finite values.
Results may differ from a plain program's by a relative error of at most 0.007.
The roundings to bfloat16 on the way count: a program that leaves them out, or rounds other values in their place, can miss the bound.
Values may be sent and summed in bfloat16 or wider, within the bound.
No kernel may reach another device: no remote copies, remote signals or barrier semaphores. Data moves between devices by JAX's collectives and lax.ppermute only.
A program may use at most 64 MiB of HBM per device.

v0:
```python
import math

import jax
import jax.numpy as jnp
from jax import lax
from jax.sharding import PartitionSpec as P

HEADS = 16
DH = 64
NR = 128


EPS = 1e-06


def padded_2(x, sides, width):
    for axis, dim in sides:
        peers, length = (lax.axis_size(axis), x.shape[dim])
        up = [(i, (i + 1) % peers) for i in range(peers - 1)]
        down = [(j, i) for i, j in up]
        last = lax.slice_in_dim(x, length - width, length, axis=dim)
        first = lax.slice_in_dim(x, 0, width, axis=dim)
        before = lax.ppermute(last, axis, up)
        after = lax.ppermute(first, axis, down)
        x = jnp.concatenate([before, x, after], axis=dim)
    return x


def from_partner(value, axis, distance):
    mask = 2**distance
    pairs = [(source, source ^ mask) for source in range(lax.axis_size(axis))]
    return lax.ppermute(value, axis, pairs)


def coarsen(array_in, level_index):
    row_count, feat_width = array_in.shape
    grouped = array_in.astype(jnp.float32).reshape(
        row_count >> level_index, 1 << level_index, feat_width
    )
    return jnp.mean(grouped, axis=1).astype(jnp.bfloat16)


def swap_pairs(blocked):
    shape_in = blocked.shape
    paired = blocked.reshape(shape_in[:-3] + (shape_in[-3] // 2, 2) + shape_in[-2:])
    return jnp.flip(paired, axis=-3).reshape(shape_in)


def spread_rows(coarse_rows, level_index):
    lead = coarse_rows.shape[:-2]
    row_count, feat_width = coarse_rows.shape[-2:]
    wide = jnp.broadcast_to(
        coarse_rows[..., :, None, :], lead + (row_count, 1 << level_index, feat_width)
    )
    return wide.reshape(lead + (row_count << level_index, feat_width)) / float(1 << level_index)


def width_sum(partial_sums):
    return lax.psum(partial_sums, "head")


def split_rows(array_in, sizes):
    cuts = []
    running = 0
    for piece_rows in sizes[:-1]:
        running = running + piece_rows
        cuts.append(running)
    return jnp.split(array_in, cuts, axis=1)


def local(queries, key_rows, value_rows, query_gain, key_gain, out_grad):
    row_count, feat_width = queries.shape
    head_size = DH
    head_local = feat_width // head_size
    leaf_size = NR
    leaf_count = row_count // leaf_size
    seq_count = lax.axis_size("seq")
    bit_count = seq_count.bit_length() - 1
    base_level = leaf_count.bit_length() - 1
    seq_index = lax.axis_index("seq")
    full_width = float(HEADS * DH)
    score_scale = 1.0 / math.sqrt(head_size)
    log_two = math.log(2.0)
    query_float = queries.astype(jnp.float32)
    key_float = key_rows.astype(jnp.float32)
    squares = width_sum(
        jnp.stack(
            [jnp.sum(query_float * query_float, axis=1), jnp.sum(key_float * key_float, axis=1)]
        )
    )
    query_rate = lax.rsqrt(squares[0] / full_width + EPS)[:, None]
    key_rate = lax.rsqrt(squares[1] / full_width + EPS)[:, None]
    query_norm = (query_float * query_rate * query_gain).astype(jnp.bfloat16)
    key_norm = (key_float * key_rate * key_gain).astype(jnp.bfloat16)
    key_value = jnp.stack([key_norm, value_rows])
    padded = padded_2(key_value, (("seq", 1),), leaf_size)
    near_sets = jnp.concatenate(
        [
            padded[:, :row_count].reshape(2, leaf_count, leaf_size, feat_width),
            padded[:, leaf_size : row_count + leaf_size].reshape(
                2, leaf_count, leaf_size, feat_width
            ),
            padded[:, 2 * leaf_size :].reshape(2, leaf_count, leaf_size, feat_width),
        ],
        axis=2,
    )
    leaf_ids = jnp.arange(leaf_count)
    left_valid = (leaf_ids > 0) | (seq_index > 0)
    right_valid = (leaf_ids < leaf_count - 1) | (seq_index < seq_count - 1)
    left_bias = jnp.broadcast_to(
        jnp.where(left_valid, 0.0, -jnp.inf).astype(jnp.float32)[:, None], (leaf_count, leaf_size)
    )
    right_bias = jnp.broadcast_to(
        jnp.where(right_valid, 0.0, -jnp.inf).astype(jnp.float32)[:, None], (leaf_count, leaf_size)
    )
    leaf_sets = [near_sets]
    leaf_biases = [left_bias, jnp.zeros((leaf_count, leaf_size), jnp.float32), right_bias]
    level_index = 1
    coarse_pair = jnp.stack([coarsen(key_norm, level_index), coarsen(value_rows, level_index)])
    block_count = (row_count >> level_index) // leaf_size
    sibling_rows = swap_pairs(coarse_pair.reshape(2, block_count, leaf_size, feat_width))
    per_leaf = jnp.broadcast_to(
        sibling_rows[:, :, None], (2, block_count, 1 << level_index, leaf_size, feat_width)
    )
    leaf_sets.append(per_leaf.reshape(2, leaf_count, leaf_size, feat_width))
    leaf_biases.append(jnp.full((leaf_count, leaf_size), level_index * log_two, jnp.float32))
    leaf_keys = jnp.concatenate(leaf_sets, axis=2)
    leaf_bias = jnp.concatenate(leaf_biases, axis=1)
    leaf_width = leaf_keys.shape[2]
    owned = [
        jnp.stack([coarsen(key_norm, base_level + j), coarsen(value_rows, base_level + j)])
        for j in range(bit_count)
    ]
    cross_sets = []
    sizes = [piece.shape[1] for piece in owned]
    total_rows = sum(sizes)
    gathered = lax.all_gather(jnp.concatenate(owned, axis=1), "seq", axis=1, tiled=True)
    gathered = gathered.reshape(2, seq_count, total_rows, feat_width)
    start_row = 0
    for j in range(bit_count):
        section = gathered[:, :, start_row : start_row + sizes[j]]
        first_device = jnp.left_shift(jnp.bitwise_xor(jnp.right_shift(seq_index, j), 1), j)
        chosen = lax.dynamic_slice_in_dim(section, first_device, 1 << j, 1)
        cross_sets.append(chosen.reshape(2, leaf_size, feat_width))
        start_row = start_row + sizes[j]
    cross_pair = jnp.concatenate(cross_sets, axis=1)
    cross_keys = cross_pair[0].reshape(-1, head_local, head_size)
    cross_values = cross_pair[1].reshape(-1, head_local, head_size)
    cross_bias = jnp.concatenate(
        [jnp.full((leaf_size,), (base_level + j) * log_two, jnp.float32) for j in range(bit_count)]
    )
    group_size = min(leaf_count, max(1, 512 // leaf_size))
    group_count = leaf_count // group_size
    query_groups = query_norm.reshape(group_count, group_size, leaf_size, head_local, head_size)
    grad_groups = out_grad.reshape(group_count, group_size, leaf_size, head_local, head_size)
    key_groups = leaf_keys[0].reshape(group_count, group_size, leaf_width, head_local, head_size)
    value_groups = leaf_keys[1].reshape(group_count, group_size, leaf_width, head_local, head_size)
    bias_groups = leaf_bias.reshape(group_count, group_size, leaf_width)

    def attend(carry, inputs):
        cross_key_grad, cross_value_grad = carry
        query_group, grad_group, key_group, value_group, bias_group = inputs
        near_scores = (
            jnp.einsum(
                "gqhe,gkhe->ghqk", query_group, key_group, preferred_element_type=jnp.float32
            )
            * score_scale
            + bias_group[:, None, None, :]
        )
        far_scores = (
            jnp.einsum(
                "gqhe,khe->ghqk", query_group, cross_keys, preferred_element_type=jnp.float32
            )
            * score_scale
            + cross_bias
        )
        top_score = jnp.maximum(
            jnp.max(near_scores, axis=-1, keepdims=True),
            jnp.max(far_scores, axis=-1, keepdims=True),
        )
        near_weights = jnp.exp(near_scores - top_score)
        far_weights = jnp.exp(far_scores - top_score)
        denominator = jnp.sum(near_weights, axis=-1, keepdims=True) + jnp.sum(
            far_weights, axis=-1, keepdims=True
        )
        near_probs = near_weights / denominator
        far_probs = far_weights / denominator
        near_low = near_probs.astype(jnp.bfloat16)
        far_low = far_probs.astype(jnp.bfloat16)
        mixed = jnp.einsum(
            "ghqk,gkhe->gqhe", near_low, value_group, preferred_element_type=jnp.float32
        )
        mixed = mixed + jnp.einsum(
            "ghqk,khe->gqhe", far_low, cross_values, preferred_element_type=jnp.float32
        )
        near_pgrad = jnp.einsum(
            "gqhe,gkhe->ghqk", grad_group, value_group, preferred_element_type=jnp.float32
        )
        far_pgrad = jnp.einsum(
            "gqhe,khe->ghqk", grad_group, cross_values, preferred_element_type=jnp.float32
        )
        delta = jnp.sum(near_probs * near_pgrad, axis=-1, keepdims=True) + jnp.sum(
            far_probs * far_pgrad, axis=-1, keepdims=True
        )
        near_sgrad = (near_probs * (near_pgrad - delta)).astype(jnp.bfloat16)
        far_sgrad = (far_probs * (far_pgrad - delta)).astype(jnp.bfloat16)
        query_part = jnp.einsum(
            "ghqk,gkhe->gqhe", near_sgrad, key_group, preferred_element_type=jnp.float32
        )
        query_part = (
            query_part
            + jnp.einsum(
                "ghqk,khe->gqhe", far_sgrad, cross_keys, preferred_element_type=jnp.float32
            )
        ) * score_scale
        key_part = (
            jnp.einsum(
                "ghqk,gqhe->gkhe", near_sgrad, query_group, preferred_element_type=jnp.float32
            )
            * score_scale
        )
        value_part = jnp.einsum(
            "ghqk,gqhe->gkhe", near_low, grad_group, preferred_element_type=jnp.float32
        )
        cross_key_grad = (
            cross_key_grad
            + jnp.einsum(
                "ghqk,gqhe->khe", far_sgrad, query_group, preferred_element_type=jnp.float32
            )
            * score_scale
        )
        cross_value_grad = cross_value_grad + jnp.einsum(
            "ghqk,gqhe->khe", far_low, grad_group, preferred_element_type=jnp.float32
        )
        return (
            (cross_key_grad, cross_value_grad),
            (mixed.astype(jnp.bfloat16), query_part, key_part, value_part),
        )

    cross_zero = jnp.zeros(cross_keys.shape, jnp.float32)
    final, stacked = lax.scan(
        attend,
        (cross_zero, cross_zero),
        (query_groups, grad_groups, key_groups, value_groups, bias_groups),
    )
    cross_key_grad, cross_value_grad = final
    attended_parts, query_parts, key_parts, value_parts = stacked
    attended = attended_parts.reshape(row_count, feat_width)
    norm_query_grad = query_parts.reshape(row_count, feat_width)
    leaf_grads = jnp.stack(
        [
            key_parts.reshape(leaf_count, leaf_width, feat_width),
            value_parts.reshape(leaf_count, leaf_width, feat_width),
        ]
    )
    near_grads = leaf_grads[:, :, : 3 * leaf_size]
    padded_grad = jnp.zeros((2, row_count + 2 * leaf_size, feat_width), jnp.float32)
    padded_grad = padded_grad.at[:, :row_count].add(
        near_grads[:, :, :leaf_size].reshape(2, row_count, feat_width)
    )
    padded_grad = padded_grad.at[:, leaf_size : row_count + leaf_size].add(
        near_grads[:, :, leaf_size : 2 * leaf_size].reshape(2, row_count, feat_width)
    )
    padded_grad = padded_grad.at[:, 2 * leaf_size :].add(
        near_grads[:, :, 2 * leaf_size :].reshape(2, row_count, feat_width)
    )
    rim_pair = jnp.concatenate(
        [padded_grad[:, :leaf_size], padded_grad[:, row_count + leaf_size :]], axis=1
    )
    returned = padded_2(rim_pair.astype(jnp.bfloat16), (("seq", 1),), leaf_size).astype(
        rim_pair.dtype
    )
    token_grad = padded_grad[:, leaf_size : row_count + leaf_size]
    token_grad = token_grad.at[:, :leaf_size].add(returned[:, :leaf_size])
    token_grad = token_grad.at[:, row_count - leaf_size :].add(returned[:, 3 * leaf_size :])
    for position, level_index in enumerate(range(1, base_level)):
        lower = (3 + position) * leaf_size
        level_part = leaf_grads[:, :, lower : lower + leaf_size]
        block_count = leaf_count >> level_index
        summed = jnp.sum(
            level_part.reshape(2, block_count, 1 << level_index, leaf_size, feat_width), axis=2
        )
        owner_rows = swap_pairs(summed).reshape(2, block_count * leaf_size, feat_width)
        token_grad = token_grad + spread_rows(owner_rows, level_index)
    cross_grad = jnp.stack(
        [cross_key_grad.reshape(-1, feat_width), cross_value_grad.reshape(-1, feat_width)]
    )
    pending = {}
    for j in reversed(range(bit_count)):
        upper_half = jnp.bitwise_and(jnp.right_shift(seq_index, j), 1) == 1
        outgoing = [cross_grad[:, j * leaf_size : (j + 1) * leaf_size]]
        keeping = []
        for i in range(j + 1, bit_count):
            whole_rows = pending[i]
            half_rows = whole_rows.shape[1] // 2
            lower_rows = whole_rows[:, :half_rows]
            upper_rows = whole_rows[:, half_rows:]
            outgoing.append(jnp.where(upper_half, lower_rows, upper_rows))
            keeping.append(jnp.where(upper_half, upper_rows, lower_rows))
        sizes = [piece.shape[1] for piece in outgoing]
        received = from_partner(
            jnp.concatenate(outgoing, axis=1).astype(jnp.bfloat16), "seq", j
        ).astype(jnp.float32)
        pieces = split_rows(received, sizes)
        pending[j] = pieces[0]
        for position, i in enumerate(range(j + 1, bit_count)):
            pending[i] = keeping[position] + pieces[position + 1]
    for j in range(bit_count):
        token_grad = token_grad + spread_rows(pending[j], base_level + j)
    norm_key_grad = token_grad[0]
    products = width_sum(
        jnp.stack(
            [
                jnp.sum(query_float * query_gain * norm_query_grad, axis=1),
                jnp.sum(key_float * key_gain * norm_key_grad, axis=1),
            ]
        )
    )
    query_inner = (products[0] / full_width)[:, None]
    key_inner = (products[1] / full_width)[:, None]
    query_grad = (
        query_rate * query_gain * norm_query_grad
        - query_float * query_rate * query_rate * query_rate * query_inner
    ).astype(jnp.bfloat16)
    key_grad = (
        key_rate * key_gain * norm_key_grad - key_float * key_rate * key_rate * key_rate * key_inner
    ).astype(jnp.bfloat16)
    return (attended, query_grad, key_grad, token_grad[1].astype(jnp.bfloat16))


def solution(mesh):
    placed = (
        P("seq", "head"),
        P("seq", "head"),
        P("seq", "head"),
        P("head"),
        P("head"),
        P("seq", "head"),
    )
    return jax.shard_map(
        local,
        mesh=mesh,
        in_specs=placed,
        out_specs=(P("seq", "head"), P("seq", "head"), P("seq", "head"), P("seq", "head")),
        check_vma=False,
    )
```

profile of v0, /device:TPU:1, one launch (start us, length us, event | category | flops | bytes accessed | tf_op | source)
XLA Modules:
  0.0 262.1 jit_solution(13717431857849499417)
XLA Ops:
  9.4 18.7 %psum.14 = f32[2,512]{1,0:T(2,128)S(1)} all-reduce(f32[2,512]{1,0:T(2,128)S(1)} %pad_maximum_fusion.15), channel_id=1, replica_groups=mesh['seq'=64,'head'=8] {'head'}, use_global_device_ids=true, to_apply=%region_2.0 | all-reduce | flops 1024 | bytes 8192 | tf_op jit(solution)/shard_map/psum | solution.py:59
  32.9 1.3 collective-permute-start
  37.3 1.9 collective-permute-done.1
  41.5 2.5 fusion.9
  44.0 86.7 %all-gather.2.cloned.1.call-done = bf16[2,16128,128]{2,0,1:T(2,128)(2,1)} async-done(((bf16[2,252,128]{2,0,1:T(2,128)(2,1)}), bf16[2,16128,128]{2,0,1:T(2,128)(2,1)}) %all-gather.2.cloned.1.call-update) | async-done | bytes 8257552 | tf_op jit(solution)/shard_map/all_gather | solution.py:137
  130.7 5.8 %slice.412 = bf16[2,64,128,128]{3,0,2,1:T(2,128)(2,1)S(1)} slice(bf16[2,64,252,128]{3,0,2,1:T(2,128)(2,1)} %bitcast.227), slice={[0:2], [0:64], [0:128], [0:128]} | slice | bytes 8388608 | tf_op jit(solution)/shard_map/slice | solution.py:141
  136.5 3.4 %slice.413 = bf16[2,64,64,128]{3,0,2,1:T(2,128)(2,1)S(1)} slice(bf16[2,64,252,128]{3,0,2,1:T(2,128)(2,1)} %bitcast.228), slice={[0:2], [0:64], [128:192], [0:128]} | slice | bytes 4194304 | tf_op jit(solution)/shard_map/slice | solution.py:141
  139.9 2.1 slice.414
  142.0 1.4 slice.415
  147.8 1.6 bitcast_reduce_fusion
  152.3 1.9 fusion.38
  154.1 2.7 %fusion.6 = (f32[4,2,128]{2,1,0:T(2,128)}, f32[4,2,512,128]{2,3,1,0:T(8,128)}) fusion(f32[4,2,128]{2,1,0:T(2,128)S(1)} %copy.265, f32[4,2,128]{2,1,0:T(2,128)S(1)} %copy.263, f32[4,512]{1,0:T(4,128)S(1)} %maximum_maximum_fusion, f32[4,2,128,512]{3,2,1,0:T(8,128)S(1)} %copy-done, bf16[4,512,2,64]{1,3,2,0:T(8,128)(2,1)S(1)} %bitcast.258, ...), kind=kOutput, calls=%fused_computation.19 | convolution fusion | flops 70253568 | bytes 4870144 | tf_op jit(solution)/shard_map/while/body/eval_jaxpr/gqhe,gkhe->ghqk/dot_general | solution.py:196
  156.9 1.7 copy.266
  158.7 2.3 fusion
  164.3 1.5 convolution_bitcast_fusion.2
  165.8 2.3 fusion.2
  173.3 7.1 %collective-permute-start.4 = (bf16[2,128,128]{2,1,0:T(8,128)(2,1)}, bf16[2,128,128]{2,1,0:T(8,128)(2,1)}, u32[]{:S(2)}, u32[]{:S(2)}) collective-permute-start(bf16[2,128,128]{2,1,0:T(8,128)(2,1)} %get-tuple-element.141), channel_id=1, source_target_pairs={{0,256},{8,264},{16,272},{24,280},{32,288},{40,296},{48,304},{56,3... | collective-permute-start | bytes 196616 | tf_op jit(solution)/shard_map/ppermute | solution.py:32
  184.9 2.2 copy.281
  187.1 2.1 constant_dynamic-update-slice_fusion.19
  189.2 2.1 constant_dynamic-update-slice_fusion.18
  191.3 1.9 collective-permute-start.2
  195.3 2.3 collective-permute-start.5
  199.4 5.1 %collective-permute-done.5 = bf16[2,192,128]{2,1,0:T(8,128)(2,1)S(1)} collective-permute-done((bf16[2,192,128]{2,1,0:T(8,128)(2,1)S(1)}, bf16[2,192,128]{2,1,0:T(8,128)(2,1)S(1)}, u32[]{:S(2)}, u32[]{:S(2)}) %collective-permute-start.5) | collective-permute-done | bytes 98336 | tf_op jit(solution)/shard_map/ppermute | solution.py:32
  204.7 1.9 collective-permute-start.6
  208.0 2.2 collective-permute-done.6
  210.4 5.3 %collective-permute-start.7 = (bf16[2,240,128]{2,1,0:T(8,128)(2,1)S(1)}, bf16[2,240,128]{2,1,0:T(8,128)(2,1)S(1)}, u32[]{:S(2)}, u32[]{:S(2)}) collective-permute-start(bf16[2,240,128]{2,1,0:T(8,128)(2,1)S(1)} %pad_maximum_fusion.7), channel_id=1, source_target_pairs={{0,32},{8,40},{16,48},{24,56},{32,0},{40,8},{48,16},{56,24},{64,96... | collective-permute-start | bytes 368648 | tf_op jit(solution)/shard_map/ppermute | solution.py:32
  215.8 4.2 %collective-permute-done.7 = bf16[2,240,128]{2,1,0:T(8,128)(2,1)S(1)} collective-permute-done((bf16[2,240,128]{2,1,0:T(8,128)(2,1)S(1)}, bf16[2,240,128]{2,1,0:T(8,128)(2,1)S(1)}, u32[]{:S(2)}, u32[]{:S(2)}) %collective-permute-start.7) | collective-permute-done | bytes 122912 | tf_op jit(solution)/shard_map/ppermute | solution.py:32
  220.1 5.3 %collective-permute-start.8 = (bf16[2,248,128]{2,1,0:T(8,128)(2,1)S(1)}, bf16[2,248,128]{2,1,0:T(8,128)(2,1)S(1)}, u32[]{:S(2)}, u32[]{:S(2)}) collective-permute-start(bf16[2,248,128]{2,1,0:T(8,128)(2,1)S(1)} %constant_dynamic-update-slice_fusion.9), channel_id=1, source_target_pairs={{0,16},{8,24},{16,0},{24,8},{32,48},{40,56},{48,32},{56,40},{64,80... | collective-permute-start | bytes 380936 | tf_op jit(solution)/shard_map/ppermute | solution.py:32
  226.4 1.3 collective-permute-done.8
  228.0 1.9 collective-permute-start.9
  229.9 3.7 %collective-permute-done.9 = bf16[2,252,128]{2,1,0:T(8,128)(2,1)S(1)} collective-permute-done((bf16[2,252,128]{2,1,0:T(8,128)(2,1)S(1)}, bf16[2,252,128]{2,1,0:T(8,128)(2,1)S(1)}, u32[]{:S(2)}, u32[]{:S(2)}) %collective-permute-start.9) | collective-permute-done | bytes 129056 | tf_op jit(solution)/shard_map/ppermute | solution.py:32
  235.5 18.0 %psum.15 = f32[2,512]{1,0:T(2,128)S(1)} all-reduce(f32[2,512]{1,0:T(2,128)S(1)} %pad_maximum_fusion.16), channel_id=1, replica_groups=mesh['seq'=64,'head'=8] {'head'}, use_global_device_ids=true, to_apply=%region_26.27 | all-reduce | flops 1024 | bytes 8192 | tf_op jit(solution)/shard_map/psum | solution.py:59
  (265 shorter events, 42.0 us)
Async XLA Ops:
  7.2 24.1 %copy-start.5 = (bf16[512,128]{1,0:T(8,128)(2,1)S(1)}, bf16[512,128]{1,0:T(8,128)(2,1)}, u32[]{:S(2)}) copy-start(bf16[512,128]{1,0:T(8,128)(2,1)} %param.18) | copy-start | bytes 393220
  7.2 123.5 %all-gather.2.cloned.1.call-start = ((), (), s32[]{:S(2)}) async-start(), calls=%async_computation | async-start | bytes 8386560 | tf_op jit(solution)/shard_map/all_gather | solution.py:137
  28.1 7.5 %copy-start.35 = (f32[1,512]{1,0:T(1,128)}, f32[1,512]{1,0:T(1,128)S(1)}, u32[]{:S(2)}) copy-start(f32[1,512]{1,0:T(1,128)S(1)} %get-tuple-element.154) | copy-start | bytes 6148
  29.2 6.4 %copy-start.42 = (f32[128]{0:T(128)S(1)}, f32[128]{0:T(128)}, u32[]{:S(2)}) copy-start(f32[128]{0:T(128)} %param.19) | copy-start | bytes 1540
  31.9 5.1 %copy-start.27 = (bf16[512,128]{1,0:T(8,128)(2,1)S(1)}, bf16[512,128]{1,0:T(8,128)(2,1)}, u32[]{:S(2)}) copy-start(bf16[512,128]{1,0:T(8,128)(2,1)} %param.21) | copy-start | bytes 393220
  32.9 4.4 %collective-permute-start = (bf16[2,128,128]{2,1,0:T(8,128)(2,1)S(1)}, bf16[2,128,128]{2,1,0:T(8,128)(2,1)S(1)}, u32[]{:S(2)}, u32[]{:S(2)}) collective-permute-start(bf16[2,128,128]{2,1,0:T(8,128)(2,1)S(1)} %get-tuple-element.150), channel_id=1, source_target_pairs={{0,8},{8,16},{16,24},{24,32},{32,40},{40,48},{48,56},{56,64},{64,7... | collective-permute-start | bytes 196616 | tf_op jit(solution)/shard_map/ppermute | solution.py:23
  34.2 5.0 %collective-permute-start.1 = (bf16[2,128,128]{2,1,0:T(8,128)(2,1)S(1)}, bf16[2,128,128]{2,1,0:T(8,128)(2,1)S(1)}, u32[]{:S(2)}, u32[]{:S(2)}) collective-permute-start(bf16[2,128,128]{2,1,0:T(8,128)(2,1)S(1)} %get-tuple-element.151), channel_id=1, source_target_pairs={{8,0},{16,8},{24,16},{32,24},{40,32},{48,40},{56,48},{64,56},{72,6... | collective-permute-start | bytes 196616 | tf_op jit(solution)/shard_map/ppermute | solution.py:24
  37.2 121.4 %copy-start.21 = (bf16[4,128,2,64]{1,0,3,2:T(4,128)(2,1)}, bf16[4,128,2,64]{1,0,3,2:T(4,128)(2,1)S(1)}, u32[]{:S(2)}) copy-start(bf16[4,128,2,64]{1,0,3,2:T(4,128)(2,1)S(1)} %squeeze.32) | copy-start | bytes 393220
  169.8 10.6 %copy-start.10 = (f32[4,2,64,512]{3,2,1,0:T(8,128)S(1)}, f32[4,2,64,512]{3,2,1,0:T(8,128)}, u32[]{:S(2)}) copy-start(f32[4,2,64,512]{3,2,1,0:T(8,128)} %convolution_multiply_fusion) | copy-start | bytes 3145732
  171.5 8.9 %copy-start.17 = (f32[4,2,512,64]{2,3,1,0:T(8,128)S(1)}, f32[4,2,512,64]{2,3,1,0:T(8,128)}, u32[]{:S(2)}) copy-start(f32[4,2,512,64]{2,3,1,0:T(8,128)} %fusion.38) | copy-start | bytes 3145732
  173.3 21.0 %collective-permute-start.4 = (bf16[2,128,128]{2,1,0:T(8,128)(2,1)}, bf16[2,128,128]{2,1,0:T(8,128)(2,1)}, u32[]{:S(2)}, u32[]{:S(2)}) collective-permute-start(bf16[2,128,128]{2,1,0:T(8,128)(2,1)} %get-tuple-element.141), channel_id=1, source_target_pairs={{0,256},{8,264},{16,272},{24,280},{32,288},{40,296},{48,304},{56,3... | collective-permute-start | bytes 196616 | tf_op jit(solution)/shard_map/ppermute | solution.py:32
  184.9 8.3 %copy-start.4 = (bf16[4,2,128,768]{2,3,0,1:T(8,128)(2,1)S(1)}, bf16[4,2,128,768]{2,3,0,1:T(8,128)(2,1)}, u32[]{:S(2)}) copy-start(bf16[4,2,128,768]{2,3,0,1:T(8,128)(2,1)} %copy-done.3) | copy-start | bytes 4718596
  184.9 8.3 %copy-start.14 = (bf16[1,768,128]{1,2,0:T(8,128)(2,1)S(1)}, bf16[1,768,128]{1,2,0:T(8,128)(2,1)}, u32[]{:S(2)}) copy-start(bf16[1,768,128]{1,2,0:T(8,128)(2,1)} %copy.260) | copy-start | bytes 589828
  187.1 6.1 %copy-start.15 = (f32[4,128,2,64]{1,3,2,0:T(8,128)S(1)}, f32[4,128,2,64]{1,3,2,0:T(8,128)}, u32[]{:S(2)}) copy-start(f32[4,128,2,64]{1,3,2,0:T(8,128)} %convolution_bitcast_fusion.1) | copy-start | bytes 786436
  189.2 6.1 %copy-start.25 = (bf16[2,128,128]{2,1,0:T(8,128)(2,1)S(1)}, bf16[2,128,128]{2,1,0:T(8,128)(2,1)}, u32[]{:S(2)}) copy-start(bf16[2,128,128]{2,1,0:T(8,128)(2,1)} %get-tuple-element.142) | copy-start | bytes 196612
  189.2 8.4 %copy-start.18 = (bf16[1,768,128]{1,2,0:T(8,128)(2,1)S(1)}, bf16[1,768,128]{1,2,0:T(8,128)(2,1)}, u32[]{:S(2)}) copy-start(bf16[1,768,128]{1,2,0:T(8,128)(2,1)} %copy.266) | copy-start | bytes 589828
  189.2 8.4 %copy-start.23 = (f32[4,128,2,64]{1,3,2,0:T(8,128)S(1)}, f32[4,128,2,64]{1,3,2,0:T(8,128)}, u32[]{:S(2)}) copy-start(f32[4,128,2,64]{1,3,2,0:T(8,128)} %convolution_bitcast_fusion.2) | copy-start | bytes 786436
  191.3 34.2 %collective-permute-start.2 = (bf16[2,128,128]{2,1,0:T(8,128)(2,1)S(1)}, bf16[2,128,128]{2,1,0:T(8,128)(2,1)}, u32[]{:S(2)}, u32[]{:S(2)}) collective-permute-start(bf16[2,128,128]{2,1,0:T(8,128)(2,1)S(1)} %slice.617), channel_id=1, source_target_pairs={{0,8},{8,16},{16,24},{24,32},{32,40},{40,48},{48,56},{56,64},{64,7... | collective-permute-start | bytes 196616 | tf_op jit(solution)/shard_map/ppermute | solution.py:23
  195.3 9.3 %collective-permute-start.5 = (bf16[2,192,128]{2,1,0:T(8,128)(2,1)S(1)}, bf16[2,192,128]{2,1,0:T(8,128)(2,1)S(1)}, u32[]{:S(2)}, u32[]{:S(2)}) collective-permute-start(bf16[2,192,128]{2,1,0:T(8,128)(2,1)S(1)} %pad_maximum_fusion.9), channel_id=1, source_target_pairs={{0,128},{8,136},{16,144},{24,152},{32,160},{40,168},{48,176},{56,1... | collective-permute-start | bytes 294920 | tf_op jit(solution)/shard_map/ppermute | solution.py:32
  197.6 7.1 %copy-start.24 = (bf16[2,128,128]{2,1,0:T(8,128)(2,1)S(1)}, bf16[2,128,128]{2,1,0:T(8,128)(2,1)}, u32[]{:S(2)}) copy-start(bf16[2,128,128]{2,1,0:T(8,128)(2,1)} %get-tuple-element.143) | copy-start | bytes 196612
  198.0 8.8 %copy-start.16 = (f32[4,128,2,64]{1,3,2,0:T(8,128)S(1)}, f32[4,128,2,64]{1,3,2,0:T(8,128)}, u32[]{:S(2)}) copy-start(f32[4,128,2,64]{1,3,2,0:T(8,128)} %fusion.29) | copy-start | bytes 786436
  198.1 27.4 %collective-permute-start.3 = (bf16[2,128,128]{2,1,0:T(8,128)(2,1)S(1)}, bf16[2,128,128]{2,1,0:T(8,128)(2,1)S(1)}, u32[]{:S(2)}, u32[]{:S(2)}) collective-permute-start(bf16[2,128,128]{2,1,0:T(8,128)(2,1)S(1)} %slice.616), channel_id=1, source_target_pairs={{8,0},{16,8},{24,16},{32,24},{40,32},{48,40},{56,48},{64,56},{72,6... | collective-permute-start | bytes 196616 | tf_op jit(solution)/shard_map/ppermute | solution.py:24
  199.4 10.9 %copy-start.26 = (bf16[2,128,128]{2,1,0:T(8,128)(2,1)S(1)}, bf16[2,128,128]{2,1,0:T(8,128)(2,1)}, u32[]{:S(2)}) copy-start(bf16[2,128,128]{2,1,0:T(8,128)(2,1)} %get-tuple-element.140) | copy-start | bytes 196612
  204.6 11.1 %copy-start.43 = (f32[128]{0:T(128)S(1)}, f32[128]{0:T(128)}, u32[]{:S(2)}) copy-start(f32[128]{0:T(128)} %param.19) | copy-start | bytes 1540
  204.7 5.5 %collective-permute-start.6 = (bf16[2,224,128]{2,1,0:T(8,128)(2,1)S(1)}, bf16[2,224,128]{2,1,0:T(8,128)(2,1)S(1)}, u32[]{:S(2)}, u32[]{:S(2)}) collective-permute-start(bf16[2,224,128]{2,1,0:T(8,128)(2,1)S(1)} %pad_maximum_fusion.8), channel_id=1, source_target_pairs={{0,64},{8,72},{16,80},{24,88},{32,96},{40,104},{48,112},{56,120},{... | collective-permute-start | bytes 344072 | tf_op jit(solution)/shard_map/ppermute | solution.py:32
  206.6 13.4 %copy-start.33 = (bf16[2,248,128]{2,1,0:T(8,128)(2,1)S(1)}, bf16[2,248,128]{2,1,0:T(8,128)(2,1)}, u32[]{:S(2)}) copy-start(bf16[2,248,128]{2,1,0:T(8,128)(2,1)} %get-tuple-element.144) | copy-start | bytes 380932
  207.2 20.7 %copy-start.34 = (bf16[2,252,128]{2,1,0:T(8,128)(2,1)S(1)}, bf16[2,252,128]{2,1,0:T(8,128)(2,1)}, u32[]{:S(2)}) copy-start(bf16[2,252,128]{2,1,0:T(8,128)(2,1)} %get-tuple-element.145) | copy-start | bytes 387076
  210.4 9.6 %collective-permute-start.7 = (bf16[2,240,128]{2,1,0:T(8,128)(2,1)S(1)}, bf16[2,240,128]{2,1,0:T(8,128)(2,1)S(1)}, u32[]{:S(2)}, u32[]{:S(2)}) collective-permute-start(bf16[2,240,128]{2,1,0:T(8,128)(2,1)S(1)} %pad_maximum_fusion.7), channel_id=1, source_target_pairs={{0,32},{8,40},{16,48},{24,56},{32,0},{40,8},{48,16},{56,24},{64,96... | collective-permute-start | bytes 368648 | tf_op jit(solution)/shard_map/ppermute | solution.py:32
  220.1 7.6 %collective-permute-start.8 = (bf16[2,248,128]{2,1,0:T(8,128)(2,1)S(1)}, bf16[2,248,128]{2,1,0:T(8,128)(2,1)S(1)}, u32[]{:S(2)}, u32[]{:S(2)}) collective-permute-start(bf16[2,248,128]{2,1,0:T(8,128)(2,1)S(1)} %constant_dynamic-update-slice_fusion.9), channel_id=1, source_target_pairs={{0,16},{8,24},{16,0},{24,8},{32,48},{40,56},{48,32},{56,40},{64,80... | collective-permute-start | bytes 380936 | tf_op jit(solution)/shard_map/ppermute | solution.py:32
  228.0 5.7 %collective-permute-start.9 = (bf16[2,252,128]{2,1,0:T(8,128)(2,1)S(1)}, bf16[2,252,128]{2,1,0:T(8,128)(2,1)S(1)}, u32[]{:S(2)}, u32[]{:S(2)}) collective-permute-start(bf16[2,252,128]{2,1,0:T(8,128)(2,1)S(1)} %constant_dynamic-update-slice_fusion.13), channel_id=1, source_target_pairs={{0,8},{8,0},{16,24},{24,16},{32,40},{40,32},{48,56},{56,48},{64,72... | collective-permute-start | bytes 387080 | tf_op jit(solution)/shard_map/ppermute | solution.py:32
  233.8 19.7 %copy-start.38 = (f32[1,512]{1,0:T(1,128)S(1)}, f32[1,512]{1,0:T(1,128)}, u32[]{:S(2)}) copy-start(f32[1,512]{1,0:T(1,128)} %copy-done.37) | copy-start | bytes 6148
  234.0 20.3 %copy-start.36 = (f32[1,512]{1,0:T(1,128)S(1)}, f32[1,512]{1,0:T(1,128)}, u32[]{:S(2)}) copy-start(f32[1,512]{1,0:T(1,128)} %copy-done.35) | copy-start | bytes 6148
  (24 other events, 52.9 us)
Sparse Core Ops, SparseCore 0:
  33.0 97.6 all-gather.1
where the time goes:
time: 263 us; the launch traced here: 262 us
  waiting for transfers between devices  105 us (40%)
  blocking collectives  36.7 us (14%)
  local copies, waits for them, and re-layouts  36 us (14%)
  starting transfers between devices  29.6 us (11%)
  other arithmetic  21.3 us (8%)
  matrix products  17.7 us (7%)
  between operations  15.5 us (6%)
    all_gather x1, waiting for transfers between devices, local(): lax.all_gather(jnp.concatenate(owned, axis=1), 'seq', axis=1, tiled=True)  86.7 us
    psum x2, blocking collectives, width_sum(): return lax.psum(partial_sums, 'head')  36.7 us
    ppermute x6, starting transfers between devices, from_partner(): return lax.ppermute(value, axis, pairs)  23.8 us
    ppermute x6, waiting for transfers between devices, from_partner(): return lax.ppermute(value, axis, pairs)  16.7 us
    slice x6, local copies, waits for them, and re-layouts, local(): section = gathered[:, :, start_row:start_row + sizes[j]]  14.9 us
    unnamed x104, local copies, waits for them, and re-layouts  6.22 us
  transfers between devices with their start and end apart: 11, of which 7 were waited for; matrix products, arithmetic and copies ran while one was open for 8% of the time, Pallas kernels for 0%

commit v1 on v0

v1 whole, which is shorter than its diff:
```python
import math

import jax
import jax.numpy as jnp
from jax import lax
from jax.experimental import pallas as pl
from jax.experimental.pallas import tpu as pltpu
from jax.sharding import PartitionSpec as P

ROWS = 512
FEAT = 128
LEAF = 128
LEAVES = 4
HEAD = 64
KEYS = 1280
EPS = 1e-06
LN2 = math.log(2.0)
F32 = jnp.float32
BF16 = jnp.bfloat16
PARAMS = pltpu.CompilerParams(vmem_limit_bytes=40 * 1024 * 1024)
ROW_LEVEL = {1: 2, 2: 3, 3: 3, 4: 4, 5: 4, 6: 4, 7: 4}
COLUMN_LEVEL = {1: 5, 2: 6, 3: 6, 4: 7, 5: 7, 6: 7, 7: 7}
FAR = 48
SLOT = 112


def dot(a, b, dims):
    return lax.dot_general(a, b, ((dims[:1], dims[1:]), ((), ())), preferred_element_type=F32)


def iota(shape, axis):
    return lax.broadcasted_iota(jnp.int32, shape, axis)


def pooling(rows, level):
    token = iota((rows, ROWS), 1)
    hit = jnp.right_shift(token, level) == iota((rows, ROWS), 0)
    return jnp.where(hit, 2.0**-level, 0.0)


def spreading(first, rows, level):
    token = iota((ROWS, rows), 0)
    hit = jnp.right_shift(token, level) == iota((ROWS, rows), 1) + first
    return jnp.where(hit, 2.0**-level, 0.0)


def far_pick(shape, far_axis):
    far = iota(shape, far_axis)
    slot_row = iota(shape, 1 - far_axis)
    mid = far - 16
    low = far - 32
    column = jnp.where(
        far < 16,
        far,
        jnp.where(
            far < 32,
            (1 + jnp.right_shift(mid, 3)) * 16 + jnp.bitwise_and(mid, 7),
            (3 + jnp.right_shift(low, 2)) * 16 + jnp.bitwise_and(low, 3),
        ),
    )
    return jnp.where(column == slot_row, 1.0, 0.0).astype(BF16)


def token_sums(x):
    return [
        jnp.sum(x[i * LEAF : (i + 1) * LEAF].T, axis=0, keepdims=True) for i in range(LEAVES)
    ]


def spread_tokens(tile, first):
    return jnp.concatenate(
        [
            jnp.broadcast_to(tile[first + i : first + i + 1], (LEAF, LEAF)).T
            for i in range(LEAVES)
        ],
        axis=0,
    )


def squares_kernel(q_ref, k_ref, out_ref):
    q = q_ref[...].astype(F32)
    k = k_ref[...].astype(F32)
    tile = jnp.concatenate(token_sums(q * q) + token_sums(k * k), axis=0)
    for i in range(out_ref.shape[0]):
        out_ref[i] = tile


def norm_kernel(width, sum_ref, q_ref, k_ref, v_ref, qg_ref, kg_ref, qn_ref, kv_ref, one_ref, lv_ref, y_ref, p1_ref, p2_ref):
    index = lax.axis_index("seq")
    column = jnp.right_shift(index, 3)
    odd = jnp.bitwise_and(index, 1)
    total = jnp.sum(sum_ref[...], axis=0)
    rate = lax.rsqrt(total / width + EPS)
    qn_ref[...] = (
        q_ref[...].astype(F32) * spread_tokens(rate, 0) * qg_ref[...]
    ).astype(BF16)
    kv_ref[:, :FEAT] = (
        k_ref[...].astype(F32) * spread_tokens(rate, 4) * kg_ref[...]
    ).astype(BF16)
    kv_ref[:, FEAT:] = v_ref[...]
    pool = jnp.concatenate(
        [pooling(ROWS >> level, level) for level in (1, 2, 3, 4)]
        + [pooling(16, COLUMN_LEVEL[d]) for d in range(1, 8)],
        axis=0,
    ).astype(BF16)
    coarse = dot(pool, kv_ref[...], (1, 0)).astype(BF16)
    one_ref[...] = coarse[:256]
    lv_ref[...] = coarse[256:480]
    y_ref[column] = jnp.zeros((16, 2 * FEAT), BF16)
    for d in range(1, 8):
        y_ref[jnp.bitwise_xor(column, d)] = coarse[464 + 16 * d : 480 + 16 * d]
    p1_ref[:LEAF] = kv_ref[pl.ds(pl.multiple_of((1 - odd) * 384, LEAF), LEAF)]
    p1_ref[LEAF:] = coarse[320:384]
    p2_ref[...] = kv_ref[pl.ds(pl.multiple_of(odd * 384, LEAF), LEAF)]


def row_kernel(y_ref, lv_ref, out_ref):
    index = lax.axis_index("seq")
    column = jnp.right_shift(index, 3)
    place = jnp.bitwise_and(index, 7)
    slots = jnp.concatenate([y_ref[jnp.bitwise_xor(column, d)] for d in range(1, 8)], axis=0)
    far = dot(far_pick((FAR, 112), 0), slots, (1, 0)).astype(BF16)
    for s in range(8):
        out_ref[s, :FAR] = far
    out_ref[place, FAR:] = jnp.zeros((64, 2 * FEAT), BF16)
    for d in range(1, 8):
        other = jnp.bitwise_xor(place, d)
        if d == 1:
            out_ref[other, FAR:] = lv_ref[:64]
        elif d < 4:
            out_ref[other, FAR:] = lv_ref[128:192]
        else:
            out_ref[other, FAR : FAR + 32] = lv_ref[192:224]
            out_ref[other, FAR + 32 :] = jnp.zeros((32, 2 * FEAT), BF16)


def attend_kernel(
    qn_ref, kv_ref, one_ref, g_ref, p1_ref, p2_ref, z_ref,
    att_ref, nqg_ref, tok_ref, p1o_ref, p2o_ref, zo_ref,
    near, cross, near_grad, one_grad, cross_grad,
):
    index = lax.axis_index("seq")
    last = lax.axis_size("seq") - 1
    place = jnp.bitwise_and(index, 7)
    odd = jnp.bitwise_and(index, 1)
    peer_side = pl.multiple_of((1 - odd) * 640, LEAF)
    other_side = pl.multiple_of(odd * 640, LEAF)
    near[LEAF : LEAF + ROWS] = kv_ref[...]
    near[pl.ds(peer_side, LEAF)] = p1_ref[:LEAF]
    near[pl.ds(other_side, LEAF)] = p2_ref[...]
    cross[:64] = z_ref[jnp.bitwise_xor(place, 1), FAR:]
    cross[64:128] = p1_ref[LEAF:]
    cross[128:192] = z_ref[jnp.bitwise_xor(place, 2), FAR:]
    cross[192:256] = z_ref[jnp.bitwise_xor(place, 3), FAR:]
    for i in range(4):
        cross[256 + 32 * i : 288 + 32 * i] = z_ref[jnp.bitwise_xor(place, 4 + i), FAR : FAR + 32]
    for s in range(8):
        cross[384 + FAR * s : 384 + FAR * (s + 1)] = z_ref[s, :FAR]

    def level_bias(rows, level):
        return jnp.full((rows, 2 * LEAF), level * LN2, F32)

    bias = jnp.concatenate(
        [level_bias(LEAF, level) for level in (1, 2, 3, 4)]
        + [level_bias(16, level) for _ in range(8) for level in (5, 6, 7)],
        axis=0,
    )
    left = jnp.where(index > 0, 0.0, -jnp.inf).astype(F32)
    right = jnp.where(index < last, 0.0, -jnp.inf).astype(F32)
    lane = iota((LEAF, FEAT), 1)
    feature = iota((FEAT, LEAF), 0)
    zero = jnp.zeros((LEAF, FEAT), BF16)

    def by_head(block):
        return jnp.concatenate(
            [jnp.where(lane < HEAD, block, zero), jnp.where(lane < HEAD, zero, block)], axis=0
        )

    def merge_heads(transposed):
        return jnp.where(feature < HEAD, transposed[:, :LEAF], transposed[:, LEAF:]).T

    near_grad[...] = jnp.zeros_like(near_grad)
    one_grad[...] = jnp.zeros_like(one_grad)
    for b in range(LEAVES):
        rows = slice(b * LEAF, (b + 1) * LEAF)
        near_rows = slice(b * LEAF, (b + 3) * LEAF)
        half = (1 - b // 2) * LEAF
        q2 = by_head(qn_ref[rows]) * jnp.asarray(0.125, BF16)
        g2 = by_head(g_ref[rows])
        kv = jnp.concatenate([near[near_rows], one_ref[half : half + LEAF], cross[...]], axis=0)
        keys = kv[:, :FEAT]
        values = kv[:, FEAT:]
        raw = dot(keys, q2, (1, 1))
        before, after = raw[:LEAF], raw[2 * LEAF : 3 * LEAF]
        if b == 0:
            before = before + left
        if b == LEAVES - 1:
            after = after + right
        scores = jnp.concatenate(
            [before, raw[LEAF : 2 * LEAF], after, raw[3 * LEAF :] + bias], axis=0
        )
        weights = jnp.exp(scores - jnp.max(scores, axis=0, keepdims=True))
        probs = weights * (1.0 / jnp.sum(weights, axis=0, keepdims=True))
        low = probs.astype(BF16)
        prob_grad = dot(values, g2, (1, 1))
        delta = jnp.sum(probs * prob_grad, axis=0, keepdims=True)
        score_grad = (probs * (prob_grad - delta)).astype(BF16)
        att_ref[rows] = merge_heads(dot(values, low, (0, 0))).astype(BF16)
        nqg_ref[rows] = merge_heads(dot(keys, score_grad, (0, 0))) * 0.125
        key_part = dot(score_grad, q2, (1, 0))
        value_part = dot(low, g2, (1, 0))
        for part, lanes in ((key_part, slice(0, FEAT)), (value_part, slice(FEAT, 2 * FEAT))):
            near_grad[near_rows, lanes] += part[: 3 * LEAF]
            one_grad[half : half + LEAF, lanes] += part[3 * LEAF : 4 * LEAF]
            if b == 0:
                cross_grad[:, lanes] = part[4 * LEAF :]
            else:
                cross_grad[:, lanes] += part[4 * LEAF :]

    spread = spreading(0, 256, 1).astype(BF16)
    high = one_grad[...].astype(BF16)
    rest = (one_grad[...] - high.astype(F32)).astype(BF16)
    tok_ref[...] = near_grad[LEAF : LEAF + ROWS] + dot(spread, high, (1, 0)) + dot(spread, rest, (1, 0))
    p1o_ref[:LEAF] = near_grad[pl.ds(peer_side, LEAF)].astype(BF16)
    p1o_ref[LEAF:] = cross_grad[64:128].astype(BF16)
    p2o_ref[...] = near_grad[pl.ds(other_side, LEAF)].astype(BF16)
    for s in range(8):
        zo_ref[s, :FAR] = cross_grad[384 + FAR * s : 384 + FAR * (s + 1)].astype(BF16)
    zo_ref[place, FAR:] = jnp.zeros((64, 2 * FEAT), BF16)
    zo_ref[jnp.bitwise_xor(place, 1), FAR:] = cross_grad[:64].astype(BF16)
    zo_ref[jnp.bitwise_xor(place, 2), FAR:] = cross_grad[128:192].astype(BF16)
    zo_ref[jnp.bitwise_xor(place, 3), FAR:] = cross_grad[192:256].astype(BF16)
    for i in range(4):
        other = jnp.bitwise_xor(place, 4 + i)
        zo_ref[other, FAR : FAR + 32] = cross_grad[256 + 32 * i : 288 + 32 * i].astype(BF16)
        zo_ref[other, FAR + 32 :] = jnp.zeros((32, 2 * FEAT), BF16)


def column_kernel(z_ref, *out_refs):
    far = jnp.sum(z_ref[:, :FAR].astype(F32), axis=0).astype(BF16)
    slots = dot(far_pick((112, FAR), 1), far, (1, 0)).astype(BF16)
    for d in range(1, 8):
        out_refs[d - 1][...] = slots[16 * (d - 1) : 16 * d]


def total_kernel(
    tok_ref, p1_ref, p2_ref, z_ref, y1, y2, y3, y4, y5, y6, y7,
    q_ref, k_ref, qg_ref, kg_ref, nqg_ref, nkg_ref, vg_ref, sum_ref, acc,
):
    index = lax.axis_index("seq")
    place = jnp.bitwise_and(index, 7)
    odd = jnp.bitwise_and(index, 1)
    pieces = [z_ref[jnp.bitwise_xor(place, 1), FAR:], p1_ref[LEAF:]]
    maps = [spreading(0, 64, 2), spreading(64, 64, 2)]
    for d in range(2, 8):
        rows = ROWS >> ROW_LEVEL[d]
        pieces.append(z_ref[jnp.bitwise_xor(place, d), FAR : FAR + rows])
        maps.append(spreading(0, rows, ROW_LEVEL[d]))
    for d, y_ref in zip(range(1, 8), (y1, y2, y3, y4, y5, y6, y7)):
        pieces.append(y_ref[...])
        maps.append(spreading(0, 16, COLUMN_LEVEL[d]))
    spread = jnp.concatenate(maps, axis=1).astype(BF16)
    acc[...] = tok_ref[...] + dot(spread, jnp.concatenate(pieces, axis=0), (1, 0))
    acc[pl.ds(pl.multiple_of((1 - odd) * 384, LEAF), LEAF)] += p1_ref[:LEAF].astype(F32)
    acc[pl.ds(pl.multiple_of(odd * 384, LEAF), LEAF)] += p2_ref[...].astype(F32)
    vg_ref[...] = acc[:, FEAT:].astype(BF16)
    key_total = acc[:, :FEAT]
    nkg_ref[...] = key_total
    tile = jnp.concatenate(
        token_sums(q_ref[...].astype(F32) * qg_ref[...] * nqg_ref[...])
        + token_sums(k_ref[...].astype(F32) * kg_ref[...] * key_total),
        axis=0,
    )
    sum_ref[...] = tile


def finish_kernel(width, sq_ref, inner_ref, q_ref, k_ref, qg_ref, kg_ref, nqg_ref, nkg_ref, dq_ref, dk_ref):
    rate = lax.rsqrt(jnp.sum(sq_ref[...], axis=0) / width + EPS)
    inner = jnp.sum(inner_ref[...], axis=0) / width
    cubed = rate * rate * rate * inner
    for first, x_ref, gain_ref, grad_ref, out_ref in (
        (0, q_ref, qg_ref, nqg_ref, dq_ref),
        (4, k_ref, kg_ref, nkg_ref, dk_ref),
    ):
        out_ref[...] = (
            spread_tokens(rate, first) * gain_ref[...] * grad_ref[...]
            - x_ref[...].astype(F32) * spread_tokens(cubed, first)
        ).astype(BF16)


def call(kernel, outs, args, scratch=(), flops=0, name=None):
    many = isinstance(outs, list)
    moved = sum(math.prod(x.shape) * x.dtype.itemsize for x in list(args) + (outs if many else [outs]))
    return pl.pallas_call(
        kernel,
        out_shape=outs,
        scratch_shapes=list(scratch),
        compiler_params=PARAMS,
        cost_estimate=pl.CostEstimate(flops=flops, bytes_accessed=moved, transcendentals=0),
        name=name,
    )(*args)


def sds(*shape, dtype=BF16):
    return jax.ShapeDtypeStruct(shape, dtype)


ROW_GROUPS = [[8 * y + z for z in range(8)] for y in range(8)]
COLUMN_GROUPS = [[8 * y + z for y in range(8)] for z in range(8)]


def exchange(x, axis, groups=None):
    return lax.all_to_all(x, axis, 0, 0, axis_index_groups=groups, tiled=True)


def local(queries, key_rows, value_rows, query_gain, key_gain, out_grad):
    seq = lax.axis_size("seq")
    heads = lax.axis_size("head")
    width = float(heads * FEAT)
    qg = query_gain.reshape(1, FEAT)
    kg = key_gain.reshape(1, FEAT)
    peer = [(i, i ^ 1) for i in range(seq)]
    beside = [(i, i + 1) for i in range(1, seq - 1, 2)] + [(i + 1, i) for i in range(1, seq - 1, 2)]

    squares = call(squares_kernel, sds(heads, 8, FEAT, dtype=F32), (queries, key_rows), name="squares")
    squares = exchange(squares, "head")
    qn, kv, one, lv, ysend, p1, p2 = call(
        lambda *refs: norm_kernel(width, *refs),
        [sds(ROWS, FEAT), sds(ROWS, 256), sds(256, 256), sds(224, 256), sds(8, 16, 256), sds(192, 256), sds(LEAF, 256)],
        (squares, queries, key_rows, value_rows, qg, kg),
        name="norm",
    )
    p1 = lax.ppermute(p1, "seq", peer)
    p2 = lax.ppermute(p2, "seq", beside)
    yrecv = exchange(ysend, "seq", COLUMN_GROUPS)
    zsend = call(row_kernel, sds(8, SLOT, 256), (yrecv, lv), name="rows")
    zrecv = exchange(zsend, "seq", ROW_GROUPS)
    attended, nqg, tok, p1, p2, zsend = call(
        attend_kernel,
        [sds(ROWS, FEAT), sds(ROWS, FEAT, dtype=F32), sds(ROWS, 256, dtype=F32), sds(192, 256), sds(LEAF, 256), sds(8, SLOT, 256)],
        (qn, kv, one, out_grad, p1, p2, zrecv),
        scratch=[
            pltpu.VMEM((768, 256), BF16),
            pltpu.VMEM((768, 256), BF16),
            pltpu.VMEM((768, 256), F32),
            pltpu.VMEM((256, 256), F32),
            pltpu.VMEM((768, 256), F32),
        ],
        flops=4 * 6 * 2 * 256 * KEYS * FEAT,
        name="attend",
    )
    p1 = lax.ppermute(p1, "seq", peer)
    p2 = lax.ppermute(p2, "seq", beside)
    zrecv = exchange(zsend, "seq", ROW_GROUPS)
    ysend = call(column_kernel, [sds(16, 256) for _ in range(7)], (zrecv,), name="columns")
    yrecv = [
        lax.ppermute(ysend[d - 1], "seq", [(i, i ^ (8 * d)) for i in range(seq)]) for d in range(1, 8)
    ]
    nkg, value_grad, inner = call(
        total_kernel,
        [sds(ROWS, FEAT, dtype=F32), sds(ROWS, FEAT), sds(8, FEAT, dtype=F32)],
        (tok, p1, p2, zrecv, *yrecv, queries, key_rows, qg, kg, nqg),
        scratch=[pltpu.VMEM((ROWS, 256), F32)],
        name="total",
    )
    inner = lax.all_gather(inner, "head", axis=0)
    query_grad, key_grad = call(
        lambda *refs: finish_kernel(width, *refs),
        [sds(ROWS, FEAT), sds(ROWS, FEAT)],
        (squares, inner, queries, key_rows, qg, kg, nqg, nkg),
        name="finish",
    )
    return (attended, query_grad, key_grad, value_grad)


def solution(mesh):
    placed = (
        P("seq", "head"),
        P("seq", "head"),
        P("seq", "head"),
        P("head"),
        P("head"),
        P("seq", "head"),
    )
    return jax.shard_map(
        local,
        mesh=mesh,
        in_specs=placed,
        out_specs=(P("seq", "head"), P("seq", "head"), P("seq", "head"), P("seq", "head")),
        check_vma=False,
    )
```

time: 263 us -> 128 us (0.49)
  waiting for transfers between devices: 105 us -> 19.3 us
  local copies, waits for them, and re-layouts: 36 us -> 2.49 us
  other arithmetic: 21.3 us -> 0 us
  starting transfers between devices: 29.6 us -> 49.1 us
  matrix products: 17.7 us -> 0 us
  between operations: 15.5 us -> 0.85 us
  Pallas kernels: 0 us -> 11.4 us
  blocking collectives: 36.7 us -> 44.3 us
    all_gather x1 -> x0, waiting for transfers between devices: 86.7 us -> none  [local(): lax.all_gather(jnp.concatenate(owned, axis=1), 'seq', axis=1, tiled=True)]
    psum x2 -> x0, blocking collectives: 36.7 us -> none  [width_sum(): return lax.psum(partial_sums, 'head')]
    slice x17 -> x0, local copies, waits for them, and re-layouts: 24.3 us -> none  [the longest x6 14.9 us: local(): section = gathered[:, :, start_row:start_row + sizes[j]]]
    all_to_all x0 -> x2, blocking collectives: none -> 24.2 us  [exchange(): return lax.all_to_all(x, axis, 0, 0, axis_index_groups=groups, tiled=True)]
    all_gather x0 -> x1, blocking collectives: none -> 20.2 us  [local(): inner = lax.all_gather(inner, 'head', axis=0)]
    dot_general x12 -> x0, matrix products: 17.7 us -> none  [the longest x1 2.73 us: attend(): jnp.einsum('gqhe,gkhe->ghqk', grad_group, value_group, preferred_element_...]
    all_to_all x0 -> x2, starting transfers between devices: none -> 15.3 us  [exchange(): return lax.all_to_all(x, axis, 0, 0, axis_index_groups=groups, tiled=True)]
    pallas_call x0 -> x7, Pallas kernels: none -> 11.4 us  [call(): pl.pallas_call(kernel, out_shape=outs, scratch_shapes=list(scratch), comp...]
  transfers between devices with their start and end apart: 11 -> 13, of which waited for: 7 -> 4; matrix products, arithmetic and copies ran while one was open for 8% -> 0% of each run, Pallas kernels for 0% -> 0%
where the time goes in v1:
time: 128 us
  starting transfers between devices  49.1 us (38%)
  blocking collectives  44.3 us (35%)
  waiting for transfers between devices  19.3 us (15%)
  Pallas kernels  11.4 us (9%)
  local copies, waits for them, and re-layouts  2.49 us (2%)
    ppermute x7, starting transfers between devices, local(): lax.ppermute(ysend[d - 1], 'seq', [(i, i ^ 8 * d) for i in range(seq)])  25.7 us
    all_to_all x2, blocking collectives, exchange(): return lax.all_to_all(x, axis, 0, 0, axis_index_groups=groups, tiled=True)  24.2 us
    all_gather x1, blocking collectives, local(): inner = lax.all_gather(inner, 'head', axis=0)  20.2 us
    all_to_all x2, starting transfers between devices, exchange(): return lax.all_to_all(x, axis, 0, 0, axis_index_groups=groups, tiled=True)  15.3 us
    pallas_call x7, Pallas kernels, call(): pl.pallas_call(kernel, out_shape=outs, scratch_shapes=list(scratch), comp...  11.4 us
    all_to_all x2, waiting for transfers between devices, exchange(): return lax.all_to_all(x, axis, 0, 0, axis_index_groups=groups, tiled=True)  9.58 us
    ppermute x2, waiting for transfers between devices, local(): p1 = lax.ppermute(p1, 'seq', peer)  7.61 us
    ppermute x2, starting transfers between devices, local(): p1 = lax.ppermute(p1, 'seq', peer)  6.71 us
  transfers between devices with their start and end apart: 13, of which 4 were waited for; matrix products, arithmetic and copies ran while one was open for 0% of the time, Pallas kernels for 0%

profile of v1, /device:TPU:1, one launch (start us, length us, event | category | flops | bytes accessed | tf_op | source)
XLA Modules:
  0.0 127.5 jit_solution(1588146532746570270)
XLA Ops:
  0.6 0.0 copy-start
  0.6 0.9 copy-done
  1.5 0.9 copy-done.2
  2.4 0.2 squares.1
  2.7 14.0 %all_to_all.20.refs_0_ = f32[8,8,128]{2,1,0:T(8,128)S(1)} all-to-all(f32[8,8,128]{2,1,0:T(8,128)S(1)} %squares.1), channel_id=1, replica_groups=mesh['seq'=64,'head'=8] {'head'}, dimensions={0} | all-to-all | bytes 65536 | tf_op jit(solution)/shard_map/all_to_all | solution.py:313
  16.6 0.6 copy-done.5
  17.3 0.0 copy-done.6
  17.3 0.5 norm.1
  17.8 10.2 %all_to_all.21.y_ref = bf16[8,16,256]{2,1,0:T(8,128)(2,1)S(1)} all-to-all(bf16[8,16,256]{2,1,0:T(8,128)(2,1)S(1)} %get-tuple-element.34), channel_id=1, replica_groups={{0,64,128,192,256,320,384,448},{8,72,136,200,264,328,392,456},{16,80,14..., dimensions={0} | all-to-all | bytes 131072 | tf_op jit(solution)/shard_map/all_to_all | solution.py:313
  28.0 1.0 rows.1
  29.0 10.2 %all-to-all-start.2 = ((bf16[8,112,256]{2,1,0:T(8,128)(2,1)}), bf16[8,112,256]{2,1,0:T(8,128)(2,1)S(1)}, u32[]{:S(2)}, u32[]{:S(2)}) async-start(bf16[8,112,256]{2,1,0:T(8,128)(2,1)} %rows.1), calls=%async_computation.2 | async-start | bytes 917504 | tf_op jit(solution)/shard_map/all_to_all | solution.py:313
  39.1 3.4 %collective-permute-start = (bf16[192,256]{1,0:T(8,128)(2,1)S(1)}, bf16[192,256]{1,0:T(8,128)(2,1)S(1)}, u32[]{:S(2)}, u32[]{:S(2)}) collective-permute-start(bf16[192,256]{1,0:T(8,128)(2,1)S(1)} %get-tuple-element.32), channel_id=1, source_target_pairs={{0,8},{8,0},{16,24},{24,16},{32,40},{40,32},{48,56},{56,48},{64,72... | collective-permute-start | bytes 294920 | tf_op jit(solution)/shard_map/ppermute | solution.py:333
  42.5 0.7 collective-permute-start.1
  43.2 7.6 %collective-permute-done.p1_ref = bf16[192,256]{1,0:T(8,128)(2,1)S(1)} collective-permute-done((bf16[192,256]{1,0:T(8,128)(2,1)S(1)}, bf16[192,256]{1,0:T(8,128)(2,1)S(1)}, u32[]{:S(2)}, u32[]{:S(2)}) %collective-permute-start) | collective-permute-done | bytes 98336 | tf_op jit(solution)/shard_map/ppermute | solution.py:333
  50.8 1.7 %all-to-all-done.2.z_ref = bf16[8,112,256]{2,1,0:T(8,128)(2,1)S(1)} async-done(((bf16[8,112,256]{2,1,0:T(8,128)(2,1)}), bf16[8,112,256]{2,1,0:T(8,128)(2,1)S(1)}, u32[]{:S(2)}, u32[]{:S(2)}) %all-to-all-start.2) | async-done | bytes 458784 | tf_op jit(solution)/shard_map/all_to_all | solution.py:313
  52.5 7.1 %attend.1 = (bf16[512,128]{1,0:T(8,128)(2,1)}, f32[512,128]{1,0:T(8,128)S(1)}, f32[512,256]{1,0:T(8,128)S(1)}, bf16[192,256]{1,0:T(8,128)(2,1)S(1)}, bf16[128,25...) custom-call(bf16[512,128]{1,0:T(8,128)(2,1)S(1)} %get-tuple-element.29.qn_ref, ...), custom_call_target="tpu_custom_call" | custom-call | flops 2013265920 | bytes 2818048 | tf_op jit(solution)/shard_map/attend/pallas_call | solution.py:294
  59.6 5.1 %all-to-all-start.3 = ((bf16[8,112,256]{2,1,0:T(8,128)(2,1)}), bf16[8,112,256]{2,1,0:T(8,128)(2,1)S(1)}, u32[]{:S(2)}, u32[]{:S(2)}) async-start(bf16[8,112,256]{2,1,0:T(8,128)(2,1)} %get-tuple-element.40), calls=%async_computation.3 | async-start | bytes 917504 | tf_op jit(solution)/shard_map/all_to_all | solution.py:313
  64.7 3.4 %collective-permute-start.2 = (bf16[192,256]{1,0:T(8,128)(2,1)S(1)}, bf16[192,256]{1,0:T(8,128)(2,1)S(1)}, u32[]{:S(2)}, u32[]{:S(2)}) collective-permute-start(bf16[192,256]{1,0:T(8,128)(2,1)S(1)} %get-tuple-element.38), channel_id=1, source_target_pairs={{0,8},{8,0},{16,24},{24,16},{32,40},{40,32},{48,56},{56,48},{64,72... | collective-permute-start | bytes 294920 | tf_op jit(solution)/shard_map/ppermute | solution.py:352
  68.1 0.8 collective-permute-start.3
  68.9 7.9 %all-to-all-done.3.z_ref = bf16[8,112,256]{2,1,0:T(8,128)(2,1)S(1)} async-done(((bf16[8,112,256]{2,1,0:T(8,128)(2,1)}), bf16[8,112,256]{2,1,0:T(8,128)(2,1)S(1)}, u32[]{:S(2)}, u32[]{:S(2)}) %all-to-all-start.3) | async-done | bytes 458784 | tf_op jit(solution)/shard_map/all_to_all | solution.py:313
  76.8 0.2 columns.1
  77.0 4.1 %collective-permute-start.4 = (bf16[16,256]{1,0:T(8,128)(2,1)S(1)}, bf16[16,256]{1,0:T(8,128)(2,1)S(1)}, u32[]{:S(2)}, u32[]{:S(2)}) collective-permute-start(bf16[16,256]{1,0:T(8,128)(2,1)S(1)} %get-tuple-element.41), channel_id=1, source_target_pairs={{0,64},{8,72},{16,80},{24,88},{32,96},{40,104},{48,112},{56,120},{... | collective-permute-start | bytes 24584 | tf_op jit(solution)/shard_map/ppermute | solution.py:357
  81.1 2.1 %collective-permute-start.5 = (bf16[16,256]{1,0:T(8,128)(2,1)S(1)}, bf16[16,256]{1,0:T(8,128)(2,1)S(1)}, u32[]{:S(2)}, u32[]{:S(2)}) collective-permute-start(bf16[16,256]{1,0:T(8,128)(2,1)S(1)} %get-tuple-element.42), channel_id=1, source_target_pairs={{0,128},{8,136},{16,144},{24,152},{32,160},{40,168},{48,176},{56,1... | collective-permute-start | bytes 24584 | tf_op jit(solution)/shard_map/ppermute | solution.py:357
  83.2 3.8 %collective-permute-start.6 = (bf16[16,256]{1,0:T(8,128)(2,1)S(1)}, bf16[16,256]{1,0:T(8,128)(2,1)S(1)}, u32[]{:S(2)}, u32[]{:S(2)}) collective-permute-start(bf16[16,256]{1,0:T(8,128)(2,1)S(1)} %get-tuple-element.43), channel_id=1, source_target_pairs={{0,192},{8,200},{16,208},{24,216},{32,224},{40,232},{48,240},{56,2... | collective-permute-start | bytes 24584 | tf_op jit(solution)/shard_map/ppermute | solution.py:357
  87.0 3.5 %collective-permute-start.7 = (bf16[16,256]{1,0:T(8,128)(2,1)S(1)}, bf16[16,256]{1,0:T(8,128)(2,1)S(1)}, u32[]{:S(2)}, u32[]{:S(2)}) collective-permute-start(bf16[16,256]{1,0:T(8,128)(2,1)S(1)} %get-tuple-element.44), channel_id=1, source_target_pairs={{0,256},{8,264},{16,272},{24,280},{32,288},{40,296},{48,304},{56,3... | collective-permute-start | bytes 24584 | tf_op jit(solution)/shard_map/ppermute | solution.py:357
  90.6 5.0 %collective-permute-start.8 = (bf16[16,256]{1,0:T(8,128)(2,1)S(1)}, bf16[16,256]{1,0:T(8,128)(2,1)S(1)}, u32[]{:S(2)}, u32[]{:S(2)}) collective-permute-start(bf16[16,256]{1,0:T(8,128)(2,1)S(1)} %get-tuple-element.45), channel_id=1, source_target_pairs={{0,320},{8,328},{16,336},{24,344},{32,352},{40,360},{48,368},{56,3... | collective-permute-start | bytes 24584 | tf_op jit(solution)/shard_map/ppermute | solution.py:357
  95.6 3.7 %collective-permute-start.9 = (bf16[16,256]{1,0:T(8,128)(2,1)S(1)}, bf16[16,256]{1,0:T(8,128)(2,1)S(1)}, u32[]{:S(2)}, u32[]{:S(2)}) collective-permute-start(bf16[16,256]{1,0:T(8,128)(2,1)S(1)} %get-tuple-element.46), channel_id=1, source_target_pairs={{0,384},{8,392},{16,400},{24,408},{32,416},{40,424},{48,432},{56,4... | collective-permute-start | bytes 24584 | tf_op jit(solution)/shard_map/ppermute | solution.py:357
  99.3 3.5 %collective-permute-start.10 = (bf16[16,256]{1,0:T(8,128)(2,1)S(1)}, bf16[16,256]{1,0:T(8,128)(2,1)S(1)}, u32[]{:S(2)}, u32[]{:S(2)}) collective-permute-start(bf16[16,256]{1,0:T(8,128)(2,1)S(1)} %get-tuple-element.47), channel_id=1, source_target_pairs={{0,448},{8,456},{16,464},{24,472},{32,480},{40,488},{48,496},{56,5... | collective-permute-start | bytes 24584 | tf_op jit(solution)/shard_map/ppermute | solution.py:357
  102.8 2.1 %collective-permute-done.10.y7 = bf16[16,256]{1,0:T(8,128)(2,1)S(1)} collective-permute-done((bf16[16,256]{1,0:T(8,128)(2,1)S(1)}, bf16[16,256]{1,0:T(8,128)(2,1)S(1)}, u32[]{:S(2)}, u32[]{:S(2)}) %collective-permute-start.10) | collective-permute-done | bytes 8224 | tf_op jit(solution)/shard_map/ppermute | solution.py:357
  104.9 1.4 %total.1 = (f32[512,128]{1,0:T(8,128)S(1)}, bf16[512,128]{1,0:T(8,128)(2,1)}, f32[8,128]{1,0:T(8,128)S(1)}) custom-call(f32[512,256]{1,0:T(8,128)S(1)} %get-tuple-element.37.tok_ref, bf16[192,256]{1,0:T(8,128)(2,1)S(1)} %collective-permute-done.2.p1_ref, bf16[128,256]{1,0:T(8,128)(2,1)S(1)} %collective-permute-done.3.p2_ref, ...), custom_call_target="tpu_custom_call" | custom-call | bytes 2126848 | tf_op jit(solution)/shard_map/total/pallas_call | solution.py:294
  106.3 20.2 %all-gather = f32[64,128]{1,0:T(8,128)S(1)} all-gather(f32[8,128]{1,0:T(8,128)S(1)} %get-tuple-element.49), channel_id=2, replica_groups=mesh['seq'=64,'head'=8] {'head'}, dimensions={0}, use_global_device_ids=true | all-gather | bytes 36864 | tf_op jit(solution)/shard_map/all_gather | solution.py:366
  126.5 1.0 finish.1
  (20 shorter events, 0.0 us)
Async XLA Ops:
  0.6 0.9 copy-start
  1.5 0.9 copy-start.2
  2.4 14.2 %copy-start.4 = (bf16[512,128]{1,0:T(8,128)(2,1)S(1)}, bf16[512,128]{1,0:T(8,128)(2,1)}, u32[]{:S(2)}) copy-start(bf16[512,128]{1,0:T(8,128)(2,1)} %refs_3_.2) | copy-start | bytes 393220
  16.6 0.7 copy-start.5
  16.6 0.7 copy-start.6
  29.0 23.5 %copy-start.7 = (bf16[512,128]{1,0:T(8,128)(2,1)S(1)}, bf16[512,128]{1,0:T(8,128)(2,1)}, u32[]{:S(2)}) copy-start(bf16[512,128]{1,0:T(8,128)(2,1)} %g_ref.1) | copy-start | bytes 393220
  29.0 23.5 %all-to-all-start.2 = ((bf16[8,112,256]{2,1,0:T(8,128)(2,1)}), bf16[8,112,256]{2,1,0:T(8,128)(2,1)S(1)}, u32[]{:S(2)}, u32[]{:S(2)}) async-start(bf16[8,112,256]{2,1,0:T(8,128)(2,1)} %rows.1), calls=%async_computation.2 | async-start | bytes 917504 | tf_op jit(solution)/shard_map/all_to_all | solution.py:313
  39.1 11.7 %collective-permute-start = (bf16[192,256]{1,0:T(8,128)(2,1)S(1)}, bf16[192,256]{1,0:T(8,128)(2,1)S(1)}, u32[]{:S(2)}, u32[]{:S(2)}) collective-permute-start(bf16[192,256]{1,0:T(8,128)(2,1)S(1)} %get-tuple-element.32), channel_id=1, source_target_pairs={{0,8},{8,0},{16,24},{24,16},{32,40},{40,32},{48,56},{56,48},{64,72... | collective-permute-start | bytes 294920 | tf_op jit(solution)/shard_map/ppermute | solution.py:333
  42.5 0.7 collective-permute-start.1
  59.6 17.2 %all-to-all-start.3 = ((bf16[8,112,256]{2,1,0:T(8,128)(2,1)}), bf16[8,112,256]{2,1,0:T(8,128)(2,1)S(1)}, u32[]{:S(2)}, u32[]{:S(2)}) async-start(bf16[8,112,256]{2,1,0:T(8,128)(2,1)} %get-tuple-element.40), calls=%async_computation.3 | async-start | bytes 917504 | tf_op jit(solution)/shard_map/all_to_all | solution.py:313
  64.7 25.9 %collective-permute-start.2 = (bf16[192,256]{1,0:T(8,128)(2,1)S(1)}, bf16[192,256]{1,0:T(8,128)(2,1)S(1)}, u32[]{:S(2)}, u32[]{:S(2)}) collective-permute-start(bf16[192,256]{1,0:T(8,128)(2,1)S(1)} %get-tuple-element.38), channel_id=1, source_target_pairs={{0,8},{8,0},{16,24},{24,16},{32,40},{40,32},{48,56},{56,48},{64,72... | collective-permute-start | bytes 294920 | tf_op jit(solution)/shard_map/ppermute | solution.py:352
  68.1 36.8 %copy-start.1 = (bf16[512,128]{1,0:T(8,128)(2,1)S(1)}, bf16[512,128]{1,0:T(8,128)(2,1)}, u32[]{:S(2)}) copy-start(bf16[512,128]{1,0:T(8,128)(2,1)} %refs_2_.3) | copy-start | bytes 393220
  68.1 36.8 %copy-start.3 = (bf16[512,128]{1,0:T(8,128)(2,1)S(1)}, bf16[512,128]{1,0:T(8,128)(2,1)}, u32[]{:S(2)}) copy-start(bf16[512,128]{1,0:T(8,128)(2,1)} %refs_3_.3) | copy-start | bytes 393220
  68.1 18.9 %collective-permute-start.3 = (bf16[128,256]{1,0:T(8,128)(2,1)S(1)}, bf16[128,256]{1,0:T(8,128)(2,1)S(1)}, u32[]{:S(2)}, u32[]{:S(2)}) collective-permute-start(bf16[128,256]{1,0:T(8,128)(2,1)S(1)} %get-tuple-element.39), channel_id=1, source_target_pairs={{8,16},{24,32},{40,48},{56,64},{72,80},{88,96},{104,112},{120,128}... | collective-permute-start | bytes 196616 | tf_op jit(solution)/shard_map/ppermute | solution.py:353
  77.0 18.6 %collective-permute-start.4 = (bf16[16,256]{1,0:T(8,128)(2,1)S(1)}, bf16[16,256]{1,0:T(8,128)(2,1)S(1)}, u32[]{:S(2)}, u32[]{:S(2)}) collective-permute-start(bf16[16,256]{1,0:T(8,128)(2,1)S(1)} %get-tuple-element.41), channel_id=1, source_target_pairs={{0,64},{8,72},{16,80},{24,88},{32,96},{40,104},{48,112},{56,120},{... | collective-permute-start | bytes 24584 | tf_op jit(solution)/shard_map/ppermute | solution.py:357
  81.1 18.2 %collective-permute-start.5 = (bf16[16,256]{1,0:T(8,128)(2,1)S(1)}, bf16[16,256]{1,0:T(8,128)(2,1)S(1)}, u32[]{:S(2)}, u32[]{:S(2)}) collective-permute-start(bf16[16,256]{1,0:T(8,128)(2,1)S(1)} %get-tuple-element.42), channel_id=1, source_target_pairs={{0,128},{8,136},{16,144},{24,152},{32,160},{40,168},{48,176},{56,1... | collective-permute-start | bytes 24584 | tf_op jit(solution)/shard_map/ppermute | solution.py:357
  83.2 19.6 %collective-permute-start.6 = (bf16[16,256]{1,0:T(8,128)(2,1)S(1)}, bf16[16,256]{1,0:T(8,128)(2,1)S(1)}, u32[]{:S(2)}, u32[]{:S(2)}) collective-permute-start(bf16[16,256]{1,0:T(8,128)(2,1)S(1)} %get-tuple-element.43), channel_id=1, source_target_pairs={{0,192},{8,200},{16,208},{24,216},{32,224},{40,232},{48,240},{56,2... | collective-permute-start | bytes 24584 | tf_op jit(solution)/shard_map/ppermute | solution.py:357
  87.0 15.8 %collective-permute-start.7 = (bf16[16,256]{1,0:T(8,128)(2,1)S(1)}, bf16[16,256]{1,0:T(8,128)(2,1)S(1)}, u32[]{:S(2)}, u32[]{:S(2)}) collective-permute-start(bf16[16,256]{1,0:T(8,128)(2,1)S(1)} %get-tuple-element.44), channel_id=1, source_target_pairs={{0,256},{8,264},{16,272},{24,280},{32,288},{40,296},{48,304},{56,3... | collective-permute-start | bytes 24584 | tf_op jit(solution)/shard_map/ppermute | solution.py:357
  90.6 12.2 %collective-permute-start.8 = (bf16[16,256]{1,0:T(8,128)(2,1)S(1)}, bf16[16,256]{1,0:T(8,128)(2,1)S(1)}, u32[]{:S(2)}, u32[]{:S(2)}) collective-permute-start(bf16[16,256]{1,0:T(8,128)(2,1)S(1)} %get-tuple-element.45), channel_id=1, source_target_pairs={{0,320},{8,328},{16,336},{24,344},{32,352},{40,360},{48,368},{56,3... | collective-permute-start | bytes 24584 | tf_op jit(solution)/shard_map/ppermute | solution.py:357
  95.6 7.2 %collective-permute-start.9 = (bf16[16,256]{1,0:T(8,128)(2,1)S(1)}, bf16[16,256]{1,0:T(8,128)(2,1)S(1)}, u32[]{:S(2)}, u32[]{:S(2)}) collective-permute-start(bf16[16,256]{1,0:T(8,128)(2,1)S(1)} %get-tuple-element.46), channel_id=1, source_target_pairs={{0,384},{8,392},{16,400},{24,408},{32,416},{40,424},{48,432},{56,4... | collective-permute-start | bytes 24584 | tf_op jit(solution)/shard_map/ppermute | solution.py:357
  99.3 5.6 %collective-permute-start.10 = (bf16[16,256]{1,0:T(8,128)(2,1)S(1)}, bf16[16,256]{1,0:T(8,128)(2,1)S(1)}, u32[]{:S(2)}, u32[]{:S(2)}) collective-permute-start(bf16[16,256]{1,0:T(8,128)(2,1)S(1)} %get-tuple-element.47), channel_id=1, source_target_pairs={{0,448},{8,456},{16,464},{24,472},{32,480},{40,488},{48,496},{56,5... | collective-permute-start | bytes 24584 | tf_op jit(solution)/shard_map/ppermute | solution.py:357

commit v2 on v1

--- a/solution.py
+++ b/solution.py
@@ -236,18 +236,21 @@
         zo_ref[other, FAR + 32 :] = jnp.zeros((32, 2 * FEAT), BF16)
 
 
-def column_kernel(z_ref, *out_refs):
+def column_kernel(z_ref, out_ref):
+    column = jnp.right_shift(lax.axis_index("seq"), 3)
     far = jnp.sum(z_ref[:, :FAR].astype(F32), axis=0).astype(BF16)
     slots = dot(far_pick((112, FAR), 1), far, (1, 0)).astype(BF16)
+    out_ref[column] = jnp.zeros((16, 2 * FEAT), BF16)
     for d in range(1, 8):
-        out_refs[d - 1][...] = slots[16 * (d - 1) : 16 * d]
+        out_ref[jnp.bitwise_xor(column, d)] = slots[16 * (d - 1) : 16 * d]
 
 
 def total_kernel(
-    tok_ref, p1_ref, p2_ref, z_ref, y1, y2, y3, y4, y5, y6, y7,
+    tok_ref, p1_ref, p2_ref, z_ref, y_ref,
     q_ref, k_ref, qg_ref, kg_ref, nqg_ref, nkg_ref, vg_ref, sum_ref, acc,
 ):
     index = lax.axis_index("seq")
+    column = jnp.right_shift(index, 3)
     place = jnp.bitwise_and(index, 7)
     odd = jnp.bitwise_and(index, 1)
     pieces = [z_ref[jnp.bitwise_xor(place, 1), FAR:], p1_ref[LEAF:]]
@@ -256,8 +259,8 @@
         rows = ROWS >> ROW_LEVEL[d]
         pieces.append(z_ref[jnp.bitwise_xor(place, d), FAR : FAR + rows])
         maps.append(spreading(0, rows, ROW_LEVEL[d]))
-    for d, y_ref in zip(range(1, 8), (y1, y2, y3, y4, y5, y6, y7)):
-        pieces.append(y_ref[...])
+    for d in range(1, 8):
+        pieces.append(y_ref[jnp.bitwise_xor(column, d)])
         maps.append(spreading(0, 16, COLUMN_LEVEL[d]))
     spread = jnp.concatenate(maps, axis=1).astype(BF16)
     acc[...] = tok_ref[...] + dot(spread, jnp.concatenate(pieces, axis=0), (1, 0))
@@ -271,7 +274,8 @@
         + token_sums(k_ref[...].astype(F32) * kg_ref[...] * key_total),
         axis=0,
     )
-    sum_ref[...] = tile
+    for i in range(sum_ref.shape[0]):
+        sum_ref[i] = tile
 
 
 def finish_kernel(width, sq_ref, inner_ref, q_ref, k_ref, qg_ref, kg_ref, nqg_ref, nkg_ref, dq_ref, dk_ref):
@@ -352,18 +356,16 @@
     p1 = lax.ppermute(p1, "seq", peer)
     p2 = lax.ppermute(p2, "seq", beside)
     zrecv = exchange(zsend, "seq", ROW_GROUPS)
-    ysend = call(column_kernel, [sds(16, 256) for _ in range(7)], (zrecv,), name="columns")
-    yrecv = [
-        lax.ppermute(ysend[d - 1], "seq", [(i, i ^ (8 * d)) for i in range(seq)]) for d in range(1, 8)
-    ]
+    ysend = call(column_kernel, sds(8, 16, 256), (zrecv,), name="columns")
+    yrecv = exchange(ysend, "seq", COLUMN_GROUPS)
     nkg, value_grad, inner = call(
         total_kernel,
-        [sds(ROWS, FEAT, dtype=F32), sds(ROWS, FEAT), sds(8, FEAT, dtype=F32)],
-        (tok, p1, p2, zrecv, *yrecv, queries, key_rows, qg, kg, nqg),
+        [sds(ROWS, FEAT, dtype=F32), sds(ROWS, FEAT), sds(heads, 8, FEAT, dtype=F32)],
+        (tok, p1, p2, zrecv, yrecv, queries, key_rows, qg, kg, nqg),
         scratch=[pltpu.VMEM((ROWS, 256), F32)],
         name="total",
     )
-    inner = lax.all_gather(inner, "head", axis=0)
+    inner = exchange(inner, "head")
     query_grad, key_grad = call(
         lambda *refs: finish_kernel(width, *refs),
         [sds(ROWS, FEAT), sds(ROWS, FEAT)],

time: 128 us -> 107 us (0.84)
  the two profiles are of different devices: /device:TPU:1 before, /device:TPU:32 now
where the time goes in v2:
time: 107 us
  blocking collectives  45.1 us (42%)
  starting transfers between devices  33.6 us (31%)
  waiting for transfers between devices  12.7 us (12%)
  Pallas kernels  12 us (11%)
  local copies, waits for them, and re-layouts  2.49 us (2%)
    all_to_all x4, blocking collectives, exchange(): return lax.all_to_all(x, axis, 0, 0, axis_index_groups=groups, tiled=True)  45.1 us
    all_to_all x2, starting transfers between devices, exchange(): return lax.all_to_all(x, axis, 0, 0, axis_index_groups=groups, tiled=True)  18.3 us
    pallas_call x7, Pallas kernels, call(): pl.pallas_call(kernel, out_shape=outs, scratch_shapes=list(scratch), comp...  12 us
    ppermute x2, waiting for transfers between devices, local(): p2 = lax.ppermute(p2, 'seq', beside)  10.4 us
    ppermute x2, starting transfers between devices, local(): p2 = lax.ppermute(p2, 'seq', beside)  8.87 us
    ppermute x2, starting transfers between devices, local(): p1 = lax.ppermute(p1, 'seq', peer)  6.38 us
    unnamed x16, local copies, waits for them, and re-layouts  2.49 us
    all_to_all x2, waiting for transfers between devices, exchange(): return lax.all_to_all(x, axis, 0, 0, axis_index_groups=groups, tiled=True)  2.27 us
  transfers between devices with their start and end apart: 6, of which 3 were waited for; matrix products, arithmetic and copies ran while one was open for 0% of the time, Pallas kernels for 0%

profile of v2, /device:TPU:32, one launch (start us, length us, event | category | flops | bytes accessed | tf_op | source)
XLA Modules:
  0.0 106.5 jit_solution(16770232367564031959)
XLA Ops:
  0.6 0.0 copy-start
  0.6 0.9 copy-done
  1.5 0.9 copy-done.2
  2.4 0.2 squares.1
  2.7 9.5 %all_to_all.30.refs_0_ = f32[8,8,128]{2,1,0:T(8,128)S(1)} all-to-all(f32[8,8,128]{2,1,0:T(8,128)S(1)} %squares.1), channel_id=1, replica_groups=mesh['seq'=64,'head'=8] {'head'}, dimensions={0} | all-to-all | bytes 65536 | tf_op jit(solution)/shard_map/all_to_all | solution.py:317
  12.2 0.0 copy-done.4
  12.2 0.6 copy-done.5
  12.9 0.0 copy-done.6
  12.9 0.5 norm.1
  13.4 9.9 %all_to_all.31.y_ref = bf16[8,16,256]{2,1,0:T(8,128)(2,1)S(1)} all-to-all(bf16[8,16,256]{2,1,0:T(8,128)(2,1)S(1)} %get-tuple-element.27), channel_id=1, replica_groups={{0,64,128,192,256,320,384,448},{8,72,136,200,264,328,392,456},{16,80,14..., dimensions={0} | all-to-all | bytes 131072 | tf_op jit(solution)/shard_map/all_to_all | solution.py:317
  23.3 0.9 rows.1
  24.3 10.4 %all-to-all-start.2 = ((bf16[8,112,256]{2,1,0:T(8,128)(2,1)}), bf16[8,112,256]{2,1,0:T(8,128)(2,1)S(1)}, u32[]{:S(2)}, u32[]{:S(2)}) async-start(bf16[8,112,256]{2,1,0:T(8,128)(2,1)} %rows.1), calls=%async_computation.2 | async-start | bytes 917504 | tf_op jit(solution)/shard_map/all_to_all | solution.py:317
  34.7 3.9 %collective-permute-start = (bf16[192,256]{1,0:T(8,128)(2,1)S(1)}, bf16[192,256]{1,0:T(8,128)(2,1)S(1)}, u32[]{:S(2)}, u32[]{:S(2)}) collective-permute-start(bf16[192,256]{1,0:T(8,128)(2,1)S(1)} %get-tuple-element.25), channel_id=1, source_target_pairs={{0,8},{8,0},{16,24},{24,16},{32,40},{40,32},{48,56},{56,48},{64,72... | collective-permute-start | bytes 294920 | tf_op jit(solution)/shard_map/ppermute | solution.py:337
  38.6 6.6 %collective-permute-start.1 = (bf16[128,256]{1,0:T(8,128)(2,1)S(1)}, bf16[128,256]{1,0:T(8,128)(2,1)S(1)}, u32[]{:S(2)}, u32[]{:S(2)}) collective-permute-start(bf16[128,256]{1,0:T(8,128)(2,1)S(1)} %get-tuple-element.26), channel_id=1, source_target_pairs={{8,16},{24,32},{40,48},{56,64},{72,80},{88,96},{104,112},{120,128}... | collective-permute-start | bytes 196616 | tf_op jit(solution)/shard_map/ppermute | solution.py:338
  45.3 3.2 %collective-permute-done.1.p2_ref = bf16[128,256]{1,0:T(8,128)(2,1)S(1)} collective-permute-done((bf16[128,256]{1,0:T(8,128)(2,1)S(1)}, bf16[128,256]{1,0:T(8,128)(2,1)S(1)}, u32[]{:S(2)}, u32[]{:S(2)}) %collective-permute-start.1) | collective-permute-done | bytes 65568 | tf_op jit(solution)/shard_map/ppermute | solution.py:338
  48.5 0.0 collective-permute-done.p1_ref
  48.5 2.3 %all-to-all-done.2.z_ref = bf16[8,112,256]{2,1,0:T(8,128)(2,1)S(1)} async-done(((bf16[8,112,256]{2,1,0:T(8,128)(2,1)}), bf16[8,112,256]{2,1,0:T(8,128)(2,1)S(1)}, u32[]{:S(2)}, u32[]{:S(2)}) %all-to-all-start.2) | async-done | bytes 458784 | tf_op jit(solution)/shard_map/all_to_all | solution.py:317
  50.7 0.0 copy-done.7
  50.7 7.1 %attend.1 = (bf16[512,128]{1,0:T(8,128)(2,1)}, f32[512,128]{1,0:T(8,128)S(1)}, f32[512,256]{1,0:T(8,128)S(1)}, bf16[192,256]{1,0:T(8,128)(2,1)S(1)}, bf16[128,25...) custom-call(bf16[512,128]{1,0:T(8,128)(2,1)S(1)} %get-tuple-element.22.qn_ref, ...), custom_call_target="tpu_custom_call" | custom-call | flops 2013265920 | bytes 2818048 | tf_op jit(solution)/shard_map/attend/pallas_call | solution.py:298
  57.9 17.8 %all_to_all.32.z_ref = bf16[8,112,256]{2,1,0:T(8,128)(2,1)S(1)} all-to-all(bf16[8,112,256]{2,1,0:T(8,128)(2,1)S(1)} %get-tuple-element.33), channel_id=1, replica_groups={{0,8,16,24,32,40,48,56},{64,72,80,88,96,104,112,120},{128,136,144,152,1..., dimensions={0} | all-to-all | bytes 917504 | tf_op jit(solution)/shard_map/all_to_all | solution.py:317
  75.6 0.8 columns.1
  76.4 7.9 %all-to-all-start.4 = ((bf16[8,16,256]{2,1,0:T(8,128)(2,1)}), bf16[8,16,256]{2,1,0:T(8,128)(2,1)S(1)}, u32[]{:S(2)}, u32[]{:S(2)}) async-start(bf16[8,16,256]{2,1,0:T(8,128)(2,1)} %columns.1), calls=%async_computation.4 | async-start | bytes 131072 | tf_op jit(solution)/shard_map/all_to_all | solution.py:317
  84.3 2.5 %collective-permute-start.2 = (bf16[192,256]{1,0:T(8,128)(2,1)S(1)}, bf16[192,256]{1,0:T(8,128)(2,1)S(1)}, u32[]{:S(2)}, u32[]{:S(2)}) collective-permute-start(bf16[192,256]{1,0:T(8,128)(2,1)S(1)} %get-tuple-element.31), channel_id=1, source_target_pairs={{0,8},{8,0},{16,24},{24,16},{32,40},{40,32},{48,56},{56,48},{64,72... | collective-permute-start | bytes 294920 | tf_op jit(solution)/shard_map/ppermute | solution.py:356
  86.8 2.2 %collective-permute-start.3 = (bf16[128,256]{1,0:T(8,128)(2,1)S(1)}, bf16[128,256]{1,0:T(8,128)(2,1)S(1)}, u32[]{:S(2)}, u32[]{:S(2)}) collective-permute-start(bf16[128,256]{1,0:T(8,128)(2,1)S(1)} %get-tuple-element.32), channel_id=1, source_target_pairs={{8,16},{24,32},{40,48},{56,64},{72,80},{88,96},{104,112},{120,128}... | collective-permute-start | bytes 196616 | tf_op jit(solution)/shard_map/ppermute | solution.py:357
  89.0 7.2 %collective-permute-done.3.p2_ref = bf16[128,256]{1,0:T(8,128)(2,1)S(1)} collective-permute-done((bf16[128,256]{1,0:T(8,128)(2,1)S(1)}, bf16[128,256]{1,0:T(8,128)(2,1)S(1)}, u32[]{:S(2)}, u32[]{:S(2)}) %collective-permute-start.3) | collective-permute-done | bytes 65568 | tf_op jit(solution)/shard_map/ppermute | solution.py:357
  96.3 0.0 collective-permute-done.2.p1_ref
  96.3 0.0 all-to-all-done.4.y_ref
  96.3 0.0 copy-done.3
  96.3 0.0 copy-done.1
  96.3 1.4 %total.1 = (f32[512,128]{1,0:T(8,128)S(1)}, bf16[512,128]{1,0:T(8,128)(2,1)}, f32[8,8,128]{2,1,0:T(8,128)S(1)}) custom-call(f32[512,256]{1,0:T(8,128)S(1)} %get-tuple-element.30.tok_ref, bf16[192,256]{1,0:T(8,128)(2,1)S(1)} %collective-permute-done.2.p1_ref, bf16[128,256]{1,0:T(8,128)(2,1)S(1)} %collective-permute-done.3.p2_ref, ...), custom_call_target="tpu_custom_call" | custom-call | bytes 2163712 | tf_op jit(solution)/shard_map/total/pallas_call | solution.py:298
  97.7 7.8 %all_to_all.33.refs_1_ = f32[8,8,128]{2,1,0:T(8,128)S(1)} all-to-all(f32[8,8,128]{2,1,0:T(8,128)S(1)} %get-tuple-element.35), channel_id=1, replica_groups=mesh['seq'=64,'head'=8] {'head'}, dimensions={0} | all-to-all | bytes 65536 | tf_op jit(solution)/shard_map/all_to_all | solution.py:317
  105.5 1.0 finish.1
  (7 shorter events, 0.0 us)
Async XLA Ops:
  0.6 0.9 copy-start
  1.5 0.9 copy-start.2
  2.4 9.8 %copy-start.4 = (bf16[512,128]{1,0:T(8,128)(2,1)S(1)}, bf16[512,128]{1,0:T(8,128)(2,1)}, u32[]{:S(2)}) copy-start(bf16[512,128]{1,0:T(8,128)(2,1)} %refs_3_.2) | copy-start | bytes 393220
  12.2 0.7 copy-start.5
  12.2 0.7 copy-start.6
  24.3 26.5 %copy-start.7 = (bf16[512,128]{1,0:T(8,128)(2,1)S(1)}, bf16[512,128]{1,0:T(8,128)(2,1)}, u32[]{:S(2)}) copy-start(bf16[512,128]{1,0:T(8,128)(2,1)} %g_ref.1) | copy-start | bytes 393220
  24.3 26.5 %all-to-all-start.2 = ((bf16[8,112,256]{2,1,0:T(8,128)(2,1)}), bf16[8,112,256]{2,1,0:T(8,128)(2,1)S(1)}, u32[]{:S(2)}, u32[]{:S(2)}) async-start(bf16[8,112,256]{2,1,0:T(8,128)(2,1)} %rows.1), calls=%async_computation.2 | async-start | bytes 917504 | tf_op jit(solution)/shard_map/all_to_all | solution.py:317
  34.7 13.8 %collective-permute-start = (bf16[192,256]{1,0:T(8,128)(2,1)S(1)}, bf16[192,256]{1,0:T(8,128)(2,1)S(1)}, u32[]{:S(2)}, u32[]{:S(2)}) collective-permute-start(bf16[192,256]{1,0:T(8,128)(2,1)S(1)} %get-tuple-element.25), channel_id=1, source_target_pairs={{0,8},{8,0},{16,24},{24,16},{32,40},{40,32},{48,56},{56,48},{64,72... | collective-permute-start | bytes 294920 | tf_op jit(solution)/shard_map/ppermute | solution.py:337
  38.6 9.8 %collective-permute-start.1 = (bf16[128,256]{1,0:T(8,128)(2,1)S(1)}, bf16[128,256]{1,0:T(8,128)(2,1)S(1)}, u32[]{:S(2)}, u32[]{:S(2)}) collective-permute-start(bf16[128,256]{1,0:T(8,128)(2,1)S(1)} %get-tuple-element.26), channel_id=1, source_target_pairs={{8,16},{24,32},{40,48},{56,64},{72,80},{88,96},{104,112},{120,128}... | collective-permute-start | bytes 196616 | tf_op jit(solution)/shard_map/ppermute | solution.py:338
  75.6 20.6 %copy-start.3 = (bf16[512,128]{1,0:T(8,128)(2,1)S(1)}, bf16[512,128]{1,0:T(8,128)(2,1)}, u32[]{:S(2)}) copy-start(bf16[512,128]{1,0:T(8,128)(2,1)} %refs_3_.3) | copy-start | bytes 393220
  76.4 19.9 %copy-start.1 = (bf16[512,128]{1,0:T(8,128)(2,1)S(1)}, bf16[512,128]{1,0:T(8,128)(2,1)}, u32[]{:S(2)}) copy-start(bf16[512,128]{1,0:T(8,128)(2,1)} %refs_2_.3) | copy-start | bytes 393220
  76.4 19.8 %all-to-all-start.4 = ((bf16[8,16,256]{2,1,0:T(8,128)(2,1)}), bf16[8,16,256]{2,1,0:T(8,128)(2,1)S(1)}, u32[]{:S(2)}, u32[]{:S(2)}) async-start(bf16[8,16,256]{2,1,0:T(8,128)(2,1)} %columns.1), calls=%async_computation.4 | async-start | bytes 131072 | tf_op jit(solution)/shard_map/all_to_all | solution.py:317
  84.3 12.0 %collective-permute-start.2 = (bf16[192,256]{1,0:T(8,128)(2,1)S(1)}, bf16[192,256]{1,0:T(8,128)(2,1)S(1)}, u32[]{:S(2)}, u32[]{:S(2)}) collective-permute-start(bf16[192,256]{1,0:T(8,128)(2,1)S(1)} %get-tuple-element.31), channel_id=1, source_target_pairs={{0,8},{8,0},{16,24},{24,16},{32,40},{40,32},{48,56},{56,48},{64,72... | collective-permute-start | bytes 294920 | tf_op jit(solution)/shard_map/ppermute | solution.py:356
  86.8 9.5 %collective-permute-start.3 = (bf16[128,256]{1,0:T(8,128)(2,1)S(1)}, bf16[128,256]{1,0:T(8,128)(2,1)S(1)}, u32[]{:S(2)}, u32[]{:S(2)}) collective-permute-start(bf16[128,256]{1,0:T(8,128)(2,1)S(1)} %get-tuple-element.32), channel_id=1, source_target_pairs={{8,16},{24,32},{40,48},{56,64},{72,80},{88,96},{104,112},{120,128}... | collective-permute-start | bytes 196616 | tf_op jit(solution)/shard_map/ppermute | solution.py:357

commit v3 on v2

--- a/solution.py
+++ b/solution.py
@@ -87,7 +87,7 @@
 
 def norm_kernel(width, sum_ref, q_ref, k_ref, v_ref, qg_ref, kg_ref, qn_ref, kv_ref, one_ref, lv_ref, y_ref, p1_ref, p2_ref):
     index = lax.axis_index("seq")
-    column = jnp.right_shift(index, 3)
+    place = jnp.bitwise_and(index, 7)
     odd = jnp.bitwise_and(index, 1)
     total = jnp.sum(sum_ref[...], axis=0)
     rate = lax.rsqrt(total / width + EPS)
@@ -105,37 +105,37 @@
     ).astype(BF16)
     coarse = dot(pool, kv_ref[...], (1, 0)).astype(BF16)
     one_ref[...] = coarse[:256]
-    lv_ref[...] = coarse[256:480]
-    y_ref[column] = jnp.zeros((16, 2 * FEAT), BF16)
+    lv_ref[place] = jnp.zeros((64, 2 * FEAT), BF16)
     for d in range(1, 8):
-        y_ref[jnp.bitwise_xor(column, d)] = coarse[464 + 16 * d : 480 + 16 * d]
+        other = jnp.bitwise_xor(place, d)
+        if d == 1:
+            lv_ref[other] = coarse[256:320]
+        elif d < 4:
+            lv_ref[other] = coarse[384:448]
+        else:
+            lv_ref[other, :32] = coarse[448:480]
+            lv_ref[other, 32:] = jnp.zeros((32, 2 * FEAT), BF16)
+    for m in range(64):
+        d = m >> 3
+        piece = coarse[464 + 16 * d : 480 + 16 * d] if d else jnp.zeros((16, 2 * FEAT), BF16)
+        y_ref[jnp.bitwise_xor(index, m)] = piece
     p1_ref[:LEAF] = kv_ref[pl.ds(pl.multiple_of((1 - odd) * 384, LEAF), LEAF)]
     p1_ref[LEAF:] = coarse[320:384]
     p2_ref[...] = kv_ref[pl.ds(pl.multiple_of(odd * 384, LEAF), LEAF)]
 
 
-def row_kernel(y_ref, lv_ref, out_ref):
+def far_kernel(y_ref, out_ref):
     index = lax.axis_index("seq")
-    column = jnp.right_shift(index, 3)
-    place = jnp.bitwise_and(index, 7)
-    slots = jnp.concatenate([y_ref[jnp.bitwise_xor(column, d)] for d in range(1, 8)], axis=0)
-    far = dot(far_pick((FAR, 112), 0), slots, (1, 0)).astype(BF16)
-    for s in range(8):
-        out_ref[s, :FAR] = far
-    out_ref[place, FAR:] = jnp.zeros((64, 2 * FEAT), BF16)
-    for d in range(1, 8):
-        other = jnp.bitwise_xor(place, d)
-        if d == 1:
-            out_ref[other, FAR:] = lv_ref[:64]
-        elif d < 4:
-            out_ref[other, FAR:] = lv_ref[128:192]
-        else:
-            out_ref[other, FAR : FAR + 32] = lv_ref[192:224]
-            out_ref[other, FAR + 32 :] = jnp.zeros((32, 2 * FEAT), BF16)
+    pick = far_pick((FAR, 112), 0)
+    for d in range(8):
+        slots = jnp.concatenate(
+            [y_ref[jnp.bitwise_xor(index, 8 * c + d)] for c in range(1, 8)], axis=0
+        )
+        out_ref[d] = dot(pick, slots, (1, 0)).astype(BF16)
 
 
 def attend_kernel(
-    qn_ref, kv_ref, one_ref, g_ref, p1_ref, p2_ref, z_ref,
+    qn_ref, kv_ref, one_ref, g_ref, p1_ref, p2_ref, z_ref, far_ref,
     att_ref, nqg_ref, tok_ref, p1o_ref, p2o_ref, zo_ref,
     near, cross, near_grad, one_grad, cross_grad,
 ):
@@ -148,14 +148,14 @@
     near[LEAF : LEAF + ROWS] = kv_ref[...]
     near[pl.ds(peer_side, LEAF)] = p1_ref[:LEAF]
     near[pl.ds(other_side, LEAF)] = p2_ref[...]
-    cross[:64] = z_ref[jnp.bitwise_xor(place, 1), FAR:]
+    cross[:64] = z_ref[jnp.bitwise_xor(place, 1)]
     cross[64:128] = p1_ref[LEAF:]
-    cross[128:192] = z_ref[jnp.bitwise_xor(place, 2), FAR:]
-    cross[192:256] = z_ref[jnp.bitwise_xor(place, 3), FAR:]
+    cross[128:192] = z_ref[jnp.bitwise_xor(place, 2)]
+    cross[192:256] = z_ref[jnp.bitwise_xor(place, 3)]
     for i in range(4):
-        cross[256 + 32 * i : 288 + 32 * i] = z_ref[jnp.bitwise_xor(place, 4 + i), FAR : FAR + 32]
-    for s in range(8):
-        cross[384 + FAR * s : 384 + FAR * (s + 1)] = z_ref[s, :FAR]
+        cross[256 + 32 * i : 288 + 32 * i] = z_ref[jnp.bitwise_xor(place, 4 + i), :32]
+    for d in range(8):
+        cross[384 + FAR * d : 384 + FAR * (d + 1)] = far_ref[d]
 
     def level_bias(rows, level):
         return jnp.full((rows, 2 * LEAF), level * LN2, F32)
@@ -224,8 +224,9 @@
     p1o_ref[:LEAF] = near_grad[pl.ds(peer_side, LEAF)].astype(BF16)
     p1o_ref[LEAF:] = cross_grad[64:128].astype(BF16)
     p2o_ref[...] = near_grad[pl.ds(other_side, LEAF)].astype(BF16)
-    for s in range(8):
-        zo_ref[s, :FAR] = cross_grad[384 + FAR * s : 384 + FAR * (s + 1)].astype(BF16)
+    for d in range(8):
+        rows = slice(384 + FAR * d, 384 + FAR * (d + 1))
+        zo_ref[jnp.bitwise_xor(place, d), :FAR] = cross_grad[rows].astype(BF16)
     zo_ref[place, FAR:] = jnp.zeros((64, 2 * FEAT), BF16)
     zo_ref[jnp.bitwise_xor(place, 1), FAR:] = cross_grad[:64].astype(BF16)
     zo_ref[jnp.bitwise_xor(place, 2), FAR:] = cross_grad[128:192].astype(BF16)
@@ -330,19 +331,19 @@
     squares = exchange(squares, "head")
     qn, kv, one, lv, ysend, p1, p2 = call(
         lambda *refs: norm_kernel(width, *refs),
-        [sds(ROWS, FEAT), sds(ROWS, 256), sds(256, 256), sds(224, 256), sds(8, 16, 256), sds(192, 256), sds(LEAF, 256)],
+        [sds(ROWS, FEAT), sds(ROWS, 256), sds(256, 256), sds(8, 64, 256), sds(seq, 16, 256), sds(192, 256), sds(LEAF, 256)],
         (squares, queries, key_rows, value_rows, qg, kg),
         name="norm",
     )
     p1 = lax.ppermute(p1, "seq", peer)
     p2 = lax.ppermute(p2, "seq", beside)
-    yrecv = exchange(ysend, "seq", COLUMN_GROUPS)
-    zsend = call(row_kernel, sds(8, SLOT, 256), (yrecv, lv), name="rows")
-    zrecv = exchange(zsend, "seq", ROW_GROUPS)
+    yrecv = exchange(ysend, "seq")
+    zrecv = exchange(lv, "seq", ROW_GROUPS)
+    far = call(far_kernel, sds(8, FAR, 256), (yrecv,), name="far")
     attended, nqg, tok, p1, p2, zsend = call(
         attend_kernel,
         [sds(ROWS, FEAT), sds(ROWS, FEAT, dtype=F32), sds(ROWS, 256, dtype=F32), sds(192, 256), sds(LEAF, 256), sds(8, SLOT, 256)],
-        (qn, kv, one, out_grad, p1, p2, zrecv),
+        (qn, kv, one, out_grad, p1, p2, zrecv, far),
         scratch=[
             pltpu.VMEM((768, 256), BF16),
             pltpu.VMEM((768, 256), BF16),

time: 107 us -> 118 us (1.10)
  blocking collectives: 45.1 us -> 66.4 us
  starting transfers between devices: 33.6 us -> 26.1 us
  waiting for transfers between devices: 12.7 us -> 9.67 us
    all_to_all x4, blocking collectives: 45.1 us -> 66.4 us  [exchange(): return lax.all_to_all(x, axis, 0, 0, axis_index_groups=groups, tiled=True)]
    all_to_all x2, starting transfers between devices: 18.3 us -> 10.7 us  [exchange(): return lax.all_to_all(x, axis, 0, 0, axis_index_groups=groups, tiled=True)]
    all_to_all x2, waiting for transfers between devices: 2.27 us -> 0.01 us  [exchange(): return lax.all_to_all(x, axis, 0, 0, axis_index_groups=groups, tiled=True)]
  transfers between devices with their start and end apart: 6 -> 6, of which waited for: 3 -> 2; matrix products, arithmetic and copies ran while one was open for 0% -> 0% of each run, Pallas kernels for 0% -> 0%
where the time goes in v3:
time: 118 us; the launch traced here: 117 us
  blocking collectives  66.4 us (56%)
  starting transfers between devices  26.1 us (22%)
  Pallas kernels  12 us (10%)
  waiting for transfers between devices  9.67 us (8%)
  local copies, waits for them, and re-layouts  2.49 us (2%)
    all_to_all x4, blocking collectives, exchange(): return lax.all_to_all(x, axis, 0, 0, axis_index_groups=groups, tiled=True)  66.4 us
    pallas_call x7, Pallas kernels, call(): pl.pallas_call(kernel, out_shape=outs, scratch_shapes=list(scratch), comp...  12 us
    all_to_all x2, starting transfers between devices, exchange(): return lax.all_to_all(x, axis, 0, 0, axis_index_groups=groups, tiled=True)  10.7 us
    ppermute x2, waiting for transfers between devices, local(): p2 = lax.ppermute(p2, 'seq', beside)  9.66 us
    ppermute x2, starting transfers between devices, local(): p2 = lax.ppermute(p2, 'seq', beside)  9.2 us
    ppermute x2, starting transfers between devices, local(): p1 = lax.ppermute(p1, 'seq', peer)  6.19 us
    unnamed x16, local copies, waits for them, and re-layouts  2.49 us
  transfers between devices with their start and end apart: 6, of which 2 were waited for; matrix products, arithmetic and copies ran while one was open for 0% of the time, Pallas kernels for 0%

profile of v3, /device:TPU:32, one launch (start us, length us, event | category | flops | bytes accessed | tf_op | source)
XLA Modules:
  0.0 117.4 jit_solution(15890541875732218439)
XLA Ops:
  0.6 0.0 copy-start
  0.6 0.9 copy-done
  1.5 0.9 copy-done.2
  2.4 0.2 squares.1
  2.7 9.5 %all_to_all.30.refs_0_ = f32[8,8,128]{2,1,0:T(8,128)S(1)} all-to-all(f32[8,8,128]{2,1,0:T(8,128)S(1)} %squares.1), channel_id=1, replica_groups=mesh['seq'=64,'head'=8] {'head'}, dimensions={0} | all-to-all | bytes 65536 | tf_op jit(solution)/shard_map/all_to_all | solution.py:318
  12.2 0.0 copy-done.4
  12.2 0.6 copy-done.5
  12.9 0.0 copy-done.6
  12.9 1.2 %norm.1 = (bf16[512,128]{1,0:T(8,128)(2,1)S(1)}, bf16[512,256]{1,0:T(8,128)(2,1)S(1)}, bf16[256,256]{1,0:T(8,128)(2,1)S(1)}, bf16[8,64,256]{2,1,0:T(8,128)(2,1)}...) custom-call(f32[8,8,128]{2,1,0:T(8,128)S(1)} %all_to_all.30.refs_0_, ...), custom_call_target="tpu_custom_call" | custom-call | bytes 1901568 | tf_op jit(solution)/shard_map/norm/pallas_call | solution.py:299
  14.1 32.6 %all_to_all.31.y_ref = bf16[64,16,256]{2,1,0:T(8,128)(2,1)S(1)} all-to-all(bf16[64,16,256]{2,1,0:T(8,128)(2,1)S(1)} %get-tuple-element.28), channel_id=1, replica_groups=mesh['seq'=64,'head'=8] {'seq'}, dimensions={0} | all-to-all | bytes 1048576 | tf_op jit(solution)/shard_map/all_to_all | solution.py:318
  46.6 3.4 %all-to-all-start.1 = ((bf16[8,64,256]{2,1,0:T(8,128)(2,1)}), bf16[8,64,256]{2,1,0:T(8,128)(2,1)S(1)}, u32[]{:S(2)}, u32[]{:S(2)}) async-start(bf16[8,64,256]{2,1,0:T(8,128)(2,1)} %get-tuple-element.27), calls=%async_computation.1 | async-start | bytes 524288 | tf_op jit(solution)/shard_map/all_to_all | solution.py:318
  50.0 3.8 %collective-permute-start = (bf16[192,256]{1,0:T(8,128)(2,1)S(1)}, bf16[192,256]{1,0:T(8,128)(2,1)S(1)}, u32[]{:S(2)}, u32[]{:S(2)}) collective-permute-start(bf16[192,256]{1,0:T(8,128)(2,1)S(1)} %get-tuple-element.25), channel_id=1, source_target_pairs={{0,8},{8,0},{16,24},{24,16},{32,40},{40,32},{48,56},{56,48},{64,72... | collective-permute-start | bytes 294920 | tf_op jit(solution)/shard_map/ppermute | solution.py:338
  53.9 0.0 copy-start.7
  53.9 6.9 %collective-permute-start.1 = (bf16[128,256]{1,0:T(8,128)(2,1)S(1)}, bf16[128,256]{1,0:T(8,128)(2,1)S(1)}, u32[]{:S(2)}, u32[]{:S(2)}) collective-permute-start(bf16[128,256]{1,0:T(8,128)(2,1)S(1)} %get-tuple-element.26), channel_id=1, source_target_pairs={{8,16},{24,32},{40,48},{56,64},{72,80},{88,96},{104,112},{120,128}... | collective-permute-start | bytes 196616 | tf_op jit(solution)/shard_map/ppermute | solution.py:339
  60.7 0.2 far.1.far_ref
  61.0 2.5 %collective-permute-done.1.p2_ref = bf16[128,256]{1,0:T(8,128)(2,1)S(1)} collective-permute-done((bf16[128,256]{1,0:T(8,128)(2,1)S(1)}, bf16[128,256]{1,0:T(8,128)(2,1)S(1)}, u32[]{:S(2)}, u32[]{:S(2)}) %collective-permute-start.1) | collective-permute-done | bytes 65568 | tf_op jit(solution)/shard_map/ppermute | solution.py:339
  63.5 0.0 collective-permute-done.p1_ref
  63.5 0.0 all-to-all-done.1.z_ref
  63.5 0.0 copy-done.7
  63.5 7.1 %attend.1 = (bf16[512,128]{1,0:T(8,128)(2,1)}, f32[512,128]{1,0:T(8,128)S(1)}, f32[512,256]{1,0:T(8,128)S(1)}, bf16[192,256]{1,0:T(8,128)(2,1)S(1)}, bf16[128,25...) custom-call(bf16[512,128]{1,0:T(8,128)(2,1)S(1)} %get-tuple-element.22.qn_ref, ...), custom_call_target="tpu_custom_call" | custom-call | flops 2013265920 | bytes 2818048 | tf_op jit(solution)/shard_map/attend/pallas_call | solution.py:299
  70.6 16.5 %all_to_all.32.z_ref = bf16[8,112,256]{2,1,0:T(8,128)(2,1)S(1)} all-to-all(bf16[8,112,256]{2,1,0:T(8,128)(2,1)S(1)} %get-tuple-element.33), channel_id=1, replica_groups={{0,8,16,24,32,40,48,56},{64,72,80,88,96,104,112,120},{128,136,144,152,1..., dimensions={0} | all-to-all | bytes 917504 | tf_op jit(solution)/shard_map/all_to_all | solution.py:318
  87.1 0.8 columns.1
  87.9 7.3 %all-to-all-start.4 = ((bf16[8,16,256]{2,1,0:T(8,128)(2,1)}), bf16[8,16,256]{2,1,0:T(8,128)(2,1)S(1)}, u32[]{:S(2)}, u32[]{:S(2)}) async-start(bf16[8,16,256]{2,1,0:T(8,128)(2,1)} %columns.1), calls=%async_computation.4 | async-start | bytes 131072 | tf_op jit(solution)/shard_map/all_to_all | solution.py:318
  95.2 2.4 %collective-permute-start.2 = (bf16[192,256]{1,0:T(8,128)(2,1)S(1)}, bf16[192,256]{1,0:T(8,128)(2,1)S(1)}, u32[]{:S(2)}, u32[]{:S(2)}) collective-permute-start(bf16[192,256]{1,0:T(8,128)(2,1)S(1)} %get-tuple-element.31), channel_id=1, source_target_pairs={{0,8},{8,0},{16,24},{24,16},{32,40},{40,32},{48,56},{56,48},{64,72... | collective-permute-start | bytes 294920 | tf_op jit(solution)/shard_map/ppermute | solution.py:357
  97.6 2.3 %collective-permute-start.3 = (bf16[128,256]{1,0:T(8,128)(2,1)S(1)}, bf16[128,256]{1,0:T(8,128)(2,1)S(1)}, u32[]{:S(2)}, u32[]{:S(2)}) collective-permute-start(bf16[128,256]{1,0:T(8,128)(2,1)S(1)} %get-tuple-element.32), channel_id=1, source_target_pairs={{8,16},{24,32},{40,48},{56,64},{72,80},{88,96},{104,112},{120,128}... | collective-permute-start | bytes 196616 | tf_op jit(solution)/shard_map/ppermute | solution.py:358
  100.0 7.1 %collective-permute-done.3.p2_ref = bf16[128,256]{1,0:T(8,128)(2,1)S(1)} collective-permute-done((bf16[128,256]{1,0:T(8,128)(2,1)S(1)}, bf16[128,256]{1,0:T(8,128)(2,1)S(1)}, u32[]{:S(2)}, u32[]{:S(2)}) %collective-permute-start.3) | collective-permute-done | bytes 65568 | tf_op jit(solution)/shard_map/ppermute | solution.py:358
  107.1 0.0 collective-permute-done.2.p1_ref
  107.1 0.0 all-to-all-done.4.y_ref
  107.1 0.0 copy-done.3
  107.1 1.4 %total.1 = (f32[512,128]{1,0:T(8,128)S(1)}, bf16[512,128]{1,0:T(8,128)(2,1)}, f32[8,8,128]{2,1,0:T(8,128)S(1)}) custom-call(f32[512,256]{1,0:T(8,128)S(1)} %get-tuple-element.30.tok_ref, bf16[192,256]{1,0:T(8,128)(2,1)S(1)} %collective-permute-done.2.p1_ref, bf16[128,256]{1,0:T(8,128)(2,1)S(1)} %collective-permute-done.3.p2_ref, ...), custom_call_target="tpu_custom_call" | custom-call | bytes 2163712 | tf_op jit(solution)/shard_map/total/pallas_call | solution.py:299
  108.5 7.8 %all_to_all.33.refs_1_ = f32[8,8,128]{2,1,0:T(8,128)S(1)} all-to-all(f32[8,8,128]{2,1,0:T(8,128)S(1)} %get-tuple-element.35), channel_id=1, replica_groups=mesh['seq'=64,'head'=8] {'head'}, dimensions={0} | all-to-all | bytes 65536 | tf_op jit(solution)/shard_map/all_to_all | solution.py:318
  116.3 1.0 finish.1
  (7 shorter events, 0.0 us)
Async XLA Ops:
  0.6 0.9 copy-start
  1.5 0.9 copy-start.2
  2.4 9.8 %copy-start.4 = (bf16[512,128]{1,0:T(8,128)(2,1)S(1)}, bf16[512,128]{1,0:T(8,128)(2,1)}, u32[]{:S(2)}) copy-start(bf16[512,128]{1,0:T(8,128)(2,1)} %refs_3_.2) | copy-start | bytes 393220
  12.2 0.7 copy-start.5
  12.2 0.7 copy-start.6
  46.6 16.9 %all-to-all-start.1 = ((bf16[8,64,256]{2,1,0:T(8,128)(2,1)}), bf16[8,64,256]{2,1,0:T(8,128)(2,1)S(1)}, u32[]{:S(2)}, u32[]{:S(2)}) async-start(bf16[8,64,256]{2,1,0:T(8,128)(2,1)} %get-tuple-element.27), calls=%async_computation.1 | async-start | bytes 524288 | tf_op jit(solution)/shard_map/all_to_all | solution.py:318
  50.0 13.5 %collective-permute-start = (bf16[192,256]{1,0:T(8,128)(2,1)S(1)}, bf16[192,256]{1,0:T(8,128)(2,1)S(1)}, u32[]{:S(2)}, u32[]{:S(2)}) collective-permute-start(bf16[192,256]{1,0:T(8,128)(2,1)S(1)} %get-tuple-element.25), channel_id=1, source_target_pairs={{0,8},{8,0},{16,24},{24,16},{32,40},{40,32},{48,56},{56,48},{64,72... | collective-permute-start | bytes 294920 | tf_op jit(solution)/shard_map/ppermute | solution.py:338
  53.9 9.6 %copy-start.7 = (bf16[512,128]{1,0:T(8,128)(2,1)S(1)}, bf16[512,128]{1,0:T(8,128)(2,1)}, u32[]{:S(2)}) copy-start(bf16[512,128]{1,0:T(8,128)(2,1)} %g_ref.1) | copy-start | bytes 393220
  53.9 9.6 %collective-permute-start.1 = (bf16[128,256]{1,0:T(8,128)(2,1)S(1)}, bf16[128,256]{1,0:T(8,128)(2,1)S(1)}, u32[]{:S(2)}, u32[]{:S(2)}) collective-permute-start(bf16[128,256]{1,0:T(8,128)(2,1)S(1)} %get-tuple-element.26), channel_id=1, source_target_pairs={{8,16},{24,32},{40,48},{56,64},{72,80},{88,96},{104,112},{120,128}... | collective-permute-start | bytes 196616 | tf_op jit(solution)/shard_map/ppermute | solution.py:339
  87.1 20.0 %copy-start.3 = (bf16[512,128]{1,0:T(8,128)(2,1)S(1)}, bf16[512,128]{1,0:T(8,128)(2,1)}, u32[]{:S(2)}) copy-start(bf16[512,128]{1,0:T(8,128)(2,1)} %refs_3_.3) | copy-start | bytes 393220
  87.9 19.2 %copy-start.1 = (bf16[512,128]{1,0:T(8,128)(2,1)S(1)}, bf16[512,128]{1,0:T(8,128)(2,1)}, u32[]{:S(2)}) copy-start(bf16[512,128]{1,0:T(8,128)(2,1)} %refs_2_.3) | copy-start | bytes 393220
  87.9 19.2 %all-to-all-start.4 = ((bf16[8,16,256]{2,1,0:T(8,128)(2,1)}), bf16[8,16,256]{2,1,0:T(8,128)(2,1)S(1)}, u32[]{:S(2)}, u32[]{:S(2)}) async-start(bf16[8,16,256]{2,1,0:T(8,128)(2,1)} %columns.1), calls=%async_computation.4 | async-start | bytes 131072 | tf_op jit(solution)/shard_map/all_to_all | solution.py:318
  95.2 11.9 %collective-permute-start.2 = (bf16[192,256]{1,0:T(8,128)(2,1)S(1)}, bf16[192,256]{1,0:T(8,128)(2,1)S(1)}, u32[]{:S(2)}, u32[]{:S(2)}) collective-permute-start(bf16[192,256]{1,0:T(8,128)(2,1)S(1)} %get-tuple-element.31), channel_id=1, source_target_pairs={{0,8},{8,0},{16,24},{24,16},{32,40},{40,32},{48,56},{56,48},{64,72... | collective-permute-start | bytes 294920 | tf_op jit(solution)/shard_map/ppermute | solution.py:357
  97.6 9.5 %collective-permute-start.3 = (bf16[128,256]{1,0:T(8,128)(2,1)S(1)}, bf16[128,256]{1,0:T(8,128)(2,1)S(1)}, u32[]{:S(2)}, u32[]{:S(2)}) collective-permute-start(bf16[128,256]{1,0:T(8,128)(2,1)S(1)} %get-tuple-element.32), channel_id=1, source_target_pairs={{8,16},{24,32},{40,48},{56,64},{72,80},{88,96},{104,112},{120,128}... | collective-permute-start | bytes 196616 | tf_op jit(solution)/shard_map/ppermute | solution.py:358

commit v4 on v2

--- a/solution.py
+++ b/solution.py
@@ -17,7 +17,7 @@
 LN2 = math.log(2.0)
 F32 = jnp.float32
 BF16 = jnp.bfloat16
-PARAMS = pltpu.CompilerParams(vmem_limit_bytes=40 * 1024 * 1024)
+MIB = 1024 * 1024
 ROW_LEVEL = {1: 2, 2: 3, 3: 3, 4: 4, 5: 4, 6: 4, 7: 4}
 COLUMN_LEVEL = {1: 5, 2: 6, 3: 6, 4: 7, 5: 7, 6: 7, 7: 7}
 FAR = 48
@@ -134,20 +134,67 @@
             out_ref[other, FAR + 32 :] = jnp.zeros((32, 2 * FEAT), BF16)
 
 
+def by_head(block):
+    lane = iota((LEAF, FEAT), 1)
+    zero = jnp.zeros((LEAF, FEAT), BF16)
+    return jnp.concatenate(
+        [jnp.where(lane < HEAD, block, zero), jnp.where(lane < HEAD, zero, block)], axis=0
+    )
+
+
+def peak(x):
+    return jnp.max(x, axis=0, keepdims=True)
+
+
+def add_up(x):
+    return jnp.sum(x, axis=0, keepdims=True)
+
+
+HALO_PIECE = {0: 0, LEAVES - 1: 2}
+
+
+def near_kernel(qn_ref, kv_ref, one_ref, g_ref, q2_ref, g2_ref, weight_ref, pgrad_ref, stat_ref):
+    for b in range(LEAVES):
+        rows = slice(b * LEAF, (b + 1) * LEAF)
+        q2 = by_head(qn_ref[rows]) * jnp.asarray(0.125, BF16)
+        g2 = by_head(g_ref[rows])
+        q2_ref[b] = q2
+        g2_ref[b] = g2
+        half = (1 - b // 2) * LEAF
+        kv = [
+            None if HALO_PIECE.get(b) == i else kv_ref[(b + i - 1) * LEAF : (b + i) * LEAF]
+            for i in range(3)
+        ] + [one_ref[half : half + LEAF]]
+        scores = {
+            i: dot(x[:, :FEAT], q2, (1, 1)) + (LN2 if i == 3 else 0.0)
+            for i, x in enumerate(kv)
+            if x is not None
+        }
+        top = peak(jnp.concatenate([peak(x) for x in scores.values()], axis=0))
+        total = jnp.zeros((1, 2 * LEAF), F32)
+        mixed = jnp.zeros((1, 2 * LEAF), F32)
+        for i, score in scores.items():
+            weight = jnp.exp(score - top)
+            pgrad = dot(kv[i][:, FEAT:], g2, (1, 1))
+            weight_ref[b, i * LEAF : (i + 1) * LEAF] = weight
+            pgrad_ref[b, i * LEAF : (i + 1) * LEAF] = pgrad
+            total = total + add_up(weight)
+            mixed = mixed + add_up(weight * pgrad)
+        stat_ref[b] = jnp.concatenate([top, total, mixed, jnp.zeros((5, 2 * LEAF), F32)], axis=0)
+
+
 def attend_kernel(
-    qn_ref, kv_ref, one_ref, g_ref, p1_ref, p2_ref, z_ref,
-    att_ref, nqg_ref, tok_ref, p1o_ref, p2o_ref, zo_ref,
-    near, cross, near_grad, one_grad, cross_grad,
+    q2_ref, g2_ref, weight_ref, pgrad_ref, stat_ref, p1_ref, p2_ref, z_ref,
+    low_ref, sgrad_ref, cross, halo, p1o_ref, p2o_ref, zo_ref,
+    score_scr, pgrad_scr, cross_grad, rims,
 ):
     index = lax.axis_index("seq")
     last = lax.axis_size("seq") - 1
     place = jnp.bitwise_and(index, 7)
     odd = jnp.bitwise_and(index, 1)
-    peer_side = pl.multiple_of((1 - odd) * 640, LEAF)
-    other_side = pl.multiple_of(odd * 640, LEAF)
-    near[LEAF : LEAF + ROWS] = kv_ref[...]
-    near[pl.ds(peer_side, LEAF)] = p1_ref[:LEAF]
-    near[pl.ds(other_side, LEAF)] = p2_ref[...]
+    peer_side = 1 - odd
+    halo[peer_side] = p1_ref[:LEAF]
+    halo[odd] = p2_ref[...]
     cross[:64] = z_ref[jnp.bitwise_xor(place, 1), FAR:]
     cross[64:128] = p1_ref[LEAF:]
     cross[128:192] = z_ref[jnp.bitwise_xor(place, 2), FAR:]
@@ -161,69 +208,74 @@
         return jnp.full((rows, 2 * LEAF), level * LN2, F32)
 
     bias = jnp.concatenate(
-        [level_bias(LEAF, level) for level in (1, 2, 3, 4)]
+        [level_bias(LEAF, level) for level in (2, 3, 4)]
         + [level_bias(16, level) for _ in range(8) for level in (5, 6, 7)],
         axis=0,
     )
-    left = jnp.where(index > 0, 0.0, -jnp.inf).astype(F32)
-    right = jnp.where(index < last, 0.0, -jnp.inf).astype(F32)
-    lane = iota((LEAF, FEAT), 1)
-    feature = iota((FEAT, LEAF), 0)
-    zero = jnp.zeros((LEAF, FEAT), BF16)
-
-    def by_head(block):
-        return jnp.concatenate(
-            [jnp.where(lane < HEAD, block, zero), jnp.where(lane < HEAD, zero, block)], axis=0
-        )
-
-    def merge_heads(transposed):
-        return jnp.where(feature < HEAD, transposed[:, :LEAF], transposed[:, LEAF:]).T
-
-    near_grad[...] = jnp.zeros_like(near_grad)
-    one_grad[...] = jnp.zeros_like(one_grad)
+    outside = {
+        0: jnp.where(index > 0, 0.0, -jnp.inf).astype(F32),
+        LEAVES - 1: jnp.where(index < last, 0.0, -jnp.inf).astype(F32),
+    }
     for b in range(LEAVES):
-        rows = slice(b * LEAF, (b + 1) * LEAF)
-        near_rows = slice(b * LEAF, (b + 3) * LEAF)
-        half = (1 - b // 2) * LEAF
-        q2 = by_head(qn_ref[rows]) * jnp.asarray(0.125, BF16)
-        g2 = by_head(g_ref[rows])
-        kv = jnp.concatenate([near[near_rows], one_ref[half : half + LEAF], cross[...]], axis=0)
-        keys = kv[:, :FEAT]
-        values = kv[:, FEAT:]
-        raw = dot(keys, q2, (1, 1))
-        before, after = raw[:LEAF], raw[2 * LEAF : 3 * LEAF]
-        if b == 0:
-            before = before + left
-        if b == LEAVES - 1:
-            after = after + right
-        scores = jnp.concatenate(
-            [before, raw[LEAF : 2 * LEAF], after, raw[3 * LEAF :] + bias], axis=0
-        )
-        weights = jnp.exp(scores - jnp.max(scores, axis=0, keepdims=True))
-        probs = weights * (1.0 / jnp.sum(weights, axis=0, keepdims=True))
-        low = probs.astype(BF16)
-        prob_grad = dot(values, g2, (1, 1))
-        delta = jnp.sum(probs * prob_grad, axis=0, keepdims=True)
-        score_grad = (probs * (prob_grad - delta)).astype(BF16)
-        att_ref[rows] = merge_heads(dot(values, low, (0, 0))).astype(BF16)
-        nqg_ref[rows] = merge_heads(dot(keys, score_grad, (0, 0))) * 0.125
-        key_part = dot(score_grad, q2, (1, 0))
-        value_part = dot(low, g2, (1, 0))
-        for part, lanes in ((key_part, slice(0, FEAT)), (value_part, slice(FEAT, 2 * FEAT))):
-            near_grad[near_rows, lanes] += part[: 3 * LEAF]
-            one_grad[half : half + LEAF, lanes] += part[3 * LEAF : 4 * LEAF]
+        q2 = q2_ref[b]
+        g2 = g2_ref[b]
+        near_top = stat_ref[b, 0:1]
+        top = near_top
+        pieces = []
+        if b in HALO_PIECE:
+            side = halo[0 if b == 0 else 1]
+            score = dot(side[:, :FEAT], q2, (1, 1)) + outside[b]
+            top = jnp.maximum(top, peak(score))
+            score_scr[6 * LEAF :] = score
+            pgrad_scr[6 * LEAF :] = dot(side[:, FEAT:], g2, (1, 1))
+            pieces.append((6 * LEAF, HALO_PIECE[b] * LEAF))
+        for i in range(6):
+            rows = slice(i * LEAF, (i + 1) * LEAF)
+            score = dot(cross[rows, :FEAT], q2, (1, 1)) + bias[rows]
+            top = jnp.maximum(top, peak(score))
+            score_scr[rows] = score
+            pgrad_scr[rows] = dot(cross[rows, FEAT:], g2, (1, 1))
+            pieces.append((i * LEAF, (4 + i) * LEAF))
+        shrink = jnp.exp(near_top - top)
+        total = stat_ref[b, 1:2] * shrink
+        mixed = stat_ref[b, 2:3] * shrink
+        for at, _ in pieces:
+            weight = jnp.exp(score_scr[at : at + LEAF] - top)
+            score_scr[at : at + LEAF] = weight
+            total = total + add_up(weight)
+            mixed = mixed + add_up(weight * pgrad_scr[at : at + LEAF])
+        inverse = 1.0 / total
+        delta = mixed * inverse
+        near_scale = shrink * inverse
+        for at, to in pieces:
+            prob = score_scr[at : at + LEAF] * inverse
+            low_ref[b, to : to + LEAF] = prob.astype(BF16)
+            sgrad_ref[b, to : to + LEAF] = (prob * (pgrad_scr[at : at + LEAF] - delta)).astype(BF16)
+        for i in range(4):
+            if HALO_PIECE.get(b) == i:
+                continue
+            rows = slice(i * LEAF, (i + 1) * LEAF)
+            prob = weight_ref[b, rows] * near_scale
+            low_ref[b, rows] = prob.astype(BF16)
+            sgrad_ref[b, rows] = (prob * (pgrad_ref[b, rows] - delta)).astype(BF16)
+        for source, other, lanes in (
+            (sgrad_ref, q2, slice(0, FEAT)),
+            (low_ref, g2, slice(FEAT, 2 * FEAT)),
+        ):
+            part = dot(source[b, 4 * LEAF :], other, (1, 0))
             if b == 0:
-                cross_grad[:, lanes] = part[4 * LEAF :]
+                cross_grad[:, lanes] = part
             else:
-                cross_grad[:, lanes] += part[4 * LEAF :]
-
-    spread = spreading(0, 256, 1).astype(BF16)
-    high = one_grad[...].astype(BF16)
-    rest = (one_grad[...] - high.astype(F32)).astype(BF16)
-    tok_ref[...] = near_grad[LEAF : LEAF + ROWS] + dot(spread, high, (1, 0)) + dot(spread, rest, (1, 0))
-    p1o_ref[:LEAF] = near_grad[pl.ds(peer_side, LEAF)].astype(BF16)
+                cross_grad[:, lanes] += part
+            if b in HALO_PIECE:
+                at = HALO_PIECE[b] * LEAF
+                rims[0 if b == 0 else 1, :, lanes] = dot(
+                    source[b, at : at + LEAF], other, (1, 0)
+                ).astype(BF16)
+
+    p1o_ref[:LEAF] = rims[peer_side]
     p1o_ref[LEAF:] = cross_grad[64:128].astype(BF16)
-    p2o_ref[...] = near_grad[pl.ds(other_side, LEAF)].astype(BF16)
+    p2o_ref[...] = rims[odd]
     for s in range(8):
         zo_ref[s, :FAR] = cross_grad[384 + FAR * s : 384 + FAR * (s + 1)].astype(BF16)
     zo_ref[place, FAR:] = jnp.zeros((64, 2 * FEAT), BF16)
@@ -236,7 +288,42 @@
         zo_ref[other, FAR + 32 :] = jnp.zeros((32, 2 * FEAT), BF16)
 
 
-def column_kernel(z_ref, out_ref):
+def after_kernel(
+    low_ref, sgrad_ref, q2_ref, g2_ref, kv_ref, one_ref, halo, cross,
+    att_ref, nqg_ref, tok_ref, near, near_grad, one_grad,
+):
+    near[:LEAF] = halo[0]
+    near[LEAF : LEAF + ROWS] = kv_ref[...]
+    near[LEAF + ROWS :] = halo[1]
+    near_grad[...] = jnp.zeros_like(near_grad)
+    one_grad[...] = jnp.zeros_like(one_grad)
+    feature = iota((FEAT, LEAF), 0)
+
+    def merge_heads(transposed):
+        return jnp.where(feature < HEAD, transposed[:, :LEAF], transposed[:, LEAF:]).T
+
+    for b in range(LEAVES):
+        rows = slice(b * LEAF, (b + 1) * LEAF)
+        near_rows = slice(b * LEAF, (b + 3) * LEAF)
+        half = (1 - b // 2) * LEAF
+        low = low_ref[b]
+        score_grad = sgrad_ref[b]
+        kv = jnp.concatenate([near[near_rows], one_ref[half : half + LEAF], cross[...]], axis=0)
+        att_ref[rows] = merge_heads(dot(kv[:, FEAT:], low, (0, 0))).astype(BF16)
+        nqg_ref[rows] = merge_heads(dot(kv[:, :FEAT], score_grad, (0, 0))) * 0.125
+        for part, lanes in (
+            (dot(score_grad[: 4 * LEAF], q2_ref[b], (1, 0)), slice(0, FEAT)),
+            (dot(low[: 4 * LEAF], g2_ref[b], (1, 0)), slice(FEAT, 2 * FEAT)),
+        ):
+            near_grad[near_rows, lanes] += part[: 3 * LEAF]
+            one_grad[half : half + LEAF, lanes] += part[3 * LEAF :]
+    spread = spreading(0, 256, 1).astype(BF16)
+    high = one_grad[...].astype(BF16)
+    rest = (one_grad[...] - high.astype(F32)).astype(BF16)
+    tok_ref[...] = near_grad[LEAF : LEAF + ROWS] + dot(spread, high, (1, 0)) + dot(spread, rest, (1, 0))
+
+
+def column_kernel(z_ref, p1_ref, p2_ref, tok_ref, out_ref):
     column = jnp.right_shift(lax.axis_index("seq"), 3)
     far = jnp.sum(z_ref[:, :FAR].astype(F32), axis=0).astype(BF16)
     slots = dot(far_pick((112, FAR), 1), far, (1, 0)).astype(BF16)
@@ -292,14 +379,15 @@
         ).astype(BF16)
 
 
-def call(kernel, outs, args, scratch=(), flops=0, name=None):
+def call(kernel, outs, args, scratch=(), flops=0, name=None, spaces=None, vmem=24 * MIB):
     many = isinstance(outs, list)
     moved = sum(math.prod(x.shape) * x.dtype.itemsize for x in list(args) + (outs if many else [outs]))
     return pl.pallas_call(
         kernel,
         out_shape=outs,
+        in_specs=[pl.BlockSpec(memory_space=space) for space in spaces or [pltpu.VMEM] * len(args)],
         scratch_shapes=list(scratch),
-        compiler_params=PARAMS,
+        compiler_params=pltpu.CompilerParams(vmem_limit_bytes=int(vmem)),
         cost_estimate=pl.CostEstimate(flops=flops, bytes_accessed=moved, transcendentals=0),
         name=name,
     )(*args)
@@ -339,24 +427,50 @@
     yrecv = exchange(ysend, "seq", COLUMN_GROUPS)
     zsend = call(row_kernel, sds(8, SLOT, 256), (yrecv, lv), name="rows")
     zrecv = exchange(zsend, "seq", ROW_GROUPS)
-    attended, nqg, tok, p1, p2, zsend = call(
+    q2, g2, weight, pgrad, stat = call(
+        near_kernel,
+        [sds(LEAVES, 256, FEAT), sds(LEAVES, 256, FEAT)]
+        + [sds(LEAVES, 512, 256, dtype=F32), sds(LEAVES, 512, 256, dtype=F32), sds(LEAVES, 8, 256, dtype=F32)],
+        (qn, kv, one, out_grad),
+        flops=4 * 2 * 2 * 256 * 512 * FEAT,
+        name="near",
+    )
+    low, sgrad, cross, halo, p1, p2, zsend = call(
         attend_kernel,
-        [sds(ROWS, FEAT), sds(ROWS, FEAT, dtype=F32), sds(ROWS, 256, dtype=F32), sds(192, 256), sds(LEAF, 256), sds(8, SLOT, 256)],
-        (qn, kv, one, out_grad, p1, p2, zrecv),
+        [sds(LEAVES, KEYS, 256), sds(LEAVES, KEYS, 256), sds(768, 256), sds(2, LEAF, 256)]
+        + [sds(192, 256), sds(LEAF, 256), sds(8, SLOT, 256)],
+        (q2, g2, weight, pgrad, stat, p1, p2, zrecv),
         scratch=[
-            pltpu.VMEM((768, 256), BF16),
+            pltpu.VMEM((896, 256), F32),
+            pltpu.VMEM((896, 256), F32),
+            pltpu.VMEM((768, 256), F32),
+            pltpu.VMEM((2, LEAF, 256), BF16),
+        ],
+        flops=4 * 4 * 2 * 256 * 768 * FEAT,
+        name="attend",
+    )
+    p1 = lax.ppermute(p1, "seq", peer)
+    p2 = lax.ppermute(p2, "seq", beside)
+    zrecv = exchange(zsend, "seq", ROW_GROUPS)
+    attended, nqg, tok = call(
+        after_kernel,
+        [sds(ROWS, FEAT), sds(ROWS, FEAT, dtype=F32), sds(ROWS, 256, dtype=F32)],
+        (low, sgrad, q2, g2, kv, one, halo, cross),
+        scratch=[
             pltpu.VMEM((768, 256), BF16),
             pltpu.VMEM((768, 256), F32),
             pltpu.VMEM((256, 256), F32),
-            pltpu.VMEM((768, 256), F32),
         ],
-        flops=4 * 6 * 2 * 256 * KEYS * FEAT,
-        name="attend",
-    )
-    p1 = lax.ppermute(p1, "seq", peer)
-    p2 = lax.ppermute(p2, "seq", beside)
-    zrecv = exchange(zsend, "seq", ROW_GROUPS)
-    ysend = call(column_kernel, sds(8, 16, 256), (zrecv,), name="columns")
+        flops=4 * 2 * 2 * 256 * (KEYS + 512) * FEAT,
+        name="after",
+    )
+    ysend = call(
+        column_kernel,
+        sds(8, 16, 256),
+        (zrecv, p1, p2, tok),
+        spaces=[pltpu.VMEM, pl.ANY, pl.ANY, pl.ANY],
+        name="columns",
+    )
     yrecv = exchange(ysend, "seq", COLUMN_GROUPS)
     nkg, value_grad, inner = call(
         total_kernel,

time: 107 us -> 126 us (1.18)
  the two profiles are of different devices: /device:TPU:32 before, /device:TPU:1 now
where the time goes in v4:
time: 126 us; the launch traced here: 124 us
  blocking collectives  52 us (41%)
  local copies, waits for them, and re-layouts  33.7 us (27%)
  starting transfers between devices  23.6 us (19%)
  Pallas kernels  12.6 us (10%)
  waiting for transfers between devices  1.61 us (1%)
    all_to_all x4, blocking collectives, exchange(): return lax.all_to_all(x, axis, 0, 0, axis_index_groups=groups, tiled=True)  52 us
    unnamed x84, local copies, waits for them, and re-layouts  33.7 us
    all_to_all x2, starting transfers between devices, exchange(): return lax.all_to_all(x, axis, 0, 0, axis_index_groups=groups, tiled=True)  15.5 us
    pallas_call x9, Pallas kernels, call(): pl.pallas_call(kernel, out_shape=outs, in_specs=[pl.BlockSpec(memory_spac...  12.6 us
    ppermute x2, starting transfers between devices, local(): p1 = lax.ppermute(p1, 'seq', peer)  6.71 us
  transfers between devices with their start and end apart: 6, of which 1 were waited for; matrix products, arithmetic and copies ran while one was open for 0% of the time, Pallas kernels for 3%

profile of v4, /device:TPU:1, one launch (start us, length us, event | category | flops | bytes accessed | tf_op | source)
XLA Modules:
  0.0 124.4 jit_solution(6990075575182096983)
XLA Ops:
  2.7 14.0 %all_to_all.30.refs_0_ = f32[8,8,128]{2,1,0:T(8,128)S(1)} all-to-all(f32[8,8,128]{2,1,0:T(8,128)S(1)} %squares.1), channel_id=1, replica_groups=mesh['seq'=64,'head'=8] {'head'}, dimensions={0} | all-to-all | bytes 65536 | tf_op jit(solution)/shard_map/all_to_all | solution.py:405
  16.6 0.9 copy-done.30
  18.8 1.1 norm.1
  21.3 10.2 %all_to_all.31.y_ref = bf16[8,16,256]{2,1,0:T(8,128)(2,1)S(1)} all-to-all(bf16[8,16,256]{2,1,0:T(8,128)(2,1)S(1)} %get-tuple-element.41), channel_id=1, replica_groups={{0,64,128,192,256,320,384,448},{8,72,136,200,264,328,392,456},{16,80,14..., dimensions={0} | all-to-all | bytes 131072 | tf_op jit(solution)/shard_map/all_to_all | solution.py:405
  31.4 0.9 rows.1
  32.4 10.0 %all-to-all-start.2 = ((bf16[8,112,256]{2,1,0:T(8,128)(2,1)}), bf16[8,112,256]{2,1,0:T(8,128)(2,1)S(1)}, u32[]{:S(2)}, u32[]{:S(2)}) async-start(bf16[8,112,256]{2,1,0:T(8,128)(2,1)} %rows.1), calls=%async_computation.2 | async-start | bytes 917504 | tf_op jit(solution)/shard_map/all_to_all | solution.py:405
  42.4 3.4 %collective-permute-start = (bf16[192,256]{1,0:T(8,128)(2,1)}, bf16[192,256]{1,0:T(8,128)(2,1)S(1)}, u32[]{:S(2)}, u32[]{:S(2)}) collective-permute-start(bf16[192,256]{1,0:T(8,128)(2,1)} %get-tuple-element.39), channel_id=1, source_target_pairs={{0,8},{8,0},{16,24},{24,16},{32,40},{40,32},{48,56},{56,48},{64,72... | collective-permute-start | bytes 294920 | tf_op jit(solution)/shard_map/ppermute | solution.py:425
  47.4 0.9 copy-done.37
  49.2 0.9 near.1
  50.1 1.3 %copy-done.9 = f32[4,512,256]{2,1,0:T(8,128)} copy-done((f32[4,512,256]{2,1,0:T(8,128)}, f32[4,512,256]{2,1,0:T(8,128)S(1)}, u32[]{:S(2)}) %copy-start.9) | copy-done | bytes 2097176
  51.5 1.4 %copy-done.11 = f32[4,512,256]{2,1,0:T(8,128)} copy-done((f32[4,512,256]{2,1,0:T(8,128)}, f32[4,512,256]{2,1,0:T(8,128)S(1)}, u32[]{:S(2)}) %copy-start.11) | copy-done | bytes 2097176
  54.2 1.6 %all-to-all-done.2.z_ref = bf16[8,112,256]{2,1,0:T(8,128)(2,1)S(1)} async-done(((bf16[8,112,256]{2,1,0:T(8,128)(2,1)}), bf16[8,112,256]{2,1,0:T(8,128)(2,1)S(1)}, u32[]{:S(2)}, u32[]{:S(2)}) %all-to-all-start.2) | async-done | bytes 458784 | tf_op jit(solution)/shard_map/all_to_all | solution.py:405
  55.8 1.6 %copy-done.10 = f32[4,512,256]{2,1,0:T(8,128)S(1)} copy-done((f32[4,512,256]{2,1,0:T(8,128)S(1)}, f32[4,512,256]{2,1,0:T(8,128)}, u32[]{:S(2)}) %copy-start.10) | copy-done | bytes 2097176
  57.4 1.6 %copy-done.12 = f32[4,512,256]{2,1,0:T(8,128)S(1)} copy-done((f32[4,512,256]{2,1,0:T(8,128)S(1)}, f32[4,512,256]{2,1,0:T(8,128)}, u32[]{:S(2)}) %copy-start.12) | copy-done | bytes 2097176
  58.9 0.9 copy-done.18
  60.7 4.5 %attend.1 = (bf16[4,1280,256]{2,1,0:T(8,128)(2,1)S(1)}, bf16[4,1280,256]{2,1,0:T(8,128)(2,1)S(1)}, bf16[768,256]{1,0:T(8,128)(2,1)S(1)}, bf16[2,128,256]{2,1,0:T...) custom-call(bf16[4,256,128]{2,1,0:T(8,128)(2,1)S(1)} %get-tuple-eleme, ...), custom_call_target="tpu_custom_call" | custom-call | flops 805306368 | bytes 11763712 | tf_op jit(solution)/shard_map/attend/pallas_call | solution.py:385
  65.2 1.5 %copy-done = bf16[4,1280,256]{2,1,0:T(8,128)(2,1)} copy-done((bf16[4,1280,256]{2,1,0:T(8,128)(2,1)}, bf16[4,1280,256]{2,1,0:T(8,128)(2,1)S(1)}, u32[]{:S(2)}) %copy-start) | copy-done | bytes 2621464
  70.1 5.5 %all-to-all-start.3 = ((bf16[8,112,256]{2,1,0:T(8,128)(2,1)}), bf16[8,112,256]{2,1,0:T(8,128)(2,1)S(1)}, u32[]{:S(2)}, u32[]{:S(2)}) async-start(bf16[8,112,256]{2,1,0:T(8,128)(2,1)} %copy-done.20), calls=%async_computation.3 | async-start | bytes 917504 | tf_op jit(solution)/shard_map/all_to_all | solution.py:405
  75.6 3.4 %collective-permute-start.2 = (bf16[192,256]{1,0:T(8,128)(2,1)}, bf16[192,256]{1,0:T(8,128)(2,1)S(1)}, u32[]{:S(2)}, u32[]{:S(2)}) collective-permute-start(bf16[192,256]{1,0:T(8,128)(2,1)} %copy-done.40), channel_id=1, source_target_pairs={{0,8},{8,0},{16,24},{24,16},{32,40},{40,32},{48,56},{56,48},{64,72... | collective-permute-start | bytes 294920 | tf_op jit(solution)/shard_map/ppermute | solution.py:452
  79.7 1.7 %copy-done.1 = bf16[4,1280,256]{2,1,0:T(8,128)(2,1)S(1)} copy-done((bf16[4,1280,256]{2,1,0:T(8,128)(2,1)S(1)}, bf16[4,1280,256]{2,1,0:T(8,128)(2,1)}, u32[]{:S(2)}) %copy-start.1) | copy-done | bytes 2621464
  81.4 0.9 copy-done.16
  82.4 0.9 copy-done.19
  83.3 1.0 copy-done.22
  84.3 0.9 copy-done.24
  87.1 2.3 %after.1 = (bf16[512,128]{1,0:T(8,128)(2,1)}, f32[512,128]{1,0:T(8,128)S(1)}, f32[512,256]{1,0:T(8,128)S(1)}) custom-call(bf16[4,1280,256]{2,1,0:T(8,128)(2,1)S(1)} %get-tuple-element.43.low_ref, bf16[4,1280,256]{2,1,0:T(8,128)(2,1)S(1)} %copy-done.1, bf16[4,256,128]{2,1,0:T(8,128)(2,1)S(1)} %copy-done.16, bf16[4,256,128]{2,1,0:T(8,128)(2,1)S(1)} %copy-done.19, ...), custom_call_target="tpu_custom_call" | custom-call | flops 939524096 | bytes 7602176 | tf_op jit(solution)/shard_map/after/pallas_call | solution.py:385
  90.9 1.0 copy-done.3
  92.1 15.5 %all_to_all.32.y_ref = bf16[8,16,256]{2,1,0:T(8,128)(2,1)S(1)} all-to-all(bf16[8,16,256]{2,1,0:T(8,128)(2,1)S(1)} %columns.1), channel_id=1, replica_groups={{0,64,128,192,256,320,384,448},{8,72,136,200,264,328,392,456},{16,80,14..., dimensions={0} | all-to-all | bytes 131072 | tf_op jit(solution)/shard_map/all_to_all | solution.py:405
  107.6 1.0 copy-done.4
  108.6 0.9 copy-done.14
  109.6 1.4 %total.1 = (f32[512,128]{1,0:T(8,128)S(1)}, bf16[512,128]{1,0:T(8,128)(2,1)}, f32[8,8,128]{2,1,0:T(8,128)S(1)}) custom-call(f32[512,256]{1,0:T(8,128)S(1)} %copy-done.4, bf16[192,256]{1,0:T(8,128)(2,1)S(1)} %collective-permute-done.2.p1_ref, bf16[128,256]{1,0:T(8,128)(2,1)S(1)} %collective-permute-done.3.p2_ref, ...), custom_call_target="tpu_custom_call" | custom-call | bytes 2163712 | tf_op jit(solution)/shard_map/total/pallas_call | solution.py:385
  111.0 12.3 %all_to_all.33.refs_1_ = f32[8,8,128]{2,1,0:T(8,128)S(1)} all-to-all(f32[8,8,128]{2,1,0:T(8,128)S(1)} %get-tuple-element.53), channel_id=1, replica_groups=mesh['seq'=64,'head'=8] {'head'}, dimensions={0} | all-to-all | bytes 65536 | tf_op jit(solution)/shard_map/all_to_all | solution.py:405
  123.4 1.0 finish.1
  (77 shorter events, 16.8 us)
Async XLA Ops:
  0.6 0.9 copy-start.5
  1.5 0.9 copy-start.7
  16.6 0.9 copy-start.30
  21.3 34.5 %copy-start.23 = (bf16[512,256]{1,0:T(8,128)(2,1)}, bf16[512,256]{1,0:T(8,128)(2,1)S(1)}, u32[]{:S(2)}) copy-start(bf16[512,256]{1,0:T(8,128)(2,1)S(1)} %get-tuple-element.32.kv_ref) | copy-start | bytes 786436
  32.4 23.4 %all-to-all-start.2 = ((bf16[8,112,256]{2,1,0:T(8,128)(2,1)}), bf16[8,112,256]{2,1,0:T(8,128)(2,1)S(1)}, u32[]{:S(2)}, u32[]{:S(2)}) async-start(bf16[8,112,256]{2,1,0:T(8,128)(2,1)} %rows.1), calls=%async_computation.2 | async-start | bytes 917504 | tf_op jit(solution)/shard_map/all_to_all | solution.py:405
  42.4 11.7 %collective-permute-start = (bf16[192,256]{1,0:T(8,128)(2,1)}, bf16[192,256]{1,0:T(8,128)(2,1)S(1)}, u32[]{:S(2)}, u32[]{:S(2)}) collective-permute-start(bf16[192,256]{1,0:T(8,128)(2,1)} %get-tuple-element.39), channel_id=1, source_target_pairs={{0,8},{8,0},{16,24},{24,16},{32,40},{40,32},{48,56},{56,48},{64,72... | collective-permute-start | bytes 294920 | tf_op jit(solution)/shard_map/ppermute | solution.py:425
  45.8 8.4 %collective-permute-start.1 = (bf16[128,256]{1,0:T(8,128)(2,1)}, bf16[128,256]{1,0:T(8,128)(2,1)S(1)}, u32[]{:S(2)}, u32[]{:S(2)}) collective-permute-start(bf16[128,256]{1,0:T(8,128)(2,1)} %get-tuple-element.40), channel_id=1, source_target_pairs={{8,16},{24,32},{40,48},{56,64},{72,80},{88,96},{104,112},{120,128}... | collective-permute-start | bytes 196616 | tf_op jit(solution)/shard_map/ppermute | solution.py:426
  46.5 0.9 copy-start.26
  47.4 0.9 copy-start.37
  50.1 1.3 %copy-start.9 = (f32[4,512,256]{2,1,0:T(8,128)}, f32[4,512,256]{2,1,0:T(8,128)S(1)}, u32[]{:S(2)}) copy-start(f32[4,512,256]{2,1,0:T(8,128)S(1)} %get-tuple-element.36.weight_ref) | copy-start | bytes 6291460
  51.5 1.4 %copy-start.11 = (f32[4,512,256]{2,1,0:T(8,128)}, f32[4,512,256]{2,1,0:T(8,128)S(1)}, u32[]{:S(2)}) copy-start(f32[4,512,256]{2,1,0:T(8,128)S(1)} %get-tuple-element.37.pgrad_ref) | copy-start | bytes 6291460
  54.2 11.0 %copy-start.15 = (bf16[4,256,128]{2,1,0:T(8,128)(2,1)}, bf16[4,256,128]{2,1,0:T(8,128)(2,1)S(1)}, u32[]{:S(2)}) copy-start(bf16[4,256,128]{2,1,0:T(8,128)(2,1)S(1)} %get-tuple-element.34.q2_ref) | copy-start | bytes 786436
  55.8 1.6 %copy-start.10 = (f32[4,512,256]{2,1,0:T(8,128)S(1)}, f32[4,512,256]{2,1,0:T(8,128)}, u32[]{:S(2)}) copy-start(f32[4,512,256]{2,1,0:T(8,128)} %copy-done.9) | copy-start | bytes 6291460
  57.4 1.6 %copy-start.12 = (f32[4,512,256]{2,1,0:T(8,128)S(1)}, f32[4,512,256]{2,1,0:T(8,128)}, u32[]{:S(2)}) copy-start(f32[4,512,256]{2,1,0:T(8,128)} %copy-done.11) | copy-start | bytes 6291460
  58.9 0.9 copy-start.18
  65.2 1.5 %copy-start = (bf16[4,1280,256]{2,1,0:T(8,128)(2,1)}, bf16[4,1280,256]{2,1,0:T(8,128)(2,1)S(1)}, u32[]{:S(2)}) copy-start(bf16[4,1280,256]{2,1,0:T(8,128)(2,1)S(1)} %get-tuple-element.44.sgrad_ref) | copy-start | bytes 7864324
  70.1 20.8 %all-to-all-start.3 = ((bf16[8,112,256]{2,1,0:T(8,128)(2,1)}), bf16[8,112,256]{2,1,0:T(8,128)(2,1)S(1)}, u32[]{:S(2)}, u32[]{:S(2)}) async-start(bf16[8,112,256]{2,1,0:T(8,128)(2,1)} %copy-done.20), calls=%async_computation.3 | async-start | bytes 917504 | tf_op jit(solution)/shard_map/all_to_all | solution.py:405
  75.6 15.2 %collective-permute-start.2 = (bf16[192,256]{1,0:T(8,128)(2,1)}, bf16[192,256]{1,0:T(8,128)(2,1)S(1)}, u32[]{:S(2)}, u32[]{:S(2)}) collective-permute-start(bf16[192,256]{1,0:T(8,128)(2,1)} %copy-done.40), channel_id=1, source_target_pairs={{0,8},{8,0},{16,24},{24,16},{32,40},{40,32},{48,56},{56,48},{64,72... | collective-permute-start | bytes 294920 | tf_op jit(solution)/shard_map/ppermute | solution.py:452
  79.0 11.9 %collective-permute-start.3 = (bf16[128,256]{1,0:T(8,128)(2,1)}, bf16[128,256]{1,0:T(8,128)(2,1)S(1)}, u32[]{:S(2)}, u32[]{:S(2)}) collective-permute-start(bf16[128,256]{1,0:T(8,128)(2,1)} %copy-done.41), channel_id=1, source_target_pairs={{8,16},{24,32},{40,48},{56,64},{72,80},{88,96},{104,112},{120,128}... | collective-permute-start | bytes 196616 | tf_op jit(solution)/shard_map/ppermute | solution.py:453
  79.7 1.7 %copy-start.1 = (bf16[4,1280,256]{2,1,0:T(8,128)(2,1)S(1)}, bf16[4,1280,256]{2,1,0:T(8,128)(2,1)}, u32[]{:S(2)}) copy-start(bf16[4,1280,256]{2,1,0:T(8,128)(2,1)} %copy-done) | copy-start | bytes 7864324
  81.4 0.9 copy-start.16
  82.4 0.9 copy-start.19
  83.3 1.0 copy-start.22
  84.3 0.9 copy-start.24
  85.3 0.9 copy-start.27
  87.1 20.5 %copy-start.6 = (bf16[512,128]{1,0:T(8,128)(2,1)S(1)}, bf16[512,128]{1,0:T(8,128)(2,1)}, u32[]{:S(2)}) copy-start(bf16[512,128]{1,0:T(8,128)(2,1)} %refs_2_.3) | copy-start | bytes 393220
  87.1 20.5 %copy-start.8 = (bf16[512,128]{1,0:T(8,128)(2,1)S(1)}, bf16[512,128]{1,0:T(8,128)(2,1)}, u32[]{:S(2)}) copy-start(bf16[512,128]{1,0:T(8,128)(2,1)} %refs_3_.3) | copy-start | bytes 393220
  87.1 20.5 %copy-start.34 = (f32[128]{0:T(128)S(1)}, f32[128]{0:T(128)}, u32[]{:S(2)}) copy-start(f32[128]{0:T(128)} %param.9) | copy-start | bytes 1540
  87.1 20.5 %copy-start.36 = (f32[128]{0:T(128)S(1)}, f32[128]{0:T(128)}, u32[]{:S(2)}) copy-start(f32[128]{0:T(128)} %param.10) | copy-start | bytes 1540
  90.9 1.0 copy-start.3
  107.6 1.0 copy-start.4
  108.6 0.9 copy-start.14
  (16 other events, 11.4 us)

commit v5 on v2

--- a/solution.py
+++ b/solution.py
@@ -18,10 +18,9 @@
 F32 = jnp.float32
 BF16 = jnp.bfloat16
 PARAMS = pltpu.CompilerParams(vmem_limit_bytes=40 * 1024 * 1024)
-ROW_LEVEL = {1: 2, 2: 3, 3: 3, 4: 4, 5: 4, 6: 4, 7: 4}
 COLUMN_LEVEL = {1: 5, 2: 6, 3: 6, 4: 7, 5: 7, 6: 7, 7: 7}
 FAR = 48
-SLOT = 112
+MID = 96
 
 
 def dot(a, b, dims):
@@ -105,38 +104,26 @@
     ).astype(BF16)
     coarse = dot(pool, kv_ref[...], (1, 0)).astype(BF16)
     one_ref[...] = coarse[:256]
-    lv_ref[...] = coarse[256:480]
+    lv_ref[...] = coarse[384:480]
     y_ref[column] = jnp.zeros((16, 2 * FEAT), BF16)
     for d in range(1, 8):
         y_ref[jnp.bitwise_xor(column, d)] = coarse[464 + 16 * d : 480 + 16 * d]
     p1_ref[:LEAF] = kv_ref[pl.ds(pl.multiple_of((1 - odd) * 384, LEAF), LEAF)]
-    p1_ref[LEAF:] = coarse[320:384]
+    p1_ref[LEAF:] = coarse[256:384]
     p2_ref[...] = kv_ref[pl.ds(pl.multiple_of(odd * 384, LEAF), LEAF)]
 
 
-def row_kernel(y_ref, lv_ref, out_ref):
-    index = lax.axis_index("seq")
-    column = jnp.right_shift(index, 3)
-    place = jnp.bitwise_and(index, 7)
+def row_kernel(y_ref, out_ref):
+    column = jnp.right_shift(lax.axis_index("seq"), 3)
     slots = jnp.concatenate([y_ref[jnp.bitwise_xor(column, d)] for d in range(1, 8)], axis=0)
     far = dot(far_pick((FAR, 112), 0), slots, (1, 0)).astype(BF16)
     for s in range(8):
-        out_ref[s, :FAR] = far
-    out_ref[place, FAR:] = jnp.zeros((64, 2 * FEAT), BF16)
-    for d in range(1, 8):
-        other = jnp.bitwise_xor(place, d)
-        if d == 1:
-            out_ref[other, FAR:] = lv_ref[:64]
-        elif d < 4:
-            out_ref[other, FAR:] = lv_ref[128:192]
-        else:
-            out_ref[other, FAR : FAR + 32] = lv_ref[192:224]
-            out_ref[other, FAR + 32 :] = jnp.zeros((32, 2 * FEAT), BF16)
+        out_ref[s] = far
 
 
 def attend_kernel(
-    qn_ref, kv_ref, one_ref, g_ref, p1_ref, p2_ref, z_ref,
-    att_ref, nqg_ref, tok_ref, p1o_ref, p2o_ref, zo_ref,
+    qn_ref, kv_ref, one_ref, g_ref, p1_ref, p2_ref, z_ref, lv_ref,
+    att_ref, nqg_ref, tok_ref, p1o_ref, p2o_ref, zo_ref, lo_ref,
     near, cross, near_grad, one_grad, cross_grad,
 ):
     index = lax.axis_index("seq")
@@ -148,14 +135,13 @@
     near[LEAF : LEAF + ROWS] = kv_ref[...]
     near[pl.ds(peer_side, LEAF)] = p1_ref[:LEAF]
     near[pl.ds(other_side, LEAF)] = p2_ref[...]
-    cross[:64] = z_ref[jnp.bitwise_xor(place, 1), FAR:]
-    cross[64:128] = p1_ref[LEAF:]
-    cross[128:192] = z_ref[jnp.bitwise_xor(place, 2), FAR:]
-    cross[192:256] = z_ref[jnp.bitwise_xor(place, 3), FAR:]
+    cross[:128] = p1_ref[LEAF:]
+    cross[128:192] = lv_ref[jnp.bitwise_xor(place, 2), :64]
+    cross[192:256] = lv_ref[jnp.bitwise_xor(place, 3), :64]
     for i in range(4):
-        cross[256 + 32 * i : 288 + 32 * i] = z_ref[jnp.bitwise_xor(place, 4 + i), FAR : FAR + 32]
+        cross[256 + 32 * i : 288 + 32 * i] = lv_ref[jnp.bitwise_xor(place, 4 + i), 64:]
     for s in range(8):
-        cross[384 + FAR * s : 384 + FAR * (s + 1)] = z_ref[s, :FAR]
+        cross[384 + FAR * s : 384 + FAR * (s + 1)] = z_ref[s]
 
     def level_bias(rows, level):
         return jnp.full((rows, 2 * LEAF), level * LN2, F32)
@@ -222,23 +208,25 @@
     rest = (one_grad[...] - high.astype(F32)).astype(BF16)
     tok_ref[...] = near_grad[LEAF : LEAF + ROWS] + dot(spread, high, (1, 0)) + dot(spread, rest, (1, 0))
     p1o_ref[:LEAF] = near_grad[pl.ds(peer_side, LEAF)].astype(BF16)
-    p1o_ref[LEAF:] = cross_grad[64:128].astype(BF16)
+    p1o_ref[LEAF:] = cross_grad[:128].astype(BF16)
     p2o_ref[...] = near_grad[pl.ds(other_side, LEAF)].astype(BF16)
     for s in range(8):
-        zo_ref[s, :FAR] = cross_grad[384 + FAR * s : 384 + FAR * (s + 1)].astype(BF16)
-    zo_ref[place, FAR:] = jnp.zeros((64, 2 * FEAT), BF16)
-    zo_ref[jnp.bitwise_xor(place, 1), FAR:] = cross_grad[:64].astype(BF16)
-    zo_ref[jnp.bitwise_xor(place, 2), FAR:] = cross_grad[128:192].astype(BF16)
-    zo_ref[jnp.bitwise_xor(place, 3), FAR:] = cross_grad[192:256].astype(BF16)
-    for i in range(4):
-        other = jnp.bitwise_xor(place, 4 + i)
-        zo_ref[other, FAR : FAR + 32] = cross_grad[256 + 32 * i : 288 + 32 * i].astype(BF16)
-        zo_ref[other, FAR + 32 :] = jnp.zeros((32, 2 * FEAT), BF16)
-
-
-def column_kernel(z_ref, out_ref):
+        zo_ref[s] = cross_grad[384 + FAR * s : 384 + FAR * (s + 1)].astype(BF16)
+    for d in range(8):
+        other = jnp.bitwise_xor(place, d)
+        high_rows = jnp.zeros((64, 2 * FEAT), BF16)
+        low_rows = jnp.zeros((32, 2 * FEAT), BF16)
+        if d in (2, 3):
+            high_rows = cross_grad[64 * d : 64 * (d + 1)].astype(BF16)
+        if d >= 4:
+            low_rows = cross_grad[128 + 32 * d : 160 + 32 * d].astype(BF16)
+        lo_ref[other, :64] = high_rows
+        lo_ref[other, 64:] = low_rows
+
+
+def column_kernel(z_ref, p1_ref, p2_ref, out_ref):
     column = jnp.right_shift(lax.axis_index("seq"), 3)
-    far = jnp.sum(z_ref[:, :FAR].astype(F32), axis=0).astype(BF16)
+    far = jnp.sum(z_ref[...].astype(F32), axis=0).astype(BF16)
     slots = dot(far_pick((112, FAR), 1), far, (1, 0)).astype(BF16)
     out_ref[column] = jnp.zeros((16, 2 * FEAT), BF16)
     for d in range(1, 8):
@@ -246,19 +234,14 @@
 
 
 def total_kernel(
-    tok_ref, p1_ref, p2_ref, z_ref, y_ref,
+    tok_ref, p1_ref, p2_ref, lv_ref, y_ref,
     q_ref, k_ref, qg_ref, kg_ref, nqg_ref, nkg_ref, vg_ref, sum_ref, acc,
 ):
     index = lax.axis_index("seq")
     column = jnp.right_shift(index, 3)
-    place = jnp.bitwise_and(index, 7)
     odd = jnp.bitwise_and(index, 1)
-    pieces = [z_ref[jnp.bitwise_xor(place, 1), FAR:], p1_ref[LEAF:]]
-    maps = [spreading(0, 64, 2), spreading(64, 64, 2)]
-    for d in range(2, 8):
-        rows = ROWS >> ROW_LEVEL[d]
-        pieces.append(z_ref[jnp.bitwise_xor(place, d), FAR : FAR + rows])
-        maps.append(spreading(0, rows, ROW_LEVEL[d]))
+    pieces = [p1_ref[LEAF:], lv_ref[...]]
+    maps = [spreading(0, 128, 2), spreading(0, 64, 3), spreading(0, 32, 4)]
     for d in range(1, 8):
         pieces.append(y_ref[jnp.bitwise_xor(column, d)])
         maps.append(spreading(0, 16, COLUMN_LEVEL[d]))
@@ -292,12 +275,13 @@
         ).astype(BF16)
 
 
-def call(kernel, outs, args, scratch=(), flops=0, name=None):
+def call(kernel, outs, args, scratch=(), flops=0, name=None, spaces=None):
     many = isinstance(outs, list)
     moved = sum(math.prod(x.shape) * x.dtype.itemsize for x in list(args) + (outs if many else [outs]))
     return pl.pallas_call(
         kernel,
         out_shape=outs,
+        in_specs=[pl.BlockSpec(memory_space=space) for space in spaces or [pltpu.VMEM] * len(args)],
         scratch_shapes=list(scratch),
         compiler_params=PARAMS,
         cost_estimate=pl.CostEstimate(flops=flops, bytes_accessed=moved, transcendentals=0),
@@ -330,19 +314,20 @@
     squares = exchange(squares, "head")
     qn, kv, one, lv, ysend, p1, p2 = call(
         lambda *refs: norm_kernel(width, *refs),
-        [sds(ROWS, FEAT), sds(ROWS, 256), sds(256, 256), sds(224, 256), sds(8, 16, 256), sds(192, 256), sds(LEAF, 256)],
+        [sds(ROWS, FEAT), sds(ROWS, 256), sds(256, 256), sds(MID, 256), sds(8, 16, 256), sds(256, 256), sds(LEAF, 256)],
         (squares, queries, key_rows, value_rows, qg, kg),
         name="norm",
     )
     p1 = lax.ppermute(p1, "seq", peer)
     p2 = lax.ppermute(p2, "seq", beside)
+    lv = lax.all_gather(lv, "seq", axis=0, axis_index_groups=ROW_GROUPS)
     yrecv = exchange(ysend, "seq", COLUMN_GROUPS)
-    zsend = call(row_kernel, sds(8, SLOT, 256), (yrecv, lv), name="rows")
+    zsend = call(row_kernel, sds(8, FAR, 256), (yrecv,), name="rows")
     zrecv = exchange(zsend, "seq", ROW_GROUPS)
-    attended, nqg, tok, p1, p2, zsend = call(
+    attended, nqg, tok, p1, p2, zsend, lv = call(
         attend_kernel,
-        [sds(ROWS, FEAT), sds(ROWS, FEAT, dtype=F32), sds(ROWS, 256, dtype=F32), sds(192, 256), sds(LEAF, 256), sds(8, SLOT, 256)],
-        (qn, kv, one, out_grad, p1, p2, zrecv),
+        [sds(ROWS, FEAT), sds(ROWS, FEAT, dtype=F32), sds(ROWS, 256, dtype=F32), sds(256, 256), sds(LEAF, 256), sds(8, FAR, 256), sds(8, MID, 256)],
+        (qn, kv, one, out_grad, p1, p2, zrecv, lv),
         scratch=[
             pltpu.VMEM((768, 256), BF16),
             pltpu.VMEM((768, 256), BF16),
@@ -355,13 +340,20 @@
     )
     p1 = lax.ppermute(p1, "seq", peer)
     p2 = lax.ppermute(p2, "seq", beside)
+    lv = lax.psum_scatter(lv, "seq", scatter_dimension=0, axis_index_groups=ROW_GROUPS)
     zrecv = exchange(zsend, "seq", ROW_GROUPS)
-    ysend = call(column_kernel, sds(8, 16, 256), (zrecv,), name="columns")
+    ysend = call(
+        column_kernel,
+        sds(8, 16, 256),
+        (zrecv, p1, p2),
+        spaces=[pltpu.VMEM, pl.ANY, pl.ANY],
+        name="columns",
+    )
     yrecv = exchange(ysend, "seq", COLUMN_GROUPS)
     nkg, value_grad, inner = call(
         total_kernel,
         [sds(ROWS, FEAT, dtype=F32), sds(ROWS, FEAT), sds(heads, 8, FEAT, dtype=F32)],
-        (tok, p1, p2, zrecv, yrecv, queries, key_rows, qg, kg, nqg),
+        (tok, p1, p2, lv, yrecv, queries, key_rows, qg, kg, nqg),
         scratch=[pltpu.VMEM((ROWS, 256), F32)],
         name="total",
     )

time: 107 us -> 141 us (1.32)
  the two profiles are of different devices: /device:TPU:32 before, /device:TPU:1 now
where the time goes in v5:
time: 141 us; the launch traced here: 140 us
  blocking collectives  70.1 us (50%)
  starting transfers between devices  25 us (18%)
  waiting for transfers between devices  16.3 us (12%)
  between operations  14.1 us (10%)
  Pallas kernels  11.1 us (8%)
  local copies, waits for them, and re-layouts  3.29 us (2%)
    all_to_all x4, blocking collectives, exchange(): return lax.all_to_all(x, axis, 0, 0, axis_index_groups=groups, tiled=True)  49.9 us
    all_gather x1, blocking collectives, local(): lv = lax.all_gather(lv, 'seq', axis=0, axis_index_groups=ROW_GROUPS)  20.2 us
    all_to_all x2, starting transfers between devices, exchange(): return lax.all_to_all(x, axis, 0, 0, axis_index_groups=groups, tiled=True)  14.5 us
    reduce_scatter x1, waiting for transfers between devices, local(): lax.psum_scatter(lv, 'seq', scatter_dimension=0, axis_index_groups=ROW_GR...  11.7 us
    pallas_call x7, Pallas kernels, call(): pl.pallas_call(kernel, out_shape=outs, in_specs=[pl.BlockSpec(memory_spac...  11.1 us
    ppermute x2, starting transfers between devices, local(): p1 = lax.ppermute(p1, 'seq', peer)  9.1 us
    unnamed x18, local copies, waits for them, and re-layouts  3.29 us
  transfers between devices with their start and end apart: 7, of which 3 were waited for; matrix products, arithmetic and copies ran while one was open for 0% of the time, Pallas kernels for 0%

profile of v5, /device:TPU:1, one launch (start us, length us, event | category | flops | bytes accessed | tf_op | source)
XLA Modules:
  0.0 139.9 jit_solution(17120338236714218472)
XLA Ops:
  7.2 0.0 copy-start
  7.2 0.9 copy-done
  8.1 0.9 copy-done.2
  9.0 0.2 squares.1
  9.2 14.0 %all_to_all.30.refs_0_ = f32[8,8,128]{2,1,0:T(8,128)S(1)} all-to-all(f32[8,8,128]{2,1,0:T(8,128)S(1)} %squares.1), channel_id=1, replica_groups=mesh['seq'=64,'head'=8] {'head'}, dimensions={0} | all-to-all | bytes 65536 | tf_op jit(solution)/shard_map/all_to_all | solution.py:301
  23.2 0.6 copy-done.6
  23.8 0.0 copy-done.7
  23.8 0.5 norm.1
  24.4 10.2 %all_to_all.31.y_ref = bf16[8,16,256]{2,1,0:T(8,128)(2,1)S(1)} all-to-all(bf16[8,16,256]{2,1,0:T(8,128)(2,1)S(1)} %get-tuple-element.28), channel_id=1, replica_groups={{0,64,128,192,256,320,384,448},{8,72,136,200,264,328,392,456},{16,80,14..., dimensions={0} | all-to-all | bytes 131072 | tf_op jit(solution)/shard_map/all_to_all | solution.py:301
  34.6 0.8 rows.1
  35.4 10.0 %all-to-all-start.2 = ((bf16[8,48,256]{2,1,0:T(8,128)(2,1)}), bf16[8,48,256]{2,1,0:T(8,128)(2,1)S(1)}, u32[]{:S(2)}, u32[]{:S(2)}) async-start(bf16[8,48,256]{2,1,0:T(8,128)(2,1)} %rows.1), calls=%async_computation.2 | async-start | bytes 393216 | tf_op jit(solution)/shard_map/all_to_all | solution.py:301
  45.4 0.0 reduce-scatter.2.cloned.1.call-start
  45.5 0.7 collective-permute-start.1
  46.1 5.7 %collective-permute-start = (bf16[256,256]{1,0:T(8,128)(2,1)S(1)}, bf16[256,256]{1,0:T(8,128)(2,1)S(1)}, u32[]{:S(2)}, u32[]{:S(2)}) collective-permute-start(bf16[256,256]{1,0:T(8,128)(2,1)S(1)} %get-tuple-element.26), channel_id=1, source_target_pairs={{0,8},{8,0},{16,24},{24,16},{32,40},{40,32},{48,56},{56,48},{64,72... | collective-permute-start | bytes 393224 | tf_op jit(solution)/shard_map/ppermute | solution.py:321
  51.9 0.0 copy-start.8
  51.9 20.2 %all-gather = bf16[768,256]{1,0:T(8,128)(2,1)S(1)} all-gather(bf16[96,256]{1,0:T(8,128)(2,1)S(1)} %get-tuple-element.29), channel_id=2, replica_groups={{0,8,16,24,32,40,48,56},{64,72,80,88,96,104,112,120},{128,136,144,152,1..., dimensions={0}, use_global_device_ids=true | all-gather | bytes 442368 | tf_op jit(solution)/shard_map/all_gather | solution.py:323
  72.1 7.2 %attend.1 = (bf16[512,128]{1,0:T(8,128)(2,1)}, f32[512,128]{1,0:T(8,128)S(1)}, f32[512,256]{1,0:T(8,128)S(1)}, bf16[256,256]{1,0:T(8,128)(2,1)S(1)}, bf16[128,25...) custom-call(bf16[512,128]{1,0:T(8,128)(2,1)S(1)} %get-tuple-element.23.qn_ref, ...), custom_call_target="tpu_custom_call" | custom-call | flops 2013265920 | bytes 3145728 | tf_op jit(solution)/shard_map/attend/pallas_call | solution.py:281
  79.3 0.0 reduce-scatter.2.cloned.1.call-update
  79.3 4.5 %all-to-all-start.3 = ((bf16[8,48,256]{2,1,0:T(8,128)(2,1)}), bf16[8,48,256]{2,1,0:T(8,128)(2,1)S(1)}, u32[]{:S(2)}, u32[]{:S(2)}) async-start(bf16[8,48,256]{2,1,0:T(8,128)(2,1)} %get-tuple-element.35), calls=%async_computation.4 | async-start | bytes 393216 | tf_op jit(solution)/shard_map/all_to_all | solution.py:301
  83.8 3.4 %collective-permute-start.2 = (bf16[256,256]{1,0:T(8,128)(2,1)S(1)}, bf16[256,256]{1,0:T(8,128)(2,1)S(1)}, u32[]{:S(2)}, u32[]{:S(2)}) collective-permute-start(bf16[256,256]{1,0:T(8,128)(2,1)S(1)} %get-tuple-element.32), channel_id=1, source_target_pairs={{0,8},{8,0},{16,24},{24,16},{32,40},{40,32},{48,56},{56,48},{64,72... | collective-permute-start | bytes 393224 | tf_op jit(solution)/shard_map/ppermute | solution.py:341
  87.2 0.7 collective-permute-start.3
  87.8 0.0 collective-permute-done.3.p2_ref
  87.8 2.2 %collective-permute-done.2.p1_ref = bf16[256,256]{1,0:T(8,128)(2,1)S(1)} collective-permute-done((bf16[256,256]{1,0:T(8,128)(2,1)S(1)}, bf16[256,256]{1,0:T(8,128)(2,1)S(1)}, u32[]{:S(2)}, u32[]{:S(2)}) %collective-permute-start.2) | collective-permute-done | bytes 131104 | tf_op jit(solution)/shard_map/ppermute | solution.py:341
  90.0 2.4 %all-to-all-done.3.z_ref = bf16[8,48,256]{2,1,0:T(8,128)(2,1)S(1)} async-done(((bf16[8,48,256]{2,1,0:T(8,128)(2,1)}), bf16[8,48,256]{2,1,0:T(8,128)(2,1)S(1)}, u32[]{:S(2)}, u32[]{:S(2)}) %all-to-all-start.3) | async-done | bytes 196640 | tf_op jit(solution)/shard_map/all_to_all | solution.py:301
  92.4 0.2 columns.1
  92.6 0.0 copy-start.1
  92.6 11.7 %all_to_all.32.y_ref = bf16[8,16,256]{2,1,0:T(8,128)(2,1)S(1)} all-to-all(bf16[8,16,256]{2,1,0:T(8,128)(2,1)S(1)} %columns.1), channel_id=1, replica_groups={{0,64,128,192,256,320,384,448},{8,72,136,200,264,328,392,456},{16,80,14..., dimensions={0} | all-to-all | bytes 131072 | tf_op jit(solution)/shard_map/all_to_all | solution.py:301
  104.3 11.7 %reduce-scatter.2.cloned.1.call-done = bf16[1,96,256]{2,1,0:T(8,128)(2,1)} async-done(((bf16[8,96,256]{2,1,0:T(8,128)(2,1)}), bf16[1,96,256]{2,1,0:T(8,128)(2,1)}) %reduce-scatter.2.cloned.1.call-update) | async-done | bytes 49168 | tf_op jit(solution)/shard_map/reduce_scatter | solution.py:343
  116.0 0.8 copy-done.5
  116.8 1.3 total.1
  118.0 14.1 %all_to_all.33.refs_1_ = f32[8,8,128]{2,1,0:T(8,128)S(1)} all-to-all(f32[8,8,128]{2,1,0:T(8,128)S(1)} %get-tuple-element.37), channel_id=1, replica_groups=mesh['seq'=64,'head'=8] {'head'}, dimensions={0} | all-to-all | bytes 65536 | tf_op jit(solution)/shard_map/all_to_all | solution.py:301
  132.1 1.0 finish.1
  (13 shorter events, 0.0 us)
Async XLA Ops:
  7.2 0.9 copy-start
  8.1 0.9 copy-start.2
  9.0 14.2 %copy-start.4 = (bf16[512,128]{1,0:T(8,128)(2,1)S(1)}, bf16[512,128]{1,0:T(8,128)(2,1)}, u32[]{:S(2)}) copy-start(bf16[512,128]{1,0:T(8,128)(2,1)} %refs_3_.2) | copy-start | bytes 393220
  23.2 0.7 copy-start.6
  23.2 0.7 copy-start.7
  35.4 36.7 %all-to-all-start.2 = ((bf16[8,48,256]{2,1,0:T(8,128)(2,1)}), bf16[8,48,256]{2,1,0:T(8,128)(2,1)S(1)}, u32[]{:S(2)}, u32[]{:S(2)}) async-start(bf16[8,48,256]{2,1,0:T(8,128)(2,1)} %rows.1), calls=%async_computation.2 | async-start | bytes 393216 | tf_op jit(solution)/shard_map/all_to_all | solution.py:301
  45.4 70.5 %reduce-scatter.2.cloned.1.call-start = ((), (), s32[]{:S(2)}) async-start(), calls=%async_computation.7 | async-start | bytes 442368 | tf_op jit(solution)/shard_map/reduce_scatter | solution.py:343
  45.5 26.6 %collective-permute-start.1 = (bf16[128,256]{1,0:T(8,128)(2,1)S(1)}, bf16[128,256]{1,0:T(8,128)(2,1)S(1)}, u32[]{:S(2)}, u32[]{:S(2)}) collective-permute-start(bf16[128,256]{1,0:T(8,128)(2,1)S(1)} %get-tuple-element.27), channel_id=1, source_target_pairs={{8,16},{24,32},{40,48},{56,64},{72,80},{88,96},{104,112},{120,128}... | collective-permute-start | bytes 196616 | tf_op jit(solution)/shard_map/ppermute | solution.py:322
  46.1 26.0 %collective-permute-start = (bf16[256,256]{1,0:T(8,128)(2,1)S(1)}, bf16[256,256]{1,0:T(8,128)(2,1)S(1)}, u32[]{:S(2)}, u32[]{:S(2)}) collective-permute-start(bf16[256,256]{1,0:T(8,128)(2,1)S(1)} %get-tuple-element.26), channel_id=1, source_target_pairs={{0,8},{8,0},{16,24},{24,16},{32,40},{40,32},{48,56},{56,48},{64,72... | collective-permute-start | bytes 393224 | tf_op jit(solution)/shard_map/ppermute | solution.py:321
  51.9 20.2 %copy-start.8 = (bf16[512,128]{1,0:T(8,128)(2,1)S(1)}, bf16[512,128]{1,0:T(8,128)(2,1)}, u32[]{:S(2)}) copy-start(bf16[512,128]{1,0:T(8,128)(2,1)} %g_ref.1) | copy-start | bytes 393220
  79.3 13.1 %all-to-all-start.3 = ((bf16[8,48,256]{2,1,0:T(8,128)(2,1)}), bf16[8,48,256]{2,1,0:T(8,128)(2,1)S(1)}, u32[]{:S(2)}, u32[]{:S(2)}) async-start(bf16[8,48,256]{2,1,0:T(8,128)(2,1)} %get-tuple-element.35), calls=%async_computation.4 | async-start | bytes 393216 | tf_op jit(solution)/shard_map/all_to_all | solution.py:301
  83.8 6.2 %collective-permute-start.2 = (bf16[256,256]{1,0:T(8,128)(2,1)S(1)}, bf16[256,256]{1,0:T(8,128)(2,1)S(1)}, u32[]{:S(2)}, u32[]{:S(2)}) collective-permute-start(bf16[256,256]{1,0:T(8,128)(2,1)S(1)} %get-tuple-element.32), channel_id=1, source_target_pairs={{0,8},{8,0},{16,24},{24,16},{32,40},{40,32},{48,56},{56,48},{64,72... | collective-permute-start | bytes 393224 | tf_op jit(solution)/shard_map/ppermute | solution.py:341
  87.2 0.7 collective-permute-start.3
  92.4 23.5 %copy-start.3 = (bf16[512,128]{1,0:T(8,128)(2,1)S(1)}, bf16[512,128]{1,0:T(8,128)(2,1)}, u32[]{:S(2)}) copy-start(bf16[512,128]{1,0:T(8,128)(2,1)} %refs_3_.3) | copy-start | bytes 393220
  92.6 23.4 %copy-start.1 = (bf16[512,128]{1,0:T(8,128)(2,1)S(1)}, bf16[512,128]{1,0:T(8,128)(2,1)}, u32[]{:S(2)}) copy-start(bf16[512,128]{1,0:T(8,128)(2,1)} %refs_2_.3) | copy-start | bytes 393220
  116.0 0.8 copy-start.5
Sparse Core Ops, SparseCore 0:
  79.4 36.4 reduce-scatter.1

commit v6 on v2

--- a/solution.py
+++ b/solution.py
@@ -134,20 +134,57 @@
             out_ref[other, FAR + 32 :] = jnp.zeros((32, 2 * FEAT), BF16)
 
 
+def by_head(block):
+    lane = iota((LEAF, FEAT), 1)
+    zero = jnp.zeros((LEAF, FEAT), BF16)
+    return jnp.concatenate(
+        [jnp.where(lane < HEAD, block, zero), jnp.where(lane < HEAD, zero, block)], axis=0
+    )
+
+
+def peak(x):
+    return jnp.max(x, axis=0, keepdims=True)
+
+
+def add_up(x):
+    return jnp.sum(x, axis=0, keepdims=True)
+
+
+HALO_PIECE = {0: 0, LEAVES - 1: 2}
+
+
+def level_bias(rows, level):
+    return jnp.full((rows, 2 * LEAF), level * LN2, F32)
+
+
+def far_bias():
+    return jnp.concatenate(
+        [level_bias(LEAF, level) for level in (2, 3, 4)]
+        + [level_bias(16, level) for _ in range(8) for level in (5, 6, 7)],
+        axis=0,
+    )
+
+
+def outside_bias():
+    index = lax.axis_index("seq")
+    last = lax.axis_size("seq") - 1
+    return {
+        0: jnp.where(index > 0, 0.0, -jnp.inf).astype(F32),
+        LEAVES - 1: jnp.where(index < last, 0.0, -jnp.inf).astype(F32),
+    }
+
+
 def attend_kernel(
     qn_ref, kv_ref, one_ref, g_ref, p1_ref, p2_ref, z_ref,
-    att_ref, nqg_ref, tok_ref, p1o_ref, p2o_ref, zo_ref,
-    near, cross, near_grad, one_grad, cross_grad,
+    stat_ref, cross, halo, p1o_ref, p2o_ref, zo_ref,
+    q2_scr, g2_scr, score_scr, pgrad_scr, low_scr, sgrad_scr, rims, cross_grad,
 ):
     index = lax.axis_index("seq")
-    last = lax.axis_size("seq") - 1
     place = jnp.bitwise_and(index, 7)
     odd = jnp.bitwise_and(index, 1)
-    peer_side = pl.multiple_of((1 - odd) * 640, LEAF)
-    other_side = pl.multiple_of(odd * 640, LEAF)
-    near[LEAF : LEAF + ROWS] = kv_ref[...]
-    near[pl.ds(peer_side, LEAF)] = p1_ref[:LEAF]
-    near[pl.ds(other_side, LEAF)] = p2_ref[...]
+    peer_side = 1 - odd
+    halo[peer_side] = p1_ref[:LEAF]
+    halo[odd] = p2_ref[...]
     cross[:64] = z_ref[jnp.bitwise_xor(place, 1), FAR:]
     cross[64:128] = p1_ref[LEAF:]
     cross[128:192] = z_ref[jnp.bitwise_xor(place, 2), FAR:]
@@ -157,30 +194,98 @@
     for s in range(8):
         cross[384 + FAR * s : 384 + FAR * (s + 1)] = z_ref[s, :FAR]
 
-    def level_bias(rows, level):
-        return jnp.full((rows, 2 * LEAF), level * LN2, F32)
-
-    bias = jnp.concatenate(
-        [level_bias(LEAF, level) for level in (1, 2, 3, 4)]
-        + [level_bias(16, level) for _ in range(8) for level in (5, 6, 7)],
-        axis=0,
-    )
-    left = jnp.where(index > 0, 0.0, -jnp.inf).astype(F32)
-    right = jnp.where(index < last, 0.0, -jnp.inf).astype(F32)
-    lane = iota((LEAF, FEAT), 1)
+    bias = far_bias()
+    outside = outside_bias()
+    for b in range(LEAVES):
+        block = slice(b * LEAF, (b + 1) * LEAF)
+        lanes = slice(2 * b * LEAF, 2 * (b + 1) * LEAF)
+        q2 = by_head(qn_ref[block]) * jnp.asarray(0.125, BF16)
+        g2 = by_head(g_ref[block])
+        q2_scr[lanes] = q2
+        g2_scr[lanes] = g2
+        half = (1 - b // 2) * LEAF
+        top = None
+        for i in range(10):
+            rows = slice(i * LEAF, (i + 1) * LEAF)
+            if HALO_PIECE.get(b) == i:
+                kv = halo[0 if b == 0 else 1]
+                extra = outside[b]
+            elif i < 3:
+                kv = kv_ref[(b + i - 1) * LEAF : (b + i) * LEAF]
+                extra = None
+            elif i == 3:
+                kv = one_ref[half : half + LEAF]
+                extra = LN2
+            else:
+                kv = cross[(i - 4) * LEAF : (i - 3) * LEAF]
+                extra = bias[(i - 4) * LEAF : (i - 3) * LEAF]
+            score = dot(kv[:, :FEAT], q2, (1, 1))
+            if extra is not None:
+                score = score + extra
+            top = peak(score) if top is None else jnp.maximum(top, peak(score))
+            score_scr[b, rows] = score
+            pgrad_scr[b, rows] = dot(kv[:, FEAT:], g2, (1, 1))
+        total = jnp.zeros((1, 2 * LEAF), F32)
+        mixed = jnp.zeros((1, 2 * LEAF), F32)
+        for i in range(10):
+            rows = slice(i * LEAF, (i + 1) * LEAF)
+            weight = jnp.exp(score_scr[b, rows] - top)
+            total = total + add_up(weight)
+            mixed = mixed + add_up(weight * pgrad_scr[b, rows])
+            if i > 3 or HALO_PIECE.get(b) == i:
+                score_scr[b, rows] = weight
+        inverse = 1.0 / total
+        delta = mixed * inverse
+        stat_ref[b] = jnp.concatenate(
+            [top, inverse, delta, jnp.zeros((5, 2 * LEAF), F32)], axis=0
+        )
+        for i in range(10):
+            rows = slice(i * LEAF, (i + 1) * LEAF)
+            if i < 4 and HALO_PIECE.get(b) != i:
+                continue
+            prob = score_scr[b, rows] * inverse
+            low = prob.astype(BF16)
+            sgrad = (prob * (pgrad_scr[b, rows] - delta)).astype(BF16)
+            if i < 4:
+                rims[0 if b == 0 else 1, :, :FEAT] = dot(sgrad, q2, (1, 0)).astype(BF16)
+                rims[0 if b == 0 else 1, :, FEAT:] = dot(low, g2, (1, 0)).astype(BF16)
+            else:
+                low_scr[(i - 4) * LEAF : (i - 3) * LEAF, lanes] = low
+                sgrad_scr[(i - 4) * LEAF : (i - 3) * LEAF, lanes] = sgrad
+
+    cross_grad[:, :FEAT] = dot(sgrad_scr[...], q2_scr[...], (1, 0)).astype(BF16)
+    cross_grad[:, FEAT:] = dot(low_scr[...], g2_scr[...], (1, 0)).astype(BF16)
+    p1o_ref[:LEAF] = rims[peer_side]
+    p1o_ref[LEAF:] = cross_grad[64:128]
+    p2o_ref[...] = rims[odd]
+    for s in range(8):
+        zo_ref[s, :FAR] = cross_grad[384 + FAR * s : 384 + FAR * (s + 1)]
+    zo_ref[place, FAR:] = jnp.zeros((64, 2 * FEAT), BF16)
+    zo_ref[jnp.bitwise_xor(place, 1), FAR:] = cross_grad[:64]
+    zo_ref[jnp.bitwise_xor(place, 2), FAR:] = cross_grad[128:192]
+    zo_ref[jnp.bitwise_xor(place, 3), FAR:] = cross_grad[192:256]
+    for i in range(4):
+        other = jnp.bitwise_xor(place, 4 + i)
+        zo_ref[other, FAR : FAR + 32] = cross_grad[256 + 32 * i : 288 + 32 * i]
+        zo_ref[other, FAR + 32 :] = jnp.zeros((32, 2 * FEAT), BF16)
+
+
+def after_kernel(
+    stat_ref, qn_ref, kv_ref, one_ref, g_ref, halo, cross,
+    att_ref, nqg_ref, tok_ref, near, near_grad, one_grad,
+):
+    near[:LEAF] = halo[0]
+    near[LEAF : LEAF + ROWS] = kv_ref[...]
+    near[LEAF + ROWS :] = halo[1]
+    near_grad[...] = jnp.zeros_like(near_grad)
+    one_grad[...] = jnp.zeros_like(one_grad)
     feature = iota((FEAT, LEAF), 0)
-    zero = jnp.zeros((LEAF, FEAT), BF16)
-
-    def by_head(block):
-        return jnp.concatenate(
-            [jnp.where(lane < HEAD, block, zero), jnp.where(lane < HEAD, zero, block)], axis=0
-        )
+    bias = jnp.concatenate([level_bias(LEAF, 1), far_bias()], axis=0)
+    outside = outside_bias()
 
     def merge_heads(transposed):
         return jnp.where(feature < HEAD, transposed[:, :LEAF], transposed[:, LEAF:]).T
 
-    near_grad[...] = jnp.zeros_like(near_grad)
-    one_grad[...] = jnp.zeros_like(one_grad)
     for b in range(LEAVES):
         rows = slice(b * LEAF, (b + 1) * LEAF)
         near_rows = slice(b * LEAF, (b + 3) * LEAF)
@@ -193,52 +298,35 @@
         raw = dot(keys, q2, (1, 1))
         before, after = raw[:LEAF], raw[2 * LEAF : 3 * LEAF]
         if b == 0:
-            before = before + left
+            before = before + outside[b]
         if b == LEAVES - 1:
-            after = after + right
+            after = after + outside[b]
         scores = jnp.concatenate(
             [before, raw[LEAF : 2 * LEAF], after, raw[3 * LEAF :] + bias], axis=0
         )
-        weights = jnp.exp(scores - jnp.max(scores, axis=0, keepdims=True))
-        probs = weights * (1.0 / jnp.sum(weights, axis=0, keepdims=True))
+        probs = jnp.exp(scores - stat_ref[b, 0:1]) * stat_ref[b, 1:2]
         low = probs.astype(BF16)
-        prob_grad = dot(values, g2, (1, 1))
-        delta = jnp.sum(probs * prob_grad, axis=0, keepdims=True)
-        score_grad = (probs * (prob_grad - delta)).astype(BF16)
+        score_grad = (probs * (dot(values, g2, (1, 1)) - stat_ref[b, 2:3])).astype(BF16)
         att_ref[rows] = merge_heads(dot(values, low, (0, 0))).astype(BF16)
         nqg_ref[rows] = merge_heads(dot(keys, score_grad, (0, 0))) * 0.125
-        key_part = dot(score_grad, q2, (1, 0))
-        value_part = dot(low, g2, (1, 0))
-        for part, lanes in ((key_part, slice(0, FEAT)), (value_part, slice(FEAT, 2 * FEAT))):
+        for part, lanes in (
+            (dot(score_grad[: 4 * LEAF], q2, (1, 0)), slice(0, FEAT)),
+            (dot(low[: 4 * LEAF], g2, (1, 0)), slice(FEAT, 2 * FEAT)),
+        ):
             near_grad[near_rows, lanes] += part[: 3 * LEAF]
-            one_grad[half : half + LEAF, lanes] += part[3 * LEAF : 4 * LEAF]
-            if b == 0:
-                cross_grad[:, lanes] = part[4 * LEAF :]
-            else:
-                cross_grad[:, lanes] += part[4 * LEAF :]
-
+            one_grad[half : half + LEAF, lanes] += part[3 * LEAF :]
     spread = spreading(0, 256, 1).astype(BF16)
     high = one_grad[...].astype(BF16)
     rest = (one_grad[...] - high.astype(F32)).astype(BF16)
     tok_ref[...] = near_grad[LEAF : LEAF + ROWS] + dot(spread, high, (1, 0)) + dot(spread, rest, (1, 0))
-    p1o_ref[:LEAF] = near_grad[pl.ds(peer_side, LEAF)].astype(BF16)
-    p1o_ref[LEAF:] = cross_grad[64:128].astype(BF16)
-    p2o_ref[...] = near_grad[pl.ds(other_side, LEAF)].astype(BF16)
-    for s in range(8):
-        zo_ref[s, :FAR] = cross_grad[384 + FAR * s : 384 + FAR * (s + 1)].astype(BF16)
-    zo_ref[place, FAR:] = jnp.zeros((64, 2 * FEAT), BF16)
-    zo_ref[jnp.bitwise_xor(place, 1), FAR:] = cross_grad[:64].astype(BF16)
-    zo_ref[jnp.bitwise_xor(place, 2), FAR:] = cross_grad[128:192].astype(BF16)
-    zo_ref[jnp.bitwise_xor(place, 3), FAR:] = cross_grad[192:256].astype(BF16)
-    for i in range(4):
-        other = jnp.bitwise_xor(place, 4 + i)
-        zo_ref[other, FAR : FAR + 32] = cross_grad[256 + 32 * i : 288 + 32 * i].astype(BF16)
-        zo_ref[other, FAR + 32 :] = jnp.zeros((32, 2 * FEAT), BF16)
-
-
-def column_kernel(z_ref, out_ref):
+
+
+def column_kernel(z_ref, p1_ref, p2_ref, tok_ref, out_ref, far_rows, sem):
     column = jnp.right_shift(lax.axis_index("seq"), 3)
-    far = jnp.sum(z_ref[:, :FAR].astype(F32), axis=0).astype(BF16)
+    copy = pltpu.make_async_copy(z_ref.at[:, pl.ds(0, FAR)], far_rows, sem)
+    copy.start()
+    copy.wait()
+    far = jnp.sum(far_rows[...].astype(F32), axis=0).astype(BF16)
     slots = dot(far_pick((112, FAR), 1), far, (1, 0)).astype(BF16)
     out_ref[column] = jnp.zeros((16, 2 * FEAT), BF16)
     for d in range(1, 8):
@@ -292,12 +380,13 @@
         ).astype(BF16)
 
 
-def call(kernel, outs, args, scratch=(), flops=0, name=None):
+def call(kernel, outs, args, scratch=(), flops=0, name=None, spaces=None):
     many = isinstance(outs, list)
     moved = sum(math.prod(x.shape) * x.dtype.itemsize for x in list(args) + (outs if many else [outs]))
     return pl.pallas_call(
         kernel,
         out_shape=outs,
+        in_specs=[pl.BlockSpec(memory_space=space) for space in spaces or [pltpu.VMEM] * len(args)],
         scratch_shapes=list(scratch),
         compiler_params=PARAMS,
         cost_estimate=pl.CostEstimate(flops=flops, bytes_accessed=moved, transcendentals=0),
@@ -339,24 +428,47 @@
     yrecv = exchange(ysend, "seq", COLUMN_GROUPS)
     zsend = call(row_kernel, sds(8, SLOT, 256), (yrecv, lv), name="rows")
     zrecv = exchange(zsend, "seq", ROW_GROUPS)
-    attended, nqg, tok, p1, p2, zsend = call(
+    stat, cross, halo, p1, p2, zsend = call(
         attend_kernel,
-        [sds(ROWS, FEAT), sds(ROWS, FEAT, dtype=F32), sds(ROWS, 256, dtype=F32), sds(192, 256), sds(LEAF, 256), sds(8, SLOT, 256)],
+        [sds(LEAVES, 8, 256, dtype=F32), sds(768, 256), sds(2, LEAF, 256)]
+        + [sds(192, 256), sds(LEAF, 256), sds(8, SLOT, 256)],
         (qn, kv, one, out_grad, p1, p2, zrecv),
         scratch=[
+            pltpu.VMEM((1024, FEAT), BF16),
+            pltpu.VMEM((1024, FEAT), BF16),
+            pltpu.VMEM((LEAVES, KEYS, 256), F32),
+            pltpu.VMEM((LEAVES, KEYS, 256), F32),
+            pltpu.VMEM((768, 1024), BF16),
+            pltpu.VMEM((768, 1024), BF16),
+            pltpu.VMEM((2, LEAF, 256), BF16),
             pltpu.VMEM((768, 256), BF16),
+        ],
+        flops=4 * 4 * 2 * 256 * KEYS * FEAT,
+        name="attend",
+    )
+    p1 = lax.ppermute(p1, "seq", peer)
+    p2 = lax.ppermute(p2, "seq", beside)
+    zrecv = exchange(zsend, "seq", ROW_GROUPS)
+    attended, nqg, tok = call(
+        after_kernel,
+        [sds(ROWS, FEAT), sds(ROWS, FEAT, dtype=F32), sds(ROWS, 256, dtype=F32)],
+        (stat, qn, kv, one, out_grad, halo, cross),
+        scratch=[
             pltpu.VMEM((768, 256), BF16),
             pltpu.VMEM((768, 256), F32),
             pltpu.VMEM((256, 256), F32),
-            pltpu.VMEM((768, 256), F32),
         ],
-        flops=4 * 6 * 2 * 256 * KEYS * FEAT,
-        name="attend",
-    )
-    p1 = lax.ppermute(p1, "seq", peer)
-    p2 = lax.ppermute(p2, "seq", beside)
-    zrecv = exchange(zsend, "seq", ROW_GROUPS)
-    ysend = call(column_kernel, sds(8, 16, 256), (zrecv,), name="columns")
+        flops=4 * 5 * 2 * 256 * KEYS * FEAT,
+        name="after",
+    )
+    ysend = call(
+        column_kernel,
+        sds(8, 16, 256),
+        (zrecv, p1, p2, tok),
+        scratch=[pltpu.VMEM((8, FAR, 256), BF16), pltpu.SemaphoreType.DMA],
+        spaces=[pl.ANY] * 4,
+        name="columns",
+    )
     yrecv = exchange(ysend, "seq", COLUMN_GROUPS)
     nkg, value_grad, inner = call(
         total_kernel,

time: 107 us -> 103 us (0.963)
  the two profiles are of different devices: /device:TPU:32 before, /device:TPU:1 now
where the time goes in v6:
time: 103 us; the launch traced here: 102 us
  blocking collectives  47.7 us (46%)
  starting transfers between devices  25.7 us (25%)
  Pallas kernels  13.7 us (13%)
  waiting for transfers between devices  11.7 us (11%)
  local copies, waits for them, and re-layouts  2.49 us (2%)
    all_to_all x4, blocking collectives, exchange(): return lax.all_to_all(x, axis, 0, 0, axis_index_groups=groups, tiled=True)  47.7 us
    all_to_all x2, starting transfers between devices, exchange(): return lax.all_to_all(x, axis, 0, 0, axis_index_groups=groups, tiled=True)  15.3 us
    pallas_call x8, Pallas kernels, call(): pl.pallas_call(kernel, out_shape=outs, in_specs=[pl.BlockSpec(memory_spac...  13.7 us
    ppermute x2, starting transfers between devices, local(): p1 = lax.ppermute(p1, 'seq', peer)  9.15 us
    ppermute x2, waiting for transfers between devices, local(): p1 = lax.ppermute(p1, 'seq', peer)  8.36 us
    all_to_all x2, waiting for transfers between devices, exchange(): return lax.all_to_all(x, axis, 0, 0, axis_index_groups=groups, tiled=True)  3.3 us
    unnamed x16, local copies, waits for them, and re-layouts  2.49 us
  transfers between devices with their start and end apart: 6, of which 4 were waited for; matrix products, arithmetic and copies ran while one was open for 0% of the time, Pallas kernels for 4%

profile of v6, /device:TPU:1, one launch (start us, length us, event | category | flops | bytes accessed | tf_op | source)
XLA Modules:
  0.0 102.0 jit_solution(2876820795507125654)
XLA Ops:
  0.6 0.0 copy-start
  0.6 0.9 copy-done
  1.5 0.9 copy-done.2
  2.4 0.2 squares.1
  2.7 14.0 %all_to_all.30.refs_0_ = f32[8,8,128]{2,1,0:T(8,128)S(1)} all-to-all(f32[8,8,128]{2,1,0:T(8,128)S(1)} %squares.1), channel_id=1, replica_groups=mesh['seq'=64,'head'=8] {'head'}, dimensions={0} | all-to-all | bytes 65536 | tf_op jit(solution)/shard_map/all_to_all | solution.py:406
  16.6 0.0 copy-done.4
  16.6 0.6 copy-done.5
  17.3 0.0 copy-done.6
  17.3 0.5 norm.1
  17.8 10.2 %all_to_all.31.y_ref = bf16[8,16,256]{2,1,0:T(8,128)(2,1)S(1)} all-to-all(bf16[8,16,256]{2,1,0:T(8,128)(2,1)S(1)} %get-tuple-element.30), channel_id=1, replica_groups={{0,64,128,192,256,320,384,448},{8,72,136,200,264,328,392,456},{16,80,14..., dimensions={0} | all-to-all | bytes 131072 | tf_op jit(solution)/shard_map/all_to_all | solution.py:406
  28.0 0.9 rows.1
  29.0 10.2 %all-to-all-start.2 = ((bf16[8,112,256]{2,1,0:T(8,128)(2,1)}), bf16[8,112,256]{2,1,0:T(8,128)(2,1)S(1)}, u32[]{:S(2)}, u32[]{:S(2)}) async-start(bf16[8,112,256]{2,1,0:T(8,128)(2,1)} %rows.1), calls=%async_computation.2 | async-start | bytes 917504 | tf_op jit(solution)/shard_map/all_to_all | solution.py:406
  39.1 3.4 %collective-permute-start = (bf16[192,256]{1,0:T(8,128)(2,1)S(1)}, bf16[192,256]{1,0:T(8,128)(2,1)S(1)}, u32[]{:S(2)}, u32[]{:S(2)}) collective-permute-start(bf16[192,256]{1,0:T(8,128)(2,1)S(1)} %get-tuple-element.28), channel_id=1, source_target_pairs={{0,8},{8,0},{16,24},{24,16},{32,40},{40,32},{48,56},{56,48},{64,72... | collective-permute-start | bytes 294920 | tf_op jit(solution)/shard_map/ppermute | solution.py:426
  42.5 0.7 collective-permute-start.1
  43.2 0.0 collective-permute-done.1.p2_ref
  43.2 7.6 %collective-permute-done.p1_ref = bf16[192,256]{1,0:T(8,128)(2,1)S(1)} collective-permute-done((bf16[192,256]{1,0:T(8,128)(2,1)S(1)}, bf16[192,256]{1,0:T(8,128)(2,1)S(1)}, u32[]{:S(2)}, u32[]{:S(2)}) %collective-permute-start) | collective-permute-done | bytes 98336 | tf_op jit(solution)/shard_map/ppermute | solution.py:426
  50.8 1.7 %all-to-all-done.2.z_ref = bf16[8,112,256]{2,1,0:T(8,128)(2,1)S(1)} async-done(((bf16[8,112,256]{2,1,0:T(8,128)(2,1)}), bf16[8,112,256]{2,1,0:T(8,128)(2,1)S(1)}, u32[]{:S(2)}, u32[]{:S(2)}) %all-to-all-start.2) | async-done | bytes 458784 | tf_op jit(solution)/shard_map/all_to_all | solution.py:406
  52.5 0.0 copy-done.7
  52.5 5.6 %attend.1 = (f32[4,8,256]{2,1,0:T(8,128)S(1)}, bf16[768,256]{1,0:T(8,128)(2,1)S(1)}, bf16[2,128,256]{2,1,0:T(8,128)(2,1)S(1)}, bf16[192,256]{1,0:T(8,128)(2,1)S(...) custom-call(bf16[512,128]{1,0:T(8,128)(2,1)S(1)} %get-tuple-element.25.qn_ref, ...), custom_call_target="tpu_custom_call" | custom-call | flops 1342177280 | bytes 2457600 | tf_op jit(solution)/shard_map/attend/pallas_call | solution.py:386
  58.0 5.1 %all-to-all-start.3 = ((bf16[8,112,256]{2,1,0:T(8,128)(2,1)}), bf16[8,112,256]{2,1,0:T(8,128)(2,1)S(1)}, u32[]{:S(2)}, u32[]{:S(2)}) async-start(bf16[8,112,256]{2,1,0:T(8,128)(2,1)} %get-tuple-element.39), calls=%async_computation.3 | async-start | bytes 917504 | tf_op jit(solution)/shard_map/all_to_all | solution.py:406
  63.1 0.7 collective-permute-start.3
  63.8 5.8 %collective-permute-start.2 = (bf16[192,256]{1,0:T(8,128)(2,1)S(1)}, bf16[192,256]{1,0:T(8,128)(2,1)S(1)}, u32[]{:S(2)}, u32[]{:S(2)}) collective-permute-start(bf16[192,256]{1,0:T(8,128)(2,1)S(1)} %get-tuple-element.37), channel_id=1, source_target_pairs={{0,8},{8,0},{16,24},{24,16},{32,40},{40,32},{48,56},{56,48},{64,72... | collective-permute-start | bytes 294920 | tf_op jit(solution)/shard_map/ppermute | solution.py:449
  69.6 3.8 %after.1 = (bf16[512,128]{1,0:T(8,128)(2,1)}, f32[512,128]{1,0:T(8,128)S(1)}, f32[512,256]{1,0:T(8,128)S(1)}) custom-call(f32[4,8,256]{2,1,0:T(8,128)S(1)} %get-tuple-element.32.stat_ref, bf16[512,128]{1,0:T(8,128)(2,1)S(1)} %get-tuple-element.25.qn_ref, bf16[512,256]{1,0:T(8,128)(2,1)S(1)} %get-tuple-element.26.kv_ref, ...), custom_call_target="tpu_custom_call" | custom-call | flops 1677721600 | bytes 2129920 | tf_op jit(solution)/shard_map/after/pallas_call | solution.py:386
  73.4 0.0 collective-permute-done.3.p2_ref
  73.4 0.8 collective-permute-done.2.p1_ref
  74.2 1.6 %all-to-all-done.3.z_ref = bf16[8,112,256]{2,1,0:T(8,128)(2,1)S(1)} async-done(((bf16[8,112,256]{2,1,0:T(8,128)(2,1)}), bf16[8,112,256]{2,1,0:T(8,128)(2,1)S(1)}, u32[]{:S(2)}, u32[]{:S(2)}) %all-to-all-start.3) | async-done | bytes 458784 | tf_op jit(solution)/shard_map/all_to_all | solution.py:406
  75.8 0.2 columns.1
  76.0 0.0 copy-start.1
  76.0 11.0 %all_to_all.32.y_ref = bf16[8,16,256]{2,1,0:T(8,128)(2,1)S(1)} all-to-all(bf16[8,16,256]{2,1,0:T(8,128)(2,1)S(1)} %columns.1), channel_id=1, replica_groups={{0,64,128,192,256,320,384,448},{8,72,136,200,264,328,392,456},{16,80,14..., dimensions={0} | all-to-all | bytes 131072 | tf_op jit(solution)/shard_map/all_to_all | solution.py:406
  87.0 1.4 %total.1 = (f32[512,128]{1,0:T(8,128)S(1)}, bf16[512,128]{1,0:T(8,128)(2,1)}, f32[8,8,128]{2,1,0:T(8,128)S(1)}) custom-call(f32[512,256]{1,0:T(8,128)S(1)} %get-tuple-element.36.tok_ref, bf16[192,256]{1,0:T(8,128)(2,1)S(1)} %collective-permute-done.2.p1_ref, bf16[128,256]{1,0:T(8,128)(2,1)S(1)} %collective-permute-done.3.p2_ref, ...), custom_call_target="tpu_custom_call" | custom-call | bytes 2163712 | tf_op jit(solution)/shard_map/total/pallas_call | solution.py:386
  88.4 12.6 %all_to_all.33.refs_1_ = f32[8,8,128]{2,1,0:T(8,128)S(1)} all-to-all(f32[8,8,128]{2,1,0:T(8,128)S(1)} %get-tuple-element.41), channel_id=1, replica_groups=mesh['seq'=64,'head'=8] {'head'}, dimensions={0} | all-to-all | bytes 65536 | tf_op jit(solution)/shard_map/all_to_all | solution.py:406
  101.0 1.0 finish.1
  (8 shorter events, 0.0 us)
Async XLA Ops:
  0.6 0.9 copy-start
  1.5 0.9 copy-start.2
  2.4 14.2 %copy-start.4 = (bf16[512,128]{1,0:T(8,128)(2,1)S(1)}, bf16[512,128]{1,0:T(8,128)(2,1)}, u32[]{:S(2)}) copy-start(bf16[512,128]{1,0:T(8,128)(2,1)} %refs_3_.2) | copy-start | bytes 393220
  16.6 0.7 copy-start.5
  16.6 0.7 copy-start.6
  29.0 23.5 %copy-start.7 = (bf16[512,128]{1,0:T(8,128)(2,1)S(1)}, bf16[512,128]{1,0:T(8,128)(2,1)}, u32[]{:S(2)}) copy-start(bf16[512,128]{1,0:T(8,128)(2,1)} %g_ref.3) | copy-start | bytes 393220
  29.0 23.5 %all-to-all-start.2 = ((bf16[8,112,256]{2,1,0:T(8,128)(2,1)}), bf16[8,112,256]{2,1,0:T(8,128)(2,1)S(1)}, u32[]{:S(2)}, u32[]{:S(2)}) async-start(bf16[8,112,256]{2,1,0:T(8,128)(2,1)} %rows.1), calls=%async_computation.2 | async-start | bytes 917504 | tf_op jit(solution)/shard_map/all_to_all | solution.py:406
  39.1 11.7 %collective-permute-start = (bf16[192,256]{1,0:T(8,128)(2,1)S(1)}, bf16[192,256]{1,0:T(8,128)(2,1)S(1)}, u32[]{:S(2)}, u32[]{:S(2)}) collective-permute-start(bf16[192,256]{1,0:T(8,128)(2,1)S(1)} %get-tuple-element.28), channel_id=1, source_target_pairs={{0,8},{8,0},{16,24},{24,16},{32,40},{40,32},{48,56},{56,48},{64,72... | collective-permute-start | bytes 294920 | tf_op jit(solution)/shard_map/ppermute | solution.py:426
  42.5 0.7 collective-permute-start.1
  58.0 17.8 %all-to-all-start.3 = ((bf16[8,112,256]{2,1,0:T(8,128)(2,1)}), bf16[8,112,256]{2,1,0:T(8,128)(2,1)S(1)}, u32[]{:S(2)}, u32[]{:S(2)}) async-start(bf16[8,112,256]{2,1,0:T(8,128)(2,1)} %get-tuple-element.39), calls=%async_computation.3 | async-start | bytes 917504 | tf_op jit(solution)/shard_map/all_to_all | solution.py:406
  63.1 10.3 %collective-permute-start.3 = (bf16[128,256]{1,0:T(8,128)(2,1)S(1)}, bf16[128,256]{1,0:T(8,128)(2,1)S(1)}, u32[]{:S(2)}, u32[]{:S(2)}) collective-permute-start(bf16[128,256]{1,0:T(8,128)(2,1)S(1)} %get-tuple-element.38), channel_id=1, source_target_pairs={{8,16},{24,32},{40,48},{56,64},{72,80},{88,96},{104,112},{120,128}... | collective-permute-start | bytes 196616 | tf_op jit(solution)/shard_map/ppermute | solution.py:450
  63.8 10.4 %collective-permute-start.2 = (bf16[192,256]{1,0:T(8,128)(2,1)S(1)}, bf16[192,256]{1,0:T(8,128)(2,1)S(1)}, u32[]{:S(2)}, u32[]{:S(2)}) collective-permute-start(bf16[192,256]{1,0:T(8,128)(2,1)S(1)} %get-tuple-element.37), channel_id=1, source_target_pairs={{0,8},{8,0},{16,24},{24,16},{32,40},{40,32},{48,56},{56,48},{64,72... | collective-permute-start | bytes 294920 | tf_op jit(solution)/shard_map/ppermute | solution.py:449
  75.8 11.2 %copy-start.3 = (bf16[512,128]{1,0:T(8,128)(2,1)S(1)}, bf16[512,128]{1,0:T(8,128)(2,1)}, u32[]{:S(2)}) copy-start(bf16[512,128]{1,0:T(8,128)(2,1)} %refs_3_.3) | copy-start | bytes 393220
  76.0 11.0 %copy-start.1 = (bf16[512,128]{1,0:T(8,128)(2,1)S(1)}, bf16[512,128]{1,0:T(8,128)(2,1)}, u32[]{:S(2)}) copy-start(bf16[512,128]{1,0:T(8,128)(2,1)} %refs_2_.3) | copy-start | bytes 393220

commit v7 on v6

--- a/solution.py
+++ b/solution.py
@@ -153,15 +153,9 @@
 HALO_PIECE = {0: 0, LEAVES - 1: 2}
 
 
-def level_bias(rows, level):
-    return jnp.full((rows, 2 * LEAF), level * LN2, F32)
-
-
 def far_bias():
     return jnp.concatenate(
-        [level_bias(LEAF, level) for level in (2, 3, 4)]
-        + [level_bias(16, level) for _ in range(8) for level in (5, 6, 7)],
-        axis=0,
+        [jnp.full((LEAF, 2 * LEAF), level * LN2, F32) for level in range(1, 8)], axis=0
     )
 
 
@@ -169,15 +163,54 @@
     index = lax.axis_index("seq")
     last = lax.axis_size("seq") - 1
     return {
-        0: jnp.where(index > 0, 0.0, -jnp.inf).astype(F32),
-        LEAVES - 1: jnp.where(index < last, 0.0, -jnp.inf).astype(F32),
+        0: jnp.where(index > 0, 0.0, -1e30).astype(F32),
+        LEAVES - 1: jnp.where(index < last, 0.0, -1e30).astype(F32),
     }
 
 
+def weigh(kv, q2, g2):
+    score = dot(kv[:, :FEAT], q2, (1, 1))
+    top = peak(score)
+    weight = jnp.exp(score - top)
+    pgrad = dot(kv[:, FEAT:], g2, (1, 1))
+    return weight, pgrad, (top, add_up(weight), add_up(weight * pgrad))
+
+
+def combine(stats):
+    top = stats[0][0]
+    for stat in stats[1:]:
+        top = jnp.maximum(top, stat[0])
+    factors = [jnp.exp(stat[0] - top) for stat in stats]
+    total = sum(factor * stat[1] for factor, stat in zip(factors, stats))
+    mixed = sum(factor * stat[2] for factor, stat in zip(factors, stats))
+    return top, total, mixed, factors
+
+
+def scaled_queries(block):
+    return by_head(block) * jnp.asarray(0.125, BF16)
+
+
+def near_kernel(qn_ref, kv_ref, one_ref, g_ref, stat_ref):
+    for b in range(LEAVES):
+        block = slice(b * LEAF, (b + 1) * LEAF)
+        q2 = scaled_queries(qn_ref[block])
+        g2 = by_head(g_ref[block])
+        half = (1 - b // 2) * LEAF
+        stats = [
+            weigh(kv_ref[(b + i - 1) * LEAF : (b + i) * LEAF], q2, g2)[2]
+            for i in range(3)
+            if HALO_PIECE.get(b) != i
+        ]
+        top, total, mixed = weigh(one_ref[half : half + LEAF], q2, g2)[2]
+        stats.append((top + LN2, total, mixed))
+        top, total, mixed, _ = combine(stats)
+        stat_ref[b] = jnp.concatenate([top, total, mixed, jnp.zeros((5, 2 * LEAF), F32)], axis=0)
+
+
 def attend_kernel(
-    qn_ref, kv_ref, one_ref, g_ref, p1_ref, p2_ref, z_ref,
+    qn_ref, g_ref, near_ref, p1_ref, p2_ref, z_ref,
     stat_ref, cross, halo, p1o_ref, p2o_ref, zo_ref,
-    q2_scr, g2_scr, score_scr, pgrad_scr, low_scr, sgrad_scr, rims, cross_grad,
+    q2_scr, g2_scr, weight_scr, pgrad_scr, low_scr, sgrad_scr, rims, cross_grad,
 ):
     index = lax.axis_index("seq")
     place = jnp.bitwise_and(index, 7)
@@ -192,66 +225,44 @@
     for i in range(4):
         cross[256 + 32 * i : 288 + 32 * i] = z_ref[jnp.bitwise_xor(place, 4 + i), FAR : FAR + 32]
     for s in range(8):
-        cross[384 + FAR * s : 384 + FAR * (s + 1)] = z_ref[s, :FAR]
-
-    bias = far_bias()
+        for j in range(3):
+            at = 384 + LEAF * j + 16 * s
+            cross[at : at + 16] = z_ref[s, 16 * j : 16 * (j + 1)]
+
     outside = outside_bias()
     for b in range(LEAVES):
         block = slice(b * LEAF, (b + 1) * LEAF)
         lanes = slice(2 * b * LEAF, 2 * (b + 1) * LEAF)
-        q2 = by_head(qn_ref[block]) * jnp.asarray(0.125, BF16)
+        q2 = scaled_queries(qn_ref[block])
         g2 = by_head(g_ref[block])
         q2_scr[lanes] = q2
         g2_scr[lanes] = g2
-        half = (1 - b // 2) * LEAF
-        top = None
-        for i in range(10):
-            rows = slice(i * LEAF, (i + 1) * LEAF)
-            if HALO_PIECE.get(b) == i:
-                kv = halo[0 if b == 0 else 1]
-                extra = outside[b]
-            elif i < 3:
-                kv = kv_ref[(b + i - 1) * LEAF : (b + i) * LEAF]
-                extra = None
-            elif i == 3:
-                kv = one_ref[half : half + LEAF]
-                extra = LN2
-            else:
-                kv = cross[(i - 4) * LEAF : (i - 3) * LEAF]
-                extra = bias[(i - 4) * LEAF : (i - 3) * LEAF]
-            score = dot(kv[:, :FEAT], q2, (1, 1))
-            if extra is not None:
-                score = score + extra
-            top = peak(score) if top is None else jnp.maximum(top, peak(score))
-            score_scr[b, rows] = score
-            pgrad_scr[b, rows] = dot(kv[:, FEAT:], g2, (1, 1))
-        total = jnp.zeros((1, 2 * LEAF), F32)
-        mixed = jnp.zeros((1, 2 * LEAF), F32)
-        for i in range(10):
-            rows = slice(i * LEAF, (i + 1) * LEAF)
-            weight = jnp.exp(score_scr[b, rows] - top)
-            total = total + add_up(weight)
-            mixed = mixed + add_up(weight * pgrad_scr[b, rows])
-            if i > 3 or HALO_PIECE.get(b) == i:
-                score_scr[b, rows] = weight
+        side = 0 if b == 0 else 1
+        pieces = list(range(7 if b in HALO_PIECE else 6))
+        stats = [(near_ref[b, 0:1], near_ref[b, 1:2], near_ref[b, 2:3])]
+        for i in pieces:
+            kv = cross[i * LEAF : (i + 1) * LEAF] if i < 6 else halo[side]
+            weight, pgrad, (top, total, mixed) = weigh(kv, q2, g2)
+            weight_scr[b, i] = weight
+            pgrad_scr[b, i] = pgrad
+            bias = (i + 2) * LN2 if i < 6 else outside[b]
+            stats.append((top + bias, total, mixed))
+        top, total, mixed, factors = combine(stats)
         inverse = 1.0 / total
         delta = mixed * inverse
         stat_ref[b] = jnp.concatenate(
             [top, inverse, delta, jnp.zeros((5, 2 * LEAF), F32)], axis=0
         )
-        for i in range(10):
-            rows = slice(i * LEAF, (i + 1) * LEAF)
-            if i < 4 and HALO_PIECE.get(b) != i:
-                continue
-            prob = score_scr[b, rows] * inverse
+        for i in pieces:
+            prob = weight_scr[b, i] * (factors[i + 1] * inverse)
             low = prob.astype(BF16)
-            sgrad = (prob * (pgrad_scr[b, rows] - delta)).astype(BF16)
-            if i < 4:
-                rims[0 if b == 0 else 1, :, :FEAT] = dot(sgrad, q2, (1, 0)).astype(BF16)
-                rims[0 if b == 0 else 1, :, FEAT:] = dot(low, g2, (1, 0)).astype(BF16)
+            sgrad = (prob * (pgrad_scr[b, i] - delta)).astype(BF16)
+            if i < 6:
+                low_scr[i * LEAF : (i + 1) * LEAF, lanes] = low
+                sgrad_scr[i * LEAF : (i + 1) * LEAF, lanes] = sgrad
             else:
-                low_scr[(i - 4) * LEAF : (i - 3) * LEAF, lanes] = low
-                sgrad_scr[(i - 4) * LEAF : (i - 3) * LEAF, lanes] = sgrad
+                rims[side, :, :FEAT] = dot(sgrad, q2, (1, 0)).astype(BF16)
+                rims[side, :, FEAT:] = dot(low, g2, (1, 0)).astype(BF16)
 
     cross_grad[:, :FEAT] = dot(sgrad_scr[...], q2_scr[...], (1, 0)).astype(BF16)
     cross_grad[:, FEAT:] = dot(low_scr[...], g2_scr[...], (1, 0)).astype(BF16)
@@ -259,7 +270,9 @@
     p1o_ref[LEAF:] = cross_grad[64:128]
     p2o_ref[...] = rims[odd]
     for s in range(8):
-        zo_ref[s, :FAR] = cross_grad[384 + FAR * s : 384 + FAR * (s + 1)]
+        for j in range(3):
+            at = 384 + LEAF * j + 16 * s
+            zo_ref[s, 16 * j : 16 * (j + 1)] = cross_grad[at : at + 16]
     zo_ref[place, FAR:] = jnp.zeros((64, 2 * FEAT), BF16)
     zo_ref[jnp.bitwise_xor(place, 1), FAR:] = cross_grad[:64]
     zo_ref[jnp.bitwise_xor(place, 2), FAR:] = cross_grad[128:192]
@@ -280,7 +293,7 @@
     near_grad[...] = jnp.zeros_like(near_grad)
     one_grad[...] = jnp.zeros_like(one_grad)
     feature = iota((FEAT, LEAF), 0)
-    bias = jnp.concatenate([level_bias(LEAF, 1), far_bias()], axis=0)
+    bias = far_bias()
     outside = outside_bias()
 
     def merge_heads(transposed):
@@ -290,7 +303,7 @@
         rows = slice(b * LEAF, (b + 1) * LEAF)
         near_rows = slice(b * LEAF, (b + 3) * LEAF)
         half = (1 - b // 2) * LEAF
-        q2 = by_head(qn_ref[rows]) * jnp.asarray(0.125, BF16)
+        q2 = scaled_queries(qn_ref[rows])
         g2 = by_head(g_ref[rows])
         kv = jnp.concatenate([near[near_rows], one_ref[half : half + LEAF], cross[...]], axis=0)
         keys = kv[:, :FEAT]
@@ -333,12 +346,8 @@
         out_ref[jnp.bitwise_xor(column, d)] = slots[16 * (d - 1) : 16 * d]
 
 
-def total_kernel(
-    tok_ref, p1_ref, p2_ref, z_ref, y_ref,
-    q_ref, k_ref, qg_ref, kg_ref, nqg_ref, nkg_ref, vg_ref, sum_ref, acc,
-):
+def middle_kernel(tok_ref, p1_ref, p2_ref, z_ref, q_ref, qg_ref, nqg_ref, acc_ref, sum_ref):
     index = lax.axis_index("seq")
-    column = jnp.right_shift(index, 3)
     place = jnp.bitwise_and(index, 7)
     odd = jnp.bitwise_and(index, 1)
     pieces = [z_ref[jnp.bitwise_xor(place, 1), FAR:], p1_ref[LEAF:]]
@@ -347,21 +356,25 @@
         rows = ROWS >> ROW_LEVEL[d]
         pieces.append(z_ref[jnp.bitwise_xor(place, d), FAR : FAR + rows])
         maps.append(spreading(0, rows, ROW_LEVEL[d]))
-    for d in range(1, 8):
-        pieces.append(y_ref[jnp.bitwise_xor(column, d)])
-        maps.append(spreading(0, 16, COLUMN_LEVEL[d]))
     spread = jnp.concatenate(maps, axis=1).astype(BF16)
-    acc[...] = tok_ref[...] + dot(spread, jnp.concatenate(pieces, axis=0), (1, 0))
-    acc[pl.ds(pl.multiple_of((1 - odd) * 384, LEAF), LEAF)] += p1_ref[:LEAF].astype(F32)
-    acc[pl.ds(pl.multiple_of(odd * 384, LEAF), LEAF)] += p2_ref[...].astype(F32)
-    vg_ref[...] = acc[:, FEAT:].astype(BF16)
-    key_total = acc[:, :FEAT]
+    acc_ref[...] = tok_ref[...] + dot(spread, jnp.concatenate(pieces, axis=0), (1, 0))
+    acc_ref[pl.ds(pl.multiple_of((1 - odd) * 384, LEAF), LEAF)] += p1_ref[:LEAF].astype(F32)
+    acc_ref[pl.ds(pl.multiple_of(odd * 384, LEAF), LEAF)] += p2_ref[...].astype(F32)
+    sums = token_sums(q_ref[...].astype(F32) * qg_ref[...] * nqg_ref[...])
+    sum_ref[...] = jnp.concatenate(sums + [jnp.zeros((LEAVES, FEAT), F32)], axis=0)
+
+
+def total_kernel(acc_ref, y_ref, k_ref, kg_ref, qsum_ref, nkg_ref, vg_ref, sum_ref):
+    column = jnp.right_shift(lax.axis_index("seq"), 3)
+    pieces = [y_ref[jnp.bitwise_xor(column, d)] for d in range(1, 8)]
+    maps = [spreading(0, 16, COLUMN_LEVEL[d]) for d in range(1, 8)]
+    spread = jnp.concatenate(maps, axis=1).astype(BF16)
+    grads = acc_ref[...] + dot(spread, jnp.concatenate(pieces, axis=0), (1, 0))
+    vg_ref[...] = grads[:, FEAT:].astype(BF16)
+    key_total = grads[:, :FEAT]
     nkg_ref[...] = key_total
-    tile = jnp.concatenate(
-        token_sums(q_ref[...].astype(F32) * qg_ref[...] * nqg_ref[...])
-        + token_sums(k_ref[...].astype(F32) * kg_ref[...] * key_total),
-        axis=0,
-    )
+    sums = token_sums(k_ref[...].astype(F32) * kg_ref[...] * key_total)
+    tile = jnp.concatenate([qsum_ref[:LEAVES]] + sums, axis=0)
     for i in range(sum_ref.shape[0]):
         sum_ref[i] = tile
 
@@ -428,22 +441,29 @@
     yrecv = exchange(ysend, "seq", COLUMN_GROUPS)
     zsend = call(row_kernel, sds(8, SLOT, 256), (yrecv, lv), name="rows")
     zrecv = exchange(zsend, "seq", ROW_GROUPS)
+    near = call(
+        near_kernel,
+        sds(LEAVES, 8, 256, dtype=F32),
+        (qn, kv, one, out_grad),
+        flops=14 * 2 * 2 * 256 * LEAF * FEAT,
+        name="near",
+    )
     stat, cross, halo, p1, p2, zsend = call(
         attend_kernel,
         [sds(LEAVES, 8, 256, dtype=F32), sds(768, 256), sds(2, LEAF, 256)]
         + [sds(192, 256), sds(LEAF, 256), sds(8, SLOT, 256)],
-        (qn, kv, one, out_grad, p1, p2, zrecv),
+        (qn, out_grad, near, p1, p2, zrecv),
         scratch=[
             pltpu.VMEM((1024, FEAT), BF16),
             pltpu.VMEM((1024, FEAT), BF16),
-            pltpu.VMEM((LEAVES, KEYS, 256), F32),
-            pltpu.VMEM((LEAVES, KEYS, 256), F32),
+            pltpu.VMEM((LEAVES, 7, LEAF, 256), F32),
+            pltpu.VMEM((LEAVES, 7, LEAF, 256), F32),
             pltpu.VMEM((768, 1024), BF16),
             pltpu.VMEM((768, 1024), BF16),
             pltpu.VMEM((2, LEAF, 256), BF16),
             pltpu.VMEM((768, 256), BF16),
         ],
-        flops=4 * 4 * 2 * 256 * KEYS * FEAT,
+        flops=4 * 4 * 2 * 256 * 768 * FEAT,
         name="attend",
     )
     p1 = lax.ppermute(p1, "seq", peer)
@@ -470,11 +490,17 @@
         name="columns",
     )
     yrecv = exchange(ysend, "seq", COLUMN_GROUPS)
+    acc, qsum = call(
+        middle_kernel,
+        [sds(ROWS, 256, dtype=F32), sds(8, FEAT, dtype=F32)],
+        (tok, p1, p2, zrecv, queries, qg, nqg),
+        flops=2 * ROWS * 384 * 256,
+        name="middle",
+    )
     nkg, value_grad, inner = call(
         total_kernel,
         [sds(ROWS, FEAT, dtype=F32), sds(ROWS, FEAT), sds(heads, 8, FEAT, dtype=F32)],
-        (tok, p1, p2, zrecv, yrecv, queries, key_rows, qg, kg, nqg),
-        scratch=[pltpu.VMEM((ROWS, 256), F32)],
+        (acc, yrecv, key_rows, kg, qsum),
         name="total",
     )
     inner = exchange(inner, "head")

time: 103 us -> 102 us (level)
  blocking collectives: 47.7 us -> 37.3 us
  waiting for transfers between devices: 11.7 us -> 17.6 us
  starting transfers between devices: 25.7 us -> 29.7 us
    all_to_all x4 -> x3, blocking collectives: 47.7 us -> 37.3 us  [exchange(): return lax.all_to_all(x, axis, 0, 0, axis_index_groups=groups, tiled=True)]
    all_to_all x2 -> x3, waiting for transfers between devices: 3.3 us -> 10 us  [exchange(): return lax.all_to_all(x, axis, 0, 0, axis_index_groups=groups, tiled=True)]
    all_to_all x2 -> x3, starting transfers between devices: 15.3 us -> 19.2 us  [exchange(): return lax.all_to_all(x, axis, 0, 0, axis_index_groups=groups, tiled=True)]
    pallas_call x8 -> x10, Pallas kernels: 13.7 us -> 13.3 us  [call(): pl.pallas_call(kernel, out_shape=outs, in_specs=[pl.BlockSpec(memory_spac...]
  transfers between devices with their start and end apart: 6 -> 7, of which waited for: 4 -> 5; matrix products, arithmetic and copies ran while one was open for 0% -> 0% of each run, Pallas kernels for 4% -> 5%
where the time goes in v7:
time: 102 us; the launch traced here: 101 us
  blocking collectives  37.3 us (37%)
  starting transfers between devices  29.7 us (29%)
  waiting for transfers between devices  17.6 us (17%)
  Pallas kernels  13.3 us (13%)
  local copies, waits for them, and re-layouts  2.49 us (2%)
    all_to_all x3, blocking collectives, exchange(): return lax.all_to_all(x, axis, 0, 0, axis_index_groups=groups, tiled=True)  37.3 us
    all_to_all x3, starting transfers between devices, exchange(): return lax.all_to_all(x, axis, 0, 0, axis_index_groups=groups, tiled=True)  19.2 us
    pallas_call x10, Pallas kernels, call(): pl.pallas_call(kernel, out_shape=outs, in_specs=[pl.BlockSpec(memory_spac...  13.3 us
    all_to_all x3, waiting for transfers between devices, exchange(): return lax.all_to_all(x, axis, 0, 0, axis_index_groups=groups, tiled=True)  10 us
    ppermute x2, starting transfers between devices, local(): p1 = lax.ppermute(p1, 'seq', peer)  9.15 us
    ppermute x2, waiting for transfers between devices, local(): p1 = lax.ppermute(p1, 'seq', peer)  7.56 us
    unnamed x16, local copies, waits for them, and re-layouts  2.49 us
  transfers between devices with their start and end apart: 7, of which 5 were waited for; matrix products, arithmetic and copies ran while one was open for 0% of the time, Pallas kernels for 5%

profile of v7, /device:TPU:1, one launch (start us, length us, event | category | flops | bytes accessed | tf_op | source)
XLA Modules:
  0.0 101.1 jit_solution(3312865665554517752)
XLA Ops:
  0.6 0.0 copy-start
  0.6 0.9 copy-done
  1.5 0.9 copy-done.2
  2.4 0.2 squares.1
  2.7 14.0 %all_to_all.30.refs_0_ = f32[8,8,128]{2,1,0:T(8,128)S(1)} all-to-all(f32[8,8,128]{2,1,0:T(8,128)S(1)} %squares.1), channel_id=1, replica_groups=mesh['seq'=64,'head'=8] {'head'}, dimensions={0} | all-to-all | bytes 65536 | tf_op jit(solution)/shard_map/all_to_all | solution.py:419
  16.6 0.6 copy-done.5
  17.3 0.0 copy-done.6
  17.3 0.5 norm.1
  17.8 10.2 %all_to_all.31.y_ref = bf16[8,16,256]{2,1,0:T(8,128)(2,1)S(1)} all-to-all(bf16[8,16,256]{2,1,0:T(8,128)(2,1)S(1)} %get-tuple-element.32), channel_id=1, replica_groups={{0,64,128,192,256,320,384,448},{8,72,136,200,264,328,392,456},{16,80,14..., dimensions={0} | all-to-all | bytes 131072 | tf_op jit(solution)/shard_map/all_to_all | solution.py:419
  28.0 0.9 rows.1
  29.0 10.2 %all-to-all-start.2 = ((bf16[8,112,256]{2,1,0:T(8,128)(2,1)}), bf16[8,112,256]{2,1,0:T(8,128)(2,1)S(1)}, u32[]{:S(2)}, u32[]{:S(2)}) async-start(bf16[8,112,256]{2,1,0:T(8,128)(2,1)} %rows.1), calls=%async_computation.2 | async-start | bytes 917504 | tf_op jit(solution)/shard_map/all_to_all | solution.py:419
  39.1 3.4 %collective-permute-start = (bf16[192,256]{1,0:T(8,128)(2,1)S(1)}, bf16[192,256]{1,0:T(8,128)(2,1)S(1)}, u32[]{:S(2)}, u32[]{:S(2)}) collective-permute-start(bf16[192,256]{1,0:T(8,128)(2,1)S(1)} %get-tuple-element.30), channel_id=1, source_target_pairs={{0,8},{8,0},{16,24},{24,16},{32,40},{40,32},{48,56},{56,48},{64,72... | collective-permute-start | bytes 294920 | tf_op jit(solution)/shard_map/ppermute | solution.py:439
  42.5 0.7 collective-permute-start.1
  43.2 0.8 near.1.near_ref
  44.0 6.8 %collective-permute-done.p1_ref = bf16[192,256]{1,0:T(8,128)(2,1)S(1)} collective-permute-done((bf16[192,256]{1,0:T(8,128)(2,1)S(1)}, bf16[192,256]{1,0:T(8,128)(2,1)S(1)}, u32[]{:S(2)}, u32[]{:S(2)}) %collective-permute-start) | collective-permute-done | bytes 98336 | tf_op jit(solution)/shard_map/ppermute | solution.py:439
  50.8 1.7 %all-to-all-done.2.z_ref = bf16[8,112,256]{2,1,0:T(8,128)(2,1)S(1)} async-done(((bf16[8,112,256]{2,1,0:T(8,128)(2,1)}), bf16[8,112,256]{2,1,0:T(8,128)(2,1)S(1)}, u32[]{:S(2)}, u32[]{:S(2)}) %all-to-all-start.2) | async-done | bytes 458784 | tf_op jit(solution)/shard_map/all_to_all | solution.py:419
  52.5 3.7 %attend.1 = (f32[4,8,256]{2,1,0:T(8,128)S(1)}, bf16[768,256]{1,0:T(8,128)(2,1)S(1)}, bf16[2,128,256]{2,1,0:T(8,128)(2,1)S(1)}, bf16[192,256]{1,0:T(8,128)(2,1)S(...) custom-call(bf16[512,128]{1,0:T(8,128)(2,1)S(1)} %get-tuple-element.27.qn_ref, ...), custom_call_target="tpu_custom_call" | custom-call | flops 805306368 | bytes 2097152 | tf_op jit(solution)/shard_map/attend/pallas_call | solution.py:399
  56.2 5.1 %all-to-all-start.3 = ((bf16[8,112,256]{2,1,0:T(8,128)(2,1)}), bf16[8,112,256]{2,1,0:T(8,128)(2,1)S(1)}, u32[]{:S(2)}, u32[]{:S(2)}) async-start(bf16[8,112,256]{2,1,0:T(8,128)(2,1)} %get-tuple-element.41), calls=%async_computation.3 | async-start | bytes 917504 | tf_op jit(solution)/shard_map/all_to_all | solution.py:419
  61.2 0.7 collective-permute-start.3
  61.9 5.8 %collective-permute-start.2 = (bf16[192,256]{1,0:T(8,128)(2,1)S(1)}, bf16[192,256]{1,0:T(8,128)(2,1)S(1)}, u32[]{:S(2)}, u32[]{:S(2)}) collective-permute-start(bf16[192,256]{1,0:T(8,128)(2,1)S(1)} %get-tuple-element.39), channel_id=1, source_target_pairs={{0,8},{8,0},{16,24},{24,16},{32,40},{40,32},{48,56},{56,48},{64,72... | collective-permute-start | bytes 294920 | tf_op jit(solution)/shard_map/ppermute | solution.py:469
  67.7 3.8 %after.1 = (bf16[512,128]{1,0:T(8,128)(2,1)}, f32[512,128]{1,0:T(8,128)S(1)}, f32[512,256]{1,0:T(8,128)S(1)}) custom-call(f32[4,8,256]{2,1,0:T(8,128)S(1)} %get-tuple-element.34.stat_ref, bf16[512,128]{1,0:T(8,128)(2,1)S(1)} %get-tuple-element.27.qn_ref, bf16[512,256]{1,0:T(8,128)(2,1)S(1)} %get-tuple-element.28.kv_ref, ...), custom_call_target="tpu_custom_call" | custom-call | flops 1677721600 | bytes 2129920 | tf_op jit(solution)/shard_map/after/pallas_call | solution.py:399
  71.5 0.8 collective-permute-done.2.p1_ref
  72.3 1.6 %all-to-all-done.3.z_ref = bf16[8,112,256]{2,1,0:T(8,128)(2,1)S(1)} async-done(((bf16[8,112,256]{2,1,0:T(8,128)(2,1)}), bf16[8,112,256]{2,1,0:T(8,128)(2,1)S(1)}, u32[]{:S(2)}, u32[]{:S(2)}) %all-to-all-start.3) | async-done | bytes 458784 | tf_op jit(solution)/shard_map/all_to_all | solution.py:419
  73.9 0.8 columns.1
  74.7 0.0 copy-start.3
  74.7 4.0 %all-to-all-start.4 = ((bf16[8,16,256]{2,1,0:T(8,128)(2,1)}), bf16[8,16,256]{2,1,0:T(8,128)(2,1)S(1)}, u32[]{:S(2)}, u32[]{:S(2)}) async-start(bf16[8,16,256]{2,1,0:T(8,128)(2,1)} %columns.1), calls=%async_computation.4 | async-start | bytes 131072 | tf_op jit(solution)/shard_map/all_to_all | solution.py:419
  78.7 0.0 copy-start.1
  78.7 0.5 middle.1
  79.2 6.7 %all-to-all-done.4.y_ref = bf16[8,16,256]{2,1,0:T(8,128)(2,1)S(1)} async-done(((bf16[8,16,256]{2,1,0:T(8,128)(2,1)}), bf16[8,16,256]{2,1,0:T(8,128)(2,1)S(1)}, u32[]{:S(2)}, u32[]{:S(2)}) %all-to-all-start.4) | async-done | bytes 65568 | tf_op jit(solution)/shard_map/all_to_all | solution.py:419
  85.9 1.1 %total.1 = (f32[512,128]{1,0:T(8,128)S(1)}, bf16[512,128]{1,0:T(8,128)(2,1)}, f32[8,8,128]{2,1,0:T(8,128)S(1)}) custom-call(f32[512,256]{1,0:T(8,128)S(1)} %get-tuple-element.43.acc_ref, bf16[8,16,256]{2,1,0:T(8,128)(2,1)S(1)} %all-to-all-done.4.y_ref, bf16[512,128]{1,0:T(8,128)(2,1)S(1)} %copy-done.1, f32[1,128]{1,0:T(1,128)S(1)} %bitcast.6, ...), custom_call_target="tpu_custom_call" | custom-call | bytes 1151488 | tf_op jit(solution)/shard_map/total/pallas_call | solution.py:399
  87.0 13.1 %all_to_all.32.refs_1_ = f32[8,8,128]{2,1,0:T(8,128)S(1)} all-to-all(f32[8,8,128]{2,1,0:T(8,128)S(1)} %get-tuple-element.45), channel_id=1, replica_groups=mesh['seq'=64,'head'=8] {'head'}, dimensions={0} | all-to-all | bytes 65536 | tf_op jit(solution)/shard_map/all_to_all | solution.py:419
  100.1 1.0 %finish.1 = (bf16[512,128]{1,0:T(8,128)(2,1)}, bf16[512,128]{1,0:T(8,128)(2,1)}) custom-call(f32[8,8,128]{2,1,0:T(8,128)S(1)} %all_to_all.30.refs_0_, f32[8,8,128]{2,1,0:T(8,128)S(1)} %all_to_all.32.refs_1_, bf16[512,128]{1,0:T(8,128)(2,1)S(1)} %copy-done.3, bf16[512,128]{1,0:T(8,128)(2,1)S(1)} %copy-done.1, f32[1,128]{1,0:T(1,128)S(1)} %bitcast.4, ...), custom_call_target="tpu_custom_call" | custom-call | bytes 1115136 | tf_op jit(solution)/shard_map/finish/pallas_call | solution.py:399
  (11 shorter events, 0.0 us)
Async XLA Ops:
  0.6 0.9 copy-start
  1.5 0.9 copy-start.2
  2.4 14.2 %copy-start.4 = (bf16[512,128]{1,0:T(8,128)(2,1)S(1)}, bf16[512,128]{1,0:T(8,128)(2,1)}, u32[]{:S(2)}) copy-start(bf16[512,128]{1,0:T(8,128)(2,1)} %refs_3_.2) | copy-start | bytes 393220
  16.6 0.7 copy-start.5
  16.6 0.7 copy-start.6
  29.0 14.2 %copy-start.7 = (bf16[512,128]{1,0:T(8,128)(2,1)S(1)}, bf16[512,128]{1,0:T(8,128)(2,1)}, u32[]{:S(2)}) copy-start(bf16[512,128]{1,0:T(8,128)(2,1)} %g_ref.5) | copy-start | bytes 393220
  29.0 23.5 %all-to-all-start.2 = ((bf16[8,112,256]{2,1,0:T(8,128)(2,1)}), bf16[8,112,256]{2,1,0:T(8,128)(2,1)S(1)}, u32[]{:S(2)}, u32[]{:S(2)}) async-start(bf16[8,112,256]{2,1,0:T(8,128)(2,1)} %rows.1), calls=%async_computation.2 | async-start | bytes 917504 | tf_op jit(solution)/shard_map/all_to_all | solution.py:419
  39.1 11.7 %collective-permute-start = (bf16[192,256]{1,0:T(8,128)(2,1)S(1)}, bf16[192,256]{1,0:T(8,128)(2,1)S(1)}, u32[]{:S(2)}, u32[]{:S(2)}) collective-permute-start(bf16[192,256]{1,0:T(8,128)(2,1)S(1)} %get-tuple-element.30), channel_id=1, source_target_pairs={{0,8},{8,0},{16,24},{24,16},{32,40},{40,32},{48,56},{56,48},{64,72... | collective-permute-start | bytes 294920 | tf_op jit(solution)/shard_map/ppermute | solution.py:439
  42.5 1.5 %collective-permute-start.1 = (bf16[128,256]{1,0:T(8,128)(2,1)S(1)}, bf16[128,256]{1,0:T(8,128)(2,1)S(1)}, u32[]{:S(2)}, u32[]{:S(2)}) collective-permute-start(bf16[128,256]{1,0:T(8,128)(2,1)S(1)} %get-tuple-element.31), channel_id=1, source_target_pairs={{8,16},{24,32},{40,48},{56,64},{72,80},{88,96},{104,112},{120,128}... | collective-permute-start | bytes 196616 | tf_op jit(solution)/shard_map/ppermute | solution.py:440
  56.2 17.7 %all-to-all-start.3 = ((bf16[8,112,256]{2,1,0:T(8,128)(2,1)}), bf16[8,112,256]{2,1,0:T(8,128)(2,1)S(1)}, u32[]{:S(2)}, u32[]{:S(2)}) async-start(bf16[8,112,256]{2,1,0:T(8,128)(2,1)} %get-tuple-element.41), calls=%async_computation.3 | async-start | bytes 917504 | tf_op jit(solution)/shard_map/all_to_all | solution.py:419
  61.2 10.3 %collective-permute-start.3 = (bf16[128,256]{1,0:T(8,128)(2,1)S(1)}, bf16[128,256]{1,0:T(8,128)(2,1)S(1)}, u32[]{:S(2)}, u32[]{:S(2)}) collective-permute-start(bf16[128,256]{1,0:T(8,128)(2,1)S(1)} %get-tuple-element.40), channel_id=1, source_target_pairs={{8,16},{24,32},{40,48},{56,64},{72,80},{88,96},{104,112},{120,128}... | collective-permute-start | bytes 196616 | tf_op jit(solution)/shard_map/ppermute | solution.py:470
  61.9 10.4 %collective-permute-start.2 = (bf16[192,256]{1,0:T(8,128)(2,1)S(1)}, bf16[192,256]{1,0:T(8,128)(2,1)S(1)}, u32[]{:S(2)}, u32[]{:S(2)}) collective-permute-start(bf16[192,256]{1,0:T(8,128)(2,1)S(1)} %get-tuple-element.39), channel_id=1, source_target_pairs={{0,8},{8,0},{16,24},{24,16},{32,40},{40,32},{48,56},{56,48},{64,72... | collective-permute-start | bytes 294920 | tf_op jit(solution)/shard_map/ppermute | solution.py:469
  74.7 4.0 %copy-start.3 = (bf16[512,128]{1,0:T(8,128)(2,1)S(1)}, bf16[512,128]{1,0:T(8,128)(2,1)}, u32[]{:S(2)}) copy-start(bf16[512,128]{1,0:T(8,128)(2,1)} %refs_2_.3) | copy-start | bytes 393220
  74.7 11.2 %all-to-all-start.4 = ((bf16[8,16,256]{2,1,0:T(8,128)(2,1)}), bf16[8,16,256]{2,1,0:T(8,128)(2,1)S(1)}, u32[]{:S(2)}, u32[]{:S(2)}) async-start(bf16[8,16,256]{2,1,0:T(8,128)(2,1)} %columns.1), calls=%async_computation.4 | async-start | bytes 131072 | tf_op jit(solution)/shard_map/all_to_all | solution.py:419
  78.7 7.2 %copy-start.1 = (bf16[512,128]{1,0:T(8,128)(2,1)S(1)}, bf16[512,128]{1,0:T(8,128)(2,1)}, u32[]{:S(2)}) copy-start(bf16[512,128]{1,0:T(8,128)(2,1)} %refs_3_.3) | copy-start | bytes 393220

commit v8 on v7

--- a/solution.py
+++ b/solution.py
@@ -19,6 +19,7 @@
 BF16 = jnp.bfloat16
 PARAMS = pltpu.CompilerParams(vmem_limit_bytes=40 * 1024 * 1024)
 ROW_LEVEL = {1: 2, 2: 3, 3: 3, 4: 4, 5: 4, 6: 4, 7: 4}
+MID_ROWS = {1: (0, 64), 2: (64, 64), 3: (128, 64), 4: (192, 32), 5: (224, 32), 6: (256, 32), 7: (288, 32)}
 COLUMN_LEVEL = {1: 5, 2: 6, 3: 6, 4: 7, 5: 7, 6: 7, 7: 7}
 FAR = 48
 SLOT = 112
@@ -77,25 +78,25 @@
     )
 
 
-def squares_kernel(q_ref, k_ref, out_ref):
-    q = q_ref[...].astype(F32)
-    k = k_ref[...].astype(F32)
+def squares_kernel(qk_ref, out_ref):
+    q = qk_ref[0].astype(F32)
+    k = qk_ref[1].astype(F32)
     tile = jnp.concatenate(token_sums(q * q) + token_sums(k * k), axis=0)
     for i in range(out_ref.shape[0]):
         out_ref[i] = tile
 
 
-def norm_kernel(width, sum_ref, q_ref, k_ref, v_ref, qg_ref, kg_ref, qn_ref, kv_ref, one_ref, lv_ref, y_ref, p1_ref, p2_ref):
+def norm_kernel(width, sum_ref, qk_ref, v_ref, qg_ref, kg_ref, qn_ref, kv_ref, one_ref, lv_ref, y_ref, p1_ref, p2_ref):
     index = lax.axis_index("seq")
     column = jnp.right_shift(index, 3)
     odd = jnp.bitwise_and(index, 1)
     total = jnp.sum(sum_ref[...], axis=0)
     rate = lax.rsqrt(total / width + EPS)
     qn_ref[...] = (
-        q_ref[...].astype(F32) * spread_tokens(rate, 0) * qg_ref[...]
+        qk_ref[0].astype(F32) * spread_tokens(rate, 0) * qg_ref[...]
     ).astype(BF16)
     kv_ref[:, :FEAT] = (
-        k_ref[...].astype(F32) * spread_tokens(rate, 4) * kg_ref[...]
+        qk_ref[1].astype(F32) * spread_tokens(rate, 4) * kg_ref[...]
     ).astype(BF16)
     kv_ref[:, FEAT:] = v_ref[...]
     pool = jnp.concatenate(
@@ -114,7 +115,7 @@
     p2_ref[...] = kv_ref[pl.ds(pl.multiple_of(odd * 384, LEAF), LEAF)]
 
 
-def row_kernel(y_ref, lv_ref, out_ref):
+def row_kernel(y_ref, lv_ref, p2_ref, out_ref):
     index = lax.axis_index("seq")
     column = jnp.right_shift(index, 3)
     place = jnp.bitwise_and(index, 7)
@@ -334,58 +335,56 @@
     tok_ref[...] = near_grad[LEAF : LEAF + ROWS] + dot(spread, high, (1, 0)) + dot(spread, rest, (1, 0))
 
 
-def column_kernel(z_ref, p1_ref, p2_ref, tok_ref, out_ref, far_rows, sem):
-    column = jnp.right_shift(lax.axis_index("seq"), 3)
-    copy = pltpu.make_async_copy(z_ref.at[:, pl.ds(0, FAR)], far_rows, sem)
-    copy.start()
-    copy.wait()
-    far = jnp.sum(far_rows[...].astype(F32), axis=0).astype(BF16)
+def column_kernel(z_ref, p1_ref, tok_ref, out_ref, mid_ref):
+    index = lax.axis_index("seq")
+    column = jnp.right_shift(index, 3)
+    place = jnp.bitwise_and(index, 7)
+    far = jnp.sum(z_ref[:, :FAR].astype(F32), axis=0).astype(BF16)
     slots = dot(far_pick((112, FAR), 1), far, (1, 0)).astype(BF16)
     out_ref[column] = jnp.zeros((16, 2 * FEAT), BF16)
     for d in range(1, 8):
         out_ref[jnp.bitwise_xor(column, d)] = slots[16 * (d - 1) : 16 * d]
-
-
-def middle_kernel(tok_ref, p1_ref, p2_ref, z_ref, q_ref, qg_ref, nqg_ref, acc_ref, sum_ref):
+    for d in range(1, 8):
+        at, rows = MID_ROWS[d]
+        mid_ref[at : at + rows] = z_ref[jnp.bitwise_xor(place, d), FAR : FAR + rows]
+
+
+def middle_kernel(tok_ref, p1_ref, mid_ref, qk_ref, qg_ref, nqg_ref, acc_ref, sum_ref):
+    odd = jnp.bitwise_and(lax.axis_index("seq"), 1)
+    maps = [spreading(0, MID_ROWS[d][1], ROW_LEVEL[d]) for d in range(1, 8)]
+    spread = jnp.concatenate(maps + [spreading(64, 64, 2)], axis=1).astype(BF16)
+    rows = jnp.concatenate([mid_ref[...], p1_ref[LEAF:]], axis=0)
+    acc_ref[...] = tok_ref[...] + dot(spread, rows, (1, 0))
+    acc_ref[pl.ds(pl.multiple_of((1 - odd) * 384, LEAF), LEAF)] += p1_ref[:LEAF].astype(F32)
+    sums = token_sums(qk_ref[0].astype(F32) * qg_ref[...] * nqg_ref[...])
+    sum_ref[...] = jnp.concatenate(sums + [jnp.zeros((LEAVES, FEAT), F32)], axis=0)
+
+
+def total_kernel(acc_ref, p2_ref, y_ref, qk_ref, kg_ref, qsum_ref, nkg_ref, vg_ref, sum_ref, grads):
     index = lax.axis_index("seq")
-    place = jnp.bitwise_and(index, 7)
+    column = jnp.right_shift(index, 3)
     odd = jnp.bitwise_and(index, 1)
-    pieces = [z_ref[jnp.bitwise_xor(place, 1), FAR:], p1_ref[LEAF:]]
-    maps = [spreading(0, 64, 2), spreading(64, 64, 2)]
-    for d in range(2, 8):
-        rows = ROWS >> ROW_LEVEL[d]
-        pieces.append(z_ref[jnp.bitwise_xor(place, d), FAR : FAR + rows])
-        maps.append(spreading(0, rows, ROW_LEVEL[d]))
-    spread = jnp.concatenate(maps, axis=1).astype(BF16)
-    acc_ref[...] = tok_ref[...] + dot(spread, jnp.concatenate(pieces, axis=0), (1, 0))
-    acc_ref[pl.ds(pl.multiple_of((1 - odd) * 384, LEAF), LEAF)] += p1_ref[:LEAF].astype(F32)
-    acc_ref[pl.ds(pl.multiple_of(odd * 384, LEAF), LEAF)] += p2_ref[...].astype(F32)
-    sums = token_sums(q_ref[...].astype(F32) * qg_ref[...] * nqg_ref[...])
-    sum_ref[...] = jnp.concatenate(sums + [jnp.zeros((LEAVES, FEAT), F32)], axis=0)
-
-
-def total_kernel(acc_ref, y_ref, k_ref, kg_ref, qsum_ref, nkg_ref, vg_ref, sum_ref):
-    column = jnp.right_shift(lax.axis_index("seq"), 3)
     pieces = [y_ref[jnp.bitwise_xor(column, d)] for d in range(1, 8)]
     maps = [spreading(0, 16, COLUMN_LEVEL[d]) for d in range(1, 8)]
     spread = jnp.concatenate(maps, axis=1).astype(BF16)
-    grads = acc_ref[...] + dot(spread, jnp.concatenate(pieces, axis=0), (1, 0))
+    grads[...] = acc_ref[...] + dot(spread, jnp.concatenate(pieces, axis=0), (1, 0))
+    grads[pl.ds(pl.multiple_of(odd * 384, LEAF), LEAF)] += p2_ref[...].astype(F32)
     vg_ref[...] = grads[:, FEAT:].astype(BF16)
     key_total = grads[:, :FEAT]
     nkg_ref[...] = key_total
-    sums = token_sums(k_ref[...].astype(F32) * kg_ref[...] * key_total)
+    sums = token_sums(qk_ref[1].astype(F32) * kg_ref[...] * key_total)
     tile = jnp.concatenate([qsum_ref[:LEAVES]] + sums, axis=0)
     for i in range(sum_ref.shape[0]):
         sum_ref[i] = tile
 
 
-def finish_kernel(width, sq_ref, inner_ref, q_ref, k_ref, qg_ref, kg_ref, nqg_ref, nkg_ref, dq_ref, dk_ref):
+def finish_kernel(width, sq_ref, inner_ref, qk_ref, qg_ref, kg_ref, nqg_ref, nkg_ref, dq_ref, dk_ref):
     rate = lax.rsqrt(jnp.sum(sq_ref[...], axis=0) / width + EPS)
     inner = jnp.sum(inner_ref[...], axis=0) / width
     cubed = rate * rate * rate * inner
     for first, x_ref, gain_ref, grad_ref, out_ref in (
-        (0, q_ref, qg_ref, nqg_ref, dq_ref),
-        (4, k_ref, kg_ref, nkg_ref, dk_ref),
+        (0, qk_ref.at[0], qg_ref, nqg_ref, dq_ref),
+        (4, qk_ref.at[1], kg_ref, nkg_ref, dk_ref),
     ):
         out_ref[...] = (
             spread_tokens(rate, first) * gain_ref[...] * grad_ref[...]
@@ -428,18 +427,25 @@
     peer = [(i, i ^ 1) for i in range(seq)]
     beside = [(i, i + 1) for i in range(1, seq - 1, 2)] + [(i + 1, i) for i in range(1, seq - 1, 2)]
 
-    squares = call(squares_kernel, sds(heads, 8, FEAT, dtype=F32), (queries, key_rows), name="squares")
+    qk = jnp.stack([queries, key_rows])
+    squares = call(squares_kernel, sds(heads, 8, FEAT, dtype=F32), (qk,), name="squares")
     squares = exchange(squares, "head")
     qn, kv, one, lv, ysend, p1, p2 = call(
         lambda *refs: norm_kernel(width, *refs),
         [sds(ROWS, FEAT), sds(ROWS, 256), sds(256, 256), sds(224, 256), sds(8, 16, 256), sds(192, 256), sds(LEAF, 256)],
-        (squares, queries, key_rows, value_rows, qg, kg),
+        (squares, qk, value_rows, qg, kg),
         name="norm",
     )
     p1 = lax.ppermute(p1, "seq", peer)
     p2 = lax.ppermute(p2, "seq", beside)
     yrecv = exchange(ysend, "seq", COLUMN_GROUPS)
-    zsend = call(row_kernel, sds(8, SLOT, 256), (yrecv, lv), name="rows")
+    zsend = call(
+        row_kernel,
+        sds(8, SLOT, 256),
+        (yrecv, lv, p2),
+        spaces=[pltpu.VMEM, pltpu.VMEM, pl.ANY],
+        name="rows",
+    )
     zrecv = exchange(zsend, "seq", ROW_GROUPS)
     near = call(
         near_kernel,
@@ -481,33 +487,33 @@
         flops=4 * 5 * 2 * 256 * KEYS * FEAT,
         name="after",
     )
-    ysend = call(
+    ysend, mid = call(
         column_kernel,
-        sds(8, 16, 256),
-        (zrecv, p1, p2, tok),
-        scratch=[pltpu.VMEM((8, FAR, 256), BF16), pltpu.SemaphoreType.DMA],
-        spaces=[pl.ANY] * 4,
+        [sds(8, 16, 256), sds(320, 256)],
+        (zrecv, p1, tok),
+        spaces=[pltpu.VMEM, pl.ANY, pl.ANY],
         name="columns",
     )
     yrecv = exchange(ysend, "seq", COLUMN_GROUPS)
     acc, qsum = call(
         middle_kernel,
         [sds(ROWS, 256, dtype=F32), sds(8, FEAT, dtype=F32)],
-        (tok, p1, p2, zrecv, queries, qg, nqg),
+        (tok, p1, mid, qk, qg, nqg),
         flops=2 * ROWS * 384 * 256,
         name="middle",
     )
     nkg, value_grad, inner = call(
         total_kernel,
         [sds(ROWS, FEAT, dtype=F32), sds(ROWS, FEAT), sds(heads, 8, FEAT, dtype=F32)],
-        (acc, yrecv, key_rows, kg, qsum),
+        (acc, p2, yrecv, qk, kg, qsum),
+        scratch=[pltpu.VMEM((ROWS, 256), F32)],
         name="total",
     )
     inner = exchange(inner, "head")
     query_grad, key_grad = call(
         lambda *refs: finish_kernel(width, *refs),
         [sds(ROWS, FEAT), sds(ROWS, FEAT)],
-        (squares, inner, queries, key_rows, qg, kg, nqg, nkg),
+        (squares, inner, qk, qg, kg, nqg, nkg),
         name="finish",
     )
     return (attended, query_grad, key_grad, value_grad)

time: 102 us -> 105 us (1.029)
  waiting for transfers between devices: 17.6 us -> 26.3 us
  blocking collectives: 37.3 us -> 28.9 us
  starting transfers between devices: 29.7 us -> 32.7 us
  local copies, waits for them, and re-layouts: 2.49 us -> 0.68 us
    all_to_all x3 -> x2, blocking collectives: 37.3 us -> 28.9 us  [exchange(): return lax.all_to_all(x, axis, 0, 0, axis_index_groups=groups, tiled=True)]
    all_to_all x3 -> x4, starting transfers between devices: 19.2 us -> 24.7 us  [exchange(): return lax.all_to_all(x, axis, 0, 0, axis_index_groups=groups, tiled=True)]
    all_to_all x3 -> x4, waiting for transfers between devices: 10 us -> 14.7 us  [exchange(): return lax.all_to_all(x, axis, 0, 0, axis_index_groups=groups, tiled=True)]
    ppermute x2, waiting for transfers between devices: 7.56 us -> 11.6 us  [local(): p1 = lax.ppermute(p1, 'seq', peer)]
    ppermute x2, starting transfers between devices: 9.15 us -> 6.71 us  [local(): p1 = lax.ppermute(p1, 'seq', peer)]
    unnamed x16 -> x8, local copies, waits for them, and re-layouts: 2.49 us -> 0.68 us
  transfers between devices with their start and end apart: 7 -> 8, of which waited for: 5 -> 6; matrix products, arithmetic and copies ran while one was open for 0% -> 0% of each run, Pallas kernels for 5% -> 5%
where the time goes in v8:
time: 105 us; the launch traced here: 104 us
  starting transfers between devices  32.7 us (31%)
  blocking collectives  28.9 us (28%)
  waiting for transfers between devices  26.3 us (25%)
  Pallas kernels  14 us (13%)
    all_to_all x2, blocking collectives, exchange(): return lax.all_to_all(x, axis, 0, 0, axis_index_groups=groups, tiled=True)  28.9 us
    all_to_all x4, starting transfers between devices, exchange(): return lax.all_to_all(x, axis, 0, 0, axis_index_groups=groups, tiled=True)  24.7 us
    all_to_all x4, waiting for transfers between devices, exchange(): return lax.all_to_all(x, axis, 0, 0, axis_index_groups=groups, tiled=True)  14.7 us
    pallas_call x10, Pallas kernels, call(): pl.pallas_call(kernel, out_shape=outs, in_specs=[pl.BlockSpec(memory_spac...  14 us
    ppermute x2, waiting for transfers between devices, local(): p1 = lax.ppermute(p1, 'seq', peer)  11.6 us
    ppermute x2, starting transfers between devices, local(): p1 = lax.ppermute(p1, 'seq', peer)  6.71 us
  transfers between devices with their start and end apart: 8, of which 6 were waited for; matrix products, arithmetic and copies ran while one was open for 0% of the time, Pallas kernels for 5%

profile of v8, /device:TPU:1, one launch (start us, length us, event | category | flops | bytes accessed | tf_op | source)
XLA Modules:
  0.0 104.4 jit_solution(10854538839670095743)
XLA Ops:
  0.6 1.0 pad_maximum_fusion.qk_ref.refs_1_.refs_2_
  1.6 0.0 copy-start
  1.6 0.2 squares.1
  1.9 14.0 %all_to_all.30.refs_0_ = f32[8,8,128]{2,1,0:T(8,128)S(1)} all-to-all(f32[8,8,128]{2,1,0:T(8,128)S(1)} %squares.1), channel_id=1, replica_groups=mesh['seq'=64,'head'=8] {'head'}, dimensions={0} | all-to-all | bytes 65536 | tf_op jit(solution)/shard_map/all_to_all | solution.py:418
  15.8 0.6 copy-done.1
  16.5 0.0 copy-done.2
  16.5 1.1 %norm.1 = (bf16[512,128]{1,0:T(8,128)(2,1)S(1)}, bf16[512,256]{1,0:T(8,128)(2,1)S(1)}, bf16[256,256]{1,0:T(8,128)(2,1)S(1)}, bf16[224,256]{1,0:T(8,128)(2,1)S(1)...) custom-call(f32[8,8,128]{2,1,0:T(8,128)S(1)} %all_to_all.30.refs_0_, ...), custom_call_target="tpu_custom_call" | custom-call | bytes 1295360 | tf_op jit(solution)/shard_map/norm/pallas_call | solution.py:398
  17.6 3.4 %all-to-all-start.1 = ((bf16[8,16,256]{2,1,0:T(8,128)(2,1)}), bf16[8,16,256]{2,1,0:T(8,128)(2,1)S(1)}, u32[]{:S(2)}, u32[]{:S(2)}) async-start(bf16[8,16,256]{2,1,0:T(8,128)(2,1)} %get-tuple-element.34), calls=%async_computation.1 | async-start | bytes 131072 | tf_op jit(solution)/shard_map/all_to_all | solution.py:418
  21.0 0.7 collective-permute-start.1
  21.7 0.0 collective-permute-done.1.p2_ref
  21.7 6.6 %all-to-all-done.1.y_ref = bf16[8,16,256]{2,1,0:T(8,128)(2,1)S(1)} async-done(((bf16[8,16,256]{2,1,0:T(8,128)(2,1)}), bf16[8,16,256]{2,1,0:T(8,128)(2,1)S(1)}, u32[]{:S(2)}, u32[]{:S(2)}) %all-to-all-start.1) | async-done | bytes 65568 | tf_op jit(solution)/shard_map/all_to_all | solution.py:418
  28.2 0.9 rows.1
  29.2 10.2 %all-to-all-start.2 = ((bf16[8,112,256]{2,1,0:T(8,128)(2,1)}), bf16[8,112,256]{2,1,0:T(8,128)(2,1)S(1)}, u32[]{:S(2)}, u32[]{:S(2)}) async-start(bf16[8,112,256]{2,1,0:T(8,128)(2,1)} %rows.1), calls=%async_computation.2 | async-start | bytes 917504 | tf_op jit(solution)/shard_map/all_to_all | solution.py:418
  39.3 3.4 %collective-permute-start = (bf16[192,256]{1,0:T(8,128)(2,1)S(1)}, bf16[192,256]{1,0:T(8,128)(2,1)S(1)}, u32[]{:S(2)}, u32[]{:S(2)}) collective-permute-start(bf16[192,256]{1,0:T(8,128)(2,1)S(1)} %get-tuple-element.32), channel_id=1, source_target_pairs={{0,8},{8,0},{16,24},{24,16},{32,40},{40,32},{48,56},{56,48},{64,72... | collective-permute-start | bytes 294920 | tf_op jit(solution)/shard_map/ppermute | solution.py:439
  42.7 0.8 near.1.near_ref
  43.5 7.5 %collective-permute-done.p1_ref = bf16[192,256]{1,0:T(8,128)(2,1)S(1)} collective-permute-done((bf16[192,256]{1,0:T(8,128)(2,1)S(1)}, bf16[192,256]{1,0:T(8,128)(2,1)S(1)}, u32[]{:S(2)}, u32[]{:S(2)}) %collective-permute-start) | collective-permute-done | bytes 98336 | tf_op jit(solution)/shard_map/ppermute | solution.py:439
  51.0 1.7 %all-to-all-done.2.z_ref = bf16[8,112,256]{2,1,0:T(8,128)(2,1)S(1)} async-done(((bf16[8,112,256]{2,1,0:T(8,128)(2,1)}), bf16[8,112,256]{2,1,0:T(8,128)(2,1)S(1)}, u32[]{:S(2)}, u32[]{:S(2)}) %all-to-all-start.2) | async-done | bytes 458784 | tf_op jit(solution)/shard_map/all_to_all | solution.py:418
  52.7 3.7 %attend.1 = (f32[4,8,256]{2,1,0:T(8,128)S(1)}, bf16[768,256]{1,0:T(8,128)(2,1)S(1)}, bf16[2,128,256]{2,1,0:T(8,128)(2,1)S(1)}, bf16[192,256]{1,0:T(8,128)(2,1)S(...) custom-call(bf16[512,128]{1,0:T(8,128)(2,1)S(1)} %get-tuple-element.29.qn_ref, ...), custom_call_target="tpu_custom_call" | custom-call | flops 805306368 | bytes 2097152 | tf_op jit(solution)/shard_map/attend/pallas_call | solution.py:398
  56.4 4.8 %all-to-all-start.3 = ((bf16[8,112,256]{2,1,0:T(8,128)(2,1)}), bf16[8,112,256]{2,1,0:T(8,128)(2,1)S(1)}, u32[]{:S(2)}, u32[]{:S(2)}) async-start(bf16[8,112,256]{2,1,0:T(8,128)(2,1)} %get-tuple-element.42), calls=%async_computation.3 | async-start | bytes 917504 | tf_op jit(solution)/shard_map/all_to_all | solution.py:418
  61.2 3.4 %collective-permute-start.2 = (bf16[192,256]{1,0:T(8,128)(2,1)S(1)}, bf16[192,256]{1,0:T(8,128)(2,1)S(1)}, u32[]{:S(2)}, u32[]{:S(2)}) collective-permute-start(bf16[192,256]{1,0:T(8,128)(2,1)S(1)} %get-tuple-element.41), channel_id=1, source_target_pairs={{0,8},{8,0},{16,24},{24,16},{32,40},{40,32},{48,56},{56,48},{64,72... | collective-permute-start | bytes 294920 | tf_op jit(solution)/shard_map/ppermute | solution.py:475
  64.6 3.8 %after.1 = (bf16[512,128]{1,0:T(8,128)(2,1)}, f32[512,128]{1,0:T(8,128)S(1)}, f32[512,256]{1,0:T(8,128)S(1)}) custom-call(f32[4,8,256]{2,1,0:T(8,128)S(1)} %get-tuple-element.36.stat_ref, bf16[512,128]{1,0:T(8,128)(2,1)S(1)} %get-tuple-element.29.qn_ref, bf16[512,256]{1,0:T(8,128)(2,1)S(1)} %get-tuple-element.30.kv_ref, ...), custom_call_target="tpu_custom_call" | custom-call | flops 1677721600 | bytes 2129920 | tf_op jit(solution)/shard_map/after/pallas_call | solution.py:398
  68.4 4.2 %collective-permute-done.2.p1_ref = bf16[192,256]{1,0:T(8,128)(2,1)S(1)} collective-permute-done((bf16[192,256]{1,0:T(8,128)(2,1)S(1)}, bf16[192,256]{1,0:T(8,128)(2,1)S(1)}, u32[]{:S(2)}, u32[]{:S(2)}) %collective-permute-start.2) | collective-permute-done | bytes 98336 | tf_op jit(solution)/shard_map/ppermute | solution.py:475
  72.5 0.4 all-to-all-done.3.z_ref
  72.9 0.8 columns.1
  73.7 6.3 %all-to-all-start.4 = ((bf16[8,16,256]{2,1,0:T(8,128)(2,1)}), bf16[8,16,256]{2,1,0:T(8,128)(2,1)S(1)}, u32[]{:S(2)}, u32[]{:S(2)}) async-start(bf16[8,16,256]{2,1,0:T(8,128)(2,1)} %get-tuple-element.47), calls=%async_computation.4 | async-start | bytes 131072 | tf_op jit(solution)/shard_map/all_to_all | solution.py:418
  80.1 0.7 collective-permute-start.3
  80.7 0.5 middle.1
  81.2 0.0 collective-permute-done.3.p2_ref
  81.2 6.1 %all-to-all-done.4.y_ref = bf16[8,16,256]{2,1,0:T(8,128)(2,1)S(1)} async-done(((bf16[8,16,256]{2,1,0:T(8,128)(2,1)}), bf16[8,16,256]{2,1,0:T(8,128)(2,1)S(1)}, u32[]{:S(2)}, u32[]{:S(2)}) %all-to-all-start.4) | async-done | bytes 65568 | tf_op jit(solution)/shard_map/all_to_all | solution.py:418
  87.3 1.2 %total.1 = (f32[512,128]{1,0:T(8,128)S(1)}, bf16[512,128]{1,0:T(8,128)(2,1)}, f32[8,8,128]{2,1,0:T(8,128)S(1)}) custom-call(f32[512,256]{1,0:T(8,128)S(1)} %get-tuple-element.45.acc_ref, bf16[128,256]{1,0:T(8,128)(2,1)S(1)} %collective-permute-done.3.p2_ref, bf16[8,16,256]{2,1,0:T(8,128)(2,1)S(1)} %all-to-all-done.4.y_ref, ...), custom_call_target="tpu_custom_call" | custom-call | bytes 1348096 | tf_op jit(solution)/shard_map/total/pallas_call | solution.py:398
  88.4 14.9 %all_to_all.31.refs_1_ = f32[8,8,128]{2,1,0:T(8,128)S(1)} all-to-all(f32[8,8,128]{2,1,0:T(8,128)S(1)} %get-tuple-element.49), channel_id=1, replica_groups=mesh['seq'=64,'head'=8] {'head'}, dimensions={0} | all-to-all | bytes 65536 | tf_op jit(solution)/shard_map/all_to_all | solution.py:418
  103.4 1.0 finish.1
  (5 shorter events, 0.0 us)
Async XLA Ops:
  1.6 14.2 %copy-start = (bf16[512,128]{1,0:T(8,128)(2,1)S(1)}, bf16[512,128]{1,0:T(8,128)(2,1)}, u32[]{:S(2)}) copy-start(bf16[512,128]{1,0:T(8,128)(2,1)} %refs_2_.1) | copy-start | bytes 393220
  15.8 0.7 copy-start.1
  15.8 0.7 copy-start.2
  17.6 10.6 %all-to-all-start.1 = ((bf16[8,16,256]{2,1,0:T(8,128)(2,1)}), bf16[8,16,256]{2,1,0:T(8,128)(2,1)S(1)}, u32[]{:S(2)}, u32[]{:S(2)}) async-start(bf16[8,16,256]{2,1,0:T(8,128)(2,1)} %get-tuple-element.34), calls=%async_computation.1 | async-start | bytes 131072 | tf_op jit(solution)/shard_map/all_to_all | solution.py:418
  21.0 0.7 collective-permute-start.1
  29.2 13.5 %copy-start.3 = (bf16[512,128]{1,0:T(8,128)(2,1)S(1)}, bf16[512,128]{1,0:T(8,128)(2,1)}, u32[]{:S(2)}) copy-start(bf16[512,128]{1,0:T(8,128)(2,1)} %g_ref.5) | copy-start | bytes 393220
  29.2 23.5 %all-to-all-start.2 = ((bf16[8,112,256]{2,1,0:T(8,128)(2,1)}), bf16[8,112,256]{2,1,0:T(8,128)(2,1)S(1)}, u32[]{:S(2)}, u32[]{:S(2)}) async-start(bf16[8,112,256]{2,1,0:T(8,128)(2,1)} %rows.1), calls=%async_computation.2 | async-start | bytes 917504 | tf_op jit(solution)/shard_map/all_to_all | solution.py:418
  39.3 11.7 %collective-permute-start = (bf16[192,256]{1,0:T(8,128)(2,1)S(1)}, bf16[192,256]{1,0:T(8,128)(2,1)S(1)}, u32[]{:S(2)}, u32[]{:S(2)}) collective-permute-start(bf16[192,256]{1,0:T(8,128)(2,1)S(1)} %get-tuple-element.32), channel_id=1, source_target_pairs={{0,8},{8,0},{16,24},{24,16},{32,40},{40,32},{48,56},{56,48},{64,72... | collective-permute-start | bytes 294920 | tf_op jit(solution)/shard_map/ppermute | solution.py:439
  56.4 16.5 %all-to-all-start.3 = ((bf16[8,112,256]{2,1,0:T(8,128)(2,1)}), bf16[8,112,256]{2,1,0:T(8,128)(2,1)S(1)}, u32[]{:S(2)}, u32[]{:S(2)}) async-start(bf16[8,112,256]{2,1,0:T(8,128)(2,1)} %get-tuple-element.42), calls=%async_computation.3 | async-start | bytes 917504 | tf_op jit(solution)/shard_map/all_to_all | solution.py:418
  61.2 11.3 %collective-permute-start.2 = (bf16[192,256]{1,0:T(8,128)(2,1)S(1)}, bf16[192,256]{1,0:T(8,128)(2,1)S(1)}, u32[]{:S(2)}, u32[]{:S(2)}) collective-permute-start(bf16[192,256]{1,0:T(8,128)(2,1)S(1)} %get-tuple-element.41), channel_id=1, source_target_pairs={{0,8},{8,0},{16,24},{24,16},{32,40},{40,32},{48,56},{56,48},{64,72... | collective-permute-start | bytes 294920 | tf_op jit(solution)/shard_map/ppermute | solution.py:475
  73.7 13.6 %all-to-all-start.4 = ((bf16[8,16,256]{2,1,0:T(8,128)(2,1)}), bf16[8,16,256]{2,1,0:T(8,128)(2,1)S(1)}, u32[]{:S(2)}, u32[]{:S(2)}) async-start(bf16[8,16,256]{2,1,0:T(8,128)(2,1)} %get-tuple-element.47), calls=%async_computation.4 | async-start | bytes 131072 | tf_op jit(solution)/shard_map/all_to_all | solution.py:418
  80.1 1.1 %collective-permute-start.3 = (bf16[128,256]{1,0:T(8,128)(2,1)S(1)}, bf16[128,256]{1,0:T(8,128)(2,1)S(1)}, u32[]{:S(2)}, u32[]{:S(2)}) collective-permute-start(bf16[128,256]{1,0:T(8,128)(2,1)S(1)} %get-tuple-element.46), channel_id=1, source_target_pairs={{8,16},{24,32},{40,48},{56,64},{72,80},{88,96},{104,112},{120,128}... | collective-permute-start | bytes 196616 | tf_op jit(solution)/shard_map/ppermute | solution.py:476

commit v9 on v7

--- a/solution.py
+++ b/solution.py
@@ -17,7 +17,7 @@
 LN2 = math.log(2.0)
 F32 = jnp.float32
 BF16 = jnp.bfloat16
-PARAMS = pltpu.CompilerParams(vmem_limit_bytes=40 * 1024 * 1024)
+BLOCKS = [pl.ds(i * LEAF, LEAF) for i in range(LEAVES)]
 ROW_LEVEL = {1: 2, 2: 3, 3: 3, 4: 4, 5: 4, 6: 4, 7: 4}
 COLUMN_LEVEL = {1: 5, 2: 6, 3: 6, 4: 7, 5: 7, 6: 7, 7: 7}
 FAR = 48
@@ -77,25 +77,38 @@
     )
 
 
-def squares_kernel(q_ref, k_ref, out_ref):
-    q = q_ref[...].astype(F32)
-    k = k_ref[...].astype(F32)
-    tile = jnp.concatenate(token_sums(q * q) + token_sums(k * k), axis=0)
+def squares_kernel(q_in, k_in, qg_in, kg_in, out_ref, rows, gains, sems):
+    copies = []
+    for i in range(2 * LEAVES):
+        source = (q_in if i < LEAVES else k_in).at[pl.ds((i % LEAVES) * LEAF, LEAF)]
+        copies.append(pltpu.make_async_copy(source, rows.at[i], sems.at[i]))
+    for i, source in enumerate((qg_in, kg_in)):
+        copies.append(pltpu.make_async_copy(source, gains.at[i], sems.at[2 * LEAVES + i]))
+    for copy in copies:
+        copy.start()
+    sums = []
+    for i in range(2 * LEAVES):
+        copies[i].wait()
+        x = rows[i].astype(F32)
+        sums.append(jnp.sum((x * x).T, axis=0, keepdims=True))
+    for copy in copies[2 * LEAVES :]:
+        copy.wait()
+    tile = jnp.concatenate(sums + [gains[0], gains[1], jnp.zeros((6, FEAT), F32)], axis=0)
     for i in range(out_ref.shape[0]):
         out_ref[i] = tile
 
 
-def norm_kernel(width, sum_ref, q_ref, k_ref, v_ref, qg_ref, kg_ref, qn_ref, kv_ref, one_ref, lv_ref, y_ref, p1_ref, p2_ref):
+def rates(width, sum_ref):
+    return lax.rsqrt(jnp.sum(sum_ref[:, :8], axis=0) / width + EPS)
+
+
+def norm_kernel(width, sum_ref, k_ref, v_ref, kv_ref, one_ref, lv_ref, y_ref, p1_ref, p2_ref):
     index = lax.axis_index("seq")
     column = jnp.right_shift(index, 3)
     odd = jnp.bitwise_and(index, 1)
-    total = jnp.sum(sum_ref[...], axis=0)
-    rate = lax.rsqrt(total / width + EPS)
-    qn_ref[...] = (
-        q_ref[...].astype(F32) * spread_tokens(rate, 0) * qg_ref[...]
-    ).astype(BF16)
+    gain = sum_ref[lax.axis_index("head"), 9:10]
     kv_ref[:, :FEAT] = (
-        k_ref[...].astype(F32) * spread_tokens(rate, 4) * kg_ref[...]
+        k_ref[...].astype(F32) * spread_tokens(rates(width, sum_ref), 4) * gain
     ).astype(BF16)
     kv_ref[:, FEAT:] = v_ref[...]
     pool = jnp.concatenate(
@@ -114,24 +127,38 @@
     p2_ref[...] = kv_ref[pl.ds(pl.multiple_of(odd * 384, LEAF), LEAF)]
 
 
-def row_kernel(y_ref, lv_ref, out_ref):
+def start_all(copies):
+    for copy in copies:
+        copy.start()
+    return copies
+
+
+def wait_all(copies):
+    for copy in copies:
+        copy.wait()
+
+
+def row_kernel(y_ref, lv_ref, out_ref, slots_scr, sems):
     index = lax.axis_index("seq")
     column = jnp.right_shift(index, 3)
     place = jnp.bitwise_and(index, 7)
     slots = jnp.concatenate([y_ref[jnp.bitwise_xor(column, d)] for d in range(1, 8)], axis=0)
     far = dot(far_pick((FAR, 112), 0), slots, (1, 0)).astype(BF16)
-    for s in range(8):
-        out_ref[s, :FAR] = far
-    out_ref[place, FAR:] = jnp.zeros((64, 2 * FEAT), BF16)
-    for d in range(1, 8):
-        other = jnp.bitwise_xor(place, d)
-        if d == 1:
-            out_ref[other, FAR:] = lv_ref[:64]
+    copies = []
+    for d in range(8):
+        slots_scr[d, :FAR] = far
+        if d == 0:
+            slots_scr[d, FAR:] = jnp.zeros((64, 2 * FEAT), BF16)
+        elif d == 1:
+            slots_scr[d, FAR:] = lv_ref[:64]
         elif d < 4:
-            out_ref[other, FAR:] = lv_ref[128:192]
+            slots_scr[d, FAR:] = lv_ref[128:192]
         else:
-            out_ref[other, FAR : FAR + 32] = lv_ref[192:224]
-            out_ref[other, FAR + 32 :] = jnp.zeros((32, 2 * FEAT), BF16)
+            slots_scr[d, FAR : FAR + 32] = lv_ref[192:224]
+            slots_scr[d, FAR + 32 :] = jnp.zeros((32, 2 * FEAT), BF16)
+        target = out_ref.at[jnp.bitwise_xor(place, d)]
+        copies += start_all([pltpu.make_async_copy(slots_scr.at[d], target, sems.at[d])])
+    wait_all(copies)
 
 
 def by_head(block):
@@ -190,7 +217,11 @@
     return by_head(block) * jnp.asarray(0.125, BF16)
 
 
-def near_kernel(qn_ref, kv_ref, one_ref, g_ref, stat_ref):
+def near_kernel(width, sum_ref, q_ref, kv_ref, one_ref, g_ref, qn_ref, stat_ref):
+    gain = sum_ref[lax.axis_index("head"), 8:9]
+    qn_ref[...] = (
+        q_ref[...].astype(F32) * spread_tokens(rates(width, sum_ref), 0) * gain
+    ).astype(BF16)
     for b in range(LEAVES):
         block = slice(b * LEAF, (b + 1) * LEAF)
         q2 = scaled_queries(qn_ref[block])
@@ -210,7 +241,7 @@
 def attend_kernel(
     qn_ref, g_ref, near_ref, p1_ref, p2_ref, z_ref,
     stat_ref, cross, halo, p1o_ref, p2o_ref, zo_ref,
-    q2_scr, g2_scr, weight_scr, pgrad_scr, low_scr, sgrad_scr, rims, cross_grad,
+    q2_scr, g2_scr, weight_scr, pgrad_scr, low_scr, sgrad_scr, rims, mid_grad, far_scr, mid_scr, sems,
 ):
     index = lax.axis_index("seq")
     place = jnp.bitwise_and(index, 7)
@@ -264,28 +295,47 @@
                 rims[side, :, :FEAT] = dot(sgrad, q2, (1, 0)).astype(BF16)
                 rims[side, :, FEAT:] = dot(low, g2, (1, 0)).astype(BF16)
 
-    cross_grad[:, :FEAT] = dot(sgrad_scr[...], q2_scr[...], (1, 0)).astype(BF16)
-    cross_grad[:, FEAT:] = dot(low_scr[...], g2_scr[...], (1, 0)).astype(BF16)
+    def grads(rows):
+        keys = dot(sgrad_scr[rows], q2_scr[...], (1, 0))
+        values = dot(low_scr[rows], g2_scr[...], (1, 0))
+        return jnp.concatenate([keys, values], axis=1).astype(BF16)
+
+    for j in range(3):
+        far = grads(slice(384 + LEAF * j, 384 + LEAF * (j + 1)))
+        for s in range(8):
+            far_scr[s, 16 * j : 16 * (j + 1)] = far[16 * s : 16 * (s + 1)]
+    copies = start_all(
+        [
+            pltpu.make_async_copy(far_scr.at[s], zo_ref.at[s, pl.ds(0, FAR)], sems.at[s])
+            for s in range(8)
+        ]
+    )
+    mid_grad[...] = grads(slice(0, 384))
+    mid_scr[...] = jnp.zeros_like(mid_scr)
+    mid_scr[1] = mid_grad[:64]
+    mid_scr[2] = mid_grad[128:192]
+    mid_scr[3] = mid_grad[192:256]
+    for i in range(4):
+        mid_scr[4 + i, :32] = mid_grad[256 + 32 * i : 288 + 32 * i]
+    copies += start_all(
+        [
+            pltpu.make_async_copy(
+                mid_scr.at[d],
+                zo_ref.at[jnp.bitwise_xor(place, d), pl.ds(FAR, 64)],
+                sems.at[8 + d],
+            )
+            for d in range(8)
+        ]
+    )
     p1o_ref[:LEAF] = rims[peer_side]
-    p1o_ref[LEAF:] = cross_grad[64:128]
+    p1o_ref[LEAF:] = mid_grad[64:128]
     p2o_ref[...] = rims[odd]
-    for s in range(8):
-        for j in range(3):
-            at = 384 + LEAF * j + 16 * s
-            zo_ref[s, 16 * j : 16 * (j + 1)] = cross_grad[at : at + 16]
-    zo_ref[place, FAR:] = jnp.zeros((64, 2 * FEAT), BF16)
-    zo_ref[jnp.bitwise_xor(place, 1), FAR:] = cross_grad[:64]
-    zo_ref[jnp.bitwise_xor(place, 2), FAR:] = cross_grad[128:192]
-    zo_ref[jnp.bitwise_xor(place, 3), FAR:] = cross_grad[192:256]
-    for i in range(4):
-        other = jnp.bitwise_xor(place, 4 + i)
-        zo_ref[other, FAR : FAR + 32] = cross_grad[256 + 32 * i : 288 + 32 * i]
-        zo_ref[other, FAR + 32 :] = jnp.zeros((32, 2 * FEAT), BF16)
+    wait_all(copies)
 
 
 def after_kernel(
-    stat_ref, qn_ref, kv_ref, one_ref, g_ref, halo, cross,
-    att_ref, nqg_ref, tok_ref, near, near_grad, one_grad,
+    stat_ref, qn_ref, kv_ref, one_ref, g_ref, halo, cross, sum_ref, q_ref,
+    att_ref, nqg_ref, tok_ref, qsum_ref, near, near_grad, one_grad,
 ):
     near[:LEAF] = halo[0]
     near[LEAF : LEAF + ROWS] = kv_ref[...]
@@ -332,6 +382,9 @@
     high = one_grad[...].astype(BF16)
     rest = (one_grad[...] - high.astype(F32)).astype(BF16)
     tok_ref[...] = near_grad[LEAF : LEAF + ROWS] + dot(spread, high, (1, 0)) + dot(spread, rest, (1, 0))
+    gains = sum_ref[lax.axis_index("head"), 8:16]
+    sums = token_sums(q_ref[...].astype(F32) * gains[0:1] * nqg_ref[...])
+    qsum_ref[...] = jnp.concatenate(sums + [gains[1:2], jnp.zeros((3, FEAT), F32)], axis=0)
 
 
 def column_kernel(z_ref, p1_ref, p2_ref, tok_ref, out_ref, far_rows, sem):
@@ -346,8 +399,12 @@
         out_ref[jnp.bitwise_xor(column, d)] = slots[16 * (d - 1) : 16 * d]
 
 
-def middle_kernel(tok_ref, p1_ref, p2_ref, z_ref, q_ref, qg_ref, nqg_ref, acc_ref, sum_ref):
+def total_kernel(
+    tok_ref, p1_ref, p2_ref, z_ref, y_ref, k_ref, qsum_ref,
+    nkg_ref, vg_ref, sum_ref, acc, value_rows, sems,
+):
     index = lax.axis_index("seq")
+    column = jnp.right_shift(index, 3)
     place = jnp.bitwise_and(index, 7)
     odd = jnp.bitwise_and(index, 1)
     pieces = [z_ref[jnp.bitwise_xor(place, 1), FAR:], p1_ref[LEAF:]]
@@ -356,52 +413,68 @@
         rows = ROWS >> ROW_LEVEL[d]
         pieces.append(z_ref[jnp.bitwise_xor(place, d), FAR : FAR + rows])
         maps.append(spreading(0, rows, ROW_LEVEL[d]))
+    for d in range(1, 8):
+        pieces.append(y_ref[jnp.bitwise_xor(column, d)])
+        maps.append(spreading(0, 16, COLUMN_LEVEL[d]))
     spread = jnp.concatenate(maps, axis=1).astype(BF16)
-    acc_ref[...] = tok_ref[...] + dot(spread, jnp.concatenate(pieces, axis=0), (1, 0))
-    acc_ref[pl.ds(pl.multiple_of((1 - odd) * 384, LEAF), LEAF)] += p1_ref[:LEAF].astype(F32)
-    acc_ref[pl.ds(pl.multiple_of(odd * 384, LEAF), LEAF)] += p2_ref[...].astype(F32)
-    sums = token_sums(q_ref[...].astype(F32) * qg_ref[...] * nqg_ref[...])
-    sum_ref[...] = jnp.concatenate(sums + [jnp.zeros((LEAVES, FEAT), F32)], axis=0)
-
-
-def total_kernel(acc_ref, y_ref, k_ref, kg_ref, qsum_ref, nkg_ref, vg_ref, sum_ref):
-    column = jnp.right_shift(lax.axis_index("seq"), 3)
-    pieces = [y_ref[jnp.bitwise_xor(column, d)] for d in range(1, 8)]
-    maps = [spreading(0, 16, COLUMN_LEVEL[d]) for d in range(1, 8)]
-    spread = jnp.concatenate(maps, axis=1).astype(BF16)
-    grads = acc_ref[...] + dot(spread, jnp.concatenate(pieces, axis=0), (1, 0))
-    vg_ref[...] = grads[:, FEAT:].astype(BF16)
-    key_total = grads[:, :FEAT]
+    acc[...] = tok_ref[...] + dot(spread, jnp.concatenate(pieces, axis=0), (1, 0))
+    acc[pl.ds(pl.multiple_of((1 - odd) * 384, LEAF), LEAF)] += p1_ref[:LEAF].astype(F32)
+    acc[pl.ds(pl.multiple_of(odd * 384, LEAF), LEAF)] += p2_ref[...].astype(F32)
+    value_rows[...] = acc[:, FEAT:].astype(BF16)
+    copies = start_all(
+        [
+            pltpu.make_async_copy(value_rows.at[rows], vg_ref.at[rows], sems.at[i])
+            for i, rows in enumerate(BLOCKS)
+        ]
+    )
+    key_total = acc[:, :FEAT]
     nkg_ref[...] = key_total
-    sums = token_sums(k_ref[...].astype(F32) * kg_ref[...] * key_total)
+    sums = token_sums(k_ref[...].astype(F32) * qsum_ref[LEAVES : LEAVES + 1] * key_total)
     tile = jnp.concatenate([qsum_ref[:LEAVES]] + sums, axis=0)
     for i in range(sum_ref.shape[0]):
         sum_ref[i] = tile
-
-
-def finish_kernel(width, sq_ref, inner_ref, q_ref, k_ref, qg_ref, kg_ref, nqg_ref, nkg_ref, dq_ref, dk_ref):
-    rate = lax.rsqrt(jnp.sum(sq_ref[...], axis=0) / width + EPS)
+    wait_all(copies)
+
+
+def finish_kernel(
+    width, sq_ref, inner_ref, q_ref, k_ref, nqg_ref, nkg_ref,
+    dq_ref, dk_ref, results, sems,
+):
+    rate = rates(width, sq_ref)
     inner = jnp.sum(inner_ref[...], axis=0) / width
     cubed = rate * rate * rate * inner
-    for first, x_ref, gain_ref, grad_ref, out_ref in (
-        (0, q_ref, qg_ref, nqg_ref, dq_ref),
-        (4, k_ref, kg_ref, nkg_ref, dk_ref),
+    copies = []
+    gains = sq_ref[lax.axis_index("head"), 8:16]
+    for side, (x_ref, grad_ref, out_ref) in enumerate(
+        ((q_ref, nqg_ref, dq_ref), (k_ref, nkg_ref, dk_ref))
     ):
-        out_ref[...] = (
-            spread_tokens(rate, first) * gain_ref[...] * grad_ref[...]
-            - x_ref[...].astype(F32) * spread_tokens(cubed, first)
+        results[side] = (
+            spread_tokens(rate, 4 * side) * gains[side : side + 1] * grad_ref[...]
+            - x_ref[...].astype(F32) * spread_tokens(cubed, 4 * side)
         ).astype(BF16)
-
-
-def call(kernel, outs, args, scratch=(), flops=0, name=None, spaces=None):
+        copies += start_all(
+            [
+                pltpu.make_async_copy(
+                    results.at[side, rows], out_ref.at[rows], sems.at[LEAVES * side + i]
+                )
+                for i, rows in enumerate(BLOCKS)
+            ]
+        )
+    wait_all(copies)
+
+
+def call(kernel, outs, args, scratch=(), flops=0, name=None, spaces=None, out_spaces=None, vmem=40):
     many = isinstance(outs, list)
     moved = sum(math.prod(x.shape) * x.dtype.itemsize for x in list(args) + (outs if many else [outs]))
+    out_spaces = out_spaces or [pltpu.VMEM] * (len(outs) if many else 1)
+    out_specs = [pl.BlockSpec(memory_space=space) for space in out_spaces]
     return pl.pallas_call(
         kernel,
         out_shape=outs,
         in_specs=[pl.BlockSpec(memory_space=space) for space in spaces or [pltpu.VMEM] * len(args)],
+        out_specs=out_specs if many else out_specs[0],
         scratch_shapes=list(scratch),
-        compiler_params=PARAMS,
+        compiler_params=pltpu.CompilerParams(vmem_limit_bytes=vmem * 1024 * 1024),
         cost_estimate=pl.CostEstimate(flops=flops, bytes_accessed=moved, transcendentals=0),
         name=name,
     )(*args)
@@ -428,23 +501,42 @@
     peer = [(i, i ^ 1) for i in range(seq)]
     beside = [(i, i + 1) for i in range(1, seq - 1, 2)] + [(i + 1, i) for i in range(1, seq - 1, 2)]
 
-    squares = call(squares_kernel, sds(heads, 8, FEAT, dtype=F32), (queries, key_rows), name="squares")
+    squares = call(
+        squares_kernel,
+        sds(heads, 16, FEAT, dtype=F32),
+        (queries, key_rows, qg, kg),
+        scratch=[
+            pltpu.VMEM((2 * LEAVES, LEAF, FEAT), BF16),
+            pltpu.VMEM((2, 1, FEAT), F32),
+            pltpu.SemaphoreType.DMA((2 * LEAVES + 2,)),
+        ],
+        spaces=[pl.ANY] * 4,
+        vmem=60,
+        name="squares",
+    )
     squares = exchange(squares, "head")
-    qn, kv, one, lv, ysend, p1, p2 = call(
+    kv, one, lv, ysend, p1, p2 = call(
         lambda *refs: norm_kernel(width, *refs),
-        [sds(ROWS, FEAT), sds(ROWS, 256), sds(256, 256), sds(224, 256), sds(8, 16, 256), sds(192, 256), sds(LEAF, 256)],
-        (squares, queries, key_rows, value_rows, qg, kg),
+        [sds(ROWS, 256), sds(256, 256), sds(224, 256), sds(8, 16, 256), sds(192, 256), sds(LEAF, 256)],
+        (squares, key_rows, value_rows),
         name="norm",
     )
     p1 = lax.ppermute(p1, "seq", peer)
     p2 = lax.ppermute(p2, "seq", beside)
     yrecv = exchange(ysend, "seq", COLUMN_GROUPS)
-    zsend = call(row_kernel, sds(8, SLOT, 256), (yrecv, lv), name="rows")
+    zsend = call(
+        row_kernel,
+        sds(8, SLOT, 256),
+        (yrecv, lv),
+        scratch=[pltpu.VMEM((8, SLOT, 256), BF16), pltpu.SemaphoreType.DMA((8,))],
+        out_spaces=[pl.ANY],
+        name="rows",
+    )
     zrecv = exchange(zsend, "seq", ROW_GROUPS)
-    near = call(
-        near_kernel,
-        sds(LEAVES, 8, 256, dtype=F32),
-        (qn, kv, one, out_grad),
+    qn, near = call(
+        lambda *refs: near_kernel(width, *refs),
+        [sds(ROWS, FEAT), sds(LEAVES, 8, 256, dtype=F32)],
+        (squares, queries, kv, one, out_grad),
         flops=14 * 2 * 2 * 256 * LEAF * FEAT,
         name="near",
     )
@@ -461,18 +553,23 @@
             pltpu.VMEM((768, 1024), BF16),
             pltpu.VMEM((768, 1024), BF16),
             pltpu.VMEM((2, LEAF, 256), BF16),
-            pltpu.VMEM((768, 256), BF16),
+            pltpu.VMEM((384, 256), BF16),
+            pltpu.VMEM((8, FAR, 256), BF16),
+            pltpu.VMEM((8, 64, 256), BF16),
+            pltpu.SemaphoreType.DMA((16,)),
         ],
+        out_spaces=[pltpu.VMEM] * 5 + [pl.ANY],
         flops=4 * 4 * 2 * 256 * 768 * FEAT,
         name="attend",
     )
     p1 = lax.ppermute(p1, "seq", peer)
     p2 = lax.ppermute(p2, "seq", beside)
     zrecv = exchange(zsend, "seq", ROW_GROUPS)
-    attended, nqg, tok = call(
+    attended, nqg, tok, qsum = call(
         after_kernel,
-        [sds(ROWS, FEAT), sds(ROWS, FEAT, dtype=F32), sds(ROWS, 256, dtype=F32)],
-        (stat, qn, kv, one, out_grad, halo, cross),
+        [sds(ROWS, FEAT), sds(ROWS, FEAT, dtype=F32), sds(ROWS, 256, dtype=F32)]
+        + [sds(8, FEAT, dtype=F32)],
+        (stat, qn, kv, one, out_grad, halo, cross, squares, queries),
         scratch=[
             pltpu.VMEM((768, 256), BF16),
             pltpu.VMEM((768, 256), F32),
@@ -490,24 +587,25 @@
         name="columns",
     )
     yrecv = exchange(ysend, "seq", COLUMN_GROUPS)
-    acc, qsum = call(
-        middle_kernel,
-        [sds(ROWS, 256, dtype=F32), sds(8, FEAT, dtype=F32)],
-        (tok, p1, p2, zrecv, queries, qg, nqg),
-        flops=2 * ROWS * 384 * 256,
-        name="middle",
-    )
     nkg, value_grad, inner = call(
         total_kernel,
         [sds(ROWS, FEAT, dtype=F32), sds(ROWS, FEAT), sds(heads, 8, FEAT, dtype=F32)],
-        (acc, yrecv, key_rows, kg, qsum),
+        (tok, p1, p2, zrecv, yrecv, key_rows, qsum),
+        scratch=[
+            pltpu.VMEM((ROWS, 256), F32),
+            pltpu.VMEM((ROWS, FEAT), BF16),
+            pltpu.SemaphoreType.DMA((LEAVES,)),
+        ],
+        out_spaces=[pltpu.VMEM, pl.ANY, pltpu.VMEM],
         name="total",
     )
     inner = exchange(inner, "head")
     query_grad, key_grad = call(
         lambda *refs: finish_kernel(width, *refs),
         [sds(ROWS, FEAT), sds(ROWS, FEAT)],
-        (squares, inner, queries, key_rows, qg, kg, nqg, nkg),
+        (squares, inner, queries, key_rows, nqg, nkg),
+        scratch=[pltpu.VMEM((2, ROWS, FEAT), BF16), pltpu.SemaphoreType.DMA((2 * LEAVES,))],
+        out_spaces=[pl.ANY, pl.ANY],
         name="finish",
     )
     return (attended, query_grad, key_grad, value_grad)

time: 102 us -> 101 us (level)
  blocking collectives: 37.3 us -> 48.2 us
  waiting for transfers between devices: 17.6 us -> 10.7 us
  starting transfers between devices: 29.7 us -> 25.7 us
  local copies, waits for them, and re-layouts: 2.49 us -> 0.02 us
  Pallas kernels: 13.3 us -> 14.9 us
    all_to_all x3 -> x4, blocking collectives: 37.3 us -> 48.2 us  [exchange(): return lax.all_to_all(x, axis, 0, 0, axis_index_groups=groups, tiled=True)]
    all_to_all x3 -> x2, waiting for transfers between devices: 10 us -> 3.29 us  [exchange(): return lax.all_to_all(x, axis, 0, 0, axis_index_groups=groups, tiled=True)]
    all_to_all x3 -> x2, starting transfers between devices: 19.2 us -> 15.3 us  [exchange(): return lax.all_to_all(x, axis, 0, 0, axis_index_groups=groups, tiled=True)]
    unnamed x16 -> x8, local copies, waits for them, and re-layouts: 2.49 us -> 0.02 us
    pallas_call x10 -> x9, Pallas kernels: 13.3 us -> 14.9 us  [call(): pl.pallas_call(kernel, out_shape=outs, in_specs=[pl.BlockSpec(memory_spac...]
  transfers between devices with their start and end apart: 7 -> 6, of which waited for: 5 -> 4; matrix products, arithmetic and copies ran while one was open for 0% -> 0% of each run, Pallas kernels for 5% -> 5%
where the time goes in v9:
time: 101 us; the launch traced here: 100 us
  blocking collectives  48.2 us (48%)
  starting transfers between devices  25.7 us (25%)
  Pallas kernels  14.9 us (15%)
  waiting for transfers between devices  10.7 us (11%)
    all_to_all x4, blocking collectives, exchange(): return lax.all_to_all(x, axis, 0, 0, axis_index_groups=groups, tiled=True)  48.2 us
    all_to_all x2, starting transfers between devices, exchange(): return lax.all_to_all(x, axis, 0, 0, axis_index_groups=groups, tiled=True)  15.3 us
    pallas_call x9, Pallas kernels, call(): pl.pallas_call(kernel, out_shape=outs, in_specs=[pl.BlockSpec(memory_spac...  14.9 us
    ppermute x2, starting transfers between devices, local(): p1 = lax.ppermute(p1, 'seq', peer)  9.15 us
    ppermute x2, waiting for transfers between devices, local(): p1 = lax.ppermute(p1, 'seq', peer)  7.46 us
    all_to_all x2, waiting for transfers between devices, exchange(): return lax.all_to_all(x, axis, 0, 0, axis_index_groups=groups, tiled=True)  3.29 us
  transfers between devices with their start and end apart: 6, of which 4 were waited for; matrix products, arithmetic and copies ran while one was open for 0% of the time, Pallas kernels for 5%

profile of v9, /device:TPU:1, one launch (start us, length us, event | category | flops | bytes accessed | tf_op | source)
XLA Modules:
  0.0 100.4 jit_solution(4885090700137352271)
XLA Ops:
  0.6 0.0 copy-start.2
  0.6 2.4 %squares.1 = f32[8,16,128]{2,1,0:T(8,128)} custom-call(bf16[512,128]{1,0:T(8,128)(2,1)} %refs_2_.3, bf16[512,128]{1,0:T(8,128)(2,1)} %refs_3_.1, f32[1,128]{1,0:T(1,128)} %bitcast.2, f32[1,128]{1,0:T(1,128)} %bitcast.3), custom_call_target="tpu_custom_call" | custom-call | bytes 328704 | tf_op jit(solution)/shard_map/squares/pallas_call | solution.py:471
  3.0 0.0 copy-start
  3.1 15.1 %all_to_all.30.refs_0_.sum_ref = f32[8,16,128]{2,1,0:T(8,128)S(1)} all-to-all(f32[8,16,128]{2,1,0:T(8,128)} %squares.1), channel_id=1, replica_groups=mesh['seq'=64,'head'=8] {'head'}, dimensions={0} | all-to-all | bytes 131072 | tf_op jit(solution)/shard_map/all_to_all | solution.py:492
  18.2 0.0 copy-done.2
  18.2 0.0 copy-done
  18.2 0.5 norm.1
  18.7 9.6 %all_to_all.31.y_ref = bf16[8,16,256]{2,1,0:T(8,128)(2,1)S(1)} all-to-all(bf16[8,16,256]{2,1,0:T(8,128)(2,1)S(1)} %get-tuple-element.33), channel_id=1, replica_groups={{0,64,128,192,256,320,384,448},{8,72,136,200,264,328,392,456},{16,80,14..., dimensions={0} | all-to-all | bytes 131072 | tf_op jit(solution)/shard_map/all_to_all | solution.py:492
  28.3 1.0 rows.1
  29.3 0.0 copy-start.1
  29.3 0.0 copy-start.3
  29.3 10.1 %all-to-all-start.2 = ((bf16[8,112,256]{2,1,0:T(8,128)(2,1)}), bf16[8,112,256]{2,1,0:T(8,128)(2,1)S(1)}, u32[]{:S(2)}, u32[]{:S(2)}) async-start(bf16[8,112,256]{2,1,0:T(8,128)(2,1)} %rows.1), calls=%async_computation.2 | async-start | bytes 917504 | tf_op jit(solution)/shard_map/all_to_all | solution.py:492
  39.4 3.4 %collective-permute-start = (bf16[192,256]{1,0:T(8,128)(2,1)S(1)}, bf16[192,256]{1,0:T(8,128)(2,1)S(1)}, u32[]{:S(2)}, u32[]{:S(2)}) collective-permute-start(bf16[192,256]{1,0:T(8,128)(2,1)S(1)} %get-tuple-element.31), channel_id=1, source_target_pairs={{0,8},{8,0},{16,24},{24,16},{32,40},{40,32},{48,56},{56,48},{64,72... | collective-permute-start | bytes 294920 | tf_op jit(solution)/shard_map/ppermute | solution.py:524
  42.8 0.7 collective-permute-start.1
  43.5 0.0 copy-done.1
  43.5 0.9 near.1
  44.4 0.0 collective-permute-done.1.p2_ref
  44.4 6.6 %collective-permute-done.p1_ref = bf16[192,256]{1,0:T(8,128)(2,1)S(1)} collective-permute-done((bf16[192,256]{1,0:T(8,128)(2,1)S(1)}, bf16[192,256]{1,0:T(8,128)(2,1)S(1)}, u32[]{:S(2)}, u32[]{:S(2)}) %collective-permute-start) | collective-permute-done | bytes 98336 | tf_op jit(solution)/shard_map/ppermute | solution.py:524
  51.0 1.7 %all-to-all-done.2.z_ref = bf16[8,112,256]{2,1,0:T(8,128)(2,1)S(1)} async-done(((bf16[8,112,256]{2,1,0:T(8,128)(2,1)}), bf16[8,112,256]{2,1,0:T(8,128)(2,1)S(1)}, u32[]{:S(2)}, u32[]{:S(2)}) %all-to-all-start.2) | async-done | bytes 458784 | tf_op jit(solution)/shard_map/all_to_all | solution.py:492
  52.7 3.7 %attend.1 = (f32[4,8,256]{2,1,0:T(8,128)S(1)}, bf16[768,256]{1,0:T(8,128)(2,1)S(1)}, bf16[2,128,256]{2,1,0:T(8,128)(2,1)S(1)}, bf16[192,256]{1,0:T(8,128)(2,1)S(...) custom-call(bf16[512,128]{1,0:T(8,128)(2,1)S(1)} %get-tuple-element.29.qn_ref, ...), custom_call_target="tpu_custom_call" | custom-call | flops 805306368 | bytes 2097152 | tf_op jit(solution)/shard_map/attend/pallas_call | solution.py:471
  56.4 5.2 %all-to-all-start.3 = ((bf16[8,112,256]{2,1,0:T(8,128)(2,1)}), bf16[8,112,256]{2,1,0:T(8,128)(2,1)S(1)}, u32[]{:S(2)}, u32[]{:S(2)}) async-start(bf16[8,112,256]{2,1,0:T(8,128)(2,1)} %get-tuple-element.42), calls=%async_computation.3 | async-start | bytes 917504 | tf_op jit(solution)/shard_map/all_to_all | solution.py:492
  61.6 0.7 collective-permute-start.3
  62.2 5.8 %collective-permute-start.2 = (bf16[192,256]{1,0:T(8,128)(2,1)S(1)}, bf16[192,256]{1,0:T(8,128)(2,1)S(1)}, u32[]{:S(2)}, u32[]{:S(2)}) collective-permute-start(bf16[192,256]{1,0:T(8,128)(2,1)S(1)} %get-tuple-element.40), channel_id=1, source_target_pairs={{0,8},{8,0},{16,24},{24,16},{32,40},{40,32},{48,56},{56,48},{64,72... | collective-permute-start | bytes 294920 | tf_op jit(solution)/shard_map/ppermute | solution.py:565
  68.0 3.7 %after.1 = (bf16[512,128]{1,0:T(8,128)(2,1)}, f32[512,128]{1,0:T(8,128)S(1)}, f32[512,256]{1,0:T(8,128)S(1)}, f32[8,128]{1,0:T(8,128)S(1)}) custom-call(f32[4,8,256]{2,1,0:T(8,128)S(1)} %get-tuple-element.35.stat_ref, bf16[512,128]{1,0:T(8,128)(2,1)S(1)} %get-tuple-element.29.qn_ref, bf16[512,256]{1,0:T(8,128)(2,1)S(1)} %get-tuple-element.27.refs_2_.kv_ref, ...), custom_call_target="tpu_custom_call" | custom-call | flops 1677721600 | bytes 2330624 | tf_op jit(solution)/shard_map/after/pallas_call | solution.py:471
  71.8 0.0 collective-permute-done.3.p2_ref
  71.8 0.8 collective-permute-done.2.p1_ref
  72.6 1.6 %all-to-all-done.3.z_ref = bf16[8,112,256]{2,1,0:T(8,128)(2,1)S(1)} async-done(((bf16[8,112,256]{2,1,0:T(8,128)(2,1)}), bf16[8,112,256]{2,1,0:T(8,128)(2,1)S(1)}, u32[]{:S(2)}, u32[]{:S(2)}) %all-to-all-start.3) | async-done | bytes 458784 | tf_op jit(solution)/shard_map/all_to_all | solution.py:492
  74.2 0.2 columns.1
  74.4 10.6 %all_to_all.32.y_ref = bf16[8,16,256]{2,1,0:T(8,128)(2,1)S(1)} all-to-all(bf16[8,16,256]{2,1,0:T(8,128)(2,1)S(1)} %columns.1), channel_id=1, replica_groups={{0,64,128,192,256,320,384,448},{8,72,136,200,264,328,392,456},{16,80,14..., dimensions={0} | all-to-all | bytes 131072 | tf_op jit(solution)/shard_map/all_to_all | solution.py:492
  85.0 1.4 %total.1 = (f32[512,128]{1,0:T(8,128)S(1)}, bf16[512,128]{1,0:T(8,128)(2,1)}, f32[8,8,128]{2,1,0:T(8,128)S(1)}) custom-call(f32[512,256]{1,0:T(8,128)S(1)} %get-tuple-element.39.tok_ref, bf16[192,256]{1,0:T(8,128)(2,1)S(1)} %collective-permute-done.2.p1_ref, bf16[128,256]{1,0:T(8,128)(2,1)S(1)} %collective-permute-done.3.p2_ref, ...), custom_call_target="tpu_custom_call" | custom-call | bytes 1773568 | tf_op jit(solution)/shard_map/total/pallas_call | solution.py:471
  86.4 12.8 %all_to_all.33.refs_1_ = f32[8,8,128]{2,1,0:T(8,128)S(1)} all-to-all(f32[8,8,128]{2,1,0:T(8,128)S(1)} %get-tuple-element.44), channel_id=1, replica_groups=mesh['seq'=64,'head'=8] {'head'}, dimensions={0} | all-to-all | bytes 65536 | tf_op jit(solution)/shard_map/all_to_all | solution.py:492
  99.3 1.1 %finish.1 = (bf16[512,128]{1,0:T(8,128)(2,1)}, bf16[512,128]{1,0:T(8,128)(2,1)}) custom-call(f32[8,16,128]{2,1,0:T(8,128)S(1)} %all_to_all.30.refs_0_.sum_ref, f32[8,8,128]{2,1,0:T(8,128)S(1)} %all_to_all.33.refs_1_, bf16[512,128]{1,0:T(8,128)(2,1)S(1)} %copy-done.1, bf16[512,128]{1,0:T(8,128)(2,1)S(1)} %copy-done, ...), custom_call_target="tpu_custom_call" | custom-call | bytes 1146880 | tf_op jit(solution)/shard_map/finish/pallas_call | solution.py:471
  (1 shorter events, 0.0 us)
Async XLA Ops:
  0.6 17.5 %copy-start.2 = (bf16[512,128]{1,0:T(8,128)(2,1)S(1)}, bf16[512,128]{1,0:T(8,128)(2,1)}, u32[]{:S(2)}) copy-start(bf16[512,128]{1,0:T(8,128)(2,1)} %refs_2_.2) | copy-start | bytes 393220
  3.0 15.1 %copy-start = (bf16[512,128]{1,0:T(8,128)(2,1)S(1)}, bf16[512,128]{1,0:T(8,128)(2,1)}, u32[]{:S(2)}) copy-start(bf16[512,128]{1,0:T(8,128)(2,1)} %refs_3_.1) | copy-start | bytes 393220
  29.3 14.2 %copy-start.1 = (bf16[512,128]{1,0:T(8,128)(2,1)S(1)}, bf16[512,128]{1,0:T(8,128)(2,1)}, u32[]{:S(2)}) copy-start(bf16[512,128]{1,0:T(8,128)(2,1)} %refs_2_.3) | copy-start | bytes 393220
  29.3 14.2 %copy-start.3 = (bf16[512,128]{1,0:T(8,128)(2,1)S(1)}, bf16[512,128]{1,0:T(8,128)(2,1)}, u32[]{:S(2)}) copy-start(bf16[512,128]{1,0:T(8,128)(2,1)} %g_ref.3) | copy-start | bytes 393220
  29.3 23.4 %all-to-all-start.2 = ((bf16[8,112,256]{2,1,0:T(8,128)(2,1)}), bf16[8,112,256]{2,1,0:T(8,128)(2,1)S(1)}, u32[]{:S(2)}, u32[]{:S(2)}) async-start(bf16[8,112,256]{2,1,0:T(8,128)(2,1)} %rows.1), calls=%async_computation.2 | async-start | bytes 917504 | tf_op jit(solution)/shard_map/all_to_all | solution.py:492
  39.4 11.6 %collective-permute-start = (bf16[192,256]{1,0:T(8,128)(2,1)S(1)}, bf16[192,256]{1,0:T(8,128)(2,1)S(1)}, u32[]{:S(2)}, u32[]{:S(2)}) collective-permute-start(bf16[192,256]{1,0:T(8,128)(2,1)S(1)} %get-tuple-element.31), channel_id=1, source_target_pairs={{0,8},{8,0},{16,24},{24,16},{32,40},{40,32},{48,56},{56,48},{64,72... | collective-permute-start | bytes 294920 | tf_op jit(solution)/shard_map/ppermute | solution.py:524
  42.8 1.6 %collective-permute-start.1 = (bf16[128,256]{1,0:T(8,128)(2,1)S(1)}, bf16[128,256]{1,0:T(8,128)(2,1)S(1)}, u32[]{:S(2)}, u32[]{:S(2)}) collective-permute-start(bf16[128,256]{1,0:T(8,128)(2,1)S(1)} %get-tuple-element.32), channel_id=1, source_target_pairs={{8,16},{24,32},{40,48},{56,64},{72,80},{88,96},{104,112},{120,128}... | collective-permute-start | bytes 196616 | tf_op jit(solution)/shard_map/ppermute | solution.py:525
  56.4 17.8 %all-to-all-start.3 = ((bf16[8,112,256]{2,1,0:T(8,128)(2,1)}), bf16[8,112,256]{2,1,0:T(8,128)(2,1)S(1)}, u32[]{:S(2)}, u32[]{:S(2)}) async-start(bf16[8,112,256]{2,1,0:T(8,128)(2,1)} %get-tuple-element.42), calls=%async_computation.3 | async-start | bytes 917504 | tf_op jit(solution)/shard_map/all_to_all | solution.py:492
  61.6 10.2 %collective-permute-start.3 = (bf16[128,256]{1,0:T(8,128)(2,1)S(1)}, bf16[128,256]{1,0:T(8,128)(2,1)S(1)}, u32[]{:S(2)}, u32[]{:S(2)}) collective-permute-start(bf16[128,256]{1,0:T(8,128)(2,1)S(1)} %get-tuple-element.41), channel_id=1, source_target_pairs={{8,16},{24,32},{40,48},{56,64},{72,80},{88,96},{104,112},{120,128}... | collective-permute-start | bytes 196616 | tf_op jit(solution)/shard_map/ppermute | solution.py:566
  62.2 10.4 %collective-permute-start.2 = (bf16[192,256]{1,0:T(8,128)(2,1)S(1)}, bf16[192,256]{1,0:T(8,128)(2,1)S(1)}, u32[]{:S(2)}, u32[]{:S(2)}) collective-permute-start(bf16[192,256]{1,0:T(8,128)(2,1)S(1)} %get-tuple-element.40), channel_id=1, source_target_pairs={{0,8},{8,0},{16,24},{24,16},{32,40},{40,32},{48,56},{56,48},{64,72... | collective-permute-start | bytes 294920 | tf_op jit(solution)/shard_map/ppermute | solution.py:565

commit v10 on v9

--- a/solution.py
+++ b/solution.py
@@ -138,26 +138,24 @@
         copy.wait()
 
 
-def row_kernel(y_ref, lv_ref, out_ref, slots_scr, sems):
+def row_kernel(y_ref, lv_ref, out_ref, far_scr, sems):
     index = lax.axis_index("seq")
     column = jnp.right_shift(index, 3)
     place = jnp.bitwise_and(index, 7)
+    copies = []
+    for d in range(1, 8):
+        first, rows = {1: (0, 64), 2: (128, 64), 3: (128, 64)}.get(d, (192, 32))
+        target = out_ref.at[jnp.bitwise_xor(place, d), pl.ds(FAR, rows)]
+        copies.append(pltpu.make_async_copy(lv_ref.at[pl.ds(first, rows)], target, sems.at[d]))
+    start_all(copies)
     slots = jnp.concatenate([y_ref[jnp.bitwise_xor(column, d)] for d in range(1, 8)], axis=0)
-    far = dot(far_pick((FAR, 112), 0), slots, (1, 0)).astype(BF16)
-    copies = []
-    for d in range(8):
-        slots_scr[d, :FAR] = far
-        if d == 0:
-            slots_scr[d, FAR:] = jnp.zeros((64, 2 * FEAT), BF16)
-        elif d == 1:
-            slots_scr[d, FAR:] = lv_ref[:64]
-        elif d < 4:
-            slots_scr[d, FAR:] = lv_ref[128:192]
-        else:
-            slots_scr[d, FAR : FAR + 32] = lv_ref[192:224]
-            slots_scr[d, FAR + 32 :] = jnp.zeros((32, 2 * FEAT), BF16)
-        target = out_ref.at[jnp.bitwise_xor(place, d)]
-        copies += start_all([pltpu.make_async_copy(slots_scr.at[d], target, sems.at[d])])
+    far_scr[...] = dot(far_pick((FAR, 112), 0), slots, (1, 0)).astype(BF16)
+    copies += start_all(
+        [
+            pltpu.make_async_copy(far_scr, out_ref.at[s, pl.ds(0, FAR)], sems.at[8 + s])
+            for s in range(8)
+        ]
+    )
     wait_all(copies)
 
 
@@ -261,6 +259,7 @@
             cross[at : at + 16] = z_ref[s, 16 * j : 16 * (j + 1)]
 
     outside = outside_bias()
+    rim_rows = []
     for b in range(LEAVES):
         block = slice(b * LEAF, (b + 1) * LEAF)
         lanes = slice(2 * b * LEAF, 2 * (b + 1) * LEAF)
@@ -284,16 +283,14 @@
         stat_ref[b] = jnp.concatenate(
             [top, inverse, delta, jnp.zeros((5, 2 * LEAF), F32)], axis=0
         )
-        for i in pieces:
+        for i in range(6):
             prob = weight_scr[b, i] * (factors[i + 1] * inverse)
-            low = prob.astype(BF16)
-            sgrad = (prob * (pgrad_scr[b, i] - delta)).astype(BF16)
-            if i < 6:
-                low_scr[i * LEAF : (i + 1) * LEAF, lanes] = low
-                sgrad_scr[i * LEAF : (i + 1) * LEAF, lanes] = sgrad
-            else:
-                rims[side, :, :FEAT] = dot(sgrad, q2, (1, 0)).astype(BF16)
-                rims[side, :, FEAT:] = dot(low, g2, (1, 0)).astype(BF16)
+            low_scr[i * LEAF : (i + 1) * LEAF, lanes] = prob.astype(BF16)
+            sgrad_scr[i * LEAF : (i + 1) * LEAF, lanes] = (
+                prob * (pgrad_scr[b, i] - delta)
+            ).astype(BF16)
+        if b in HALO_PIECE:
+            rim_rows.append((b, side, lanes, factors[7] * inverse, delta))
 
     def grads(rows):
         keys = dot(sgrad_scr[rows], q2_scr[...], (1, 0))
@@ -327,6 +324,11 @@
             for d in range(8)
         ]
     )
+    for b, side, lanes, factor, delta in rim_rows:
+        prob = weight_scr[b, 6] * factor
+        sgrad = (prob * (pgrad_scr[b, 6] - delta)).astype(BF16)
+        rims[side, :, :FEAT] = dot(sgrad, q2_scr[lanes], (1, 0)).astype(BF16)
+        rims[side, :, FEAT:] = dot(prob.astype(BF16), g2_scr[lanes], (1, 0)).astype(BF16)
     p1o_ref[:LEAF] = rims[peer_side]
     p1o_ref[LEAF:] = mid_grad[64:128]
     p2o_ref[...] = rims[odd]
@@ -401,7 +403,7 @@
 
 def total_kernel(
     tok_ref, p1_ref, p2_ref, z_ref, y_ref, k_ref, qsum_ref,
-    nkg_ref, vg_ref, sum_ref, acc, value_rows, sems,
+    nkg_ref, vg_ref, sum_ref, acc,
 ):
     index = lax.axis_index("seq")
     column = jnp.right_shift(index, 3)
@@ -420,30 +422,23 @@
     acc[...] = tok_ref[...] + dot(spread, jnp.concatenate(pieces, axis=0), (1, 0))
     acc[pl.ds(pl.multiple_of((1 - odd) * 384, LEAF), LEAF)] += p1_ref[:LEAF].astype(F32)
     acc[pl.ds(pl.multiple_of(odd * 384, LEAF), LEAF)] += p2_ref[...].astype(F32)
-    value_rows[...] = acc[:, FEAT:].astype(BF16)
-    copies = start_all(
-        [
-            pltpu.make_async_copy(value_rows.at[rows], vg_ref.at[rows], sems.at[i])
-            for i, rows in enumerate(BLOCKS)
-        ]
-    )
+    vg_ref[...] = acc[:, FEAT:].astype(BF16)
     key_total = acc[:, :FEAT]
     nkg_ref[...] = key_total
     sums = token_sums(k_ref[...].astype(F32) * qsum_ref[LEAVES : LEAVES + 1] * key_total)
     tile = jnp.concatenate([qsum_ref[:LEAVES]] + sums, axis=0)
     for i in range(sum_ref.shape[0]):
         sum_ref[i] = tile
-    wait_all(copies)
 
 
 def finish_kernel(
-    width, sq_ref, inner_ref, q_ref, k_ref, nqg_ref, nkg_ref,
-    dq_ref, dk_ref, results, sems,
+    width, sq_ref, inner_ref, q_ref, k_ref, nqg_ref, nkg_ref, value_ref,
+    dq_ref, dk_ref, vg_ref, results, sems,
 ):
+    copies = start_all([pltpu.make_async_copy(value_ref, vg_ref, sems.at[2 * LEAVES])])
     rate = rates(width, sq_ref)
     inner = jnp.sum(inner_ref[...], axis=0) / width
     cubed = rate * rate * rate * inner
-    copies = []
     gains = sq_ref[lax.axis_index("head"), 8:16]
     for side, (x_ref, grad_ref, out_ref) in enumerate(
         ((q_ref, nqg_ref, dq_ref), (k_ref, nkg_ref, dk_ref))
@@ -528,7 +523,7 @@
         row_kernel,
         sds(8, SLOT, 256),
         (yrecv, lv),
-        scratch=[pltpu.VMEM((8, SLOT, 256), BF16), pltpu.SemaphoreType.DMA((8,))],
+        scratch=[pltpu.VMEM((FAR, 256), BF16), pltpu.SemaphoreType.DMA((16,))],
         out_spaces=[pl.ANY],
         name="rows",
     )
@@ -593,19 +588,16 @@
         (tok, p1, p2, zrecv, yrecv, key_rows, qsum),
         scratch=[
             pltpu.VMEM((ROWS, 256), F32),
-            pltpu.VMEM((ROWS, FEAT), BF16),
-            pltpu.SemaphoreType.DMA((LEAVES,)),
         ],
-        out_spaces=[pltpu.VMEM, pl.ANY, pltpu.VMEM],
         name="total",
     )
     inner = exchange(inner, "head")
-    query_grad, key_grad = call(
+    query_grad, key_grad, value_grad = call(
         lambda *refs: finish_kernel(width, *refs),
-        [sds(ROWS, FEAT), sds(ROWS, FEAT)],
-        (squares, inner, queries, key_rows, nqg, nkg),
-        scratch=[pltpu.VMEM((2, ROWS, FEAT), BF16), pltpu.SemaphoreType.DMA((2 * LEAVES,))],
-        out_spaces=[pl.ANY, pl.ANY],
+        [sds(ROWS, FEAT), sds(ROWS, FEAT), sds(ROWS, FEAT)],
+        (squares, inner, queries, key_rows, nqg, nkg, value_grad),
+        scratch=[pltpu.VMEM((2, ROWS, FEAT), BF16), pltpu.SemaphoreType.DMA((2 * LEAVES + 1,))],
+        out_spaces=[pl.ANY] * 3,
         name="finish",
     )
     return (attended, query_grad, key_grad, value_grad)

time: 101 us -> 100 us (0.990)
  no operation moved by 1% of the time
where the time goes in v10:
time: 100 us; the launch traced here: 99.7 us
  blocking collectives  48.2 us (48%)
  starting transfers between devices  25.7 us (26%)
  Pallas kernels  14.3 us (14%)
  waiting for transfers between devices  10.7 us (11%)
    all_to_all x4, blocking collectives, exchange(): return lax.all_to_all(x, axis, 0, 0, axis_index_groups=groups, tiled=True)  48.2 us
    all_to_all x2, starting transfers between devices, exchange(): return lax.all_to_all(x, axis, 0, 0, axis_index_groups=groups, tiled=True)  15.3 us
    pallas_call x9, Pallas kernels, call(): pl.pallas_call(kernel, out_shape=outs, in_specs=[pl.BlockSpec(memory_spac...  14.3 us
    ppermute x2, starting transfers between devices, local(): p1 = lax.ppermute(p1, 'seq', peer)  9.15 us
    ppermute x2, waiting for transfers between devices, local(): p1 = lax.ppermute(p1, 'seq', peer)  7.46 us
    all_to_all x2, waiting for transfers between devices, exchange(): return lax.all_to_all(x, axis, 0, 0, axis_index_groups=groups, tiled=True)  3.28 us
  transfers between devices with their start and end apart: 6, of which 4 were waited for; matrix products, arithmetic and copies ran while one was open for 0% of the time, Pallas kernels for 5%

profile of v10, /device:TPU:1, one launch (start us, length us, event | category | flops | bytes accessed | tf_op | source)
XLA Modules:
  0.0 99.7 jit_solution(9928680740049598521)
XLA Ops:
  0.6 0.0 copy-start.2
  0.6 2.4 %squares.1 = f32[8,16,128]{2,1,0:T(8,128)} custom-call(bf16[512,128]{1,0:T(8,128)(2,1)} %refs_2_.3, bf16[512,128]{1,0:T(8,128)(2,1)} %refs_3_.1, f32[1,128]{1,0:T(1,128)} %bitcast.2, f32[1,128]{1,0:T(1,128)} %bitcast.3), custom_call_target="tpu_custom_call" | custom-call | bytes 328704 | tf_op jit(solution)/shard_map/squares/pallas_call | solution.py:466
  3.0 0.0 copy-start
  3.1 15.1 %all_to_all.30.refs_0_.sum_ref = f32[8,16,128]{2,1,0:T(8,128)S(1)} all-to-all(f32[8,16,128]{2,1,0:T(8,128)} %squares.1), channel_id=1, replica_groups=mesh['seq'=64,'head'=8] {'head'}, dimensions={0} | all-to-all | bytes 131072 | tf_op jit(solution)/shard_map/all_to_all | solution.py:487
  18.2 0.0 copy-done.2
  18.2 0.0 copy-done
  18.2 0.5 norm.1
  18.7 9.6 %all_to_all.31.y_ref = bf16[8,16,256]{2,1,0:T(8,128)(2,1)S(1)} all-to-all(bf16[8,16,256]{2,1,0:T(8,128)(2,1)S(1)} %get-tuple-element.34), channel_id=1, replica_groups={{0,64,128,192,256,320,384,448},{8,72,136,200,264,328,392,456},{16,80,14..., dimensions={0} | all-to-all | bytes 131072 | tf_op jit(solution)/shard_map/all_to_all | solution.py:487
  28.3 1.0 rows.1
  29.3 0.0 copy-start.1
  29.3 0.0 copy-start.3
  29.3 10.1 %all-to-all-start.2 = ((bf16[8,112,256]{2,1,0:T(8,128)(2,1)}), bf16[8,112,256]{2,1,0:T(8,128)(2,1)S(1)}, u32[]{:S(2)}, u32[]{:S(2)}) async-start(bf16[8,112,256]{2,1,0:T(8,128)(2,1)} %rows.1), calls=%async_computation.2 | async-start | bytes 917504 | tf_op jit(solution)/shard_map/all_to_all | solution.py:487
  39.4 3.4 %collective-permute-start = (bf16[192,256]{1,0:T(8,128)(2,1)S(1)}, bf16[192,256]{1,0:T(8,128)(2,1)S(1)}, u32[]{:S(2)}, u32[]{:S(2)}) collective-permute-start(bf16[192,256]{1,0:T(8,128)(2,1)S(1)} %get-tuple-element.32), channel_id=1, source_target_pairs={{0,8},{8,0},{16,24},{24,16},{32,40},{40,32},{48,56},{56,48},{64,72... | collective-permute-start | bytes 294920 | tf_op jit(solution)/shard_map/ppermute | solution.py:519
  42.8 0.7 collective-permute-start.1
  43.4 0.0 copy-done.1
  43.5 0.9 near.1
  44.4 0.0 collective-permute-done.1.p2_ref
  44.4 6.6 %collective-permute-done.p1_ref = bf16[192,256]{1,0:T(8,128)(2,1)S(1)} collective-permute-done((bf16[192,256]{1,0:T(8,128)(2,1)S(1)}, bf16[192,256]{1,0:T(8,128)(2,1)S(1)}, u32[]{:S(2)}, u32[]{:S(2)}) %collective-permute-start) | collective-permute-done | bytes 98336 | tf_op jit(solution)/shard_map/ppermute | solution.py:519
  51.0 1.7 %all-to-all-done.2.z_ref = bf16[8,112,256]{2,1,0:T(8,128)(2,1)S(1)} async-done(((bf16[8,112,256]{2,1,0:T(8,128)(2,1)}), bf16[8,112,256]{2,1,0:T(8,128)(2,1)S(1)}, u32[]{:S(2)}, u32[]{:S(2)}) %all-to-all-start.2) | async-done | bytes 458784 | tf_op jit(solution)/shard_map/all_to_all | solution.py:487
  52.7 3.7 %attend.1 = (f32[4,8,256]{2,1,0:T(8,128)S(1)}, bf16[768,256]{1,0:T(8,128)(2,1)S(1)}, bf16[2,128,256]{2,1,0:T(8,128)(2,1)S(1)}, bf16[192,256]{1,0:T(8,128)(2,1)S(...) custom-call(bf16[512,128]{1,0:T(8,128)(2,1)S(1)} %get-tuple-element.30.qn_ref, ...), custom_call_target="tpu_custom_call" | custom-call | flops 805306368 | bytes 2097152 | tf_op jit(solution)/shard_map/attend/pallas_call | solution.py:466
  56.4 5.2 %all-to-all-start.3 = ((bf16[8,112,256]{2,1,0:T(8,128)(2,1)}), bf16[8,112,256]{2,1,0:T(8,128)(2,1)S(1)}, u32[]{:S(2)}, u32[]{:S(2)}) async-start(bf16[8,112,256]{2,1,0:T(8,128)(2,1)} %get-tuple-element.43), calls=%async_computation.3 | async-start | bytes 917504 | tf_op jit(solution)/shard_map/all_to_all | solution.py:487
  61.5 0.7 collective-permute-start.3
  62.2 5.8 %collective-permute-start.2 = (bf16[192,256]{1,0:T(8,128)(2,1)S(1)}, bf16[192,256]{1,0:T(8,128)(2,1)S(1)}, u32[]{:S(2)}, u32[]{:S(2)}) collective-permute-start(bf16[192,256]{1,0:T(8,128)(2,1)S(1)} %get-tuple-element.41), channel_id=1, source_target_pairs={{0,8},{8,0},{16,24},{24,16},{32,40},{40,32},{48,56},{56,48},{64,72... | collective-permute-start | bytes 294920 | tf_op jit(solution)/shard_map/ppermute | solution.py:560
  68.0 3.7 %after.1 = (bf16[512,128]{1,0:T(8,128)(2,1)}, f32[512,128]{1,0:T(8,128)S(1)}, f32[512,256]{1,0:T(8,128)S(1)}, f32[8,128]{1,0:T(8,128)S(1)}) custom-call(f32[4,8,256]{2,1,0:T(8,128)S(1)} %get-tuple-element.36.stat_ref, bf16[512,128]{1,0:T(8,128)(2,1)S(1)} %get-tuple-element.30.qn_ref, bf16[512,256]{1,0:T(8,128)(2,1)S(1)} %get-tuple-element.28.refs_2_.kv_ref, ...), custom_call_target="tpu_custom_call" | custom-call | flops 1677721600 | bytes 2330624 | tf_op jit(solution)/shard_map/after/pallas_call | solution.py:466
  71.7 0.0 collective-permute-done.3.p2_ref
  71.7 0.8 collective-permute-done.2.p1_ref
  72.6 1.6 %all-to-all-done.3.z_ref = bf16[8,112,256]{2,1,0:T(8,128)(2,1)S(1)} async-done(((bf16[8,112,256]{2,1,0:T(8,128)(2,1)}), bf16[8,112,256]{2,1,0:T(8,128)(2,1)S(1)}, u32[]{:S(2)}, u32[]{:S(2)}) %all-to-all-start.3) | async-done | bytes 458784 | tf_op jit(solution)/shard_map/all_to_all | solution.py:487
  74.2 0.2 columns.1
  74.4 10.6 %all_to_all.32.y_ref = bf16[8,16,256]{2,1,0:T(8,128)(2,1)S(1)} all-to-all(bf16[8,16,256]{2,1,0:T(8,128)(2,1)S(1)} %columns.1), channel_id=1, replica_groups={{0,64,128,192,256,320,384,448},{8,72,136,200,264,328,392,456},{16,80,14..., dimensions={0} | all-to-all | bytes 131072 | tf_op jit(solution)/shard_map/all_to_all | solution.py:487
  85.0 0.8 total.1
  85.8 12.8 %all_to_all.33.refs_1_ = f32[8,8,128]{2,1,0:T(8,128)S(1)} all-to-all(f32[8,8,128]{2,1,0:T(8,128)S(1)} %get-tuple-element.45), channel_id=1, replica_groups=mesh['seq'=64,'head'=8] {'head'}, dimensions={0} | all-to-all | bytes 65536 | tf_op jit(solution)/shard_map/all_to_all | solution.py:487
  98.7 1.1 %finish.1 = (bf16[512,128]{1,0:T(8,128)(2,1)}, bf16[512,128]{1,0:T(8,128)(2,1)}, bf16[512,128]{1,0:T(8,128)(2,1)}) custom-call(f32[8,16,128]{2,1,0:T(8,128)S(1)} %all_to_all.30.refs_0_.sum_ref, f32[8,8,128]{2,1,0:T(8,128)S(1)} %all_to_all.33.refs_1_, bf16[512,128]{1,0:T(8,128)(2,1)S(1)} %copy-done.1, bf16[512,128]{1,0:T(8,128)(2,1)S(1)} %copy-done, ...), custom_call_target="tpu_custom_call" | custom-call | bytes 1409024 | tf_op jit(solution)/shard_map/finish/pallas_call | solution.py:466
  (1 shorter events, 0.0 us)
Async XLA Ops:
  0.6 17.5 %copy-start.2 = (bf16[512,128]{1,0:T(8,128)(2,1)S(1)}, bf16[512,128]{1,0:T(8,128)(2,1)}, u32[]{:S(2)}) copy-start(bf16[512,128]{1,0:T(8,128)(2,1)} %refs_2_.2) | copy-start | bytes 393220
  3.0 15.1 %copy-start = (bf16[512,128]{1,0:T(8,128)(2,1)S(1)}, bf16[512,128]{1,0:T(8,128)(2,1)}, u32[]{:S(2)}) copy-start(bf16[512,128]{1,0:T(8,128)(2,1)} %refs_3_.1) | copy-start | bytes 393220
  29.3 14.2 %copy-start.1 = (bf16[512,128]{1,0:T(8,128)(2,1)S(1)}, bf16[512,128]{1,0:T(8,128)(2,1)}, u32[]{:S(2)}) copy-start(bf16[512,128]{1,0:T(8,128)(2,1)} %refs_2_.3) | copy-start | bytes 393220
  29.3 14.1 %copy-start.3 = (bf16[512,128]{1,0:T(8,128)(2,1)S(1)}, bf16[512,128]{1,0:T(8,128)(2,1)}, u32[]{:S(2)}) copy-start(bf16[512,128]{1,0:T(8,128)(2,1)} %g_ref.3) | copy-start | bytes 393220
  29.3 23.4 %all-to-all-start.2 = ((bf16[8,112,256]{2,1,0:T(8,128)(2,1)}), bf16[8,112,256]{2,1,0:T(8,128)(2,1)S(1)}, u32[]{:S(2)}, u32[]{:S(2)}) async-start(bf16[8,112,256]{2,1,0:T(8,128)(2,1)} %rows.1), calls=%async_computation.2 | async-start | bytes 917504 | tf_op jit(solution)/shard_map/all_to_all | solution.py:487
  39.4 11.6 %collective-permute-start = (bf16[192,256]{1,0:T(8,128)(2,1)S(1)}, bf16[192,256]{1,0:T(8,128)(2,1)S(1)}, u32[]{:S(2)}, u32[]{:S(2)}) collective-permute-start(bf16[192,256]{1,0:T(8,128)(2,1)S(1)} %get-tuple-element.32), channel_id=1, source_target_pairs={{0,8},{8,0},{16,24},{24,16},{32,40},{40,32},{48,56},{56,48},{64,72... | collective-permute-start | bytes 294920 | tf_op jit(solution)/shard_map/ppermute | solution.py:519
  42.8 1.6 %collective-permute-start.1 = (bf16[128,256]{1,0:T(8,128)(2,1)S(1)}, bf16[128,256]{1,0:T(8,128)(2,1)S(1)}, u32[]{:S(2)}, u32[]{:S(2)}) collective-permute-start(bf16[128,256]{1,0:T(8,128)(2,1)S(1)} %get-tuple-element.33), channel_id=1, source_target_pairs={{8,16},{24,32},{40,48},{56,64},{72,80},{88,96},{104,112},{120,128}... | collective-permute-start | bytes 196616 | tf_op jit(solution)/shard_map/ppermute | solution.py:520
  56.4 17.8 %all-to-all-start.3 = ((bf16[8,112,256]{2,1,0:T(8,128)(2,1)}), bf16[8,112,256]{2,1,0:T(8,128)(2,1)S(1)}, u32[]{:S(2)}, u32[]{:S(2)}) async-start(bf16[8,112,256]{2,1,0:T(8,128)(2,1)} %get-tuple-element.43), calls=%async_computation.3 | async-start | bytes 917504 | tf_op jit(solution)/shard_map/all_to_all | solution.py:487
  61.5 10.2 %collective-permute-start.3 = (bf16[128,256]{1,0:T(8,128)(2,1)S(1)}, bf16[128,256]{1,0:T(8,128)(2,1)S(1)}, u32[]{:S(2)}, u32[]{:S(2)}) collective-permute-start(bf16[128,256]{1,0:T(8,128)(2,1)S(1)} %get-tuple-element.42), channel_id=1, source_target_pairs={{8,16},{24,32},{40,48},{56,64},{72,80},{88,96},{104,112},{120,128}... | collective-permute-start | bytes 196616 | tf_op jit(solution)/shard_map/ppermute | solution.py:561
  62.2 10.4 %collective-permute-start.2 = (bf16[192,256]{1,0:T(8,128)(2,1)S(1)}, bf16[192,256]{1,0:T(8,128)(2,1)S(1)}, u32[]{:S(2)}, u32[]{:S(2)}) collective-permute-start(bf16[192,256]{1,0:T(8,128)(2,1)S(1)} %get-tuple-element.41), channel_id=1, source_target_pairs={{0,8},{8,0},{16,24},{24,16},{32,40},{40,32},{48,56},{56,48},{64,72... | collective-permute-start | bytes 294920 | tf_op jit(solution)/shard_map/ppermute | solution.py:560

commit v11 on v10

--- a/solution.py
+++ b/solution.py
@@ -239,7 +239,7 @@
 def attend_kernel(
     qn_ref, g_ref, near_ref, p1_ref, p2_ref, z_ref,
     stat_ref, cross, halo, p1o_ref, p2o_ref, zo_ref,
-    q2_scr, g2_scr, weight_scr, pgrad_scr, low_scr, sgrad_scr, rims, mid_grad, far_scr, mid_scr, sems,
+    q2_scr, g2_scr, score_scr, weight_scr, pgrad_scr, low_scr, sgrad_scr, rims, mid_grad, far_scr, mid_scr, sems,
 ):
     index = lax.axis_index("seq")
     place = jnp.bitwise_and(index, 7)
@@ -268,15 +268,22 @@
         q2_scr[lanes] = q2
         g2_scr[lanes] = g2
         side = 0 if b == 0 else 1
-        pieces = list(range(7 if b in HALO_PIECE else 6))
         stats = [(near_ref[b, 0:1], near_ref[b, 1:2], near_ref[b, 2:3])]
-        for i in pieces:
-            kv = cross[i * LEAF : (i + 1) * LEAF] if i < 6 else halo[side]
-            weight, pgrad, (top, total, mixed) = weigh(kv, q2, g2)
-            weight_scr[b, i] = weight
-            pgrad_scr[b, i] = pgrad
-            bias = (i + 2) * LN2 if i < 6 else outside[b]
-            stats.append((top + bias, total, mixed))
+        score_scr[...] = dot(cross[:, :FEAT], q2, (1, 1))
+        pgrad_scr[b, : 6 * LEAF] = dot(cross[:, FEAT:], g2, (1, 1))
+        for i in range(6):
+            rows = slice(i * LEAF, (i + 1) * LEAF)
+            score = score_scr[rows]
+            top = peak(score)
+            weight = jnp.exp(score - top)
+            weight_scr[b, rows] = weight
+            mixed = add_up(weight * pgrad_scr[b, rows])
+            stats.append((top + (i + 2) * LN2, add_up(weight), mixed))
+        if b in HALO_PIECE:
+            weight, pgrad, (top, total, mixed) = weigh(halo[side], q2, g2)
+            weight_scr[b, 6 * LEAF :] = weight
+            pgrad_scr[b, 6 * LEAF :] = pgrad
+            stats.append((top + outside[b], total, mixed))
         top, total, mixed, factors = combine(stats)
         inverse = 1.0 / total
         delta = mixed * inverse
@@ -284,11 +291,10 @@
             [top, inverse, delta, jnp.zeros((5, 2 * LEAF), F32)], axis=0
         )
         for i in range(6):
-            prob = weight_scr[b, i] * (factors[i + 1] * inverse)
-            low_scr[i * LEAF : (i + 1) * LEAF, lanes] = prob.astype(BF16)
-            sgrad_scr[i * LEAF : (i + 1) * LEAF, lanes] = (
-                prob * (pgrad_scr[b, i] - delta)
-            ).astype(BF16)
+            rows = slice(i * LEAF, (i + 1) * LEAF)
+            prob = weight_scr[b, rows] * (factors[i + 1] * inverse)
+            low_scr[rows, lanes] = prob.astype(BF16)
+            sgrad_scr[rows, lanes] = (prob * (pgrad_scr[b, rows] - delta)).astype(BF16)
         if b in HALO_PIECE:
             rim_rows.append((b, side, lanes, factors[7] * inverse, delta))
 
@@ -297,10 +303,11 @@
         values = dot(low_scr[rows], g2_scr[...], (1, 0))
         return jnp.concatenate([keys, values], axis=1).astype(BF16)
 
+    far = grads(slice(384, 768))
     for j in range(3):
-        far = grads(slice(384 + LEAF * j, 384 + LEAF * (j + 1)))
         for s in range(8):
-            far_scr[s, 16 * j : 16 * (j + 1)] = far[16 * s : 16 * (s + 1)]
+            at = LEAF * j + 16 * s
+            far_scr[s, 16 * j : 16 * (j + 1)] = far[at : at + 16]
     copies = start_all(
         [
             pltpu.make_async_copy(far_scr.at[s], zo_ref.at[s, pl.ds(0, FAR)], sems.at[s])
@@ -325,8 +332,8 @@
         ]
     )
     for b, side, lanes, factor, delta in rim_rows:
-        prob = weight_scr[b, 6] * factor
-        sgrad = (prob * (pgrad_scr[b, 6] - delta)).astype(BF16)
+        prob = weight_scr[b, 6 * LEAF :] * factor
+        sgrad = (prob * (pgrad_scr[b, 6 * LEAF :] - delta)).astype(BF16)
         rims[side, :, :FEAT] = dot(sgrad, q2_scr[lanes], (1, 0)).astype(BF16)
         rims[side, :, FEAT:] = dot(prob.astype(BF16), g2_scr[lanes], (1, 0)).astype(BF16)
     p1o_ref[:LEAF] = rims[peer_side]
@@ -543,8 +550,9 @@
         scratch=[
             pltpu.VMEM((1024, FEAT), BF16),
             pltpu.VMEM((1024, FEAT), BF16),
-            pltpu.VMEM((LEAVES, 7, LEAF, 256), F32),
-            pltpu.VMEM((LEAVES, 7, LEAF, 256), F32),
+            pltpu.VMEM((768, 256), F32),
+            pltpu.VMEM((LEAVES, 7 * LEAF, 256), F32),
+            pltpu.VMEM((LEAVES, 7 * LEAF, 256), F32),
             pltpu.VMEM((768, 1024), BF16),
             pltpu.VMEM((768, 1024), BF16),
             pltpu.VMEM((2, LEAF, 256), BF16),

time: 100 us -> 99.9 us (level)
  no operation moved by 1% of the time
where the time goes in v11:
time: 99.9 us; the launch traced here: 99.4 us
  blocking collectives  48.2 us (48%)
  starting transfers between devices  25.7 us (26%)
  Pallas kernels  13.9 us (14%)
  waiting for transfers between devices  10.7 us (11%)
    all_to_all x4, blocking collectives, exchange(): return lax.all_to_all(x, axis, 0, 0, axis_index_groups=groups, tiled=True)  48.2 us
    all_to_all x2, starting transfers between devices, exchange(): return lax.all_to_all(x, axis, 0, 0, axis_index_groups=groups, tiled=True)  15.2 us
    pallas_call x9, Pallas kernels, call(): pl.pallas_call(kernel, out_shape=outs, in_specs=[pl.BlockSpec(memory_spac...  13.9 us
    ppermute x2, starting transfers between devices, local(): p1 = lax.ppermute(p1, 'seq', peer)  9.15 us
    ppermute x2, waiting for transfers between devices, local(): p1 = lax.ppermute(p1, 'seq', peer)  7.46 us
    all_to_all x2, waiting for transfers between devices, exchange(): return lax.all_to_all(x, axis, 0, 0, axis_index_groups=groups, tiled=True)  3.28 us
  transfers between devices with their start and end apart: 6, of which 4 were waited for; matrix products, arithmetic and copies ran while one was open for 0% of the time, Pallas kernels for 5%

profile of v11, /device:TPU:1, one launch (start us, length us, event | category | flops | bytes accessed | tf_op | source)
XLA Modules:
  0.0 99.4 jit_solution(11787719871584115137)
XLA Ops:
  0.6 0.0 copy-start.2
  0.6 2.4 %squares.1 = f32[8,16,128]{2,1,0:T(8,128)} custom-call(bf16[512,128]{1,0:T(8,128)(2,1)} %refs_2_.3, bf16[512,128]{1,0:T(8,128)(2,1)} %refs_3_.1, f32[1,128]{1,0:T(1,128)} %bitcast.2, f32[1,128]{1,0:T(1,128)} %bitcast.3), custom_call_target="tpu_custom_call" | custom-call | bytes 328704 | tf_op jit(solution)/shard_map/squares/pallas_call | solution.py:473
  3.0 0.0 copy-start
  3.1 15.1 %all_to_all.30.refs_0_.sum_ref = f32[8,16,128]{2,1,0:T(8,128)S(1)} all-to-all(f32[8,16,128]{2,1,0:T(8,128)} %squares.1), channel_id=1, replica_groups=mesh['seq'=64,'head'=8] {'head'}, dimensions={0} | all-to-all | bytes 131072 | tf_op jit(solution)/shard_map/all_to_all | solution.py:494
  18.2 0.0 copy-done.2
  18.2 0.0 copy-done
  18.2 0.5 norm.1
  18.7 9.6 %all_to_all.31.y_ref = bf16[8,16,256]{2,1,0:T(8,128)(2,1)S(1)} all-to-all(bf16[8,16,256]{2,1,0:T(8,128)(2,1)S(1)} %get-tuple-element.34), channel_id=1, replica_groups={{0,64,128,192,256,320,384,448},{8,72,136,200,264,328,392,456},{16,80,14..., dimensions={0} | all-to-all | bytes 131072 | tf_op jit(solution)/shard_map/all_to_all | solution.py:494
  28.3 1.0 rows.1
  29.3 0.0 copy-start.1
  29.3 0.0 copy-start.3
  29.3 10.1 %all-to-all-start.2 = ((bf16[8,112,256]{2,1,0:T(8,128)(2,1)}), bf16[8,112,256]{2,1,0:T(8,128)(2,1)S(1)}, u32[]{:S(2)}, u32[]{:S(2)}) async-start(bf16[8,112,256]{2,1,0:T(8,128)(2,1)} %rows.1), calls=%async_computation.2 | async-start | bytes 917504 | tf_op jit(solution)/shard_map/all_to_all | solution.py:494
  39.4 3.4 %collective-permute-start = (bf16[192,256]{1,0:T(8,128)(2,1)S(1)}, bf16[192,256]{1,0:T(8,128)(2,1)S(1)}, u32[]{:S(2)}, u32[]{:S(2)}) collective-permute-start(bf16[192,256]{1,0:T(8,128)(2,1)S(1)} %get-tuple-element.32), channel_id=1, source_target_pairs={{0,8},{8,0},{16,24},{24,16},{32,40},{40,32},{48,56},{56,48},{64,72... | collective-permute-start | bytes 294920 | tf_op jit(solution)/shard_map/ppermute | solution.py:526
  42.8 0.7 collective-permute-start.1
  43.4 0.0 copy-done.1
  43.5 0.9 near.1
  44.4 0.0 collective-permute-done.1.p2_ref
  44.4 6.6 %collective-permute-done.p1_ref = bf16[192,256]{1,0:T(8,128)(2,1)S(1)} collective-permute-done((bf16[192,256]{1,0:T(8,128)(2,1)S(1)}, bf16[192,256]{1,0:T(8,128)(2,1)S(1)}, u32[]{:S(2)}, u32[]{:S(2)}) %collective-permute-start) | collective-permute-done | bytes 98336 | tf_op jit(solution)/shard_map/ppermute | solution.py:526
  51.0 1.7 %all-to-all-done.2.z_ref = bf16[8,112,256]{2,1,0:T(8,128)(2,1)S(1)} async-done(((bf16[8,112,256]{2,1,0:T(8,128)(2,1)}), bf16[8,112,256]{2,1,0:T(8,128)(2,1)S(1)}, u32[]{:S(2)}, u32[]{:S(2)}) %all-to-all-start.2) | async-done | bytes 458784 | tf_op jit(solution)/shard_map/all_to_all | solution.py:494
  52.7 3.3 %attend.1 = (f32[4,8,256]{2,1,0:T(8,128)S(1)}, bf16[768,256]{1,0:T(8,128)(2,1)S(1)}, bf16[2,128,256]{2,1,0:T(8,128)(2,1)S(1)}, bf16[192,256]{1,0:T(8,128)(2,1)S(...) custom-call(bf16[512,128]{1,0:T(8,128)(2,1)S(1)} %get-tuple-element.30.qn_ref, ...), custom_call_target="tpu_custom_call" | custom-call | flops 805306368 | bytes 2097152 | tf_op jit(solution)/shard_map/attend/pallas_call | solution.py:473
  56.0 5.2 %all-to-all-start.3 = ((bf16[8,112,256]{2,1,0:T(8,128)(2,1)}), bf16[8,112,256]{2,1,0:T(8,128)(2,1)S(1)}, u32[]{:S(2)}, u32[]{:S(2)}) async-start(bf16[8,112,256]{2,1,0:T(8,128)(2,1)} %get-tuple-element.43), calls=%async_computation.3 | async-start | bytes 917504 | tf_op jit(solution)/shard_map/all_to_all | solution.py:494
  61.1 0.7 collective-permute-start.3
  61.8 5.8 %collective-permute-start.2 = (bf16[192,256]{1,0:T(8,128)(2,1)S(1)}, bf16[192,256]{1,0:T(8,128)(2,1)S(1)}, u32[]{:S(2)}, u32[]{:S(2)}) collective-permute-start(bf16[192,256]{1,0:T(8,128)(2,1)S(1)} %get-tuple-element.41), channel_id=1, source_target_pairs={{0,8},{8,0},{16,24},{24,16},{32,40},{40,32},{48,56},{56,48},{64,72... | collective-permute-start | bytes 294920 | tf_op jit(solution)/shard_map/ppermute | solution.py:568
  67.6 3.7 %after.1 = (bf16[512,128]{1,0:T(8,128)(2,1)}, f32[512,128]{1,0:T(8,128)S(1)}, f32[512,256]{1,0:T(8,128)S(1)}, f32[8,128]{1,0:T(8,128)S(1)}) custom-call(f32[4,8,256]{2,1,0:T(8,128)S(1)} %get-tuple-element.36.stat_ref, bf16[512,128]{1,0:T(8,128)(2,1)S(1)} %get-tuple-element.30.qn_ref, bf16[512,256]{1,0:T(8,128)(2,1)S(1)} %get-tuple-element.28.refs_2_.kv_ref, ...), custom_call_target="tpu_custom_call" | custom-call | flops 1677721600 | bytes 2330624 | tf_op jit(solution)/shard_map/after/pallas_call | solution.py:473
  71.3 0.0 collective-permute-done.3.p2_ref
  71.3 0.8 collective-permute-done.2.p1_ref
  72.2 1.6 %all-to-all-done.3.z_ref = bf16[8,112,256]{2,1,0:T(8,128)(2,1)S(1)} async-done(((bf16[8,112,256]{2,1,0:T(8,128)(2,1)}), bf16[8,112,256]{2,1,0:T(8,128)(2,1)S(1)}, u32[]{:S(2)}, u32[]{:S(2)}) %all-to-all-start.3) | async-done | bytes 458784 | tf_op jit(solution)/shard_map/all_to_all | solution.py:494
  73.8 0.2 columns.1
  74.0 10.6 %all_to_all.32.y_ref = bf16[8,16,256]{2,1,0:T(8,128)(2,1)S(1)} all-to-all(bf16[8,16,256]{2,1,0:T(8,128)(2,1)S(1)} %columns.1), channel_id=1, replica_groups={{0,64,128,192,256,320,384,448},{8,72,136,200,264,328,392,456},{16,80,14..., dimensions={0} | all-to-all | bytes 131072 | tf_op jit(solution)/shard_map/all_to_all | solution.py:494
  84.6 0.8 total.1
  85.4 12.8 %all_to_all.33.refs_1_ = f32[8,8,128]{2,1,0:T(8,128)S(1)} all-to-all(f32[8,8,128]{2,1,0:T(8,128)S(1)} %get-tuple-element.45), channel_id=1, replica_groups=mesh['seq'=64,'head'=8] {'head'}, dimensions={0} | all-to-all | bytes 65536 | tf_op jit(solution)/shard_map/all_to_all | solution.py:494
  98.3 1.1 %finish.1 = (bf16[512,128]{1,0:T(8,128)(2,1)}, bf16[512,128]{1,0:T(8,128)(2,1)}, bf16[512,128]{1,0:T(8,128)(2,1)}) custom-call(f32[8,16,128]{2,1,0:T(8,128)S(1)} %all_to_all.30.refs_0_.sum_ref, f32[8,8,128]{2,1,0:T(8,128)S(1)} %all_to_all.33.refs_1_, bf16[512,128]{1,0:T(8,128)(2,1)S(1)} %copy-done.1, bf16[512,128]{1,0:T(8,128)(2,1)S(1)} %copy-done, ...), custom_call_target="tpu_custom_call" | custom-call | bytes 1409024 | tf_op jit(solution)/shard_map/finish/pallas_call | solution.py:473
  (1 shorter events, 0.0 us)
Async XLA Ops:
  0.6 17.5 %copy-start.2 = (bf16[512,128]{1,0:T(8,128)(2,1)S(1)}, bf16[512,128]{1,0:T(8,128)(2,1)}, u32[]{:S(2)}) copy-start(bf16[512,128]{1,0:T(8,128)(2,1)} %refs_2_.2) | copy-start | bytes 393220
  3.0 15.1 %copy-start = (bf16[512,128]{1,0:T(8,128)(2,1)S(1)}, bf16[512,128]{1,0:T(8,128)(2,1)}, u32[]{:S(2)}) copy-start(bf16[512,128]{1,0:T(8,128)(2,1)} %refs_3_.1) | copy-start | bytes 393220
  29.3 14.2 %copy-start.1 = (bf16[512,128]{1,0:T(8,128)(2,1)S(1)}, bf16[512,128]{1,0:T(8,128)(2,1)}, u32[]{:S(2)}) copy-start(bf16[512,128]{1,0:T(8,128)(2,1)} %refs_2_.3) | copy-start | bytes 393220
  29.3 14.1 %copy-start.3 = (bf16[512,128]{1,0:T(8,128)(2,1)S(1)}, bf16[512,128]{1,0:T(8,128)(2,1)}, u32[]{:S(2)}) copy-start(bf16[512,128]{1,0:T(8,128)(2,1)} %g_ref.3) | copy-start | bytes 393220
  29.3 23.4 %all-to-all-start.2 = ((bf16[8,112,256]{2,1,0:T(8,128)(2,1)}), bf16[8,112,256]{2,1,0:T(8,128)(2,1)S(1)}, u32[]{:S(2)}, u32[]{:S(2)}) async-start(bf16[8,112,256]{2,1,0:T(8,128)(2,1)} %rows.1), calls=%async_computation.2 | async-start | bytes 917504 | tf_op jit(solution)/shard_map/all_to_all | solution.py:494
  39.4 11.6 %collective-permute-start = (bf16[192,256]{1,0:T(8,128)(2,1)S(1)}, bf16[192,256]{1,0:T(8,128)(2,1)S(1)}, u32[]{:S(2)}, u32[]{:S(2)}) collective-permute-start(bf16[192,256]{1,0:T(8,128)(2,1)S(1)} %get-tuple-element.32), channel_id=1, source_target_pairs={{0,8},{8,0},{16,24},{24,16},{32,40},{40,32},{48,56},{56,48},{64,72... | collective-permute-start | bytes 294920 | tf_op jit(solution)/shard_map/ppermute | solution.py:526
  42.8 1.6 %collective-permute-start.1 = (bf16[128,256]{1,0:T(8,128)(2,1)S(1)}, bf16[128,256]{1,0:T(8,128)(2,1)S(1)}, u32[]{:S(2)}, u32[]{:S(2)}) collective-permute-start(bf16[128,256]{1,0:T(8,128)(2,1)S(1)} %get-tuple-element.33), channel_id=1, source_target_pairs={{8,16},{24,32},{40,48},{56,64},{72,80},{88,96},{104,112},{120,128}... | collective-permute-start | bytes 196616 | tf_op jit(solution)/shard_map/ppermute | solution.py:527
  56.0 17.8 %all-to-all-start.3 = ((bf16[8,112,256]{2,1,0:T(8,128)(2,1)}), bf16[8,112,256]{2,1,0:T(8,128)(2,1)S(1)}, u32[]{:S(2)}, u32[]{:S(2)}) async-start(bf16[8,112,256]{2,1,0:T(8,128)(2,1)} %get-tuple-element.43), calls=%async_computation.3 | async-start | bytes 917504 | tf_op jit(solution)/shard_map/all_to_all | solution.py:494
  61.1 10.2 %collective-permute-start.3 = (bf16[128,256]{1,0:T(8,128)(2,1)S(1)}, bf16[128,256]{1,0:T(8,128)(2,1)S(1)}, u32[]{:S(2)}, u32[]{:S(2)}) collective-permute-start(bf16[128,256]{1,0:T(8,128)(2,1)S(1)} %get-tuple-element.42), channel_id=1, source_target_pairs={{8,16},{24,32},{40,48},{56,64},{72,80},{88,96},{104,112},{120,128}... | collective-permute-start | bytes 196616 | tf_op jit(solution)/shard_map/ppermute | solution.py:569
  61.8 10.4 %collective-permute-start.2 = (bf16[192,256]{1,0:T(8,128)(2,1)S(1)}, bf16[192,256]{1,0:T(8,128)(2,1)S(1)}, u32[]{:S(2)}, u32[]{:S(2)}) collective-permute-start(bf16[192,256]{1,0:T(8,128)(2,1)S(1)} %get-tuple-element.41), channel_id=1, source_target_pairs={{0,8},{8,0},{16,24},{24,16},{32,40},{40,32},{48,56},{56,48},{64,72... | collective-permute-start | bytes 294920 | tf_op jit(solution)/shard_map/ppermute | solution.py:568

commit v12 on v11

--- a/solution.py
+++ b/solution.py
@@ -17,7 +17,6 @@
 LN2 = math.log(2.0)
 F32 = jnp.float32
 BF16 = jnp.bfloat16
-BLOCKS = [pl.ds(i * LEAF, LEAF) for i in range(LEAVES)]
 ROW_LEVEL = {1: 2, 2: 3, 3: 3, 4: 4, 5: 4, 6: 4, 7: 4}
 COLUMN_LEVEL = {1: 5, 2: 6, 3: 6, 4: 7, 5: 7, 6: 7, 7: 7}
 FAR = 48
@@ -78,20 +77,20 @@
 
 
 def squares_kernel(q_in, k_in, qg_in, kg_in, out_ref, rows, gains, sems):
-    copies = []
-    for i in range(2 * LEAVES):
-        source = (q_in if i < LEAVES else k_in).at[pl.ds((i % LEAVES) * LEAF, LEAF)]
-        copies.append(pltpu.make_async_copy(source, rows.at[i], sems.at[i]))
-    for i, source in enumerate((qg_in, kg_in)):
-        copies.append(pltpu.make_async_copy(source, gains.at[i], sems.at[2 * LEAVES + i]))
+    copies = [
+        pltpu.make_async_copy(source, target, sems.at[i])
+        for i, (source, target) in enumerate(
+            ((q_in, rows.at[0]), (k_in, rows.at[1]), (qg_in, gains.at[0]), (kg_in, gains.at[1]))
+        )
+    ]
     for copy in copies:
         copy.start()
     sums = []
-    for i in range(2 * LEAVES):
+    for i in range(2):
         copies[i].wait()
         x = rows[i].astype(F32)
-        sums.append(jnp.sum((x * x).T, axis=0, keepdims=True))
-    for copy in copies[2 * LEAVES :]:
+        sums += token_sums(x * x)
+    for copy in copies[2:]:
         copy.wait()
     tile = jnp.concatenate(sums + [gains[0], gains[1], jnp.zeros((6, FEAT), F32)], axis=0)
     for i in range(out_ref.shape[0]):
@@ -138,24 +137,24 @@
         copy.wait()
 
 
-def row_kernel(y_ref, lv_ref, out_ref, far_scr, sems):
+def row_kernel(y_ref, lv_ref, out_ref, far_scr, mid_scr, sems):
     index = lax.axis_index("seq")
     column = jnp.right_shift(index, 3)
     place = jnp.bitwise_and(index, 7)
-    copies = []
+    mid_scr[place] = jnp.zeros((64, 2 * FEAT), BF16)
     for d in range(1, 8):
-        first, rows = {1: (0, 64), 2: (128, 64), 3: (128, 64)}.get(d, (192, 32))
-        target = out_ref.at[jnp.bitwise_xor(place, d), pl.ds(FAR, rows)]
-        copies.append(pltpu.make_async_copy(lv_ref.at[pl.ds(first, rows)], target, sems.at[d]))
-    start_all(copies)
+        other = jnp.bitwise_xor(place, d)
+        if d < 4:
+            mid_scr[other] = lv_ref[:64] if d == 1 else lv_ref[128:192]
+        else:
+            mid_scr[other, :32] = lv_ref[192:224]
+            mid_scr[other, 32:] = jnp.zeros((32, 2 * FEAT), BF16)
+    copies = start_all([pltpu.make_async_copy(mid_scr, out_ref.at[:, pl.ds(FAR, 64)], sems.at[0])])
     slots = jnp.concatenate([y_ref[jnp.bitwise_xor(column, d)] for d in range(1, 8)], axis=0)
-    far_scr[...] = dot(far_pick((FAR, 112), 0), slots, (1, 0)).astype(BF16)
-    copies += start_all(
-        [
-            pltpu.make_async_copy(far_scr, out_ref.at[s, pl.ds(0, FAR)], sems.at[8 + s])
-            for s in range(8)
-        ]
-    )
+    far = dot(far_pick((FAR, 112), 0), slots, (1, 0)).astype(BF16)
+    for s in range(8):
+        far_scr[s] = far
+    copies += start_all([pltpu.make_async_copy(far_scr, out_ref.at[:, pl.ds(0, FAR)], sems.at[1])])
     wait_all(copies)
 
 
@@ -308,29 +307,17 @@
         for s in range(8):
             at = LEAF * j + 16 * s
             far_scr[s, 16 * j : 16 * (j + 1)] = far[at : at + 16]
-    copies = start_all(
-        [
-            pltpu.make_async_copy(far_scr.at[s], zo_ref.at[s, pl.ds(0, FAR)], sems.at[s])
-            for s in range(8)
-        ]
-    )
+    copies = start_all([pltpu.make_async_copy(far_scr, zo_ref.at[:, pl.ds(0, FAR)], sems.at[0])])
     mid_grad[...] = grads(slice(0, 384))
-    mid_scr[...] = jnp.zeros_like(mid_scr)
-    mid_scr[1] = mid_grad[:64]
-    mid_scr[2] = mid_grad[128:192]
-    mid_scr[3] = mid_grad[192:256]
+    mid_scr[place] = jnp.zeros((64, 2 * FEAT), BF16)
+    mid_scr[jnp.bitwise_xor(place, 1)] = mid_grad[:64]
+    mid_scr[jnp.bitwise_xor(place, 2)] = mid_grad[128:192]
+    mid_scr[jnp.bitwise_xor(place, 3)] = mid_grad[192:256]
     for i in range(4):
-        mid_scr[4 + i, :32] = mid_grad[256 + 32 * i : 288 + 32 * i]
-    copies += start_all(
-        [
-            pltpu.make_async_copy(
-                mid_scr.at[d],
-                zo_ref.at[jnp.bitwise_xor(place, d), pl.ds(FAR, 64)],
-                sems.at[8 + d],
-            )
-            for d in range(8)
-        ]
-    )
+        other = jnp.bitwise_xor(place, 4 + i)
+        mid_scr[other, :32] = mid_grad[256 + 32 * i : 288 + 32 * i]
+        mid_scr[other, 32:] = jnp.zeros((32, 2 * FEAT), BF16)
+    copies += start_all([pltpu.make_async_copy(mid_scr, zo_ref.at[:, pl.ds(FAR, 64)], sems.at[1])])
     for b, side, lanes, factor, delta in rim_rows:
         prob = weight_scr[b, 6 * LEAF :] * factor
         sgrad = (prob * (pgrad_scr[b, 6 * LEAF :] - delta)).astype(BF16)
@@ -442,7 +429,7 @@
     width, sq_ref, inner_ref, q_ref, k_ref, nqg_ref, nkg_ref, value_ref,
     dq_ref, dk_ref, vg_ref, results, sems,
 ):
-    copies = start_all([pltpu.make_async_copy(value_ref, vg_ref, sems.at[2 * LEAVES])])
+    copies = start_all([pltpu.make_async_copy(value_ref, vg_ref, sems.at[2])])
     rate = rates(width, sq_ref)
     inner = jnp.sum(inner_ref[...], axis=0) / width
     cubed = rate * rate * rate * inner
@@ -454,14 +441,7 @@
             spread_tokens(rate, 4 * side) * gains[side : side + 1] * grad_ref[...]
             - x_ref[...].astype(F32) * spread_tokens(cubed, 4 * side)
         ).astype(BF16)
-        copies += start_all(
-            [
-                pltpu.make_async_copy(
-                    results.at[side, rows], out_ref.at[rows], sems.at[LEAVES * side + i]
-                )
-                for i, rows in enumerate(BLOCKS)
-            ]
-        )
+        copies += start_all([pltpu.make_async_copy(results.at[side], out_ref, sems.at[side])])
     wait_all(copies)
 
 
@@ -508,9 +488,9 @@
         sds(heads, 16, FEAT, dtype=F32),
         (queries, key_rows, qg, kg),
         scratch=[
-            pltpu.VMEM((2 * LEAVES, LEAF, FEAT), BF16),
+            pltpu.VMEM((2, ROWS, FEAT), BF16),
             pltpu.VMEM((2, 1, FEAT), F32),
-            pltpu.SemaphoreType.DMA((2 * LEAVES + 2,)),
+            pltpu.SemaphoreType.DMA((4,)),
         ],
         spaces=[pl.ANY] * 4,
         vmem=60,
@@ -530,7 +510,11 @@
         row_kernel,
         sds(8, SLOT, 256),
         (yrecv, lv),
-        scratch=[pltpu.VMEM((FAR, 256), BF16), pltpu.SemaphoreType.DMA((16,))],
+        scratch=[
+            pltpu.VMEM((8, FAR, 256), BF16),
+            pltpu.VMEM((8, 64, 256), BF16),
+            pltpu.SemaphoreType.DMA((2,)),
+        ],
         out_spaces=[pl.ANY],
         name="rows",
     )
@@ -559,7 +543,7 @@
             pltpu.VMEM((384, 256), BF16),
             pltpu.VMEM((8, FAR, 256), BF16),
             pltpu.VMEM((8, 64, 256), BF16),
-            pltpu.SemaphoreType.DMA((16,)),
+            pltpu.SemaphoreType.DMA((2,)),
         ],
         out_spaces=[pltpu.VMEM] * 5 + [pl.ANY],
         flops=4 * 4 * 2 * 256 * 768 * FEAT,
@@ -604,7 +588,7 @@
         lambda *refs: finish_kernel(width, *refs),
         [sds(ROWS, FEAT), sds(ROWS, FEAT), sds(ROWS, FEAT)],
         (squares, inner, queries, key_rows, nqg, nkg, value_grad),
-        scratch=[pltpu.VMEM((2, ROWS, FEAT), BF16), pltpu.SemaphoreType.DMA((2 * LEAVES + 1,))],
+        scratch=[pltpu.VMEM((2, ROWS, FEAT), BF16), pltpu.SemaphoreType.DMA((3,))],
         out_spaces=[pl.ANY] * 3,
         name="finish",
     )

time: 99.9 us -> 99.1 us (level)
  no operation moved by 1% of the time
where the time goes in v12:
time: 99.1 us; the launch traced here: 98.6 us
  blocking collectives  48.2 us (49%)
  starting transfers between devices  25.7 us (26%)
  Pallas kernels  13.1 us (13%)
  waiting for transfers between devices  10.7 us (11%)
    all_to_all x4, blocking collectives, exchange(): return lax.all_to_all(x, axis, 0, 0, axis_index_groups=groups, tiled=True)  48.2 us
    all_to_all x2, starting transfers between devices, exchange(): return lax.all_to_all(x, axis, 0, 0, axis_index_groups=groups, tiled=True)  15.2 us
    pallas_call x9, Pallas kernels, call(): pl.pallas_call(kernel, out_shape=outs, in_specs=[pl.BlockSpec(memory_spac...  13.1 us
    ppermute x2, starting transfers between devices, local(): p1 = lax.ppermute(p1, 'seq', peer)  9.15 us
    ppermute x2, waiting for transfers between devices, local(): p1 = lax.ppermute(p1, 'seq', peer)  7.46 us
    all_to_all x2, waiting for transfers between devices, exchange(): return lax.all_to_all(x, axis, 0, 0, axis_index_groups=groups, tiled=True)  3.28 us
  transfers between devices with their start and end apart: 6, of which 4 were waited for; matrix products, arithmetic and copies ran while one was open for 0% of the time, Pallas kernels for 5%

profile of v12, /device:TPU:1, one launch (start us, length us, event | category | flops | bytes accessed | tf_op | source)
XLA Modules:
  0.0 98.6 jit_solution(5428328076159049857)
XLA Ops:
  0.6 0.0 copy-start.2
  0.6 1.9 %squares.1 = f32[8,16,128]{2,1,0:T(8,128)} custom-call(bf16[512,128]{1,0:T(8,128)(2,1)} %refs_2_.3, bf16[512,128]{1,0:T(8,128)(2,1)} %refs_3_.1, f32[1,128]{1,0:T(1,128)} %bitcast.2, f32[1,128]{1,0:T(1,128)} %bitcast.3), custom_call_target="tpu_custom_call" | custom-call | bytes 328704 | tf_op jit(solution)/shard_map/squares/pallas_call | solution.py:453
  2.5 0.0 copy-start
  2.6 15.1 %all_to_all.30.refs_0_.sum_ref = f32[8,16,128]{2,1,0:T(8,128)S(1)} all-to-all(f32[8,16,128]{2,1,0:T(8,128)} %squares.1), channel_id=1, replica_groups=mesh['seq'=64,'head'=8] {'head'}, dimensions={0} | all-to-all | bytes 131072 | tf_op jit(solution)/shard_map/all_to_all | solution.py:474
  17.7 0.0 copy-done.2
  17.7 0.5 norm.1
  18.2 9.6 %all_to_all.31.y_ref = bf16[8,16,256]{2,1,0:T(8,128)(2,1)S(1)} all-to-all(bf16[8,16,256]{2,1,0:T(8,128)(2,1)S(1)} %get-tuple-element.34), channel_id=1, replica_groups={{0,64,128,192,256,320,384,448},{8,72,136,200,264,328,392,456},{16,80,14..., dimensions={0} | all-to-all | bytes 131072 | tf_op jit(solution)/shard_map/all_to_all | solution.py:474
  27.8 0.9 rows.1
  28.7 0.0 copy-start.1
  28.7 0.0 copy-start.3
  28.7 10.1 %all-to-all-start.2 = ((bf16[8,112,256]{2,1,0:T(8,128)(2,1)}), bf16[8,112,256]{2,1,0:T(8,128)(2,1)S(1)}, u32[]{:S(2)}, u32[]{:S(2)}) async-start(bf16[8,112,256]{2,1,0:T(8,128)(2,1)} %rows.1), calls=%async_computation.2 | async-start | bytes 917504 | tf_op jit(solution)/shard_map/all_to_all | solution.py:474
  38.8 3.4 %collective-permute-start = (bf16[192,256]{1,0:T(8,128)(2,1)S(1)}, bf16[192,256]{1,0:T(8,128)(2,1)S(1)}, u32[]{:S(2)}, u32[]{:S(2)}) collective-permute-start(bf16[192,256]{1,0:T(8,128)(2,1)S(1)} %get-tuple-element.32), channel_id=1, source_target_pairs={{0,8},{8,0},{16,24},{24,16},{32,40},{40,32},{48,56},{56,48},{64,72... | collective-permute-start | bytes 294920 | tf_op jit(solution)/shard_map/ppermute | solution.py:506
  42.2 0.7 collective-permute-start.1
  42.8 0.0 copy-done.1
  42.8 0.0 copy-done.3
  42.9 0.9 near.1
  43.8 0.0 collective-permute-done.1.p2_ref
  43.8 6.6 %collective-permute-done.p1_ref = bf16[192,256]{1,0:T(8,128)(2,1)S(1)} collective-permute-done((bf16[192,256]{1,0:T(8,128)(2,1)S(1)}, bf16[192,256]{1,0:T(8,128)(2,1)S(1)}, u32[]{:S(2)}, u32[]{:S(2)}) %collective-permute-start) | collective-permute-done | bytes 98336 | tf_op jit(solution)/shard_map/ppermute | solution.py:506
  50.4 1.7 %all-to-all-done.2.z_ref = bf16[8,112,256]{2,1,0:T(8,128)(2,1)S(1)} async-done(((bf16[8,112,256]{2,1,0:T(8,128)(2,1)}), bf16[8,112,256]{2,1,0:T(8,128)(2,1)S(1)}, u32[]{:S(2)}, u32[]{:S(2)}) %all-to-all-start.2) | async-done | bytes 458784 | tf_op jit(solution)/shard_map/all_to_all | solution.py:474
  52.1 3.1 %attend.1 = (f32[4,8,256]{2,1,0:T(8,128)S(1)}, bf16[768,256]{1,0:T(8,128)(2,1)S(1)}, bf16[2,128,256]{2,1,0:T(8,128)(2,1)S(1)}, bf16[192,256]{1,0:T(8,128)(2,1)S(...) custom-call(bf16[512,128]{1,0:T(8,128)(2,1)S(1)} %get-tuple-element.30.qn_ref, ...), custom_call_target="tpu_custom_call" | custom-call | flops 805306368 | bytes 2097152 | tf_op jit(solution)/shard_map/attend/pallas_call | solution.py:453
  55.2 5.2 %all-to-all-start.3 = ((bf16[8,112,256]{2,1,0:T(8,128)(2,1)}), bf16[8,112,256]{2,1,0:T(8,128)(2,1)S(1)}, u32[]{:S(2)}, u32[]{:S(2)}) async-start(bf16[8,112,256]{2,1,0:T(8,128)(2,1)} %get-tuple-element.43), calls=%async_computation.3 | async-start | bytes 917504 | tf_op jit(solution)/shard_map/all_to_all | solution.py:474
  60.4 0.7 collective-permute-start.3
  61.0 5.8 %collective-permute-start.2 = (bf16[192,256]{1,0:T(8,128)(2,1)S(1)}, bf16[192,256]{1,0:T(8,128)(2,1)S(1)}, u32[]{:S(2)}, u32[]{:S(2)}) collective-permute-start(bf16[192,256]{1,0:T(8,128)(2,1)S(1)} %get-tuple-element.41), channel_id=1, source_target_pairs={{0,8},{8,0},{16,24},{24,16},{32,40},{40,32},{48,56},{56,48},{64,72... | collective-permute-start | bytes 294920 | tf_op jit(solution)/shard_map/ppermute | solution.py:552
  66.8 3.7 %after.1 = (bf16[512,128]{1,0:T(8,128)(2,1)}, f32[512,128]{1,0:T(8,128)S(1)}, f32[512,256]{1,0:T(8,128)S(1)}, f32[8,128]{1,0:T(8,128)S(1)}) custom-call(f32[4,8,256]{2,1,0:T(8,128)S(1)} %get-tuple-element.36.stat_ref, bf16[512,128]{1,0:T(8,128)(2,1)S(1)} %get-tuple-element.30.qn_ref, bf16[512,256]{1,0:T(8,128)(2,1)S(1)} %get-tuple-element.28.refs_2_.kv_ref, ...), custom_call_target="tpu_custom_call" | custom-call | flops 1677721600 | bytes 2330624 | tf_op jit(solution)/shard_map/after/pallas_call | solution.py:453
  70.6 0.0 collective-permute-done.3.p2_ref
  70.6 0.8 collective-permute-done.2.p1_ref
  71.4 1.6 %all-to-all-done.3.z_ref = bf16[8,112,256]{2,1,0:T(8,128)(2,1)S(1)} async-done(((bf16[8,112,256]{2,1,0:T(8,128)(2,1)}), bf16[8,112,256]{2,1,0:T(8,128)(2,1)S(1)}, u32[]{:S(2)}, u32[]{:S(2)}) %all-to-all-start.3) | async-done | bytes 458784 | tf_op jit(solution)/shard_map/all_to_all | solution.py:474
  73.0 0.2 columns.1
  73.2 10.6 %all_to_all.32.y_ref = bf16[8,16,256]{2,1,0:T(8,128)(2,1)S(1)} all-to-all(bf16[8,16,256]{2,1,0:T(8,128)(2,1)S(1)} %columns.1), channel_id=1, replica_groups={{0,64,128,192,256,320,384,448},{8,72,136,200,264,328,392,456},{16,80,14..., dimensions={0} | all-to-all | bytes 131072 | tf_op jit(solution)/shard_map/all_to_all | solution.py:474
  83.9 0.8 total.1
  84.7 12.8 %all_to_all.33.refs_1_ = f32[8,8,128]{2,1,0:T(8,128)S(1)} all-to-all(f32[8,8,128]{2,1,0:T(8,128)S(1)} %get-tuple-element.45), channel_id=1, replica_groups=mesh['seq'=64,'head'=8] {'head'}, dimensions={0} | all-to-all | bytes 65536 | tf_op jit(solution)/shard_map/all_to_all | solution.py:474
  97.5 1.0 %finish.1 = (bf16[512,128]{1,0:T(8,128)(2,1)}, bf16[512,128]{1,0:T(8,128)(2,1)}, bf16[512,128]{1,0:T(8,128)(2,1)}) custom-call(f32[8,16,128]{2,1,0:T(8,128)S(1)} %all_to_all.30.refs_0_.sum_ref, f32[8,8,128]{2,1,0:T(8,128)S(1)} %all_to_all.33.refs_1_, bf16[512,128]{1,0:T(8,128)(2,1)S(1)} %copy-done.1, bf16[512,128]{1,0:T(8,128)(2,1)S(1)} %copy-done, ...), custom_call_target="tpu_custom_call" | custom-call | bytes 1409024 | tf_op jit(solution)/shard_map/finish/pallas_call | solution.py:453
  (1 shorter events, 0.0 us)
Async XLA Ops:
  0.6 17.1 %copy-start.2 = (bf16[512,128]{1,0:T(8,128)(2,1)S(1)}, bf16[512,128]{1,0:T(8,128)(2,1)}, u32[]{:S(2)}) copy-start(bf16[512,128]{1,0:T(8,128)(2,1)} %refs_2_.2) | copy-start | bytes 393220
  2.5 15.1 %copy-start = (bf16[512,128]{1,0:T(8,128)(2,1)S(1)}, bf16[512,128]{1,0:T(8,128)(2,1)}, u32[]{:S(2)}) copy-start(bf16[512,128]{1,0:T(8,128)(2,1)} %refs_3_.1) | copy-start | bytes 393220
  28.7 14.2 %copy-start.1 = (bf16[512,128]{1,0:T(8,128)(2,1)S(1)}, bf16[512,128]{1,0:T(8,128)(2,1)}, u32[]{:S(2)}) copy-start(bf16[512,128]{1,0:T(8,128)(2,1)} %refs_2_.3) | copy-start | bytes 393220
  28.7 14.1 %copy-start.3 = (bf16[512,128]{1,0:T(8,128)(2,1)S(1)}, bf16[512,128]{1,0:T(8,128)(2,1)}, u32[]{:S(2)}) copy-start(bf16[512,128]{1,0:T(8,128)(2,1)} %g_ref.3) | copy-start | bytes 393220
  28.7 23.4 %all-to-all-start.2 = ((bf16[8,112,256]{2,1,0:T(8,128)(2,1)}), bf16[8,112,256]{2,1,0:T(8,128)(2,1)S(1)}, u32[]{:S(2)}, u32[]{:S(2)}) async-start(bf16[8,112,256]{2,1,0:T(8,128)(2,1)} %rows.1), calls=%async_computation.2 | async-start | bytes 917504 | tf_op jit(solution)/shard_map/all_to_all | solution.py:474
  38.8 11.6 %collective-permute-start = (bf16[192,256]{1,0:T(8,128)(2,1)S(1)}, bf16[192,256]{1,0:T(8,128)(2,1)S(1)}, u32[]{:S(2)}, u32[]{:S(2)}) collective-permute-start(bf16[192,256]{1,0:T(8,128)(2,1)S(1)} %get-tuple-element.32), channel_id=1, source_target_pairs={{0,8},{8,0},{16,24},{24,16},{32,40},{40,32},{48,56},{56,48},{64,72... | collective-permute-start | bytes 294920 | tf_op jit(solution)/shard_map/ppermute | solution.py:506
  42.2 1.6 %collective-permute-start.1 = (bf16[128,256]{1,0:T(8,128)(2,1)S(1)}, bf16[128,256]{1,0:T(8,128)(2,1)S(1)}, u32[]{:S(2)}, u32[]{:S(2)}) collective-permute-start(bf16[128,256]{1,0:T(8,128)(2,1)S(1)} %get-tuple-element.33), channel_id=1, source_target_pairs={{8,16},{24,32},{40,48},{56,64},{72,80},{88,96},{104,112},{120,128}... | collective-permute-start | bytes 196616 | tf_op jit(solution)/shard_map/ppermute | solution.py:507
  55.2 17.8 %all-to-all-start.3 = ((bf16[8,112,256]{2,1,0:T(8,128)(2,1)}), bf16[8,112,256]{2,1,0:T(8,128)(2,1)S(1)}, u32[]{:S(2)}, u32[]{:S(2)}) async-start(bf16[8,112,256]{2,1,0:T(8,128)(2,1)} %get-tuple-element.43), calls=%async_computation.3 | async-start | bytes 917504 | tf_op jit(solution)/shard_map/all_to_all | solution.py:474
  60.4 10.2 %collective-permute-start.3 = (bf16[128,256]{1,0:T(8,128)(2,1)S(1)}, bf16[128,256]{1,0:T(8,128)(2,1)S(1)}, u32[]{:S(2)}, u32[]{:S(2)}) collective-permute-start(bf16[128,256]{1,0:T(8,128)(2,1)S(1)} %get-tuple-element.42), channel_id=1, source_target_pairs={{8,16},{24,32},{40,48},{56,64},{72,80},{88,96},{104,112},{120,128}... | collective-permute-start | bytes 196616 | tf_op jit(solution)/shard_map/ppermute | solution.py:553
  61.0 10.4 %collective-permute-start.2 = (bf16[192,256]{1,0:T(8,128)(2,1)S(1)}, bf16[192,256]{1,0:T(8,128)(2,1)S(1)}, u32[]{:S(2)}, u32[]{:S(2)}) collective-permute-start(bf16[192,256]{1,0:T(8,128)(2,1)S(1)} %get-tuple-element.41), channel_id=1, source_target_pairs={{0,8},{8,0},{16,24},{24,16},{32,40},{40,32},{48,56},{56,48},{64,72... | collective-permute-start | bytes 294920 | tf_op jit(solution)/shard_map/ppermute | solution.py:552

commit v13 on v12

--- a/solution.py
+++ b/solution.py
@@ -238,7 +238,8 @@
 def attend_kernel(
     qn_ref, g_ref, near_ref, p1_ref, p2_ref, z_ref,
     stat_ref, cross, halo, p1o_ref, p2o_ref, zo_ref,
-    q2_scr, g2_scr, score_scr, weight_scr, pgrad_scr, low_scr, sgrad_scr, rims, mid_grad, far_scr, mid_scr, sems,
+    q2_scr, g2_scr, score_scr, weight_scr, pgrad_scr, low_scr, sgrad_scr, half_scr, rims, mid_grad,
+    far_scr, mid_scr, sems,
 ):
     index = lax.axis_index("seq")
     place = jnp.bitwise_and(index, 7)
@@ -268,11 +269,11 @@
         g2_scr[lanes] = g2
         side = 0 if b == 0 else 1
         stats = [(near_ref[b, 0:1], near_ref[b, 1:2], near_ref[b, 2:3])]
-        score_scr[...] = dot(cross[:, :FEAT], q2, (1, 1))
+        score_scr[b] = dot(cross[:, :FEAT], q2, (1, 1))
         pgrad_scr[b, : 6 * LEAF] = dot(cross[:, FEAT:], g2, (1, 1))
         for i in range(6):
             rows = slice(i * LEAF, (i + 1) * LEAF)
-            score = score_scr[rows]
+            score = score_scr[b, rows]
             top = peak(score)
             weight = jnp.exp(score - top)
             weight_scr[b, rows] = weight
@@ -296,10 +297,13 @@
             sgrad_scr[rows, lanes] = (prob * (pgrad_scr[b, rows] - delta)).astype(BF16)
         if b in HALO_PIECE:
             rim_rows.append((b, side, lanes, factors[7] * inverse, delta))
+        if b == 1:
+            half_scr[:, :FEAT] = dot(sgrad_scr[:, :512], q2_scr[:512], (1, 0))
+            half_scr[:, FEAT:] = dot(low_scr[:, :512], g2_scr[:512], (1, 0))
 
     def grads(rows):
-        keys = dot(sgrad_scr[rows], q2_scr[...], (1, 0))
-        values = dot(low_scr[rows], g2_scr[...], (1, 0))
+        keys = half_scr[rows, :FEAT] + dot(sgrad_scr[rows, 512:], q2_scr[512:], (1, 0))
+        values = half_scr[rows, FEAT:] + dot(low_scr[rows, 512:], g2_scr[512:], (1, 0))
         return jnp.concatenate([keys, values], axis=1).astype(BF16)
 
     far = grads(slice(384, 768))
@@ -534,11 +538,12 @@
         scratch=[
             pltpu.VMEM((1024, FEAT), BF16),
             pltpu.VMEM((1024, FEAT), BF16),
-            pltpu.VMEM((768, 256), F32),
+            pltpu.VMEM((LEAVES, 768, 256), F32),
             pltpu.VMEM((LEAVES, 7 * LEAF, 256), F32),
             pltpu.VMEM((LEAVES, 7 * LEAF, 256), F32),
             pltpu.VMEM((768, 1024), BF16),
             pltpu.VMEM((768, 1024), BF16),
+            pltpu.VMEM((768, 256), F32),
             pltpu.VMEM((2, LEAF, 256), BF16),
             pltpu.VMEM((384, 256), BF16),
             pltpu.VMEM((8, FAR, 256), BF16),

time: 99.1 us -> 99.3 us (level)
  no operation moved by 1% of the time
where the time goes in v13:
time: 99.3 us; the launch traced here: 98.7 us
  blocking collectives  48.2 us (49%)
  starting transfers between devices  25.7 us (26%)
  Pallas kernels  13.3 us (13%)
  waiting for transfers between devices  10.7 us (11%)
    all_to_all x4, blocking collectives, exchange(): return lax.all_to_all(x, axis, 0, 0, axis_index_groups=groups, tiled=True)  48.2 us
    all_to_all x2, starting transfers between devices, exchange(): return lax.all_to_all(x, axis, 0, 0, axis_index_groups=groups, tiled=True)  15.2 us
    pallas_call x9, Pallas kernels, call(): pl.pallas_call(kernel, out_shape=outs, in_specs=[pl.BlockSpec(memory_spac...  13.3 us
    ppermute x2, starting transfers between devices, local(): p1 = lax.ppermute(p1, 'seq', peer)  9.15 us
    ppermute x2, waiting for transfers between devices, local(): p1 = lax.ppermute(p1, 'seq', peer)  7.46 us
    all_to_all x2, waiting for transfers between devices, exchange(): return lax.all_to_all(x, axis, 0, 0, axis_index_groups=groups, tiled=True)  3.28 us
  transfers between devices with their start and end apart: 6, of which 4 were waited for; matrix products, arithmetic and copies ran while one was open for 0% of the time, Pallas kernels for 5%

profile of v13, /device:TPU:1, one launch (start us, length us, event | category | flops | bytes accessed | tf_op | source)
XLA Modules:
  0.0 98.7 jit_solution(14461979238936745274)
XLA Ops:
  0.6 0.0 copy-start.2
  0.6 1.9 %squares.1 = f32[8,16,128]{2,1,0:T(8,128)} custom-call(bf16[512,128]{1,0:T(8,128)(2,1)} %refs_2_.3, bf16[512,128]{1,0:T(8,128)(2,1)} %refs_3_.1, f32[1,128]{1,0:T(1,128)} %bitcast.2, f32[1,128]{1,0:T(1,128)} %bitcast.3), custom_call_target="tpu_custom_call" | custom-call | bytes 328704 | tf_op jit(solution)/shard_map/squares/pallas_call | solution.py:457
  2.5 0.0 copy-start
  2.6 15.1 %all_to_all.30.refs_0_.sum_ref = f32[8,16,128]{2,1,0:T(8,128)S(1)} all-to-all(f32[8,16,128]{2,1,0:T(8,128)} %squares.1), channel_id=1, replica_groups=mesh['seq'=64,'head'=8] {'head'}, dimensions={0} | all-to-all | bytes 131072 | tf_op jit(solution)/shard_map/all_to_all | solution.py:478
  17.7 0.0 copy-done.2
  17.7 0.5 norm.1
  18.2 9.6 %all_to_all.31.y_ref = bf16[8,16,256]{2,1,0:T(8,128)(2,1)S(1)} all-to-all(bf16[8,16,256]{2,1,0:T(8,128)(2,1)S(1)} %get-tuple-element.34), channel_id=1, replica_groups={{0,64,128,192,256,320,384,448},{8,72,136,200,264,328,392,456},{16,80,14..., dimensions={0} | all-to-all | bytes 131072 | tf_op jit(solution)/shard_map/all_to_all | solution.py:478
  27.8 0.9 rows.1
  28.7 0.0 copy-start.1
  28.7 0.0 copy-start.3
  28.7 10.1 %all-to-all-start.2 = ((bf16[8,112,256]{2,1,0:T(8,128)(2,1)}), bf16[8,112,256]{2,1,0:T(8,128)(2,1)S(1)}, u32[]{:S(2)}, u32[]{:S(2)}) async-start(bf16[8,112,256]{2,1,0:T(8,128)(2,1)} %rows.1), calls=%async_computation.2 | async-start | bytes 917504 | tf_op jit(solution)/shard_map/all_to_all | solution.py:478
  38.8 3.4 %collective-permute-start = (bf16[192,256]{1,0:T(8,128)(2,1)S(1)}, bf16[192,256]{1,0:T(8,128)(2,1)S(1)}, u32[]{:S(2)}, u32[]{:S(2)}) collective-permute-start(bf16[192,256]{1,0:T(8,128)(2,1)S(1)} %get-tuple-element.32), channel_id=1, source_target_pairs={{0,8},{8,0},{16,24},{24,16},{32,40},{40,32},{48,56},{56,48},{64,72... | collective-permute-start | bytes 294920 | tf_op jit(solution)/shard_map/ppermute | solution.py:510
  42.2 0.7 collective-permute-start.1
  42.8 0.0 copy-done.1
  42.8 0.0 copy-done.3
  42.9 0.9 near.1
  43.8 0.0 collective-permute-done.1.p2_ref
  43.8 6.6 %collective-permute-done.p1_ref = bf16[192,256]{1,0:T(8,128)(2,1)S(1)} collective-permute-done((bf16[192,256]{1,0:T(8,128)(2,1)S(1)}, bf16[192,256]{1,0:T(8,128)(2,1)S(1)}, u32[]{:S(2)}, u32[]{:S(2)}) %collective-permute-start) | collective-permute-done | bytes 98336 | tf_op jit(solution)/shard_map/ppermute | solution.py:510
  50.4 1.7 %all-to-all-done.2.z_ref = bf16[8,112,256]{2,1,0:T(8,128)(2,1)S(1)} async-done(((bf16[8,112,256]{2,1,0:T(8,128)(2,1)}), bf16[8,112,256]{2,1,0:T(8,128)(2,1)S(1)}, u32[]{:S(2)}, u32[]{:S(2)}) %all-to-all-start.2) | async-done | bytes 458784 | tf_op jit(solution)/shard_map/all_to_all | solution.py:478
  52.1 3.3 %attend.1 = (f32[4,8,256]{2,1,0:T(8,128)S(1)}, bf16[768,256]{1,0:T(8,128)(2,1)S(1)}, bf16[2,128,256]{2,1,0:T(8,128)(2,1)S(1)}, bf16[192,256]{1,0:T(8,128)(2,1)S(...) custom-call(bf16[512,128]{1,0:T(8,128)(2,1)S(1)} %get-tuple-element.30.qn_ref, ...), custom_call_target="tpu_custom_call" | custom-call | flops 805306368 | bytes 2097152 | tf_op jit(solution)/shard_map/attend/pallas_call | solution.py:457
  55.4 5.2 %all-to-all-start.3 = ((bf16[8,112,256]{2,1,0:T(8,128)(2,1)}), bf16[8,112,256]{2,1,0:T(8,128)(2,1)S(1)}, u32[]{:S(2)}, u32[]{:S(2)}) async-start(bf16[8,112,256]{2,1,0:T(8,128)(2,1)} %get-tuple-element.43), calls=%async_computation.3 | async-start | bytes 917504 | tf_op jit(solution)/shard_map/all_to_all | solution.py:478
  60.6 0.7 collective-permute-start.3
  61.2 5.8 %collective-permute-start.2 = (bf16[192,256]{1,0:T(8,128)(2,1)S(1)}, bf16[192,256]{1,0:T(8,128)(2,1)S(1)}, u32[]{:S(2)}, u32[]{:S(2)}) collective-permute-start(bf16[192,256]{1,0:T(8,128)(2,1)S(1)} %get-tuple-element.41), channel_id=1, source_target_pairs={{0,8},{8,0},{16,24},{24,16},{32,40},{40,32},{48,56},{56,48},{64,72... | collective-permute-start | bytes 294920 | tf_op jit(solution)/shard_map/ppermute | solution.py:557
  67.0 3.7 %after.1 = (bf16[512,128]{1,0:T(8,128)(2,1)}, f32[512,128]{1,0:T(8,128)S(1)}, f32[512,256]{1,0:T(8,128)S(1)}, f32[8,128]{1,0:T(8,128)S(1)}) custom-call(f32[4,8,256]{2,1,0:T(8,128)S(1)} %get-tuple-element.36.stat_ref, bf16[512,128]{1,0:T(8,128)(2,1)S(1)} %get-tuple-element.30.qn_ref, bf16[512,256]{1,0:T(8,128)(2,1)S(1)} %get-tuple-element.28.refs_2_.kv_ref, ...), custom_call_target="tpu_custom_call" | custom-call | flops 1677721600 | bytes 2330624 | tf_op jit(solution)/shard_map/after/pallas_call | solution.py:457
  70.7 0.0 collective-permute-done.3.p2_ref
  70.8 0.8 collective-permute-done.2.p1_ref
  71.6 1.6 %all-to-all-done.3.z_ref = bf16[8,112,256]{2,1,0:T(8,128)(2,1)S(1)} async-done(((bf16[8,112,256]{2,1,0:T(8,128)(2,1)}), bf16[8,112,256]{2,1,0:T(8,128)(2,1)S(1)}, u32[]{:S(2)}, u32[]{:S(2)}) %all-to-all-start.3) | async-done | bytes 458784 | tf_op jit(solution)/shard_map/all_to_all | solution.py:478
  73.2 0.2 columns.1
  73.4 10.6 %all_to_all.32.y_ref = bf16[8,16,256]{2,1,0:T(8,128)(2,1)S(1)} all-to-all(bf16[8,16,256]{2,1,0:T(8,128)(2,1)S(1)} %columns.1), channel_id=1, replica_groups={{0,64,128,192,256,320,384,448},{8,72,136,200,264,328,392,456},{16,80,14..., dimensions={0} | all-to-all | bytes 131072 | tf_op jit(solution)/shard_map/all_to_all | solution.py:478
  84.0 0.8 total.1
  84.8 12.8 %all_to_all.33.refs_1_ = f32[8,8,128]{2,1,0:T(8,128)S(1)} all-to-all(f32[8,8,128]{2,1,0:T(8,128)S(1)} %get-tuple-element.45), channel_id=1, replica_groups=mesh['seq'=64,'head'=8] {'head'}, dimensions={0} | all-to-all | bytes 65536 | tf_op jit(solution)/shard_map/all_to_all | solution.py:478
  97.7 1.0 %finish.1 = (bf16[512,128]{1,0:T(8,128)(2,1)}, bf16[512,128]{1,0:T(8,128)(2,1)}, bf16[512,128]{1,0:T(8,128)(2,1)}) custom-call(f32[8,16,128]{2,1,0:T(8,128)S(1)} %all_to_all.30.refs_0_.sum_ref, f32[8,8,128]{2,1,0:T(8,128)S(1)} %all_to_all.33.refs_1_, bf16[512,128]{1,0:T(8,128)(2,1)S(1)} %copy-done.1, bf16[512,128]{1,0:T(8,128)(2,1)S(1)} %copy-done, ...), custom_call_target="tpu_custom_call" | custom-call | bytes 1409024 | tf_op jit(solution)/shard_map/finish/pallas_call | solution.py:457
  (1 shorter events, 0.0 us)
Async XLA Ops:
  0.6 17.1 %copy-start.2 = (bf16[512,128]{1,0:T(8,128)(2,1)S(1)}, bf16[512,128]{1,0:T(8,128)(2,1)}, u32[]{:S(2)}) copy-start(bf16[512,128]{1,0:T(8,128)(2,1)} %refs_2_.2) | copy-start | bytes 393220
  2.5 15.1 %copy-start = (bf16[512,128]{1,0:T(8,128)(2,1)S(1)}, bf16[512,128]{1,0:T(8,128)(2,1)}, u32[]{:S(2)}) copy-start(bf16[512,128]{1,0:T(8,128)(2,1)} %refs_3_.1) | copy-start | bytes 393220
  28.7 14.2 %copy-start.1 = (bf16[512,128]{1,0:T(8,128)(2,1)S(1)}, bf16[512,128]{1,0:T(8,128)(2,1)}, u32[]{:S(2)}) copy-start(bf16[512,128]{1,0:T(8,128)(2,1)} %refs_2_.3) | copy-start | bytes 393220
  28.7 14.1 %copy-start.3 = (bf16[512,128]{1,0:T(8,128)(2,1)S(1)}, bf16[512,128]{1,0:T(8,128)(2,1)}, u32[]{:S(2)}) copy-start(bf16[512,128]{1,0:T(8,128)(2,1)} %g_ref.3) | copy-start | bytes 393220
  28.7 23.4 %all-to-all-start.2 = ((bf16[8,112,256]{2,1,0:T(8,128)(2,1)}), bf16[8,112,256]{2,1,0:T(8,128)(2,1)S(1)}, u32[]{:S(2)}, u32[]{:S(2)}) async-start(bf16[8,112,256]{2,1,0:T(8,128)(2,1)} %rows.1), calls=%async_computation.2 | async-start | bytes 917504 | tf_op jit(solution)/shard_map/all_to_all | solution.py:478
  38.8 11.6 %collective-permute-start = (bf16[192,256]{1,0:T(8,128)(2,1)S(1)}, bf16[192,256]{1,0:T(8,128)(2,1)S(1)}, u32[]{:S(2)}, u32[]{:S(2)}) collective-permute-start(bf16[192,256]{1,0:T(8,128)(2,1)S(1)} %get-tuple-element.32), channel_id=1, source_target_pairs={{0,8},{8,0},{16,24},{24,16},{32,40},{40,32},{48,56},{56,48},{64,72... | collective-permute-start | bytes 294920 | tf_op jit(solution)/shard_map/ppermute | solution.py:510
  42.2 1.6 %collective-permute-start.1 = (bf16[128,256]{1,0:T(8,128)(2,1)S(1)}, bf16[128,256]{1,0:T(8,128)(2,1)S(1)}, u32[]{:S(2)}, u32[]{:S(2)}) collective-permute-start(bf16[128,256]{1,0:T(8,128)(2,1)S(1)} %get-tuple-element.33), channel_id=1, source_target_pairs={{8,16},{24,32},{40,48},{56,64},{72,80},{88,96},{104,112},{120,128}... | collective-permute-start | bytes 196616 | tf_op jit(solution)/shard_map/ppermute | solution.py:511
  55.4 17.8 %all-to-all-start.3 = ((bf16[8,112,256]{2,1,0:T(8,128)(2,1)}), bf16[8,112,256]{2,1,0:T(8,128)(2,1)S(1)}, u32[]{:S(2)}, u32[]{:S(2)}) async-start(bf16[8,112,256]{2,1,0:T(8,128)(2,1)} %get-tuple-element.43), calls=%async_computation.3 | async-start | bytes 917504 | tf_op jit(solution)/shard_map/all_to_all | solution.py:478
  60.6 10.2 %collective-permute-start.3 = (bf16[128,256]{1,0:T(8,128)(2,1)S(1)}, bf16[128,256]{1,0:T(8,128)(2,1)S(1)}, u32[]{:S(2)}, u32[]{:S(2)}) collective-permute-start(bf16[128,256]{1,0:T(8,128)(2,1)S(1)} %get-tuple-element.42), channel_id=1, source_target_pairs={{8,16},{24,32},{40,48},{56,64},{72,80},{88,96},{104,112},{120,128}... | collective-permute-start | bytes 196616 | tf_op jit(solution)/shard_map/ppermute | solution.py:558
  61.2 10.4 %collective-permute-start.2 = (bf16[192,256]{1,0:T(8,128)(2,1)S(1)}, bf16[192,256]{1,0:T(8,128)(2,1)S(1)}, u32[]{:S(2)}, u32[]{:S(2)}) collective-permute-start(bf16[192,256]{1,0:T(8,128)(2,1)S(1)} %get-tuple-element.41), channel_id=1, source_target_pairs={{0,8},{8,0},{16,24},{24,16},{32,40},{40,32},{48,56},{56,48},{64,72... | collective-permute-start | bytes 294920 | tf_op jit(solution)/shard_map/ppermute | solution.py:557

commit v14 on v12

--- a/solution.py
+++ b/solution.py
@@ -31,15 +31,15 @@
     return lax.broadcasted_iota(jnp.int32, shape, axis)
 
 
-def pooling(rows, level):
-    token = iota((rows, ROWS), 1)
-    hit = jnp.right_shift(token, level) == iota((rows, ROWS), 0)
+def pooling(rows, level, tokens=ROWS):
+    token = iota((rows, tokens), 1)
+    hit = jnp.right_shift(token, level) == iota((rows, tokens), 0)
     return jnp.where(hit, 2.0**-level, 0.0)
 
 
-def spreading(first, rows, level):
-    token = iota((ROWS, rows), 0)
-    hit = jnp.right_shift(token, level) == iota((ROWS, rows), 1) + first
+def spreading(first, rows, level, tokens=ROWS):
+    token = iota((tokens, rows), 0)
+    hit = jnp.right_shift(token, level) == iota((tokens, rows), 1) + first
     return jnp.where(hit, 2.0**-level, 0.0)
 
 
@@ -122,7 +122,7 @@
     for d in range(1, 8):
         y_ref[jnp.bitwise_xor(column, d)] = coarse[464 + 16 * d : 480 + 16 * d]
     p1_ref[:LEAF] = kv_ref[pl.ds(pl.multiple_of((1 - odd) * 384, LEAF), LEAF)]
-    p1_ref[LEAF:] = coarse[320:384]
+    p1_ref[LEAF:] = lv_ref[pl.ds(pl.multiple_of(64 + 32 * odd, 32), 32)]
     p2_ref[...] = kv_ref[pl.ds(pl.multiple_of(odd * 384, LEAF), LEAF)]
 
 
@@ -141,11 +141,13 @@
     index = lax.axis_index("seq")
     column = jnp.right_shift(index, 3)
     place = jnp.bitwise_and(index, 7)
+    odd = jnp.bitwise_and(index, 1)
     mid_scr[place] = jnp.zeros((64, 2 * FEAT), BF16)
     for d in range(1, 8):
         other = jnp.bitwise_xor(place, d)
         if d < 4:
-            mid_scr[other] = lv_ref[:64] if d == 1 else lv_ref[128:192]
+            first = pl.multiple_of(32 * odd, 32) if d == 1 else 128
+            mid_scr[other] = lv_ref[pl.ds(first, 64)]
         else:
             mid_scr[other, :32] = lv_ref[192:224]
             mid_scr[other, 32:] = jnp.zeros((32, 2 * FEAT), BF16)
@@ -247,7 +249,8 @@
     halo[peer_side] = p1_ref[:LEAF]
     halo[odd] = p2_ref[...]
     cross[:64] = z_ref[jnp.bitwise_xor(place, 1), FAR:]
-    cross[64:128] = p1_ref[LEAF:]
+    cross[64:96] = p1_ref[LEAF:]
+    cross[96:128] = dot(pooling(32, 2, LEAF).astype(BF16), p1_ref[:LEAF], (1, 0)).astype(BF16)
     cross[128:192] = z_ref[jnp.bitwise_xor(place, 2), FAR:]
     cross[192:256] = z_ref[jnp.bitwise_xor(place, 3), FAR:]
     for i in range(4):
@@ -321,11 +324,12 @@
     for b, side, lanes, factor, delta in rim_rows:
         prob = weight_scr[b, 6 * LEAF :] * factor
         sgrad = (prob * (pgrad_scr[b, 6 * LEAF :] - delta)).astype(BF16)
-        rims[side, :, :FEAT] = dot(sgrad, q2_scr[lanes], (1, 0)).astype(BF16)
-        rims[side, :, FEAT:] = dot(prob.astype(BF16), g2_scr[lanes], (1, 0)).astype(BF16)
-    p1o_ref[:LEAF] = rims[peer_side]
-    p1o_ref[LEAF:] = mid_grad[64:128]
-    p2o_ref[...] = rims[odd]
+        rims[side, :, :FEAT] = dot(sgrad, q2_scr[lanes], (1, 0))
+        rims[side, :, FEAT:] = dot(prob.astype(BF16), g2_scr[lanes], (1, 0))
+    own_rows = dot(spreading(0, 32, 2, LEAF).astype(BF16), mid_grad[96:128], (1, 0))
+    p1o_ref[:LEAF] = (rims[peer_side] + own_rows).astype(BF16)
+    p1o_ref[LEAF:] = mid_grad[64:96]
+    p2o_ref[...] = rims[odd].astype(BF16)
     wait_all(copies)
 
 
@@ -404,7 +408,7 @@
     place = jnp.bitwise_and(index, 7)
     odd = jnp.bitwise_and(index, 1)
     pieces = [z_ref[jnp.bitwise_xor(place, 1), FAR:], p1_ref[LEAF:]]
-    maps = [spreading(0, 64, 2), spreading(64, 64, 2)]
+    maps = [spreading(32 * odd, 64, 2), spreading(64 + 32 * odd, 32, 2)]
     for d in range(2, 8):
         rows = ROWS >> ROW_LEVEL[d]
         pieces.append(z_ref[jnp.bitwise_xor(place, d), FAR : FAR + rows])
@@ -499,7 +503,7 @@
     squares = exchange(squares, "head")
     kv, one, lv, ysend, p1, p2 = call(
         lambda *refs: norm_kernel(width, *refs),
-        [sds(ROWS, 256), sds(256, 256), sds(224, 256), sds(8, 16, 256), sds(192, 256), sds(LEAF, 256)],
+        [sds(ROWS, 256), sds(256, 256), sds(224, 256), sds(8, 16, 256), sds(160, 256), sds(LEAF, 256)],
         (squares, key_rows, value_rows),
         name="norm",
     )
@@ -529,7 +533,7 @@
     stat, cross, halo, p1, p2, zsend = call(
         attend_kernel,
         [sds(LEAVES, 8, 256, dtype=F32), sds(768, 256), sds(2, LEAF, 256)]
-        + [sds(192, 256), sds(LEAF, 256), sds(8, SLOT, 256)],
+        + [sds(160, 256), sds(LEAF, 256), sds(8, SLOT, 256)],
         (qn, out_grad, near, p1, p2, zrecv),
         scratch=[
             pltpu.VMEM((1024, FEAT), BF16),
@@ -539,7 +543,7 @@
             pltpu.VMEM((LEAVES, 7 * LEAF, 256), F32),
             pltpu.VMEM((768, 1024), BF16),
             pltpu.VMEM((768, 1024), BF16),
-            pltpu.VMEM((2, LEAF, 256), BF16),
+            pltpu.VMEM((2, LEAF, 256), F32),
             pltpu.VMEM((384, 256), BF16),
             pltpu.VMEM((8, FAR, 256), BF16),
             pltpu.VMEM((8, 64, 256), BF16),

time: 99.1 us -> 99.6 us (level)
  blocking collectives: 48.2 us -> 47.1 us
    all_to_all x2, waiting for transfers between devices: 3.28 us -> 4.57 us  [exchange(): return lax.all_to_all(x, axis, 0, 0, axis_index_groups=groups, tiled=True)]
    all_to_all x4, blocking collectives: 48.2 us -> 47.1 us  [exchange(): return lax.all_to_all(x, axis, 0, 0, axis_index_groups=groups, tiled=True)]
where the time goes in v14:
time: 99.6 us; the launch traced here: 99.1 us
  blocking collectives  47.1 us (47%)
  starting transfers between devices  26.3 us (26%)
  Pallas kernels  13.4 us (13%)
  waiting for transfers between devices  11.5 us (12%)
    all_to_all x4, blocking collectives, exchange(): return lax.all_to_all(x, axis, 0, 0, axis_index_groups=groups, tiled=True)  47.1 us
    all_to_all x2, starting transfers between devices, exchange(): return lax.all_to_all(x, axis, 0, 0, axis_index_groups=groups, tiled=True)  15.8 us
    pallas_call x9, Pallas kernels, call(): pl.pallas_call(kernel, out_shape=outs, in_specs=[pl.BlockSpec(memory_spac...  13.4 us
    ppermute x2, starting transfers between devices, local(): p1 = lax.ppermute(p1, 'seq', peer)  9.15 us
    ppermute x2, waiting for transfers between devices, local(): p1 = lax.ppermute(p1, 'seq', peer)  6.95 us
    all_to_all x2, waiting for transfers between devices, exchange(): return lax.all_to_all(x, axis, 0, 0, axis_index_groups=groups, tiled=True)  4.57 us
  transfers between devices with their start and end apart: 6, of which 4 were waited for; matrix products, arithmetic and copies ran while one was open for 0% of the time, Pallas kernels for 5%

profile of v14, /device:TPU:1, one launch (start us, length us, event | category | flops | bytes accessed | tf_op | source)
XLA Modules:
  0.0 99.1 jit_solution(1223870848084657697)
XLA Ops:
  0.6 0.0 copy-start.2
  0.6 1.9 %squares.1 = f32[8,16,128]{2,1,0:T(8,128)} custom-call(bf16[512,128]{1,0:T(8,128)(2,1)} %refs_2_.3, bf16[512,128]{1,0:T(8,128)(2,1)} %refs_3_.1, f32[1,128]{1,0:T(1,128)} %bitcast.2, f32[1,128]{1,0:T(1,128)} %bitcast.3), custom_call_target="tpu_custom_call" | custom-call | bytes 328704 | tf_op jit(solution)/shard_map/squares/pallas_call | solution.py:457
  2.5 0.0 copy-start
  2.6 15.1 %all_to_all.30.refs_0_.sum_ref = f32[8,16,128]{2,1,0:T(8,128)S(1)} all-to-all(f32[8,16,128]{2,1,0:T(8,128)} %squares.1), channel_id=1, replica_groups=mesh['seq'=64,'head'=8] {'head'}, dimensions={0} | all-to-all | bytes 131072 | tf_op jit(solution)/shard_map/all_to_all | solution.py:478
  17.7 0.0 copy-done.2
  17.7 0.5 norm.1
  18.2 9.6 %all_to_all.31.y_ref = bf16[8,16,256]{2,1,0:T(8,128)(2,1)S(1)} all-to-all(bf16[8,16,256]{2,1,0:T(8,128)(2,1)S(1)} %get-tuple-element.34), channel_id=1, replica_groups={{0,64,128,192,256,320,384,448},{8,72,136,200,264,328,392,456},{16,80,14..., dimensions={0} | all-to-all | bytes 131072 | tf_op jit(solution)/shard_map/all_to_all | solution.py:478
  27.8 0.9 rows.1
  28.7 0.0 copy-start.1
  28.7 0.0 copy-start.3
  28.7 10.1 %all-to-all-start.2 = ((bf16[8,112,256]{2,1,0:T(8,128)(2,1)}), bf16[8,112,256]{2,1,0:T(8,128)(2,1)S(1)}, u32[]{:S(2)}, u32[]{:S(2)}) async-start(bf16[8,112,256]{2,1,0:T(8,128)(2,1)} %rows.1), calls=%async_computation.2 | async-start | bytes 917504 | tf_op jit(solution)/shard_map/all_to_all | solution.py:478
  38.8 3.4 %collective-permute-start = (bf16[160,256]{1,0:T(8,128)(2,1)S(1)}, bf16[160,256]{1,0:T(8,128)(2,1)S(1)}, u32[]{:S(2)}, u32[]{:S(2)}) collective-permute-start(bf16[160,256]{1,0:T(8,128)(2,1)S(1)} %get-tuple-element.32), channel_id=1, source_target_pairs={{0,8},{8,0},{16,24},{24,16},{32,40},{40,32},{48,56},{56,48},{64,72... | collective-permute-start | bytes 245768 | tf_op jit(solution)/shard_map/ppermute | solution.py:510
  42.2 0.7 collective-permute-start.1
  42.8 0.0 copy-done.1
  42.8 0.0 copy-done.3
  42.9 0.9 near.1
  43.8 0.0 collective-permute-done.1.p2_ref
  43.8 6.2 %collective-permute-done.p1_ref = bf16[160,256]{1,0:T(8,128)(2,1)S(1)} collective-permute-done((bf16[160,256]{1,0:T(8,128)(2,1)S(1)}, bf16[160,256]{1,0:T(8,128)(2,1)S(1)}, u32[]{:S(2)}, u32[]{:S(2)}) %collective-permute-start) | collective-permute-done | bytes 81952 | tf_op jit(solution)/shard_map/ppermute | solution.py:510
  50.0 2.1 %all-to-all-done.2.z_ref = bf16[8,112,256]{2,1,0:T(8,128)(2,1)S(1)} async-done(((bf16[8,112,256]{2,1,0:T(8,128)(2,1)}), bf16[8,112,256]{2,1,0:T(8,128)(2,1)S(1)}, u32[]{:S(2)}, u32[]{:S(2)}) %all-to-all-start.2) | async-done | bytes 458784 | tf_op jit(solution)/shard_map/all_to_all | solution.py:478
  52.1 3.4 %attend.1 = (f32[4,8,256]{2,1,0:T(8,128)S(1)}, bf16[768,256]{1,0:T(8,128)(2,1)S(1)}, bf16[2,128,256]{2,1,0:T(8,128)(2,1)S(1)}, bf16[160,256]{1,0:T(8,128)(2,1)S(...) custom-call(bf16[512,128]{1,0:T(8,128)(2,1)S(1)} %get-tuple-element.30.qn_ref, ...), custom_call_target="tpu_custom_call" | custom-call | flops 805306368 | bytes 2064384 | tf_op jit(solution)/shard_map/attend/pallas_call | solution.py:457
  55.5 5.7 %all-to-all-start.3 = ((bf16[8,112,256]{2,1,0:T(8,128)(2,1)}), bf16[8,112,256]{2,1,0:T(8,128)(2,1)S(1)}, u32[]{:S(2)}, u32[]{:S(2)}) async-start(bf16[8,112,256]{2,1,0:T(8,128)(2,1)} %get-tuple-element.43), calls=%async_computation.3 | async-start | bytes 917504 | tf_op jit(solution)/shard_map/all_to_all | solution.py:478
  61.2 0.7 collective-permute-start.3
  61.8 5.8 %collective-permute-start.2 = (bf16[160,256]{1,0:T(8,128)(2,1)S(1)}, bf16[160,256]{1,0:T(8,128)(2,1)S(1)}, u32[]{:S(2)}, u32[]{:S(2)}) collective-permute-start(bf16[160,256]{1,0:T(8,128)(2,1)S(1)} %get-tuple-element.41), channel_id=1, source_target_pairs={{0,8},{8,0},{16,24},{24,16},{32,40},{40,32},{48,56},{56,48},{64,72... | collective-permute-start | bytes 245768 | tf_op jit(solution)/shard_map/ppermute | solution.py:556
  67.6 3.7 %after.1 = (bf16[512,128]{1,0:T(8,128)(2,1)}, f32[512,128]{1,0:T(8,128)S(1)}, f32[512,256]{1,0:T(8,128)S(1)}, f32[8,128]{1,0:T(8,128)S(1)}) custom-call(f32[4,8,256]{2,1,0:T(8,128)S(1)} %get-tuple-element.36.stat_ref, bf16[512,128]{1,0:T(8,128)(2,1)S(1)} %get-tuple-element.30.qn_ref, bf16[512,256]{1,0:T(8,128)(2,1)S(1)} %get-tuple-element.28.refs_2_.kv_ref, ...), custom_call_target="tpu_custom_call" | custom-call | flops 1677721600 | bytes 2330624 | tf_op jit(solution)/shard_map/after/pallas_call | solution.py:457
  71.4 0.0 collective-permute-done.3.p2_ref
  71.4 0.8 collective-permute-done.2.p1_ref
  72.1 2.5 %all-to-all-done.3.z_ref = bf16[8,112,256]{2,1,0:T(8,128)(2,1)S(1)} async-done(((bf16[8,112,256]{2,1,0:T(8,128)(2,1)}), bf16[8,112,256]{2,1,0:T(8,128)(2,1)S(1)}, u32[]{:S(2)}, u32[]{:S(2)}) %all-to-all-start.3) | async-done | bytes 458784 | tf_op jit(solution)/shard_map/all_to_all | solution.py:478
  74.6 0.2 columns.1
  74.8 9.6 %all_to_all.32.y_ref = bf16[8,16,256]{2,1,0:T(8,128)(2,1)S(1)} all-to-all(bf16[8,16,256]{2,1,0:T(8,128)(2,1)S(1)} %columns.1), channel_id=1, replica_groups={{0,64,128,192,256,320,384,448},{8,72,136,200,264,328,392,456},{16,80,14..., dimensions={0} | all-to-all | bytes 131072 | tf_op jit(solution)/shard_map/all_to_all | solution.py:478
  84.4 0.9 total.1
  85.3 12.7 %all_to_all.33.refs_1_ = f32[8,8,128]{2,1,0:T(8,128)S(1)} all-to-all(f32[8,8,128]{2,1,0:T(8,128)S(1)} %get-tuple-element.45), channel_id=1, replica_groups=mesh['seq'=64,'head'=8] {'head'}, dimensions={0} | all-to-all | bytes 65536 | tf_op jit(solution)/shard_map/all_to_all | solution.py:478
  98.0 1.0 %finish.1 = (bf16[512,128]{1,0:T(8,128)(2,1)}, bf16[512,128]{1,0:T(8,128)(2,1)}, bf16[512,128]{1,0:T(8,128)(2,1)}) custom-call(f32[8,16,128]{2,1,0:T(8,128)S(1)} %all_to_all.30.refs_0_.sum_ref, f32[8,8,128]{2,1,0:T(8,128)S(1)} %all_to_all.33.refs_1_, bf16[512,128]{1,0:T(8,128)(2,1)S(1)} %copy-done.1, bf16[512,128]{1,0:T(8,128)(2,1)S(1)} %copy-done, ...), custom_call_target="tpu_custom_call" | custom-call | bytes 1409024 | tf_op jit(solution)/shard_map/finish/pallas_call | solution.py:457
  (1 shorter events, 0.0 us)
Async XLA Ops:
  0.6 17.1 %copy-start.2 = (bf16[512,128]{1,0:T(8,128)(2,1)S(1)}, bf16[512,128]{1,0:T(8,128)(2,1)}, u32[]{:S(2)}) copy-start(bf16[512,128]{1,0:T(8,128)(2,1)} %refs_2_.2) | copy-start | bytes 393220
  2.5 15.1 %copy-start = (bf16[512,128]{1,0:T(8,128)(2,1)S(1)}, bf16[512,128]{1,0:T(8,128)(2,1)}, u32[]{:S(2)}) copy-start(bf16[512,128]{1,0:T(8,128)(2,1)} %refs_3_.1) | copy-start | bytes 393220
  28.7 14.2 %copy-start.1 = (bf16[512,128]{1,0:T(8,128)(2,1)S(1)}, bf16[512,128]{1,0:T(8,128)(2,1)}, u32[]{:S(2)}) copy-start(bf16[512,128]{1,0:T(8,128)(2,1)} %refs_2_.3) | copy-start | bytes 393220
  28.7 14.1 %copy-start.3 = (bf16[512,128]{1,0:T(8,128)(2,1)S(1)}, bf16[512,128]{1,0:T(8,128)(2,1)}, u32[]{:S(2)}) copy-start(bf16[512,128]{1,0:T(8,128)(2,1)} %g_ref.3) | copy-start | bytes 393220
  28.7 23.4 %all-to-all-start.2 = ((bf16[8,112,256]{2,1,0:T(8,128)(2,1)}), bf16[8,112,256]{2,1,0:T(8,128)(2,1)S(1)}, u32[]{:S(2)}, u32[]{:S(2)}) async-start(bf16[8,112,256]{2,1,0:T(8,128)(2,1)} %rows.1), calls=%async_computation.2 | async-start | bytes 917504 | tf_op jit(solution)/shard_map/all_to_all | solution.py:478
  38.8 11.2 %collective-permute-start = (bf16[160,256]{1,0:T(8,128)(2,1)S(1)}, bf16[160,256]{1,0:T(8,128)(2,1)S(1)}, u32[]{:S(2)}, u32[]{:S(2)}) collective-permute-start(bf16[160,256]{1,0:T(8,128)(2,1)S(1)} %get-tuple-element.32), channel_id=1, source_target_pairs={{0,8},{8,0},{16,24},{24,16},{32,40},{40,32},{48,56},{56,48},{64,72... | collective-permute-start | bytes 245768 | tf_op jit(solution)/shard_map/ppermute | solution.py:510
  42.2 1.6 %collective-permute-start.1 = (bf16[128,256]{1,0:T(8,128)(2,1)S(1)}, bf16[128,256]{1,0:T(8,128)(2,1)S(1)}, u32[]{:S(2)}, u32[]{:S(2)}) collective-permute-start(bf16[128,256]{1,0:T(8,128)(2,1)S(1)} %get-tuple-element.33), channel_id=1, source_target_pairs={{8,16},{24,32},{40,48},{56,64},{72,80},{88,96},{104,112},{120,128}... | collective-permute-start | bytes 196616 | tf_op jit(solution)/shard_map/ppermute | solution.py:511
  55.5 19.2 %all-to-all-start.3 = ((bf16[8,112,256]{2,1,0:T(8,128)(2,1)}), bf16[8,112,256]{2,1,0:T(8,128)(2,1)S(1)}, u32[]{:S(2)}, u32[]{:S(2)}) async-start(bf16[8,112,256]{2,1,0:T(8,128)(2,1)} %get-tuple-element.43), calls=%async_computation.3 | async-start | bytes 917504 | tf_op jit(solution)/shard_map/all_to_all | solution.py:478
  61.2 10.2 %collective-permute-start.3 = (bf16[128,256]{1,0:T(8,128)(2,1)S(1)}, bf16[128,256]{1,0:T(8,128)(2,1)S(1)}, u32[]{:S(2)}, u32[]{:S(2)}) collective-permute-start(bf16[128,256]{1,0:T(8,128)(2,1)S(1)} %get-tuple-element.42), channel_id=1, source_target_pairs={{8,16},{24,32},{40,48},{56,64},{72,80},{88,96},{104,112},{120,128}... | collective-permute-start | bytes 196616 | tf_op jit(solution)/shard_map/ppermute | solution.py:557
  61.8 10.3 %collective-permute-start.2 = (bf16[160,256]{1,0:T(8,128)(2,1)S(1)}, bf16[160,256]{1,0:T(8,128)(2,1)S(1)}, u32[]{:S(2)}, u32[]{:S(2)}) collective-permute-start(bf16[160,256]{1,0:T(8,128)(2,1)S(1)} %get-tuple-element.41), channel_id=1, source_target_pairs={{0,8},{8,0},{16,24},{24,16},{32,40},{40,32},{48,56},{56,48},{64,72... | collective-permute-start | bytes 245768 | tf_op jit(solution)/shard_map/ppermute | solution.py:556

commit v15 on v13

--- a/solution.py
+++ b/solution.py
@@ -238,8 +238,7 @@
 def attend_kernel(
     qn_ref, g_ref, near_ref, p1_ref, p2_ref, z_ref,
     stat_ref, cross, halo, p1o_ref, p2o_ref, zo_ref,
-    q2_scr, g2_scr, score_scr, weight_scr, pgrad_scr, low_scr, sgrad_scr, half_scr, rims, mid_grad,
-    far_scr, mid_scr, sems,
+    q2_scr, g2_scr, score_scr, weight_scr, pgrad_scr, low_scr, sgrad_scr, rims, cross_grad, far_scr, mid_scr, sems,
 ):
     index = lax.axis_index("seq")
     place = jnp.bitwise_and(index, 7)
@@ -297,29 +296,21 @@
             sgrad_scr[rows, lanes] = (prob * (pgrad_scr[b, rows] - delta)).astype(BF16)
         if b in HALO_PIECE:
             rim_rows.append((b, side, lanes, factors[7] * inverse, delta))
-        if b == 1:
-            half_scr[:, :FEAT] = dot(sgrad_scr[:, :512], q2_scr[:512], (1, 0))
-            half_scr[:, FEAT:] = dot(low_scr[:, :512], g2_scr[:512], (1, 0))
-
-    def grads(rows):
-        keys = half_scr[rows, :FEAT] + dot(sgrad_scr[rows, 512:], q2_scr[512:], (1, 0))
-        values = half_scr[rows, FEAT:] + dot(low_scr[rows, 512:], g2_scr[512:], (1, 0))
-        return jnp.concatenate([keys, values], axis=1).astype(BF16)
-
-    far = grads(slice(384, 768))
+
+    cross_grad[:, :FEAT] = dot(sgrad_scr[...], q2_scr[...], (1, 0)).astype(BF16)
+    cross_grad[:, FEAT:] = dot(low_scr[...], g2_scr[...], (1, 0)).astype(BF16)
     for j in range(3):
         for s in range(8):
-            at = LEAF * j + 16 * s
-            far_scr[s, 16 * j : 16 * (j + 1)] = far[at : at + 16]
+            at = 384 + LEAF * j + 16 * s
+            far_scr[s, 16 * j : 16 * (j + 1)] = cross_grad[at : at + 16]
     copies = start_all([pltpu.make_async_copy(far_scr, zo_ref.at[:, pl.ds(0, FAR)], sems.at[0])])
-    mid_grad[...] = grads(slice(0, 384))
     mid_scr[place] = jnp.zeros((64, 2 * FEAT), BF16)
-    mid_scr[jnp.bitwise_xor(place, 1)] = mid_grad[:64]
-    mid_scr[jnp.bitwise_xor(place, 2)] = mid_grad[128:192]
-    mid_scr[jnp.bitwise_xor(place, 3)] = mid_grad[192:256]
+    mid_scr[jnp.bitwise_xor(place, 1)] = cross_grad[:64]
+    mid_scr[jnp.bitwise_xor(place, 2)] = cross_grad[128:192]
+    mid_scr[jnp.bitwise_xor(place, 3)] = cross_grad[192:256]
     for i in range(4):
         other = jnp.bitwise_xor(place, 4 + i)
-        mid_scr[other, :32] = mid_grad[256 + 32 * i : 288 + 32 * i]
+        mid_scr[other, :32] = cross_grad[256 + 32 * i : 288 + 32 * i]
         mid_scr[other, 32:] = jnp.zeros((32, 2 * FEAT), BF16)
     copies += start_all([pltpu.make_async_copy(mid_scr, zo_ref.at[:, pl.ds(FAR, 64)], sems.at[1])])
     for b, side, lanes, factor, delta in rim_rows:
@@ -328,7 +319,7 @@
         rims[side, :, :FEAT] = dot(sgrad, q2_scr[lanes], (1, 0)).astype(BF16)
         rims[side, :, FEAT:] = dot(prob.astype(BF16), g2_scr[lanes], (1, 0)).astype(BF16)
     p1o_ref[:LEAF] = rims[peer_side]
-    p1o_ref[LEAF:] = mid_grad[64:128]
+    p1o_ref[LEAF:] = cross_grad[64:128]
     p2o_ref[...] = rims[odd]
     wait_all(copies)
 
@@ -543,9 +534,8 @@
             pltpu.VMEM((LEAVES, 7 * LEAF, 256), F32),
             pltpu.VMEM((768, 1024), BF16),
             pltpu.VMEM((768, 1024), BF16),
-            pltpu.VMEM((768, 256), F32),
             pltpu.VMEM((2, LEAF, 256), BF16),
-            pltpu.VMEM((384, 256), BF16),
+            pltpu.VMEM((768, 256), BF16),
             pltpu.VMEM((8, FAR, 256), BF16),
             pltpu.VMEM((8, 64, 256), BF16),
             pltpu.SemaphoreType.DMA((2,)),

time: 99.3 us -> 99.2 us (level)
  no operation moved by 1% of the time
where the time goes in v15:
time: 99.2 us; the launch traced here: 98.6 us
  blocking collectives  48.2 us (49%)
  starting transfers between devices  25.7 us (26%)
  Pallas kernels  13.2 us (13%)
  waiting for transfers between devices  10.7 us (11%)
    all_to_all x4, blocking collectives, exchange(): return lax.all_to_all(x, axis, 0, 0, axis_index_groups=groups, tiled=True)  48.2 us
    all_to_all x2, starting transfers between devices, exchange(): return lax.all_to_all(x, axis, 0, 0, axis_index_groups=groups, tiled=True)  15.2 us
    pallas_call x9, Pallas kernels, call(): pl.pallas_call(kernel, out_shape=outs, in_specs=[pl.BlockSpec(memory_spac...  13.2 us
    ppermute x2, starting transfers between devices, local(): p1 = lax.ppermute(p1, 'seq', peer)  9.15 us
    ppermute x2, waiting for transfers between devices, local(): p1 = lax.ppermute(p1, 'seq', peer)  7.46 us
    all_to_all x2, waiting for transfers between devices, exchange(): return lax.all_to_all(x, axis, 0, 0, axis_index_groups=groups, tiled=True)  3.28 us
  transfers between devices with their start and end apart: 6, of which 4 were waited for; matrix products, arithmetic and copies ran while one was open for 0% of the time, Pallas kernels for 5%

profile of v15, /device:TPU:1, one launch (start us, length us, event | category | flops | bytes accessed | tf_op | source)
XLA Modules:
  0.0 98.6 jit_solution(15849517338781710290)
XLA Ops:
  0.6 0.0 copy-start.2
  0.6 1.9 %squares.1 = f32[8,16,128]{2,1,0:T(8,128)} custom-call(bf16[512,128]{1,0:T(8,128)(2,1)} %refs_2_.3, bf16[512,128]{1,0:T(8,128)(2,1)} %refs_3_.1, f32[1,128]{1,0:T(1,128)} %bitcast.2, f32[1,128]{1,0:T(1,128)} %bitcast.3), custom_call_target="tpu_custom_call" | custom-call | bytes 328704 | tf_op jit(solution)/shard_map/squares/pallas_call | solution.py:448
  2.5 0.0 copy-start
  2.6 15.1 %all_to_all.30.refs_0_.sum_ref = f32[8,16,128]{2,1,0:T(8,128)S(1)} all-to-all(f32[8,16,128]{2,1,0:T(8,128)} %squares.1), channel_id=1, replica_groups=mesh['seq'=64,'head'=8] {'head'}, dimensions={0} | all-to-all | bytes 131072 | tf_op jit(solution)/shard_map/all_to_all | solution.py:469
  17.7 0.0 copy-done.2
  17.7 0.5 norm.1
  18.2 9.6 %all_to_all.31.y_ref = bf16[8,16,256]{2,1,0:T(8,128)(2,1)S(1)} all-to-all(bf16[8,16,256]{2,1,0:T(8,128)(2,1)S(1)} %get-tuple-element.34), channel_id=1, replica_groups={{0,64,128,192,256,320,384,448},{8,72,136,200,264,328,392,456},{16,80,14..., dimensions={0} | all-to-all | bytes 131072 | tf_op jit(solution)/shard_map/all_to_all | solution.py:469
  27.8 0.9 rows.1
  28.7 0.0 copy-start.1
  28.7 0.0 copy-start.3
  28.7 10.1 %all-to-all-start.2 = ((bf16[8,112,256]{2,1,0:T(8,128)(2,1)}), bf16[8,112,256]{2,1,0:T(8,128)(2,1)S(1)}, u32[]{:S(2)}, u32[]{:S(2)}) async-start(bf16[8,112,256]{2,1,0:T(8,128)(2,1)} %rows.1), calls=%async_computation.2 | async-start | bytes 917504 | tf_op jit(solution)/shard_map/all_to_all | solution.py:469
  38.8 3.4 %collective-permute-start = (bf16[192,256]{1,0:T(8,128)(2,1)S(1)}, bf16[192,256]{1,0:T(8,128)(2,1)S(1)}, u32[]{:S(2)}, u32[]{:S(2)}) collective-permute-start(bf16[192,256]{1,0:T(8,128)(2,1)S(1)} %get-tuple-element.32), channel_id=1, source_target_pairs={{0,8},{8,0},{16,24},{24,16},{32,40},{40,32},{48,56},{56,48},{64,72... | collective-permute-start | bytes 294920 | tf_op jit(solution)/shard_map/ppermute | solution.py:501
  42.2 0.7 collective-permute-start.1
  42.8 0.0 copy-done.1
  42.8 0.0 copy-done.3
  42.9 0.9 near.1
  43.8 0.0 collective-permute-done.1.p2_ref
  43.8 6.6 %collective-permute-done.p1_ref = bf16[192,256]{1,0:T(8,128)(2,1)S(1)} collective-permute-done((bf16[192,256]{1,0:T(8,128)(2,1)S(1)}, bf16[192,256]{1,0:T(8,128)(2,1)S(1)}, u32[]{:S(2)}, u32[]{:S(2)}) %collective-permute-start) | collective-permute-done | bytes 98336 | tf_op jit(solution)/shard_map/ppermute | solution.py:501
  50.4 1.7 %all-to-all-done.2.z_ref = bf16[8,112,256]{2,1,0:T(8,128)(2,1)S(1)} async-done(((bf16[8,112,256]{2,1,0:T(8,128)(2,1)}), bf16[8,112,256]{2,1,0:T(8,128)(2,1)S(1)}, u32[]{:S(2)}, u32[]{:S(2)}) %all-to-all-start.2) | async-done | bytes 458784 | tf_op jit(solution)/shard_map/all_to_all | solution.py:469
  52.1 3.2 %attend.1 = (f32[4,8,256]{2,1,0:T(8,128)S(1)}, bf16[768,256]{1,0:T(8,128)(2,1)S(1)}, bf16[2,128,256]{2,1,0:T(8,128)(2,1)S(1)}, bf16[192,256]{1,0:T(8,128)(2,1)S(...) custom-call(bf16[512,128]{1,0:T(8,128)(2,1)S(1)} %get-tuple-element.30.qn_ref, ...), custom_call_target="tpu_custom_call" | custom-call | flops 805306368 | bytes 2097152 | tf_op jit(solution)/shard_map/attend/pallas_call | solution.py:448
  55.3 5.2 %all-to-all-start.3 = ((bf16[8,112,256]{2,1,0:T(8,128)(2,1)}), bf16[8,112,256]{2,1,0:T(8,128)(2,1)S(1)}, u32[]{:S(2)}, u32[]{:S(2)}) async-start(bf16[8,112,256]{2,1,0:T(8,128)(2,1)} %get-tuple-element.43), calls=%async_computation.3 | async-start | bytes 917504 | tf_op jit(solution)/shard_map/all_to_all | solution.py:469
  60.4 0.7 collective-permute-start.3
  61.1 5.8 %collective-permute-start.2 = (bf16[192,256]{1,0:T(8,128)(2,1)S(1)}, bf16[192,256]{1,0:T(8,128)(2,1)S(1)}, u32[]{:S(2)}, u32[]{:S(2)}) collective-permute-start(bf16[192,256]{1,0:T(8,128)(2,1)S(1)} %get-tuple-element.41), channel_id=1, source_target_pairs={{0,8},{8,0},{16,24},{24,16},{32,40},{40,32},{48,56},{56,48},{64,72... | collective-permute-start | bytes 294920 | tf_op jit(solution)/shard_map/ppermute | solution.py:547
  66.9 3.7 %after.1 = (bf16[512,128]{1,0:T(8,128)(2,1)}, f32[512,128]{1,0:T(8,128)S(1)}, f32[512,256]{1,0:T(8,128)S(1)}, f32[8,128]{1,0:T(8,128)S(1)}) custom-call(f32[4,8,256]{2,1,0:T(8,128)S(1)} %get-tuple-element.36.stat_ref, bf16[512,128]{1,0:T(8,128)(2,1)S(1)} %get-tuple-element.30.qn_ref, bf16[512,256]{1,0:T(8,128)(2,1)S(1)} %get-tuple-element.28.refs_2_.kv_ref, ...), custom_call_target="tpu_custom_call" | custom-call | flops 1677721600 | bytes 2330624 | tf_op jit(solution)/shard_map/after/pallas_call | solution.py:448
  70.6 0.0 collective-permute-done.3.p2_ref
  70.6 0.8 collective-permute-done.2.p1_ref
  71.5 1.6 %all-to-all-done.3.z_ref = bf16[8,112,256]{2,1,0:T(8,128)(2,1)S(1)} async-done(((bf16[8,112,256]{2,1,0:T(8,128)(2,1)}), bf16[8,112,256]{2,1,0:T(8,128)(2,1)S(1)}, u32[]{:S(2)}, u32[]{:S(2)}) %all-to-all-start.3) | async-done | bytes 458784 | tf_op jit(solution)/shard_map/all_to_all | solution.py:469
  73.1 0.2 columns.1
  73.3 10.6 %all_to_all.32.y_ref = bf16[8,16,256]{2,1,0:T(8,128)(2,1)S(1)} all-to-all(bf16[8,16,256]{2,1,0:T(8,128)(2,1)S(1)} %columns.1), channel_id=1, replica_groups={{0,64,128,192,256,320,384,448},{8,72,136,200,264,328,392,456},{16,80,14..., dimensions={0} | all-to-all | bytes 131072 | tf_op jit(solution)/shard_map/all_to_all | solution.py:469
  83.9 0.8 total.1
  84.7 12.8 %all_to_all.33.refs_1_ = f32[8,8,128]{2,1,0:T(8,128)S(1)} all-to-all(f32[8,8,128]{2,1,0:T(8,128)S(1)} %get-tuple-element.45), channel_id=1, replica_groups=mesh['seq'=64,'head'=8] {'head'}, dimensions={0} | all-to-all | bytes 65536 | tf_op jit(solution)/shard_map/all_to_all | solution.py:469
  97.6 1.0 %finish.1 = (bf16[512,128]{1,0:T(8,128)(2,1)}, bf16[512,128]{1,0:T(8,128)(2,1)}, bf16[512,128]{1,0:T(8,128)(2,1)}) custom-call(f32[8,16,128]{2,1,0:T(8,128)S(1)} %all_to_all.30.refs_0_.sum_ref, f32[8,8,128]{2,1,0:T(8,128)S(1)} %all_to_all.33.refs_1_, bf16[512,128]{1,0:T(8,128)(2,1)S(1)} %copy-done.1, bf16[512,128]{1,0:T(8,128)(2,1)S(1)} %copy-done, ...), custom_call_target="tpu_custom_call" | custom-call | bytes 1409024 | tf_op jit(solution)/shard_map/finish/pallas_call | solution.py:448
  (1 shorter events, 0.0 us)
Async XLA Ops:
  0.6 17.1 %copy-start.2 = (bf16[512,128]{1,0:T(8,128)(2,1)S(1)}, bf16[512,128]{1,0:T(8,128)(2,1)}, u32[]{:S(2)}) copy-start(bf16[512,128]{1,0:T(8,128)(2,1)} %refs_2_.2) | copy-start | bytes 393220
  2.5 15.1 %copy-start = (bf16[512,128]{1,0:T(8,128)(2,1)S(1)}, bf16[512,128]{1,0:T(8,128)(2,1)}, u32[]{:S(2)}) copy-start(bf16[512,128]{1,0:T(8,128)(2,1)} %refs_3_.1) | copy-start | bytes 393220
  28.7 14.2 %copy-start.1 = (bf16[512,128]{1,0:T(8,128)(2,1)S(1)}, bf16[512,128]{1,0:T(8,128)(2,1)}, u32[]{:S(2)}) copy-start(bf16[512,128]{1,0:T(8,128)(2,1)} %refs_2_.3) | copy-start | bytes 393220
  28.7 14.1 %copy-start.3 = (bf16[512,128]{1,0:T(8,128)(2,1)S(1)}, bf16[512,128]{1,0:T(8,128)(2,1)}, u32[]{:S(2)}) copy-start(bf16[512,128]{1,0:T(8,128)(2,1)} %g_ref.3) | copy-start | bytes 393220
  28.7 23.4 %all-to-all-start.2 = ((bf16[8,112,256]{2,1,0:T(8,128)(2,1)}), bf16[8,112,256]{2,1,0:T(8,128)(2,1)S(1)}, u32[]{:S(2)}, u32[]{:S(2)}) async-start(bf16[8,112,256]{2,1,0:T(8,128)(2,1)} %rows.1), calls=%async_computation.2 | async-start | bytes 917504 | tf_op jit(solution)/shard_map/all_to_all | solution.py:469
  38.8 11.6 %collective-permute-start = (bf16[192,256]{1,0:T(8,128)(2,1)S(1)}, bf16[192,256]{1,0:T(8,128)(2,1)S(1)}, u32[]{:S(2)}, u32[]{:S(2)}) collective-permute-start(bf16[192,256]{1,0:T(8,128)(2,1)S(1)} %get-tuple-element.32), channel_id=1, source_target_pairs={{0,8},{8,0},{16,24},{24,16},{32,40},{40,32},{48,56},{56,48},{64,72... | collective-permute-start | bytes 294920 | tf_op jit(solution)/shard_map/ppermute | solution.py:501
  42.2 1.6 %collective-permute-start.1 = (bf16[128,256]{1,0:T(8,128)(2,1)S(1)}, bf16[128,256]{1,0:T(8,128)(2,1)S(1)}, u32[]{:S(2)}, u32[]{:S(2)}) collective-permute-start(bf16[128,256]{1,0:T(8,128)(2,1)S(1)} %get-tuple-element.33), channel_id=1, source_target_pairs={{8,16},{24,32},{40,48},{56,64},{72,80},{88,96},{104,112},{120,128}... | collective-permute-start | bytes 196616 | tf_op jit(solution)/shard_map/ppermute | solution.py:502
  55.3 17.8 %all-to-all-start.3 = ((bf16[8,112,256]{2,1,0:T(8,128)(2,1)}), bf16[8,112,256]{2,1,0:T(8,128)(2,1)S(1)}, u32[]{:S(2)}, u32[]{:S(2)}) async-start(bf16[8,112,256]{2,1,0:T(8,128)(2,1)} %get-tuple-element.43), calls=%async_computation.3 | async-start | bytes 917504 | tf_op jit(solution)/shard_map/all_to_all | solution.py:469
  60.4 10.2 %collective-permute-start.3 = (bf16[128,256]{1,0:T(8,128)(2,1)S(1)}, bf16[128,256]{1,0:T(8,128)(2,1)S(1)}, u32[]{:S(2)}, u32[]{:S(2)}) collective-permute-start(bf16[128,256]{1,0:T(8,128)(2,1)S(1)} %get-tuple-element.42), channel_id=1, source_target_pairs={{8,16},{24,32},{40,48},{56,64},{72,80},{88,96},{104,112},{120,128}... | collective-permute-start | bytes 196616 | tf_op jit(solution)/shard_map/ppermute | solution.py:548
  61.1 10.4 %collective-permute-start.2 = (bf16[192,256]{1,0:T(8,128)(2,1)S(1)}, bf16[192,256]{1,0:T(8,128)(2,1)S(1)}, u32[]{:S(2)}, u32[]{:S(2)}) collective-permute-start(bf16[192,256]{1,0:T(8,128)(2,1)S(1)} %get-tuple-element.41), channel_id=1, source_target_pairs={{0,8},{8,0},{16,24},{24,16},{32,40},{40,32},{48,56},{56,48},{64,72... | collective-permute-start | bytes 294920 | tf_op jit(solution)/shard_map/ppermute | solution.py:547

commit v16 on v15

--- a/solution.py
+++ b/solution.py
@@ -21,6 +21,8 @@
 COLUMN_LEVEL = {1: 5, 2: 6, 3: 6, 4: 7, 5: 7, 6: 7, 7: 7}
 FAR = 48
 SLOT = 112
+FIRST_Z = 7
+FIRST_Y = 4
 
 
 def dot(a, b, dims):
@@ -103,7 +105,7 @@
 
 def norm_kernel(width, sum_ref, k_ref, v_ref, kv_ref, one_ref, lv_ref, y_ref, p1_ref, p2_ref):
     index = lax.axis_index("seq")
-    column = jnp.right_shift(index, 3)
+    column = jnp.bitwise_xor(jnp.right_shift(index, 3), FIRST_Y)
     odd = jnp.bitwise_and(index, 1)
     gain = sum_ref[lax.axis_index("head"), 9:10]
     kv_ref[:, :FEAT] = (
@@ -139,8 +141,8 @@
 
 def row_kernel(y_ref, lv_ref, out_ref, far_scr, mid_scr, sems):
     index = lax.axis_index("seq")
-    column = jnp.right_shift(index, 3)
-    place = jnp.bitwise_and(index, 7)
+    column = jnp.bitwise_xor(jnp.right_shift(index, 3), FIRST_Y)
+    place = jnp.bitwise_xor(jnp.bitwise_and(index, 7), FIRST_Z)
     mid_scr[place] = jnp.zeros((64, 2 * FEAT), BF16)
     for d in range(1, 8):
         other = jnp.bitwise_xor(place, d)
@@ -242,16 +244,17 @@
 ):
     index = lax.axis_index("seq")
     place = jnp.bitwise_and(index, 7)
+    slot = jnp.bitwise_xor(place, FIRST_Z)
     odd = jnp.bitwise_and(index, 1)
     peer_side = 1 - odd
     halo[peer_side] = p1_ref[:LEAF]
     halo[odd] = p2_ref[...]
-    cross[:64] = z_ref[jnp.bitwise_xor(place, 1), FAR:]
+    cross[:64] = z_ref[jnp.bitwise_xor(slot, 1), FAR:]
     cross[64:128] = p1_ref[LEAF:]
-    cross[128:192] = z_ref[jnp.bitwise_xor(place, 2), FAR:]
-    cross[192:256] = z_ref[jnp.bitwise_xor(place, 3), FAR:]
+    cross[128:192] = z_ref[jnp.bitwise_xor(slot, 2), FAR:]
+    cross[192:256] = z_ref[jnp.bitwise_xor(slot, 3), FAR:]
     for i in range(4):
-        cross[256 + 32 * i : 288 + 32 * i] = z_ref[jnp.bitwise_xor(place, 4 + i), FAR : FAR + 32]
+        cross[256 + 32 * i : 288 + 32 * i] = z_ref[jnp.bitwise_xor(slot, 4 + i), FAR : FAR + 32]
     for s in range(8):
         for j in range(3):
             at = 384 + LEAF * j + 16 * s
@@ -302,7 +305,7 @@
     for j in range(3):
         for s in range(8):
             at = 384 + LEAF * j + 16 * s
-            far_scr[s, 16 * j : 16 * (j + 1)] = cross_grad[at : at + 16]
+            far_scr[s ^ FIRST_Z, 16 * j : 16 * (j + 1)] = cross_grad[at : at + 16]
     copies = start_all([pltpu.make_async_copy(far_scr, zo_ref.at[:, pl.ds(0, FAR)], sems.at[0])])
     mid_scr[place] = jnp.zeros((64, 2 * FEAT), BF16)
     mid_scr[jnp.bitwise_xor(place, 1)] = cross_grad[:64]
@@ -461,6 +464,8 @@
     return jax.ShapeDtypeStruct(shape, dtype)
 
 
+FORWARD_ROWS = [[8 * y + (p ^ FIRST_Z) for p in range(8)] for y in range(8)]
+FORWARD_COLUMNS = [[8 * (p ^ FIRST_Y) + z for p in range(8)] for z in range(8)]
 ROW_GROUPS = [[8 * y + z for z in range(8)] for y in range(8)]
 COLUMN_GROUPS = [[8 * y + z for y in range(8)] for z in range(8)]
 
@@ -500,7 +505,7 @@
     )
     p1 = lax.ppermute(p1, "seq", peer)
     p2 = lax.ppermute(p2, "seq", beside)
-    yrecv = exchange(ysend, "seq", COLUMN_GROUPS)
+    yrecv = exchange(ysend, "seq", FORWARD_COLUMNS)
     zsend = call(
         row_kernel,
         sds(8, SLOT, 256),
@@ -513,7 +518,7 @@
         out_spaces=[pl.ANY],
         name="rows",
     )
-    zrecv = exchange(zsend, "seq", ROW_GROUPS)
+    zrecv = exchange(zsend, "seq", FORWARD_ROWS)
     qn, near = call(
         lambda *refs: near_kernel(width, *refs),
         [sds(ROWS, FEAT), sds(LEAVES, 8, 256, dtype=F32)],

time: 99.2 us -> 100 us (level)
  blocking collectives: 48.2 us -> 50.9 us
  starting transfers between devices: 25.7 us -> 23.8 us
    all_to_all x4, blocking collectives: 48.2 us -> 50.9 us  [exchange(): return lax.all_to_all(x, axis, 0, 0, axis_index_groups=groups, tiled=True)]
    ppermute x2, waiting for transfers between devices: 7.46 us -> 9.1 us  [local(): p1 = lax.ppermute(p1, 'seq', peer)]
    all_to_all x2, starting transfers between devices: 15.2 us -> 13.6 us  [exchange(): return lax.all_to_all(x, axis, 0, 0, axis_index_groups=groups, tiled=True)]
    all_to_all x2, waiting for transfers between devices: 3.28 us -> 1.74 us  [exchange(): return lax.all_to_all(x, axis, 0, 0, axis_index_groups=groups, tiled=True)]
  transfers between devices with their start and end apart: 6 -> 6, of which waited for: 4 -> 3; matrix products, arithmetic and copies ran while one was open for 0% -> 0% of each run, Pallas kernels for 5% -> 5%
where the time goes in v16:
time: 100 us; the launch traced here: 99.5 us
  blocking collectives  50.9 us (51%)
  starting transfers between devices  23.8 us (24%)
  Pallas kernels  13.2 us (13%)
  waiting for transfers between devices  10.8 us (11%)
    all_to_all x4, blocking collectives, exchange(): return lax.all_to_all(x, axis, 0, 0, axis_index_groups=groups, tiled=True)  50.9 us
    all_to_all x2, starting transfers between devices, exchange(): return lax.all_to_all(x, axis, 0, 0, axis_index_groups=groups, tiled=True)  13.6 us
    pallas_call x9, Pallas kernels, call(): pl.pallas_call(kernel, out_shape=outs, in_specs=[pl.BlockSpec(memory_spac...  13.2 us
    ppermute x2, waiting for transfers between devices, local(): p1 = lax.ppermute(p1, 'seq', peer)  9.1 us
    ppermute x2, starting transfers between devices, local(): p1 = lax.ppermute(p1, 'seq', peer)  8.87 us
  transfers between devices with their start and end apart: 6, of which 3 were waited for; matrix products, arithmetic and copies ran while one was open for 0% of the time, Pallas kernels for 5%

profile of v16, /device:TPU:1, one launch (start us, length us, event | category | flops | bytes accessed | tf_op | source)
XLA Modules:
  0.0 99.5 jit_solution(17207166224952345541)
XLA Ops:
  0.6 0.0 copy-start.2
  0.6 1.9 %squares.1 = f32[8,16,128]{2,1,0:T(8,128)} custom-call(bf16[512,128]{1,0:T(8,128)(2,1)} %refs_2_.3, bf16[512,128]{1,0:T(8,128)(2,1)} %refs_3_.1, f32[1,128]{1,0:T(1,128)} %bitcast.2, f32[1,128]{1,0:T(1,128)} %bitcast.3), custom_call_target="tpu_custom_call" | custom-call | bytes 328704 | tf_op jit(solution)/shard_map/squares/pallas_call | solution.py:451
  2.5 0.0 copy-start
  2.6 15.1 %all_to_all.30.refs_0_.sum_ref = f32[8,16,128]{2,1,0:T(8,128)S(1)} all-to-all(f32[8,16,128]{2,1,0:T(8,128)} %squares.1), channel_id=1, replica_groups=mesh['seq'=64,'head'=8] {'head'}, dimensions={0} | all-to-all | bytes 131072 | tf_op jit(solution)/shard_map/all_to_all | solution.py:474
  17.7 0.0 copy-done.2
  17.7 0.5 norm.1
  18.2 8.9 %all_to_all.31.y_ref = bf16[8,16,256]{2,1,0:T(8,128)(2,1)S(1)} all-to-all(bf16[8,16,256]{2,1,0:T(8,128)(2,1)S(1)} %get-tuple-element.34), channel_id=1, replica_groups={{256,320,384,448,0,64,128,192},{264,328,392,456,8,72,136,200},{272,336,..., dimensions={0} | all-to-all | bytes 131072 | tf_op jit(solution)/shard_map/all_to_all | solution.py:474
  27.1 0.9 rows.1
  27.9 0.0 copy-start.1
  27.9 0.0 copy-start.3
  28.0 9.5 %all-to-all-start.2 = ((bf16[8,112,256]{2,1,0:T(8,128)(2,1)}), bf16[8,112,256]{2,1,0:T(8,128)(2,1)S(1)}, u32[]{:S(2)}, u32[]{:S(2)}) async-start(bf16[8,112,256]{2,1,0:T(8,128)(2,1)} %rows.1), calls=%async_computation.2 | async-start | bytes 917504 | tf_op jit(solution)/shard_map/all_to_all | solution.py:474
  37.4 3.1 %collective-permute-start = (bf16[192,256]{1,0:T(8,128)(2,1)S(1)}, bf16[192,256]{1,0:T(8,128)(2,1)S(1)}, u32[]{:S(2)}, u32[]{:S(2)}) collective-permute-start(bf16[192,256]{1,0:T(8,128)(2,1)S(1)} %get-tuple-element.32), channel_id=1, source_target_pairs={{0,8},{8,0},{16,24},{24,16},{32,40},{40,32},{48,56},{56,48},{64,72... | collective-permute-start | bytes 294920 | tf_op jit(solution)/shard_map/ppermute | solution.py:506
  40.5 0.7 collective-permute-start.1
  41.2 0.0 copy-done.1
  41.2 0.0 copy-done.3
  41.2 0.9 near.1
  42.1 0.0 collective-permute-done.1.p2_ref
  42.1 8.3 %collective-permute-done.p1_ref = bf16[192,256]{1,0:T(8,128)(2,1)S(1)} collective-permute-done((bf16[192,256]{1,0:T(8,128)(2,1)S(1)}, bf16[192,256]{1,0:T(8,128)(2,1)S(1)}, u32[]{:S(2)}, u32[]{:S(2)}) %collective-permute-start) | collective-permute-done | bytes 98336 | tf_op jit(solution)/shard_map/ppermute | solution.py:506
  50.4 0.0 all-to-all-done.2.z_ref
  50.4 3.2 %attend.1 = (f32[4,8,256]{2,1,0:T(8,128)S(1)}, bf16[768,256]{1,0:T(8,128)(2,1)S(1)}, bf16[2,128,256]{2,1,0:T(8,128)(2,1)S(1)}, bf16[192,256]{1,0:T(8,128)(2,1)S(...) custom-call(bf16[512,128]{1,0:T(8,128)(2,1)S(1)} %get-tuple-element.30.qn_ref, ...), custom_call_target="tpu_custom_call" | custom-call | flops 805306368 | bytes 2097152 | tf_op jit(solution)/shard_map/attend/pallas_call | solution.py:451
  53.6 4.2 %all-to-all-start.3 = ((bf16[8,112,256]{2,1,0:T(8,128)(2,1)}), bf16[8,112,256]{2,1,0:T(8,128)(2,1)S(1)}, u32[]{:S(2)}, u32[]{:S(2)}) async-start(bf16[8,112,256]{2,1,0:T(8,128)(2,1)} %get-tuple-element.43), calls=%async_computation.3 | async-start | bytes 917504 | tf_op jit(solution)/shard_map/all_to_all | solution.py:474
  57.8 0.7 collective-permute-start.3
  58.4 5.8 %collective-permute-start.2 = (bf16[192,256]{1,0:T(8,128)(2,1)S(1)}, bf16[192,256]{1,0:T(8,128)(2,1)S(1)}, u32[]{:S(2)}, u32[]{:S(2)}) collective-permute-start(bf16[192,256]{1,0:T(8,128)(2,1)S(1)} %get-tuple-element.41), channel_id=1, source_target_pairs={{0,8},{8,0},{16,24},{24,16},{32,40},{40,32},{48,56},{56,48},{64,72... | collective-permute-start | bytes 294920 | tf_op jit(solution)/shard_map/ppermute | solution.py:552
  64.2 3.7 %after.1 = (bf16[512,128]{1,0:T(8,128)(2,1)}, f32[512,128]{1,0:T(8,128)S(1)}, f32[512,256]{1,0:T(8,128)S(1)}, f32[8,128]{1,0:T(8,128)S(1)}) custom-call(f32[4,8,256]{2,1,0:T(8,128)S(1)} %get-tuple-element.36.stat_ref, bf16[512,128]{1,0:T(8,128)(2,1)S(1)} %get-tuple-element.30.qn_ref, bf16[512,256]{1,0:T(8,128)(2,1)S(1)} %get-tuple-element.28.refs_2_.kv_ref, ...), custom_call_target="tpu_custom_call" | custom-call | flops 1677721600 | bytes 2330624 | tf_op jit(solution)/shard_map/after/pallas_call | solution.py:451
  67.9 0.0 collective-permute-done.3.p2_ref
  67.9 0.8 collective-permute-done.2.p1_ref
  68.8 1.7 %all-to-all-done.3.z_ref = bf16[8,112,256]{2,1,0:T(8,128)(2,1)S(1)} async-done(((bf16[8,112,256]{2,1,0:T(8,128)(2,1)}), bf16[8,112,256]{2,1,0:T(8,128)(2,1)S(1)}, u32[]{:S(2)}, u32[]{:S(2)}) %all-to-all-start.3) | async-done | bytes 458784 | tf_op jit(solution)/shard_map/all_to_all | solution.py:474
  70.5 0.2 columns.1
  70.7 13.1 %all_to_all.32.y_ref = bf16[8,16,256]{2,1,0:T(8,128)(2,1)S(1)} all-to-all(bf16[8,16,256]{2,1,0:T(8,128)(2,1)S(1)} %columns.1), channel_id=1, replica_groups={{0,64,128,192,256,320,384,448},{8,72,136,200,264,328,392,456},{16,80,14..., dimensions={0} | all-to-all | bytes 131072 | tf_op jit(solution)/shard_map/all_to_all | solution.py:474
  83.8 0.8 total.1
  84.6 13.8 %all_to_all.33.refs_1_ = f32[8,8,128]{2,1,0:T(8,128)S(1)} all-to-all(f32[8,8,128]{2,1,0:T(8,128)S(1)} %get-tuple-element.45), channel_id=1, replica_groups=mesh['seq'=64,'head'=8] {'head'}, dimensions={0} | all-to-all | bytes 65536 | tf_op jit(solution)/shard_map/all_to_all | solution.py:474
  98.5 1.0 %finish.1 = (bf16[512,128]{1,0:T(8,128)(2,1)}, bf16[512,128]{1,0:T(8,128)(2,1)}, bf16[512,128]{1,0:T(8,128)(2,1)}) custom-call(f32[8,16,128]{2,1,0:T(8,128)S(1)} %all_to_all.30.refs_0_.sum_ref, f32[8,8,128]{2,1,0:T(8,128)S(1)} %all_to_all.33.refs_1_, bf16[512,128]{1,0:T(8,128)(2,1)S(1)} %copy-done.1, bf16[512,128]{1,0:T(8,128)(2,1)S(1)} %copy-done, ...), custom_call_target="tpu_custom_call" | custom-call | bytes 1409024 | tf_op jit(solution)/shard_map/finish/pallas_call | solution.py:451
  (1 shorter events, 0.0 us)
Async XLA Ops:
  0.6 17.1 %copy-start.2 = (bf16[512,128]{1,0:T(8,128)(2,1)S(1)}, bf16[512,128]{1,0:T(8,128)(2,1)}, u32[]{:S(2)}) copy-start(bf16[512,128]{1,0:T(8,128)(2,1)} %refs_2_.2) | copy-start | bytes 393220
  2.5 15.1 %copy-start = (bf16[512,128]{1,0:T(8,128)(2,1)S(1)}, bf16[512,128]{1,0:T(8,128)(2,1)}, u32[]{:S(2)}) copy-start(bf16[512,128]{1,0:T(8,128)(2,1)} %refs_3_.1) | copy-start | bytes 393220
  27.9 13.3 %copy-start.1 = (bf16[512,128]{1,0:T(8,128)(2,1)S(1)}, bf16[512,128]{1,0:T(8,128)(2,1)}, u32[]{:S(2)}) copy-start(bf16[512,128]{1,0:T(8,128)(2,1)} %refs_2_.3) | copy-start | bytes 393220
  27.9 13.2 %copy-start.3 = (bf16[512,128]{1,0:T(8,128)(2,1)S(1)}, bf16[512,128]{1,0:T(8,128)(2,1)}, u32[]{:S(2)}) copy-start(bf16[512,128]{1,0:T(8,128)(2,1)} %g_ref.3) | copy-start | bytes 393220
  28.0 22.4 %all-to-all-start.2 = ((bf16[8,112,256]{2,1,0:T(8,128)(2,1)}), bf16[8,112,256]{2,1,0:T(8,128)(2,1)S(1)}, u32[]{:S(2)}, u32[]{:S(2)}) async-start(bf16[8,112,256]{2,1,0:T(8,128)(2,1)} %rows.1), calls=%async_computation.2 | async-start | bytes 917504 | tf_op jit(solution)/shard_map/all_to_all | solution.py:474
  37.4 13.0 %collective-permute-start = (bf16[192,256]{1,0:T(8,128)(2,1)S(1)}, bf16[192,256]{1,0:T(8,128)(2,1)S(1)}, u32[]{:S(2)}, u32[]{:S(2)}) collective-permute-start(bf16[192,256]{1,0:T(8,128)(2,1)S(1)} %get-tuple-element.32), channel_id=1, source_target_pairs={{0,8},{8,0},{16,24},{24,16},{32,40},{40,32},{48,56},{56,48},{64,72... | collective-permute-start | bytes 294920 | tf_op jit(solution)/shard_map/ppermute | solution.py:506
  40.5 1.6 %collective-permute-start.1 = (bf16[128,256]{1,0:T(8,128)(2,1)S(1)}, bf16[128,256]{1,0:T(8,128)(2,1)S(1)}, u32[]{:S(2)}, u32[]{:S(2)}) collective-permute-start(bf16[128,256]{1,0:T(8,128)(2,1)S(1)} %get-tuple-element.33), channel_id=1, source_target_pairs={{8,16},{24,32},{40,48},{56,64},{72,80},{88,96},{104,112},{120,128}... | collective-permute-start | bytes 196616 | tf_op jit(solution)/shard_map/ppermute | solution.py:507
  53.6 16.9 %all-to-all-start.3 = ((bf16[8,112,256]{2,1,0:T(8,128)(2,1)}), bf16[8,112,256]{2,1,0:T(8,128)(2,1)S(1)}, u32[]{:S(2)}, u32[]{:S(2)}) async-start(bf16[8,112,256]{2,1,0:T(8,128)(2,1)} %get-tuple-element.43), calls=%async_computation.3 | async-start | bytes 917504 | tf_op jit(solution)/shard_map/all_to_all | solution.py:474
  57.8 10.2 %collective-permute-start.3 = (bf16[128,256]{1,0:T(8,128)(2,1)S(1)}, bf16[128,256]{1,0:T(8,128)(2,1)S(1)}, u32[]{:S(2)}, u32[]{:S(2)}) collective-permute-start(bf16[128,256]{1,0:T(8,128)(2,1)S(1)} %get-tuple-element.42), channel_id=1, source_target_pairs={{8,16},{24,32},{40,48},{56,64},{72,80},{88,96},{104,112},{120,128}... | collective-permute-start | bytes 196616 | tf_op jit(solution)/shard_map/ppermute | solution.py:553
  58.4 10.4 %collective-permute-start.2 = (bf16[192,256]{1,0:T(8,128)(2,1)S(1)}, bf16[192,256]{1,0:T(8,128)(2,1)S(1)}, u32[]{:S(2)}, u32[]{:S(2)}) collective-permute-start(bf16[192,256]{1,0:T(8,128)(2,1)S(1)} %get-tuple-element.41), channel_id=1, source_target_pairs={{0,8},{8,0},{16,24},{24,16},{32,40},{40,32},{48,56},{56,48},{64,72... | collective-permute-start | bytes 294920 | tf_op jit(solution)/shard_map/ppermute | solution.py:552

commit v17 on v15

--- a/solution.py
+++ b/solution.py
@@ -21,6 +21,7 @@
 COLUMN_LEVEL = {1: 5, 2: 6, 3: 6, 4: 7, 5: 7, 6: 7, 7: 7}
 FAR = 48
 SLOT = 112
+FIRST_Z = 7
 
 
 def dot(a, b, dims):
@@ -242,6 +243,7 @@
 ):
     index = lax.axis_index("seq")
     place = jnp.bitwise_and(index, 7)
+    slot = jnp.bitwise_xor(place, FIRST_Z)
     odd = jnp.bitwise_and(index, 1)
     peer_side = 1 - odd
     halo[peer_side] = p1_ref[:LEAF]
@@ -302,14 +304,14 @@
     for j in range(3):
         for s in range(8):
             at = 384 + LEAF * j + 16 * s
-            far_scr[s, 16 * j : 16 * (j + 1)] = cross_grad[at : at + 16]
+            far_scr[s ^ FIRST_Z, 16 * j : 16 * (j + 1)] = cross_grad[at : at + 16]
     copies = start_all([pltpu.make_async_copy(far_scr, zo_ref.at[:, pl.ds(0, FAR)], sems.at[0])])
-    mid_scr[place] = jnp.zeros((64, 2 * FEAT), BF16)
-    mid_scr[jnp.bitwise_xor(place, 1)] = cross_grad[:64]
-    mid_scr[jnp.bitwise_xor(place, 2)] = cross_grad[128:192]
-    mid_scr[jnp.bitwise_xor(place, 3)] = cross_grad[192:256]
+    mid_scr[slot] = jnp.zeros((64, 2 * FEAT), BF16)
+    mid_scr[jnp.bitwise_xor(slot, 1)] = cross_grad[:64]
+    mid_scr[jnp.bitwise_xor(slot, 2)] = cross_grad[128:192]
+    mid_scr[jnp.bitwise_xor(slot, 3)] = cross_grad[192:256]
     for i in range(4):
-        other = jnp.bitwise_xor(place, 4 + i)
+        other = jnp.bitwise_xor(slot, 4 + i)
         mid_scr[other, :32] = cross_grad[256 + 32 * i : 288 + 32 * i]
         mid_scr[other, 32:] = jnp.zeros((32, 2 * FEAT), BF16)
     copies += start_all([pltpu.make_async_copy(mid_scr, zo_ref.at[:, pl.ds(FAR, 64)], sems.at[1])])
@@ -396,7 +398,7 @@
 ):
     index = lax.axis_index("seq")
     column = jnp.right_shift(index, 3)
-    place = jnp.bitwise_and(index, 7)
+    place = jnp.bitwise_xor(jnp.bitwise_and(index, 7), FIRST_Z)
     odd = jnp.bitwise_and(index, 1)
     pieces = [z_ref[jnp.bitwise_xor(place, 1), FAR:], p1_ref[LEAF:]]
     maps = [spreading(0, 64, 2), spreading(64, 64, 2)]
@@ -461,6 +463,7 @@
     return jax.ShapeDtypeStruct(shape, dtype)
 
 
+BACKWARD_ROWS = [[8 * y + (p ^ FIRST_Z) for p in range(8)] for y in range(8)]
 ROW_GROUPS = [[8 * y + z for z in range(8)] for y in range(8)]
 COLUMN_GROUPS = [[8 * y + z for y in range(8)] for z in range(8)]
 
@@ -546,7 +549,7 @@
     )
     p1 = lax.ppermute(p1, "seq", peer)
     p2 = lax.ppermute(p2, "seq", beside)
-    zrecv = exchange(zsend, "seq", ROW_GROUPS)
+    zrecv = exchange(zsend, "seq", BACKWARD_ROWS)
     attended, nqg, tok, qsum = call(
         after_kernel,
         [sds(ROWS, FEAT), sds(ROWS, FEAT, dtype=F32), sds(ROWS, 256, dtype=F32)]

time: 99.2 us -> 97.3 us (0.981)
  blocking collectives: 48.2 us -> 46.4 us
    all_to_all x4, blocking collectives: 48.2 us -> 46.4 us  [exchange(): return lax.all_to_all(x, axis, 0, 0, axis_index_groups=groups, tiled=True)]
    all_to_all x2, waiting for transfers between devices: 3.28 us -> 1.67 us  [exchange(): return lax.all_to_all(x, axis, 0, 0, axis_index_groups=groups, tiled=True)]
    ppermute x2, waiting for transfers between devices: 7.46 us -> 8.64 us  [local(): p1 = lax.ppermute(p1, 'seq', peer)]
  transfers between devices with their start and end apart: 6 -> 6, of which waited for: 4 -> 3; matrix products, arithmetic and copies ran while one was open for 0% -> 0% of each run, Pallas kernels for 5% -> 5%
where the time goes in v17:
time: 97.3 us; the launch traced here: 96.7 us
  blocking collectives  46.4 us (48%)
  starting transfers between devices  26 us (27%)
  Pallas kernels  13.2 us (14%)
  waiting for transfers between devices  10.3 us (11%)
    all_to_all x4, blocking collectives, exchange(): return lax.all_to_all(x, axis, 0, 0, axis_index_groups=groups, tiled=True)  46.4 us
    all_to_all x2, starting transfers between devices, exchange(): return lax.all_to_all(x, axis, 0, 0, axis_index_groups=groups, tiled=True)  15.9 us
    pallas_call x9, Pallas kernels, call(): pl.pallas_call(kernel, out_shape=outs, in_specs=[pl.BlockSpec(memory_spac...  13.2 us
    ppermute x2, starting transfers between devices, local(): p1 = lax.ppermute(p1, 'seq', peer)  8.87 us
    ppermute x2, waiting for transfers between devices, local(): p1 = lax.ppermute(p1, 'seq', peer)  8.64 us
  transfers between devices with their start and end apart: 6, of which 3 were waited for; matrix products, arithmetic and copies ran while one was open for 0% of the time, Pallas kernels for 5%

profile of v17, /device:TPU:1, one launch (start us, length us, event | category | flops | bytes accessed | tf_op | source)
XLA Modules:
  0.0 96.7 jit_solution(2152934920240533900)
XLA Ops:
  0.6 0.0 copy-start.2
  0.6 1.9 %squares.1 = f32[8,16,128]{2,1,0:T(8,128)} custom-call(bf16[512,128]{1,0:T(8,128)(2,1)} %refs_2_.3, bf16[512,128]{1,0:T(8,128)(2,1)} %refs_3_.1, f32[1,128]{1,0:T(1,128)} %bitcast.2, f32[1,128]{1,0:T(1,128)} %bitcast.3), custom_call_target="tpu_custom_call" | custom-call | bytes 328704 | tf_op jit(solution)/shard_map/squares/pallas_call | solution.py:450
  2.5 0.0 copy-start
  2.6 15.1 %all_to_all.30.refs_0_.sum_ref = f32[8,16,128]{2,1,0:T(8,128)S(1)} all-to-all(f32[8,16,128]{2,1,0:T(8,128)} %squares.1), channel_id=1, replica_groups=mesh['seq'=64,'head'=8] {'head'}, dimensions={0} | all-to-all | bytes 131072 | tf_op jit(solution)/shard_map/all_to_all | solution.py:472
  17.7 0.0 copy-done.2
  17.7 0.5 norm.1
  18.2 9.6 %all_to_all.31.y_ref = bf16[8,16,256]{2,1,0:T(8,128)(2,1)S(1)} all-to-all(bf16[8,16,256]{2,1,0:T(8,128)(2,1)S(1)} %get-tuple-element.34), channel_id=1, replica_groups={{0,64,128,192,256,320,384,448},{8,72,136,200,264,328,392,456},{16,80,14..., dimensions={0} | all-to-all | bytes 131072 | tf_op jit(solution)/shard_map/all_to_all | solution.py:472
  27.8 0.9 rows.1
  28.7 0.0 copy-start.1
  28.7 0.0 copy-start.3
  28.7 10.1 %all-to-all-start.2 = ((bf16[8,112,256]{2,1,0:T(8,128)(2,1)}), bf16[8,112,256]{2,1,0:T(8,128)(2,1)S(1)}, u32[]{:S(2)}, u32[]{:S(2)}) async-start(bf16[8,112,256]{2,1,0:T(8,128)(2,1)} %rows.1), calls=%async_computation.2 | async-start | bytes 917504 | tf_op jit(solution)/shard_map/all_to_all | solution.py:472
  38.8 3.4 %collective-permute-start = (bf16[192,256]{1,0:T(8,128)(2,1)S(1)}, bf16[192,256]{1,0:T(8,128)(2,1)S(1)}, u32[]{:S(2)}, u32[]{:S(2)}) collective-permute-start(bf16[192,256]{1,0:T(8,128)(2,1)S(1)} %get-tuple-element.32), channel_id=1, source_target_pairs={{0,8},{8,0},{16,24},{24,16},{32,40},{40,32},{48,56},{56,48},{64,72... | collective-permute-start | bytes 294920 | tf_op jit(solution)/shard_map/ppermute | solution.py:504
  42.2 0.7 collective-permute-start.1
  42.8 0.0 copy-done.1
  42.8 0.0 copy-done.3
  42.9 0.9 near.1
  43.8 0.0 collective-permute-done.1.p2_ref
  43.8 6.6 %collective-permute-done.p1_ref = bf16[192,256]{1,0:T(8,128)(2,1)S(1)} collective-permute-done((bf16[192,256]{1,0:T(8,128)(2,1)S(1)}, bf16[192,256]{1,0:T(8,128)(2,1)S(1)}, u32[]{:S(2)}, u32[]{:S(2)}) %collective-permute-start) | collective-permute-done | bytes 98336 | tf_op jit(solution)/shard_map/ppermute | solution.py:504
  50.4 1.7 %all-to-all-done.2.z_ref = bf16[8,112,256]{2,1,0:T(8,128)(2,1)S(1)} async-done(((bf16[8,112,256]{2,1,0:T(8,128)(2,1)}), bf16[8,112,256]{2,1,0:T(8,128)(2,1)S(1)}, u32[]{:S(2)}, u32[]{:S(2)}) %all-to-all-start.2) | async-done | bytes 458784 | tf_op jit(solution)/shard_map/all_to_all | solution.py:472
  52.1 3.2 %attend.1 = (f32[4,8,256]{2,1,0:T(8,128)S(1)}, bf16[768,256]{1,0:T(8,128)(2,1)S(1)}, bf16[2,128,256]{2,1,0:T(8,128)(2,1)S(1)}, bf16[192,256]{1,0:T(8,128)(2,1)S(...) custom-call(bf16[512,128]{1,0:T(8,128)(2,1)S(1)} %get-tuple-element.30.qn_ref, ...), custom_call_target="tpu_custom_call" | custom-call | flops 805306368 | bytes 2097152 | tf_op jit(solution)/shard_map/attend/pallas_call | solution.py:450
  55.3 5.8 %all-to-all-start.3 = ((bf16[8,112,256]{2,1,0:T(8,128)(2,1)}), bf16[8,112,256]{2,1,0:T(8,128)(2,1)S(1)}, u32[]{:S(2)}, u32[]{:S(2)}) async-start(bf16[8,112,256]{2,1,0:T(8,128)(2,1)} %get-tuple-element.43), calls=%async_computation.3 | async-start | bytes 917504 | tf_op jit(solution)/shard_map/all_to_all | solution.py:472
  61.0 0.7 collective-permute-start.3
  61.7 5.5 %collective-permute-start.2 = (bf16[192,256]{1,0:T(8,128)(2,1)S(1)}, bf16[192,256]{1,0:T(8,128)(2,1)S(1)}, u32[]{:S(2)}, u32[]{:S(2)}) collective-permute-start(bf16[192,256]{1,0:T(8,128)(2,1)S(1)} %get-tuple-element.41), channel_id=1, source_target_pairs={{0,8},{8,0},{16,24},{24,16},{32,40},{40,32},{48,56},{56,48},{64,72... | collective-permute-start | bytes 294920 | tf_op jit(solution)/shard_map/ppermute | solution.py:550
  67.2 3.7 %after.1 = (bf16[512,128]{1,0:T(8,128)(2,1)}, f32[512,128]{1,0:T(8,128)S(1)}, f32[512,256]{1,0:T(8,128)S(1)}, f32[8,128]{1,0:T(8,128)S(1)}) custom-call(f32[4,8,256]{2,1,0:T(8,128)S(1)} %get-tuple-element.36.stat_ref, bf16[512,128]{1,0:T(8,128)(2,1)S(1)} %get-tuple-element.30.qn_ref, bf16[512,256]{1,0:T(8,128)(2,1)S(1)} %get-tuple-element.28.refs_2_.kv_ref, ...), custom_call_target="tpu_custom_call" | custom-call | flops 1677721600 | bytes 2330624 | tf_op jit(solution)/shard_map/after/pallas_call | solution.py:450
  71.0 0.0 collective-permute-done.3.p2_ref
  71.0 2.0 %collective-permute-done.2.p1_ref = bf16[192,256]{1,0:T(8,128)(2,1)S(1)} collective-permute-done((bf16[192,256]{1,0:T(8,128)(2,1)S(1)}, bf16[192,256]{1,0:T(8,128)(2,1)S(1)}, u32[]{:S(2)}, u32[]{:S(2)}) %collective-permute-start.2) | collective-permute-done | bytes 98336 | tf_op jit(solution)/shard_map/ppermute | solution.py:550
  73.0 0.0 all-to-all-done.3.z_ref
  73.0 0.2 columns.1
  73.2 9.7 %all_to_all.32.y_ref = bf16[8,16,256]{2,1,0:T(8,128)(2,1)S(1)} all-to-all(bf16[8,16,256]{2,1,0:T(8,128)(2,1)S(1)} %columns.1), channel_id=1, replica_groups={{0,64,128,192,256,320,384,448},{8,72,136,200,264,328,392,456},{16,80,14..., dimensions={0} | all-to-all | bytes 131072 | tf_op jit(solution)/shard_map/all_to_all | solution.py:472
  82.9 0.8 total.1
  83.7 11.9 %all_to_all.33.refs_1_ = f32[8,8,128]{2,1,0:T(8,128)S(1)} all-to-all(f32[8,8,128]{2,1,0:T(8,128)S(1)} %get-tuple-element.45), channel_id=1, replica_groups=mesh['seq'=64,'head'=8] {'head'}, dimensions={0} | all-to-all | bytes 65536 | tf_op jit(solution)/shard_map/all_to_all | solution.py:472
  95.7 1.0 %finish.1 = (bf16[512,128]{1,0:T(8,128)(2,1)}, bf16[512,128]{1,0:T(8,128)(2,1)}, bf16[512,128]{1,0:T(8,128)(2,1)}) custom-call(f32[8,16,128]{2,1,0:T(8,128)S(1)} %all_to_all.30.refs_0_.sum_ref, f32[8,8,128]{2,1,0:T(8,128)S(1)} %all_to_all.33.refs_1_, bf16[512,128]{1,0:T(8,128)(2,1)S(1)} %copy-done.1, bf16[512,128]{1,0:T(8,128)(2,1)S(1)} %copy-done, ...), custom_call_target="tpu_custom_call" | custom-call | bytes 1409024 | tf_op jit(solution)/shard_map/finish/pallas_call | solution.py:450
  (1 shorter events, 0.0 us)
Async XLA Ops:
  0.6 17.1 %copy-start.2 = (bf16[512,128]{1,0:T(8,128)(2,1)S(1)}, bf16[512,128]{1,0:T(8,128)(2,1)}, u32[]{:S(2)}) copy-start(bf16[512,128]{1,0:T(8,128)(2,1)} %refs_2_.2) | copy-start | bytes 393220
  2.5 15.1 %copy-start = (bf16[512,128]{1,0:T(8,128)(2,1)S(1)}, bf16[512,128]{1,0:T(8,128)(2,1)}, u32[]{:S(2)}) copy-start(bf16[512,128]{1,0:T(8,128)(2,1)} %refs_3_.1) | copy-start | bytes 393220
  28.7 14.2 %copy-start.1 = (bf16[512,128]{1,0:T(8,128)(2,1)S(1)}, bf16[512,128]{1,0:T(8,128)(2,1)}, u32[]{:S(2)}) copy-start(bf16[512,128]{1,0:T(8,128)(2,1)} %refs_2_.3) | copy-start | bytes 393220
  28.7 14.1 %copy-start.3 = (bf16[512,128]{1,0:T(8,128)(2,1)S(1)}, bf16[512,128]{1,0:T(8,128)(2,1)}, u32[]{:S(2)}) copy-start(bf16[512,128]{1,0:T(8,128)(2,1)} %g_ref.3) | copy-start | bytes 393220
  28.7 23.4 %all-to-all-start.2 = ((bf16[8,112,256]{2,1,0:T(8,128)(2,1)}), bf16[8,112,256]{2,1,0:T(8,128)(2,1)S(1)}, u32[]{:S(2)}, u32[]{:S(2)}) async-start(bf16[8,112,256]{2,1,0:T(8,128)(2,1)} %rows.1), calls=%async_computation.2 | async-start | bytes 917504 | tf_op jit(solution)/shard_map/all_to_all | solution.py:472
  38.8 11.6 %collective-permute-start = (bf16[192,256]{1,0:T(8,128)(2,1)S(1)}, bf16[192,256]{1,0:T(8,128)(2,1)S(1)}, u32[]{:S(2)}, u32[]{:S(2)}) collective-permute-start(bf16[192,256]{1,0:T(8,128)(2,1)S(1)} %get-tuple-element.32), channel_id=1, source_target_pairs={{0,8},{8,0},{16,24},{24,16},{32,40},{40,32},{48,56},{56,48},{64,72... | collective-permute-start | bytes 294920 | tf_op jit(solution)/shard_map/ppermute | solution.py:504
  42.2 1.6 %collective-permute-start.1 = (bf16[128,256]{1,0:T(8,128)(2,1)S(1)}, bf16[128,256]{1,0:T(8,128)(2,1)S(1)}, u32[]{:S(2)}, u32[]{:S(2)}) collective-permute-start(bf16[128,256]{1,0:T(8,128)(2,1)S(1)} %get-tuple-element.33), channel_id=1, source_target_pairs={{8,16},{24,32},{40,48},{56,64},{72,80},{88,96},{104,112},{120,128}... | collective-permute-start | bytes 196616 | tf_op jit(solution)/shard_map/ppermute | solution.py:505
  55.3 17.7 %all-to-all-start.3 = ((bf16[8,112,256]{2,1,0:T(8,128)(2,1)}), bf16[8,112,256]{2,1,0:T(8,128)(2,1)S(1)}, u32[]{:S(2)}, u32[]{:S(2)}) async-start(bf16[8,112,256]{2,1,0:T(8,128)(2,1)} %get-tuple-element.43), calls=%async_computation.3 | async-start | bytes 917504 | tf_op jit(solution)/shard_map/all_to_all | solution.py:472
  61.0 9.9 %collective-permute-start.3 = (bf16[128,256]{1,0:T(8,128)(2,1)S(1)}, bf16[128,256]{1,0:T(8,128)(2,1)S(1)}, u32[]{:S(2)}, u32[]{:S(2)}) collective-permute-start(bf16[128,256]{1,0:T(8,128)(2,1)S(1)} %get-tuple-element.42), channel_id=1, source_target_pairs={{8,16},{24,32},{40,48},{56,64},{72,80},{88,96},{104,112},{120,128}... | collective-permute-start | bytes 196616 | tf_op jit(solution)/shard_map/ppermute | solution.py:551
  61.7 11.3 %collective-permute-start.2 = (bf16[192,256]{1,0:T(8,128)(2,1)S(1)}, bf16[192,256]{1,0:T(8,128)(2,1)S(1)}, u32[]{:S(2)}, u32[]{:S(2)}) collective-permute-start(bf16[192,256]{1,0:T(8,128)(2,1)S(1)} %get-tuple-element.41), channel_id=1, source_target_pairs={{0,8},{8,0},{16,24},{24,16},{32,40},{40,32},{48,56},{56,48},{64,72... | collective-permute-start | bytes 294920 | tf_op jit(solution)/shard_map/ppermute | solution.py:550

commit v18 on v17

--- a/solution.py
+++ b/solution.py
@@ -581,7 +581,8 @@
         ],
         name="total",
     )
-    inner = exchange(inner, "head")
+    odd_first = [[p ^ 1 for p in range(heads)]] if heads > 1 else None
+    inner = exchange(inner, "head", odd_first)
     query_grad, key_grad, value_grad = call(
         lambda *refs: finish_kernel(width, *refs),
         [sds(ROWS, FEAT), sds(ROWS, FEAT), sds(ROWS, FEAT)],

time: 97.3 us -> 96.8 us (level)
  no operation moved by 1% of the time
where the time goes in v18:
time: 96.8 us; the launch traced here: 96.3 us
  blocking collectives  45.9 us (47%)
  starting transfers between devices  26 us (27%)
  Pallas kernels  13.2 us (14%)
  waiting for transfers between devices  10.3 us (11%)
    all_to_all x4, blocking collectives, exchange(): return lax.all_to_all(x, axis, 0, 0, axis_index_groups=groups, tiled=True)  45.9 us
    all_to_all x2, starting transfers between devices, exchange(): return lax.all_to_all(x, axis, 0, 0, axis_index_groups=groups, tiled=True)  15.9 us
    pallas_call x9, Pallas kernels, call(): pl.pallas_call(kernel, out_shape=outs, in_specs=[pl.BlockSpec(memory_spac...  13.2 us
    ppermute x2, starting transfers between devices, local(): p1 = lax.ppermute(p1, 'seq', peer)  8.87 us
    ppermute x2, waiting for transfers between devices, local(): p1 = lax.ppermute(p1, 'seq', peer)  8.64 us
  transfers between devices with their start and end apart: 6, of which 3 were waited for; matrix products, arithmetic and copies ran while one was open for 0% of the time, Pallas kernels for 5%

profile of v18, /device:TPU:1, one launch (start us, length us, event | category | flops | bytes accessed | tf_op | source)
XLA Modules:
  0.0 96.3 jit_solution(15672096016218289691)
XLA Ops:
  0.6 0.0 copy-start.2
  0.6 1.9 %squares.1 = f32[8,16,128]{2,1,0:T(8,128)} custom-call(bf16[512,128]{1,0:T(8,128)(2,1)} %refs_2_.3, bf16[512,128]{1,0:T(8,128)(2,1)} %refs_3_.1, f32[1,128]{1,0:T(1,128)} %bitcast.2, f32[1,128]{1,0:T(1,128)} %bitcast.3), custom_call_target="tpu_custom_call" | custom-call | bytes 328704 | tf_op jit(solution)/shard_map/squares/pallas_call | solution.py:450
  2.5 0.0 copy-start
  2.6 15.1 %all_to_all.30.refs_0_.sum_ref = f32[8,16,128]{2,1,0:T(8,128)S(1)} all-to-all(f32[8,16,128]{2,1,0:T(8,128)} %squares.1), channel_id=1, replica_groups=mesh['seq'=64,'head'=8] {'head'}, dimensions={0} | all-to-all | bytes 131072 | tf_op jit(solution)/shard_map/all_to_all | solution.py:472
  17.7 0.0 copy-done.2
  17.7 0.5 norm.1
  18.2 9.6 %all_to_all.31.y_ref = bf16[8,16,256]{2,1,0:T(8,128)(2,1)S(1)} all-to-all(bf16[8,16,256]{2,1,0:T(8,128)(2,1)S(1)} %get-tuple-element.34), channel_id=1, replica_groups={{0,64,128,192,256,320,384,448},{8,72,136,200,264,328,392,456},{16,80,14..., dimensions={0} | all-to-all | bytes 131072 | tf_op jit(solution)/shard_map/all_to_all | solution.py:472
  27.8 0.9 rows.1
  28.7 0.0 copy-start.1
  28.7 0.0 copy-start.3
  28.7 10.1 %all-to-all-start.2 = ((bf16[8,112,256]{2,1,0:T(8,128)(2,1)}), bf16[8,112,256]{2,1,0:T(8,128)(2,1)S(1)}, u32[]{:S(2)}, u32[]{:S(2)}) async-start(bf16[8,112,256]{2,1,0:T(8,128)(2,1)} %rows.1), calls=%async_computation.2 | async-start | bytes 917504 | tf_op jit(solution)/shard_map/all_to_all | solution.py:472
  38.8 3.4 %collective-permute-start = (bf16[192,256]{1,0:T(8,128)(2,1)S(1)}, bf16[192,256]{1,0:T(8,128)(2,1)S(1)}, u32[]{:S(2)}, u32[]{:S(2)}) collective-permute-start(bf16[192,256]{1,0:T(8,128)(2,1)S(1)} %get-tuple-element.32), channel_id=1, source_target_pairs={{0,8},{8,0},{16,24},{24,16},{32,40},{40,32},{48,56},{56,48},{64,72... | collective-permute-start | bytes 294920 | tf_op jit(solution)/shard_map/ppermute | solution.py:504
  42.2 0.7 collective-permute-start.1
  42.8 0.0 copy-done.1
  42.8 0.0 copy-done.3
  42.9 0.9 near.1
  43.8 0.0 collective-permute-done.1.p2_ref
  43.8 6.6 %collective-permute-done.p1_ref = bf16[192,256]{1,0:T(8,128)(2,1)S(1)} collective-permute-done((bf16[192,256]{1,0:T(8,128)(2,1)S(1)}, bf16[192,256]{1,0:T(8,128)(2,1)S(1)}, u32[]{:S(2)}, u32[]{:S(2)}) %collective-permute-start) | collective-permute-done | bytes 98336 | tf_op jit(solution)/shard_map/ppermute | solution.py:504
  50.4 1.7 %all-to-all-done.2.z_ref = bf16[8,112,256]{2,1,0:T(8,128)(2,1)S(1)} async-done(((bf16[8,112,256]{2,1,0:T(8,128)(2,1)}), bf16[8,112,256]{2,1,0:T(8,128)(2,1)S(1)}, u32[]{:S(2)}, u32[]{:S(2)}) %all-to-all-start.2) | async-done | bytes 458784 | tf_op jit(solution)/shard_map/all_to_all | solution.py:472
  52.1 3.2 %attend.1 = (f32[4,8,256]{2,1,0:T(8,128)S(1)}, bf16[768,256]{1,0:T(8,128)(2,1)S(1)}, bf16[2,128,256]{2,1,0:T(8,128)(2,1)S(1)}, bf16[192,256]{1,0:T(8,128)(2,1)S(...) custom-call(bf16[512,128]{1,0:T(8,128)(2,1)S(1)} %get-tuple-element.30.qn_ref, ...), custom_call_target="tpu_custom_call" | custom-call | flops 805306368 | bytes 2097152 | tf_op jit(solution)/shard_map/attend/pallas_call | solution.py:450
  55.3 5.8 %all-to-all-start.3 = ((bf16[8,112,256]{2,1,0:T(8,128)(2,1)}), bf16[8,112,256]{2,1,0:T(8,128)(2,1)S(1)}, u32[]{:S(2)}, u32[]{:S(2)}) async-start(bf16[8,112,256]{2,1,0:T(8,128)(2,1)} %get-tuple-element.43), calls=%async_computation.3 | async-start | bytes 917504 | tf_op jit(solution)/shard_map/all_to_all | solution.py:472
  61.0 0.7 collective-permute-start.3
  61.7 5.5 %collective-permute-start.2 = (bf16[192,256]{1,0:T(8,128)(2,1)S(1)}, bf16[192,256]{1,0:T(8,128)(2,1)S(1)}, u32[]{:S(2)}, u32[]{:S(2)}) collective-permute-start(bf16[192,256]{1,0:T(8,128)(2,1)S(1)} %get-tuple-element.41), channel_id=1, source_target_pairs={{0,8},{8,0},{16,24},{24,16},{32,40},{40,32},{48,56},{56,48},{64,72... | collective-permute-start | bytes 294920 | tf_op jit(solution)/shard_map/ppermute | solution.py:550
  67.2 3.7 %after.1 = (bf16[512,128]{1,0:T(8,128)(2,1)}, f32[512,128]{1,0:T(8,128)S(1)}, f32[512,256]{1,0:T(8,128)S(1)}, f32[8,128]{1,0:T(8,128)S(1)}) custom-call(f32[4,8,256]{2,1,0:T(8,128)S(1)} %get-tuple-element.36.stat_ref, bf16[512,128]{1,0:T(8,128)(2,1)S(1)} %get-tuple-element.30.qn_ref, bf16[512,256]{1,0:T(8,128)(2,1)S(1)} %get-tuple-element.28.refs_2_.kv_ref, ...), custom_call_target="tpu_custom_call" | custom-call | flops 1677721600 | bytes 2330624 | tf_op jit(solution)/shard_map/after/pallas_call | solution.py:450
  71.0 0.0 collective-permute-done.3.p2_ref
  71.0 2.0 %collective-permute-done.2.p1_ref = bf16[192,256]{1,0:T(8,128)(2,1)S(1)} collective-permute-done((bf16[192,256]{1,0:T(8,128)(2,1)S(1)}, bf16[192,256]{1,0:T(8,128)(2,1)S(1)}, u32[]{:S(2)}, u32[]{:S(2)}) %collective-permute-start.2) | collective-permute-done | bytes 98336 | tf_op jit(solution)/shard_map/ppermute | solution.py:550
  73.0 0.0 all-to-all-done.3.z_ref
  73.0 0.2 columns.1
  73.2 9.7 %all_to_all.32.y_ref = bf16[8,16,256]{2,1,0:T(8,128)(2,1)S(1)} all-to-all(bf16[8,16,256]{2,1,0:T(8,128)(2,1)S(1)} %columns.1), channel_id=1, replica_groups={{0,64,128,192,256,320,384,448},{8,72,136,200,264,328,392,456},{16,80,14..., dimensions={0} | all-to-all | bytes 131072 | tf_op jit(solution)/shard_map/all_to_all | solution.py:472
  82.9 0.8 total.1
  83.7 11.5 %all_to_all.33.refs_1_ = f32[8,8,128]{2,1,0:T(8,128)S(1)} all-to-all(f32[8,8,128]{2,1,0:T(8,128)S(1)} %get-tuple-element.45), channel_id=1, replica_groups={{1,0,3,2,5,4,7,6},{9,8,11,10,13,12,15,14},{17,16,19,18,21,20,23,22},{25..., dimensions={0} | all-to-all | bytes 65536 | tf_op jit(solution)/shard_map/all_to_all | solution.py:472
  95.2 1.0 %finish.1 = (bf16[512,128]{1,0:T(8,128)(2,1)}, bf16[512,128]{1,0:T(8,128)(2,1)}, bf16[512,128]{1,0:T(8,128)(2,1)}) custom-call(f32[8,16,128]{2,1,0:T(8,128)S(1)} %all_to_all.30.refs_0_.sum_ref, f32[8,8,128]{2,1,0:T(8,128)S(1)} %all_to_all.33.refs_1_, bf16[512,128]{1,0:T(8,128)(2,1)S(1)} %copy-done.1, bf16[512,128]{1,0:T(8,128)(2,1)S(1)} %copy-done, ...), custom_call_target="tpu_custom_call" | custom-call | bytes 1409024 | tf_op jit(solution)/shard_map/finish/pallas_call | solution.py:450
  (1 shorter events, 0.0 us)
Async XLA Ops:
  0.6 17.1 %copy-start.2 = (bf16[512,128]{1,0:T(8,128)(2,1)S(1)}, bf16[512,128]{1,0:T(8,128)(2,1)}, u32[]{:S(2)}) copy-start(bf16[512,128]{1,0:T(8,128)(2,1)} %refs_2_.2) | copy-start | bytes 393220
  2.5 15.1 %copy-start = (bf16[512,128]{1,0:T(8,128)(2,1)S(1)}, bf16[512,128]{1,0:T(8,128)(2,1)}, u32[]{:S(2)}) copy-start(bf16[512,128]{1,0:T(8,128)(2,1)} %refs_3_.1) | copy-start | bytes 393220
  28.7 14.2 %copy-start.1 = (bf16[512,128]{1,0:T(8,128)(2,1)S(1)}, bf16[512,128]{1,0:T(8,128)(2,1)}, u32[]{:S(2)}) copy-start(bf16[512,128]{1,0:T(8,128)(2,1)} %refs_2_.3) | copy-start | bytes 393220
  28.7 14.1 %copy-start.3 = (bf16[512,128]{1,0:T(8,128)(2,1)S(1)}, bf16[512,128]{1,0:T(8,128)(2,1)}, u32[]{:S(2)}) copy-start(bf16[512,128]{1,0:T(8,128)(2,1)} %g_ref.3) | copy-start | bytes 393220
  28.7 23.4 %all-to-all-start.2 = ((bf16[8,112,256]{2,1,0:T(8,128)(2,1)}), bf16[8,112,256]{2,1,0:T(8,128)(2,1)S(1)}, u32[]{:S(2)}, u32[]{:S(2)}) async-start(bf16[8,112,256]{2,1,0:T(8,128)(2,1)} %rows.1), calls=%async_computation.2 | async-start | bytes 917504 | tf_op jit(solution)/shard_map/all_to_all | solution.py:472
  38.8 11.6 %collective-permute-start = (bf16[192,256]{1,0:T(8,128)(2,1)S(1)}, bf16[192,256]{1,0:T(8,128)(2,1)S(1)}, u32[]{:S(2)}, u32[]{:S(2)}) collective-permute-start(bf16[192,256]{1,0:T(8,128)(2,1)S(1)} %get-tuple-element.32), channel_id=1, source_target_pairs={{0,8},{8,0},{16,24},{24,16},{32,40},{40,32},{48,56},{56,48},{64,72... | collective-permute-start | bytes 294920 | tf_op jit(solution)/shard_map/ppermute | solution.py:504
  42.2 1.6 %collective-permute-start.1 = (bf16[128,256]{1,0:T(8,128)(2,1)S(1)}, bf16[128,256]{1,0:T(8,128)(2,1)S(1)}, u32[]{:S(2)}, u32[]{:S(2)}) collective-permute-start(bf16[128,256]{1,0:T(8,128)(2,1)S(1)} %get-tuple-element.33), channel_id=1, source_target_pairs={{8,16},{24,32},{40,48},{56,64},{72,80},{88,96},{104,112},{120,128}... | collective-permute-start | bytes 196616 | tf_op jit(solution)/shard_map/ppermute | solution.py:505
  55.3 17.7 %all-to-all-start.3 = ((bf16[8,112,256]{2,1,0:T(8,128)(2,1)}), bf16[8,112,256]{2,1,0:T(8,128)(2,1)S(1)}, u32[]{:S(2)}, u32[]{:S(2)}) async-start(bf16[8,112,256]{2,1,0:T(8,128)(2,1)} %get-tuple-element.43), calls=%async_computation.3 | async-start | bytes 917504 | tf_op jit(solution)/shard_map/all_to_all | solution.py:472
  61.0 9.9 %collective-permute-start.3 = (bf16[128,256]{1,0:T(8,128)(2,1)S(1)}, bf16[128,256]{1,0:T(8,128)(2,1)S(1)}, u32[]{:S(2)}, u32[]{:S(2)}) collective-permute-start(bf16[128,256]{1,0:T(8,128)(2,1)S(1)} %get-tuple-element.42), channel_id=1, source_target_pairs={{8,16},{24,32},{40,48},{56,64},{72,80},{88,96},{104,112},{120,128}... | collective-permute-start | bytes 196616 | tf_op jit(solution)/shard_map/ppermute | solution.py:551
  61.7 11.3 %collective-permute-start.2 = (bf16[192,256]{1,0:T(8,128)(2,1)S(1)}, bf16[192,256]{1,0:T(8,128)(2,1)S(1)}, u32[]{:S(2)}, u32[]{:S(2)}) collective-permute-start(bf16[192,256]{1,0:T(8,128)(2,1)S(1)} %get-tuple-element.41), channel_id=1, source_target_pairs={{0,8},{8,0},{16,24},{24,16},{32,40},{40,32},{48,56},{56,48},{64,72... | collective-permute-start | bytes 294920 | tf_op jit(solution)/shard_map/ppermute | solution.py:550

commit v19 on v18

--- a/solution.py
+++ b/solution.py
@@ -22,6 +22,7 @@
 FAR = 48
 SLOT = 112
 FIRST_Z = 7
+FIRST_Y = 5
 
 
 def dot(a, b, dims):
@@ -104,7 +105,7 @@
 
 def norm_kernel(width, sum_ref, k_ref, v_ref, kv_ref, one_ref, lv_ref, y_ref, p1_ref, p2_ref):
     index = lax.axis_index("seq")
-    column = jnp.right_shift(index, 3)
+    column = jnp.bitwise_xor(jnp.right_shift(index, 3), FIRST_Y)
     odd = jnp.bitwise_and(index, 1)
     gain = sum_ref[lax.axis_index("head"), 9:10]
     kv_ref[:, :FEAT] = (
@@ -140,7 +141,7 @@
 
 def row_kernel(y_ref, lv_ref, out_ref, far_scr, mid_scr, sems):
     index = lax.axis_index("seq")
-    column = jnp.right_shift(index, 3)
+    column = jnp.bitwise_xor(jnp.right_shift(index, 3), FIRST_Y)
     place = jnp.bitwise_and(index, 7)
     mid_scr[place] = jnp.zeros((64, 2 * FEAT), BF16)
     for d in range(1, 8):
@@ -381,7 +382,7 @@
 
 
 def column_kernel(z_ref, p1_ref, p2_ref, tok_ref, out_ref, far_rows, sem):
-    column = jnp.right_shift(lax.axis_index("seq"), 3)
+    column = jnp.bitwise_xor(jnp.right_shift(lax.axis_index("seq"), 3), FIRST_Y)
     copy = pltpu.make_async_copy(z_ref.at[:, pl.ds(0, FAR)], far_rows, sem)
     copy.start()
     copy.wait()
@@ -397,7 +398,7 @@
     nkg_ref, vg_ref, sum_ref, acc,
 ):
     index = lax.axis_index("seq")
-    column = jnp.right_shift(index, 3)
+    column = jnp.bitwise_xor(jnp.right_shift(index, 3), FIRST_Y)
     place = jnp.bitwise_xor(jnp.bitwise_and(index, 7), FIRST_Z)
     odd = jnp.bitwise_and(index, 1)
     pieces = [z_ref[jnp.bitwise_xor(place, 1), FAR:], p1_ref[LEAF:]]
@@ -465,7 +466,7 @@
 
 BACKWARD_ROWS = [[8 * y + (p ^ FIRST_Z) for p in range(8)] for y in range(8)]
 ROW_GROUPS = [[8 * y + z for z in range(8)] for y in range(8)]
-COLUMN_GROUPS = [[8 * y + z for y in range(8)] for z in range(8)]
+COLUMN_GROUPS = [[8 * (p ^ FIRST_Y) + z for p in range(8)] for z in range(8)]
 
 
 def exchange(x, axis, groups=None):

time: 96.8 us -> 93.2 us (0.963)
  starting transfers between devices: 26 us -> 23.3 us
  blocking collectives: 45.9 us -> 44.3 us
    all_to_all x2, starting transfers between devices: 15.9 us -> 13.1 us  [exchange(): return lax.all_to_all(x, axis, 0, 0, axis_index_groups=groups, tiled=True)]
    all_to_all x4, blocking collectives: 45.9 us -> 44.3 us  [exchange(): return lax.all_to_all(x, axis, 0, 0, axis_index_groups=groups, tiled=True)]
where the time goes in v19:
time: 93.2 us; the launch traced here: 92.6 us
  blocking collectives  44.3 us (48%)
  starting transfers between devices  23.3 us (25%)
  Pallas kernels  13.2 us (14%)
  waiting for transfers between devices  11.1 us (12%)
    all_to_all x4, blocking collectives, exchange(): return lax.all_to_all(x, axis, 0, 0, axis_index_groups=groups, tiled=True)  44.3 us
    pallas_call x9, Pallas kernels, call(): pl.pallas_call(kernel, out_shape=outs, in_specs=[pl.BlockSpec(memory_spac...  13.2 us
    all_to_all x2, starting transfers between devices, exchange(): return lax.all_to_all(x, axis, 0, 0, axis_index_groups=groups, tiled=True)  13.1 us
    ppermute x2, waiting for transfers between devices, local(): p1 = lax.ppermute(p1, 'seq', peer)  9.21 us
    ppermute x2, starting transfers between devices, local(): p1 = lax.ppermute(p1, 'seq', peer)  8.87 us
  transfers between devices with their start and end apart: 6, of which 3 were waited for; matrix products, arithmetic and copies ran while one was open for 0% of the time, Pallas kernels for 5%

profile of v19, /device:TPU:1, one launch (start us, length us, event | category | flops | bytes accessed | tf_op | source)
XLA Modules:
  0.0 92.6 jit_solution(13002438292579044330)
XLA Ops:
  0.6 0.0 copy-start.2
  0.6 1.9 %squares.1 = f32[8,16,128]{2,1,0:T(8,128)} custom-call(bf16[512,128]{1,0:T(8,128)(2,1)} %refs_2_.3, bf16[512,128]{1,0:T(8,128)(2,1)} %refs_3_.1, f32[1,128]{1,0:T(1,128)} %bitcast.2, f32[1,128]{1,0:T(1,128)} %bitcast.3), custom_call_target="tpu_custom_call" | custom-call | bytes 328704 | tf_op jit(solution)/shard_map/squares/pallas_call | solution.py:451
  2.5 0.0 copy-start
  2.6 15.1 %all_to_all.30.refs_0_.sum_ref = f32[8,16,128]{2,1,0:T(8,128)S(1)} all-to-all(f32[8,16,128]{2,1,0:T(8,128)} %squares.1), channel_id=1, replica_groups=mesh['seq'=64,'head'=8] {'head'}, dimensions={0} | all-to-all | bytes 131072 | tf_op jit(solution)/shard_map/all_to_all | solution.py:473
  17.7 0.0 copy-done.2
  17.7 0.0 copy-done
  17.7 0.5 norm.1
  18.2 8.7 %all_to_all.31.y_ref = bf16[8,16,256]{2,1,0:T(8,128)(2,1)S(1)} all-to-all(bf16[8,16,256]{2,1,0:T(8,128)(2,1)S(1)} %get-tuple-element.34), channel_id=1, replica_groups={{320,256,448,384,64,0,192,128},{328,264,456,392,72,8,200,136},{336,272,..., dimensions={0} | all-to-all | bytes 131072 | tf_op jit(solution)/shard_map/all_to_all | solution.py:473
  26.9 0.9 rows.1
  27.8 0.0 copy-start.1
  27.8 0.0 copy-start.3
  27.8 7.4 %all-to-all-start.2 = ((bf16[8,112,256]{2,1,0:T(8,128)(2,1)}), bf16[8,112,256]{2,1,0:T(8,128)(2,1)S(1)}, u32[]{:S(2)}, u32[]{:S(2)}) async-start(bf16[8,112,256]{2,1,0:T(8,128)(2,1)} %rows.1), calls=%async_computation.2 | async-start | bytes 917504 | tf_op jit(solution)/shard_map/all_to_all | solution.py:473
  35.2 3.4 %collective-permute-start = (bf16[192,256]{1,0:T(8,128)(2,1)S(1)}, bf16[192,256]{1,0:T(8,128)(2,1)S(1)}, u32[]{:S(2)}, u32[]{:S(2)}) collective-permute-start(bf16[192,256]{1,0:T(8,128)(2,1)S(1)} %get-tuple-element.32), channel_id=1, source_target_pairs={{0,8},{8,0},{16,24},{24,16},{32,40},{40,32},{48,56},{56,48},{64,72... | collective-permute-start | bytes 294920 | tf_op jit(solution)/shard_map/ppermute | solution.py:505
  38.6 0.7 collective-permute-start.1
  39.3 0.0 copy-done.1
  39.3 0.9 near.1
  40.2 0.0 collective-permute-done.1.p2_ref
  40.2 7.0 %collective-permute-done.p1_ref = bf16[192,256]{1,0:T(8,128)(2,1)S(1)} collective-permute-done((bf16[192,256]{1,0:T(8,128)(2,1)S(1)}, bf16[192,256]{1,0:T(8,128)(2,1)S(1)}, u32[]{:S(2)}, u32[]{:S(2)}) %collective-permute-start) | collective-permute-done | bytes 98336 | tf_op jit(solution)/shard_map/ppermute | solution.py:505
  47.2 1.8 %all-to-all-done.2.z_ref = bf16[8,112,256]{2,1,0:T(8,128)(2,1)S(1)} async-done(((bf16[8,112,256]{2,1,0:T(8,128)(2,1)}), bf16[8,112,256]{2,1,0:T(8,128)(2,1)S(1)}, u32[]{:S(2)}, u32[]{:S(2)}) %all-to-all-start.2) | async-done | bytes 458784 | tf_op jit(solution)/shard_map/all_to_all | solution.py:473
  49.0 3.2 %attend.1 = (f32[4,8,256]{2,1,0:T(8,128)S(1)}, bf16[768,256]{1,0:T(8,128)(2,1)S(1)}, bf16[2,128,256]{2,1,0:T(8,128)(2,1)S(1)}, bf16[192,256]{1,0:T(8,128)(2,1)S(...) custom-call(bf16[512,128]{1,0:T(8,128)(2,1)S(1)} %get-tuple-element.30.qn_ref, ...), custom_call_target="tpu_custom_call" | custom-call | flops 805306368 | bytes 2097152 | tf_op jit(solution)/shard_map/attend/pallas_call | solution.py:451
  52.2 5.6 %all-to-all-start.3 = ((bf16[8,112,256]{2,1,0:T(8,128)(2,1)}), bf16[8,112,256]{2,1,0:T(8,128)(2,1)S(1)}, u32[]{:S(2)}, u32[]{:S(2)}) async-start(bf16[8,112,256]{2,1,0:T(8,128)(2,1)} %get-tuple-element.43), calls=%async_computation.3 | async-start | bytes 917504 | tf_op jit(solution)/shard_map/all_to_all | solution.py:473
  57.9 0.7 collective-permute-start.3
  58.5 5.5 %collective-permute-start.2 = (bf16[192,256]{1,0:T(8,128)(2,1)S(1)}, bf16[192,256]{1,0:T(8,128)(2,1)S(1)}, u32[]{:S(2)}, u32[]{:S(2)}) collective-permute-start(bf16[192,256]{1,0:T(8,128)(2,1)S(1)} %get-tuple-element.41), channel_id=1, source_target_pairs={{0,8},{8,0},{16,24},{24,16},{32,40},{40,32},{48,56},{56,48},{64,72... | collective-permute-start | bytes 294920 | tf_op jit(solution)/shard_map/ppermute | solution.py:551
  64.1 3.7 %after.1 = (bf16[512,128]{1,0:T(8,128)(2,1)}, f32[512,128]{1,0:T(8,128)S(1)}, f32[512,256]{1,0:T(8,128)S(1)}, f32[8,128]{1,0:T(8,128)S(1)}) custom-call(f32[4,8,256]{2,1,0:T(8,128)S(1)} %get-tuple-element.36.stat_ref, bf16[512,128]{1,0:T(8,128)(2,1)S(1)} %get-tuple-element.30.qn_ref, bf16[512,256]{1,0:T(8,128)(2,1)S(1)} %get-tuple-element.28.refs_2_.kv_ref, ...), custom_call_target="tpu_custom_call" | custom-call | flops 1677721600 | bytes 2330624 | tf_op jit(solution)/shard_map/after/pallas_call | solution.py:451
  67.8 0.0 collective-permute-done.3.p2_ref
  67.8 2.2 %collective-permute-done.2.p1_ref = bf16[192,256]{1,0:T(8,128)(2,1)S(1)} collective-permute-done((bf16[192,256]{1,0:T(8,128)(2,1)S(1)}, bf16[192,256]{1,0:T(8,128)(2,1)S(1)}, u32[]{:S(2)}, u32[]{:S(2)}) %collective-permute-start.2) | collective-permute-done | bytes 98336 | tf_op jit(solution)/shard_map/ppermute | solution.py:551
  70.0 0.0 all-to-all-done.3.z_ref
  70.0 0.2 columns.1
  70.2 9.3 %all_to_all.32.y_ref = bf16[8,16,256]{2,1,0:T(8,128)(2,1)S(1)} all-to-all(bf16[8,16,256]{2,1,0:T(8,128)(2,1)S(1)} %columns.1), channel_id=1, replica_groups={{320,256,448,384,64,0,192,128},{328,264,456,392,72,8,200,136},{336,272,..., dimensions={0} | all-to-all | bytes 131072 | tf_op jit(solution)/shard_map/all_to_all | solution.py:473
  79.5 0.8 total.1
  80.3 11.3 %all_to_all.33.refs_1_ = f32[8,8,128]{2,1,0:T(8,128)S(1)} all-to-all(f32[8,8,128]{2,1,0:T(8,128)S(1)} %get-tuple-element.45), channel_id=1, replica_groups={{1,0,3,2,5,4,7,6},{9,8,11,10,13,12,15,14},{17,16,19,18,21,20,23,22},{25..., dimensions={0} | all-to-all | bytes 65536 | tf_op jit(solution)/shard_map/all_to_all | solution.py:473
  91.6 1.0 %finish.1 = (bf16[512,128]{1,0:T(8,128)(2,1)}, bf16[512,128]{1,0:T(8,128)(2,1)}, bf16[512,128]{1,0:T(8,128)(2,1)}) custom-call(f32[8,16,128]{2,1,0:T(8,128)S(1)} %all_to_all.30.refs_0_.sum_ref, f32[8,8,128]{2,1,0:T(8,128)S(1)} %all_to_all.33.refs_1_, bf16[512,128]{1,0:T(8,128)(2,1)S(1)} %copy-done.1, bf16[512,128]{1,0:T(8,128)(2,1)S(1)} %copy-done, ...), custom_call_target="tpu_custom_call" | custom-call | bytes 1409024 | tf_op jit(solution)/shard_map/finish/pallas_call | solution.py:451
  (1 shorter events, 0.0 us)
Async XLA Ops:
  0.6 17.1 %copy-start.2 = (bf16[512,128]{1,0:T(8,128)(2,1)S(1)}, bf16[512,128]{1,0:T(8,128)(2,1)}, u32[]{:S(2)}) copy-start(bf16[512,128]{1,0:T(8,128)(2,1)} %refs_2_.2) | copy-start | bytes 393220
  2.5 15.1 %copy-start = (bf16[512,128]{1,0:T(8,128)(2,1)S(1)}, bf16[512,128]{1,0:T(8,128)(2,1)}, u32[]{:S(2)}) copy-start(bf16[512,128]{1,0:T(8,128)(2,1)} %refs_3_.1) | copy-start | bytes 393220
  27.8 11.5 %copy-start.1 = (bf16[512,128]{1,0:T(8,128)(2,1)S(1)}, bf16[512,128]{1,0:T(8,128)(2,1)}, u32[]{:S(2)}) copy-start(bf16[512,128]{1,0:T(8,128)(2,1)} %refs_2_.3) | copy-start | bytes 393220
  27.8 11.5 %copy-start.3 = (bf16[512,128]{1,0:T(8,128)(2,1)S(1)}, bf16[512,128]{1,0:T(8,128)(2,1)}, u32[]{:S(2)}) copy-start(bf16[512,128]{1,0:T(8,128)(2,1)} %g_ref.3) | copy-start | bytes 393220
  27.8 21.2 %all-to-all-start.2 = ((bf16[8,112,256]{2,1,0:T(8,128)(2,1)}), bf16[8,112,256]{2,1,0:T(8,128)(2,1)S(1)}, u32[]{:S(2)}, u32[]{:S(2)}) async-start(bf16[8,112,256]{2,1,0:T(8,128)(2,1)} %rows.1), calls=%async_computation.2 | async-start | bytes 917504 | tf_op jit(solution)/shard_map/all_to_all | solution.py:473
  35.2 12.0 %collective-permute-start = (bf16[192,256]{1,0:T(8,128)(2,1)S(1)}, bf16[192,256]{1,0:T(8,128)(2,1)S(1)}, u32[]{:S(2)}, u32[]{:S(2)}) collective-permute-start(bf16[192,256]{1,0:T(8,128)(2,1)S(1)} %get-tuple-element.32), channel_id=1, source_target_pairs={{0,8},{8,0},{16,24},{24,16},{32,40},{40,32},{48,56},{56,48},{64,72... | collective-permute-start | bytes 294920 | tf_op jit(solution)/shard_map/ppermute | solution.py:505
  38.6 1.6 %collective-permute-start.1 = (bf16[128,256]{1,0:T(8,128)(2,1)S(1)}, bf16[128,256]{1,0:T(8,128)(2,1)S(1)}, u32[]{:S(2)}, u32[]{:S(2)}) collective-permute-start(bf16[128,256]{1,0:T(8,128)(2,1)S(1)} %get-tuple-element.33), channel_id=1, source_target_pairs={{8,16},{24,32},{40,48},{56,64},{72,80},{88,96},{104,112},{120,128}... | collective-permute-start | bytes 196616 | tf_op jit(solution)/shard_map/ppermute | solution.py:506
  52.2 17.8 %all-to-all-start.3 = ((bf16[8,112,256]{2,1,0:T(8,128)(2,1)}), bf16[8,112,256]{2,1,0:T(8,128)(2,1)S(1)}, u32[]{:S(2)}, u32[]{:S(2)}) async-start(bf16[8,112,256]{2,1,0:T(8,128)(2,1)} %get-tuple-element.43), calls=%async_computation.3 | async-start | bytes 917504 | tf_op jit(solution)/shard_map/all_to_all | solution.py:473
  57.9 9.9 %collective-permute-start.3 = (bf16[128,256]{1,0:T(8,128)(2,1)S(1)}, bf16[128,256]{1,0:T(8,128)(2,1)S(1)}, u32[]{:S(2)}, u32[]{:S(2)}) collective-permute-start(bf16[128,256]{1,0:T(8,128)(2,1)S(1)} %get-tuple-element.42), channel_id=1, source_target_pairs={{8,16},{24,32},{40,48},{56,64},{72,80},{88,96},{104,112},{120,128}... | collective-permute-start | bytes 196616 | tf_op jit(solution)/shard_map/ppermute | solution.py:552
  58.5 11.5 %collective-permute-start.2 = (bf16[192,256]{1,0:T(8,128)(2,1)S(1)}, bf16[192,256]{1,0:T(8,128)(2,1)S(1)}, u32[]{:S(2)}, u32[]{:S(2)}) collective-permute-start(bf16[192,256]{1,0:T(8,128)(2,1)S(1)} %get-tuple-element.41), channel_id=1, source_target_pairs={{0,8},{8,0},{16,24},{24,16},{32,40},{40,32},{48,56},{56,48},{64,72... | collective-permute-start | bytes 294920 | tf_op jit(solution)/shard_map/ppermute | solution.py:551

commit v20 on v19

--- a/solution.py
+++ b/solution.py
@@ -23,6 +23,7 @@
 SLOT = 112
 FIRST_Z = 7
 FIRST_Y = 5
+FIRST_HEAD = 3
 
 
 def dot(a, b, dims):
@@ -99,6 +100,11 @@
         out_ref[i] = tile
 
 
+def own_slot():
+    head = lax.axis_index("head")
+    return jnp.bitwise_xor(head, FIRST_HEAD) if lax.axis_size("head") > 1 else head
+
+
 def rates(width, sum_ref):
     return lax.rsqrt(jnp.sum(sum_ref[:, :8], axis=0) / width + EPS)
 
@@ -107,7 +113,7 @@
     index = lax.axis_index("seq")
     column = jnp.bitwise_xor(jnp.right_shift(index, 3), FIRST_Y)
     odd = jnp.bitwise_and(index, 1)
-    gain = sum_ref[lax.axis_index("head"), 9:10]
+    gain = sum_ref[own_slot(), 9:10]
     kv_ref[:, :FEAT] = (
         k_ref[...].astype(F32) * spread_tokens(rates(width, sum_ref), 4) * gain
     ).astype(BF16)
@@ -217,7 +223,7 @@
 
 
 def near_kernel(width, sum_ref, q_ref, kv_ref, one_ref, g_ref, qn_ref, stat_ref):
-    gain = sum_ref[lax.axis_index("head"), 8:9]
+    gain = sum_ref[own_slot(), 8:9]
     qn_ref[...] = (
         q_ref[...].astype(F32) * spread_tokens(rates(width, sum_ref), 0) * gain
     ).astype(BF16)
@@ -376,7 +382,7 @@
     high = one_grad[...].astype(BF16)
     rest = (one_grad[...] - high.astype(F32)).astype(BF16)
     tok_ref[...] = near_grad[LEAF : LEAF + ROWS] + dot(spread, high, (1, 0)) + dot(spread, rest, (1, 0))
-    gains = sum_ref[lax.axis_index("head"), 8:16]
+    gains = sum_ref[own_slot(), 8:16]
     sums = token_sums(q_ref[...].astype(F32) * gains[0:1] * nqg_ref[...])
     qsum_ref[...] = jnp.concatenate(sums + [gains[1:2], jnp.zeros((3, FEAT), F32)], axis=0)
 
@@ -431,7 +437,7 @@
     rate = rates(width, sq_ref)
     inner = jnp.sum(inner_ref[...], axis=0) / width
     cubed = rate * rate * rate * inner
-    gains = sq_ref[lax.axis_index("head"), 8:16]
+    gains = sq_ref[own_slot(), 8:16]
     for side, (x_ref, grad_ref, out_ref) in enumerate(
         ((q_ref, nqg_ref, dq_ref), (k_ref, nkg_ref, dk_ref))
     ):
@@ -495,7 +501,8 @@
         vmem=60,
         name="squares",
     )
-    squares = exchange(squares, "head")
+    head_group = [[p ^ FIRST_HEAD for p in range(heads)]] if heads > 1 else None
+    squares = exchange(squares, "head", head_group)
     kv, one, lv, ysend, p1, p2 = call(
         lambda *refs: norm_kernel(width, *refs),
         [sds(ROWS, 256), sds(256, 256), sds(224, 256), sds(8, 16, 256), sds(192, 256), sds(LEAF, 256)],
@@ -582,8 +589,7 @@
         ],
         name="total",
     )
-    odd_first = [[p ^ 1 for p in range(heads)]] if heads > 1 else None
-    inner = exchange(inner, "head", odd_first)
+    inner = exchange(inner, "head", head_group)
     query_grad, key_grad, value_grad = call(
         lambda *refs: finish_kernel(width, *refs),
         [sds(ROWS, FEAT), sds(ROWS, FEAT), sds(ROWS, FEAT)],

time: 93.2 us -> 92.9 us (level)
  blocking collectives: 44.3 us -> 43 us
  waiting for transfers between devices: 11.1 us -> 12.2 us
    all_to_all x4, blocking collectives: 44.3 us -> 43 us  [exchange(): return lax.all_to_all(x, axis, 0, 0, axis_index_groups=groups, tiled=True)]
where the time goes in v20:
time: 92.9 us; the launch traced here: 92.3 us
  blocking collectives  43 us (46%)
  starting transfers between devices  23.1 us (25%)
  Pallas kernels  13.2 us (14%)
  waiting for transfers between devices  12.2 us (13%)
    all_to_all x4, blocking collectives, exchange(): return lax.all_to_all(x, axis, 0, 0, axis_index_groups=groups, tiled=True)  43 us
    pallas_call x9, Pallas kernels, call(): pl.pallas_call(kernel, out_shape=outs, in_specs=[pl.BlockSpec(memory_spac...  13.2 us
    all_to_all x2, starting transfers between devices, exchange(): return lax.all_to_all(x, axis, 0, 0, axis_index_groups=groups, tiled=True)  12.9 us
    ppermute x2, waiting for transfers between devices, local(): p1 = lax.ppermute(p1, 'seq', peer)  9.51 us
    ppermute x2, starting transfers between devices, local(): p1 = lax.ppermute(p1, 'seq', peer)  8.87 us
    all_to_all x2, waiting for transfers between devices, exchange(): return lax.all_to_all(x, axis, 0, 0, axis_index_groups=groups, tiled=True)  2.73 us
  transfers between devices with their start and end apart: 6, of which 3 were waited for; matrix products, arithmetic and copies ran while one was open for 0% of the time, Pallas kernels for 5%

profile of v20, /device:TPU:1, one launch (start us, length us, event | category | flops | bytes accessed | tf_op | source)
XLA Modules:
  0.0 92.3 jit_solution(11357486655969167736)
XLA Ops:
  0.6 0.0 copy-start.2
  0.6 1.9 %squares.1 = f32[8,16,128]{2,1,0:T(8,128)} custom-call(bf16[512,128]{1,0:T(8,128)(2,1)} %refs_2_.3, bf16[512,128]{1,0:T(8,128)(2,1)} %refs_3_.1, f32[1,128]{1,0:T(1,128)} %bitcast.2, f32[1,128]{1,0:T(1,128)} %bitcast.3), custom_call_target="tpu_custom_call" | custom-call | bytes 328704 | tf_op jit(solution)/shard_map/squares/pallas_call | solution.py:457
  2.5 0.0 copy-start
  2.6 14.2 %all_to_all.30.refs_0_.sum_ref = f32[8,16,128]{2,1,0:T(8,128)S(1)} all-to-all(f32[8,16,128]{2,1,0:T(8,128)} %squares.1), channel_id=1, replica_groups={{3,2,1,0,7,6,5,4},{11,10,9,8,15,14,13,12},{19,18,17,16,23,22,21,20},{27..., dimensions={0} | all-to-all | bytes 131072 | tf_op jit(solution)/shard_map/all_to_all | solution.py:479
  16.7 0.0 copy-done.2
  16.7 0.0 copy-done
  16.7 0.5 norm.1
  17.3 8.7 %all_to_all.31.y_ref = bf16[8,16,256]{2,1,0:T(8,128)(2,1)S(1)} all-to-all(bf16[8,16,256]{2,1,0:T(8,128)(2,1)S(1)} %get-tuple-element.34), channel_id=1, replica_groups={{320,256,448,384,64,0,192,128},{328,264,456,392,72,8,200,136},{336,272,..., dimensions={0} | all-to-all | bytes 131072 | tf_op jit(solution)/shard_map/all_to_all | solution.py:479
  25.9 0.9 rows.1
  26.8 0.0 copy-start.1
  26.8 0.0 copy-start.3
  26.8 8.0 %all-to-all-start.2 = ((bf16[8,112,256]{2,1,0:T(8,128)(2,1)}), bf16[8,112,256]{2,1,0:T(8,128)(2,1)S(1)}, u32[]{:S(2)}, u32[]{:S(2)}) async-start(bf16[8,112,256]{2,1,0:T(8,128)(2,1)} %rows.1), calls=%async_computation.2 | async-start | bytes 917504 | tf_op jit(solution)/shard_map/all_to_all | solution.py:479
  34.8 3.4 %collective-permute-start = (bf16[192,256]{1,0:T(8,128)(2,1)S(1)}, bf16[192,256]{1,0:T(8,128)(2,1)S(1)}, u32[]{:S(2)}, u32[]{:S(2)}) collective-permute-start(bf16[192,256]{1,0:T(8,128)(2,1)S(1)} %get-tuple-element.32), channel_id=1, source_target_pairs={{0,8},{8,0},{16,24},{24,16},{32,40},{40,32},{48,56},{56,48},{64,72... | collective-permute-start | bytes 294920 | tf_op jit(solution)/shard_map/ppermute | solution.py:512
  38.2 0.7 collective-permute-start.1
  38.9 0.0 copy-done.1
  38.9 0.9 near.1
  39.8 0.0 collective-permute-done.1.p2_ref
  39.8 7.1 %collective-permute-done.p1_ref = bf16[192,256]{1,0:T(8,128)(2,1)S(1)} collective-permute-done((bf16[192,256]{1,0:T(8,128)(2,1)S(1)}, bf16[192,256]{1,0:T(8,128)(2,1)S(1)}, u32[]{:S(2)}, u32[]{:S(2)}) %collective-permute-start) | collective-permute-done | bytes 98336 | tf_op jit(solution)/shard_map/ppermute | solution.py:512
  46.9 2.7 %all-to-all-done.2.z_ref = bf16[8,112,256]{2,1,0:T(8,128)(2,1)S(1)} async-done(((bf16[8,112,256]{2,1,0:T(8,128)(2,1)}), bf16[8,112,256]{2,1,0:T(8,128)(2,1)S(1)}, u32[]{:S(2)}, u32[]{:S(2)}) %all-to-all-start.2) | async-done | bytes 458784 | tf_op jit(solution)/shard_map/all_to_all | solution.py:479
  49.6 3.2 %attend.1 = (f32[4,8,256]{2,1,0:T(8,128)S(1)}, bf16[768,256]{1,0:T(8,128)(2,1)S(1)}, bf16[2,128,256]{2,1,0:T(8,128)(2,1)S(1)}, bf16[192,256]{1,0:T(8,128)(2,1)S(...) custom-call(bf16[512,128]{1,0:T(8,128)(2,1)S(1)} %get-tuple-element.30.qn_ref, ...), custom_call_target="tpu_custom_call" | custom-call | flops 805306368 | bytes 2097152 | tf_op jit(solution)/shard_map/attend/pallas_call | solution.py:457
  52.9 4.9 %all-to-all-start.3 = ((bf16[8,112,256]{2,1,0:T(8,128)(2,1)}), bf16[8,112,256]{2,1,0:T(8,128)(2,1)S(1)}, u32[]{:S(2)}, u32[]{:S(2)}) async-start(bf16[8,112,256]{2,1,0:T(8,128)(2,1)} %get-tuple-element.43), calls=%async_computation.3 | async-start | bytes 917504 | tf_op jit(solution)/shard_map/all_to_all | solution.py:479
  57.7 0.7 collective-permute-start.3
  58.4 5.5 %collective-permute-start.2 = (bf16[192,256]{1,0:T(8,128)(2,1)S(1)}, bf16[192,256]{1,0:T(8,128)(2,1)S(1)}, u32[]{:S(2)}, u32[]{:S(2)}) collective-permute-start(bf16[192,256]{1,0:T(8,128)(2,1)S(1)} %get-tuple-element.41), channel_id=1, source_target_pairs={{0,8},{8,0},{16,24},{24,16},{32,40},{40,32},{48,56},{56,48},{64,72... | collective-permute-start | bytes 294920 | tf_op jit(solution)/shard_map/ppermute | solution.py:558
  63.9 3.7 %after.1 = (bf16[512,128]{1,0:T(8,128)(2,1)}, f32[512,128]{1,0:T(8,128)S(1)}, f32[512,256]{1,0:T(8,128)S(1)}, f32[8,128]{1,0:T(8,128)S(1)}) custom-call(f32[4,8,256]{2,1,0:T(8,128)S(1)} %get-tuple-element.36.stat_ref, bf16[512,128]{1,0:T(8,128)(2,1)S(1)} %get-tuple-element.30.qn_ref, bf16[512,256]{1,0:T(8,128)(2,1)S(1)} %get-tuple-element.28.refs_2_.kv_ref, ...), custom_call_target="tpu_custom_call" | custom-call | flops 1677721600 | bytes 2330624 | tf_op jit(solution)/shard_map/after/pallas_call | solution.py:457
  67.6 0.0 collective-permute-done.3.p2_ref
  67.6 2.4 %collective-permute-done.2.p1_ref = bf16[192,256]{1,0:T(8,128)(2,1)S(1)} collective-permute-done((bf16[192,256]{1,0:T(8,128)(2,1)S(1)}, bf16[192,256]{1,0:T(8,128)(2,1)S(1)}, u32[]{:S(2)}, u32[]{:S(2)}) %collective-permute-start.2) | collective-permute-done | bytes 98336 | tf_op jit(solution)/shard_map/ppermute | solution.py:558
  70.1 0.0 all-to-all-done.3.z_ref
  70.1 0.2 columns.1
  70.3 9.0 %all_to_all.32.y_ref = bf16[8,16,256]{2,1,0:T(8,128)(2,1)S(1)} all-to-all(bf16[8,16,256]{2,1,0:T(8,128)(2,1)S(1)} %columns.1), channel_id=1, replica_groups={{320,256,448,384,64,0,192,128},{328,264,456,392,72,8,200,136},{336,272,..., dimensions={0} | all-to-all | bytes 131072 | tf_op jit(solution)/shard_map/all_to_all | solution.py:479
  79.2 0.8 total.1
  80.1 11.2 %all_to_all.33.refs_1_ = f32[8,8,128]{2,1,0:T(8,128)S(1)} all-to-all(f32[8,8,128]{2,1,0:T(8,128)S(1)} %get-tuple-element.45), channel_id=1, replica_groups={{3,2,1,0,7,6,5,4},{11,10,9,8,15,14,13,12},{19,18,17,16,23,22,21,20},{27..., dimensions={0} | all-to-all | bytes 65536 | tf_op jit(solution)/shard_map/all_to_all | solution.py:479
  91.3 1.0 %finish.1 = (bf16[512,128]{1,0:T(8,128)(2,1)}, bf16[512,128]{1,0:T(8,128)(2,1)}, bf16[512,128]{1,0:T(8,128)(2,1)}) custom-call(f32[8,16,128]{2,1,0:T(8,128)S(1)} %all_to_all.30.refs_0_.sum_ref, f32[8,8,128]{2,1,0:T(8,128)S(1)} %all_to_all.33.refs_1_, bf16[512,128]{1,0:T(8,128)(2,1)S(1)} %copy-done.1, bf16[512,128]{1,0:T(8,128)(2,1)S(1)} %copy-done, ...), custom_call_target="tpu_custom_call" | custom-call | bytes 1409024 | tf_op jit(solution)/shard_map/finish/pallas_call | solution.py:457
  (1 shorter events, 0.0 us)
Async XLA Ops:
  0.6 16.1 %copy-start.2 = (bf16[512,128]{1,0:T(8,128)(2,1)S(1)}, bf16[512,128]{1,0:T(8,128)(2,1)}, u32[]{:S(2)}) copy-start(bf16[512,128]{1,0:T(8,128)(2,1)} %refs_2_.2) | copy-start | bytes 393220
  2.5 14.2 %copy-start = (bf16[512,128]{1,0:T(8,128)(2,1)S(1)}, bf16[512,128]{1,0:T(8,128)(2,1)}, u32[]{:S(2)}) copy-start(bf16[512,128]{1,0:T(8,128)(2,1)} %refs_3_.1) | copy-start | bytes 393220
  26.8 12.1 %copy-start.1 = (bf16[512,128]{1,0:T(8,128)(2,1)S(1)}, bf16[512,128]{1,0:T(8,128)(2,1)}, u32[]{:S(2)}) copy-start(bf16[512,128]{1,0:T(8,128)(2,1)} %refs_2_.3) | copy-start | bytes 393220
  26.8 12.1 %copy-start.3 = (bf16[512,128]{1,0:T(8,128)(2,1)S(1)}, bf16[512,128]{1,0:T(8,128)(2,1)}, u32[]{:S(2)}) copy-start(bf16[512,128]{1,0:T(8,128)(2,1)} %g_ref.3) | copy-start | bytes 393220
  26.8 22.8 %all-to-all-start.2 = ((bf16[8,112,256]{2,1,0:T(8,128)(2,1)}), bf16[8,112,256]{2,1,0:T(8,128)(2,1)S(1)}, u32[]{:S(2)}, u32[]{:S(2)}) async-start(bf16[8,112,256]{2,1,0:T(8,128)(2,1)} %rows.1), calls=%async_computation.2 | async-start | bytes 917504 | tf_op jit(solution)/shard_map/all_to_all | solution.py:479
  34.8 12.1 %collective-permute-start = (bf16[192,256]{1,0:T(8,128)(2,1)S(1)}, bf16[192,256]{1,0:T(8,128)(2,1)S(1)}, u32[]{:S(2)}, u32[]{:S(2)}) collective-permute-start(bf16[192,256]{1,0:T(8,128)(2,1)S(1)} %get-tuple-element.32), channel_id=1, source_target_pairs={{0,8},{8,0},{16,24},{24,16},{32,40},{40,32},{48,56},{56,48},{64,72... | collective-permute-start | bytes 294920 | tf_op jit(solution)/shard_map/ppermute | solution.py:512
  38.2 1.6 %collective-permute-start.1 = (bf16[128,256]{1,0:T(8,128)(2,1)S(1)}, bf16[128,256]{1,0:T(8,128)(2,1)S(1)}, u32[]{:S(2)}, u32[]{:S(2)}) collective-permute-start(bf16[128,256]{1,0:T(8,128)(2,1)S(1)} %get-tuple-element.33), channel_id=1, source_target_pairs={{8,16},{24,32},{40,48},{56,64},{72,80},{88,96},{104,112},{120,128}... | collective-permute-start | bytes 196616 | tf_op jit(solution)/shard_map/ppermute | solution.py:513
  52.9 17.2 %all-to-all-start.3 = ((bf16[8,112,256]{2,1,0:T(8,128)(2,1)}), bf16[8,112,256]{2,1,0:T(8,128)(2,1)S(1)}, u32[]{:S(2)}, u32[]{:S(2)}) async-start(bf16[8,112,256]{2,1,0:T(8,128)(2,1)} %get-tuple-element.43), calls=%async_computation.3 | async-start | bytes 917504 | tf_op jit(solution)/shard_map/all_to_all | solution.py:479
  57.7 9.9 %collective-permute-start.3 = (bf16[128,256]{1,0:T(8,128)(2,1)S(1)}, bf16[128,256]{1,0:T(8,128)(2,1)S(1)}, u32[]{:S(2)}, u32[]{:S(2)}) collective-permute-start(bf16[128,256]{1,0:T(8,128)(2,1)S(1)} %get-tuple-element.42), channel_id=1, source_target_pairs={{8,16},{24,32},{40,48},{56,64},{72,80},{88,96},{104,112},{120,128}... | collective-permute-start | bytes 196616 | tf_op jit(solution)/shard_map/ppermute | solution.py:559
  58.4 11.7 %collective-permute-start.2 = (bf16[192,256]{1,0:T(8,128)(2,1)S(1)}, bf16[192,256]{1,0:T(8,128)(2,1)S(1)}, u32[]{:S(2)}, u32[]{:S(2)}) collective-permute-start(bf16[192,256]{1,0:T(8,128)(2,1)S(1)} %get-tuple-element.41), channel_id=1, source_target_pairs={{0,8},{8,0},{16,24},{24,16},{32,40},{40,32},{48,56},{56,48},{64,72... | collective-permute-start | bytes 294920 | tf_op jit(solution)/shard_map/ppermute | solution.py:558
